TPU v7x, 32 devices: a whole 2x2x4 slice. The times are simulated.
32 devices in a mesh: experts: 4 (over y, x), context: 2 (over core), dp: 4 (over z).
Axes of the slice: x: 2, y: 2, z: 4, core: 2. Of those that a mesh axis runs over, the one named last changes fastest.
Arguments:
- hidden: bfloat16 [16, 1024, 2048], P(('experts', 'dp'), 'context'), may hold values from -6 to 6
- cotangent: bfloat16 [16, 1024, 2048], P(('experts', 'dp'), 'context'), may hold values from -6 to 6
- segments: int32 [16, 1024], P(('experts', 'dp'), 'context'), may hold values from 0 to 1023, as said below
- padding: int32 [16, 1024], P(('experts', 'dp'), 'context'), may hold values 0 or 1
- routes: int32 [16, 1024, 4], P(('experts', 'dp'), 'context'), may hold values from 0 to 7, all different within a row
- order: int32 [16, 2, 512], P(('experts', 'dp'), 'context'), may hold values from 0 to 511, each once within a row
- norm1_gain: bfloat16 [2048], P('dp'), may hold values from 0.5 to 1.5
- w_query: bfloat16 [2048, 2048], P('dp'), may hold values from -0.125 to 0.125
- w_key: bfloat16 [2048, 2048], P('dp'), may hold values from -0.125 to 0.125
- w_value: bfloat16 [2048, 2048], P('dp'), may hold values from -0.125 to 0.125
- w_out: bfloat16 [2048, 2048], P('dp'), may hold values from -1 to 1
- norm2_gain: bfloat16 [2048], P('dp'), may hold values from 0.5 to 1.5
- router: bfloat16 [2048, 8], P('dp'), may hold values from -0.0625 to 0.0625
- shared_gate_vec: bfloat16 [2048], P('dp'), may hold values from -0.125 to 0.125
- shared_w_gate: bfloat16 [2048, 5632], P('dp', 'experts'), may hold values from -0.125 to 0.125
- shared_w_up: bfloat16 [2048, 5632], P('dp', 'experts'), may hold values from -0.125 to 0.125
- shared_w_down: bfloat16 [5632, 2048], P(('experts', 'dp')), may hold values from -0.15625 to 0.15625
- expert_w_gate: bfloat16 [8, 2048, 1408], P(('experts', 'context'), 'dp'), may hold values from -0.125 to 0.125
- expert_w_up: bfloat16 [8, 2048, 1408], P(('experts', 'context'), 'dp'), may hold values from -0.125 to 0.125
- expert_w_down: bfloat16 [8, 1408, 2048], P(('experts', 'context'), None, 'dp'), may hold values from -0.625 to 0.625
Outputs:
- output: bfloat16 [16, 1024, 2048], P(('experts', 'dp'), 'context')
- input_grad: bfloat16 [16, 1024, 2048], P(('experts', 'dp'), 'context')
- grad_norm1_gain: float32 [2048], P(('experts', 'context', 'dp'))
- grad_w_query: float32 [2048, 2048], P(('experts', 'context', 'dp'))
- grad_w_key: float32 [2048, 2048], P(('experts', 'context', 'dp'))
- grad_w_value: float32 [2048, 2048], P(('experts', 'context', 'dp'))
- grad_w_out: float32 [2048, 2048], P(('experts', 'context', 'dp'))
- grad_norm2_gain: float32 [2048], P(('experts', 'context', 'dp'))
- grad_router: float32 [2048, 8], P(('experts', 'context', 'dp'))
- grad_shared_gate_vec: float32 [2048], P(('experts', 'context', 'dp'))
- grad_shared_w_gate: float32 [2048, 5632], P(('context', 'dp'), 'experts')
- grad_shared_w_up: float32 [2048, 5632], P(('context', 'dp'), 'experts')
- grad_shared_w_down: float32 [5632, 2048], P('experts', ('context', 'dp'))
- grad_expert_w_gate: float32 [8, 2048, 1408], P(('experts', 'context'), 'dp')
- grad_expert_w_up: float32 [8, 2048, 1408], P(('experts', 'context'), 'dp')
- grad_expert_w_down: float32 [8, 1408, 2048], P(('experts', 'context'), None, 'dp')
Inputs may be any that keep to these rules, and one draw needn't show every extreme that they name: `segments`: along a sequence segment numbers never fall; the last token of every sequence has number 1024 - 1. `routes`: each token names 4 different experts. `order`: each row is a permutation of the 512 ranks of a block.
All inputs are finite; a program needn't handle non-finite values. No bound on the sum of `padding` on one device may be relied on, other than what follows from the above.
Results may differ from a plain program's by a relative error of at most 0.015.
Values may be sent and summed in bfloat16 or wider, within the bound.
A program may use at most 576 MiB of HBM per device.

v0:
```python
from functools import partial

import jax
import jax.numpy as jnp
from jax import lax
from jax.sharding import PartitionSpec as P

HEADS = 16
HEAD_DIM = 128
TOP = 4


EPS = 1e-06
NEG = -1e30


def silu_grad(pre_act):
    logistic = jax.nn.sigmoid(pre_act)
    return logistic * (1.0 + pre_act * (1.0 - logistic))


def block_slots(route_row, priority, expert_count):
    matches = (route_row[:, None] == jnp.arange(expert_count, dtype=jnp.int32)[None, :]).astype(
        jnp.int32
    )
    ordered = jnp.zeros_like(matches).at[priority].set(matches)
    before = jnp.cumsum(ordered, axis=0) - ordered
    return jnp.sum(before[priority] * matches, axis=1)


def norm_back(values_in, inv_rms, gain_vec, gradient):
    weighted = gradient * gain_vec
    inner_sum = jnp.mean(weighted * values_in, axis=1, keepdims=True)
    d_value = inv_rms * weighted - values_in * inv_rms**3 * inner_sum
    d_gain = jnp.sum(gradient * values_in * inv_rms, axis=0)
    return (d_value, d_gain)


def attend_head(packed, allowed, scale_factor):
    query_h, key_h, value_h = packed
    raw_scores = jnp.einsum("th,lh->tl", query_h, key_h, preferred_element_type=jnp.float32)
    logits = jnp.where(allowed, raw_scores * scale_factor, NEG)
    row_max = jnp.max(logits, axis=1, keepdims=True)
    exp_scores = jnp.exp(logits - row_max)
    row_total = jnp.sum(exp_scores, axis=1, keepdims=True)
    attn_probs = (exp_scores / row_total).astype(jnp.bfloat16)
    head_out = jnp.dot(attn_probs, value_h, preferred_element_type=jnp.float32).astype(jnp.bfloat16)
    return (head_out, row_max + jnp.log(row_total))


def attend_back(packed, allowed, scale_factor):
    query_h, key_h, value_h, out_grad, log_total = packed
    raw_scores = jnp.einsum("th,lh->tl", query_h, key_h, preferred_element_type=jnp.float32)
    logits = jnp.where(allowed, raw_scores * scale_factor, NEG)
    attn_probs = jnp.exp(logits - log_total)
    prob_grad = jnp.einsum("th,lh->tl", out_grad, value_h, preferred_element_type=jnp.float32)
    inner_sum = jnp.sum(attn_probs * prob_grad, axis=1, keepdims=True)
    score_grad = (attn_probs * (prob_grad - inner_sum) * scale_factor).astype(jnp.bfloat16)
    query_grad = jnp.dot(score_grad, key_h, preferred_element_type=jnp.float32)
    key_grad = jnp.einsum("tl,th->lh", score_grad, query_h, preferred_element_type=jnp.float32)
    value_grad = jnp.einsum(
        "tl,th->lh", attn_probs.astype(jnp.bfloat16), out_grad, preferred_element_type=jnp.float32
    )
    return (query_grad, key_grad, value_grad)


def local(
    hidden,
    cotangent,
    segments,
    padding,
    routes,
    order,
    norm1_gain,
    w_query,
    w_key,
    w_value,
    w_out,
    norm2_gain,
    router,
    shared_gate_vec,
    shared_w_gate,
    shared_w_up,
    shared_w_down,
    expert_w_gate,
    expert_w_up,
    expert_w_down,
):
    fetched = (
        lax.all_gather(norm1_gain, "dp", axis=0, tiled=True),
        lax.all_gather(w_query, "dp", axis=0, tiled=True),
        lax.all_gather(w_key, "dp", axis=0, tiled=True),
        lax.all_gather(w_value, "dp", axis=0, tiled=True),
        lax.all_gather(w_out, "dp", axis=0, tiled=True),
        lax.all_gather(norm2_gain, "dp", axis=0, tiled=True),
        lax.all_gather(router, "dp", axis=0, tiled=True),
        lax.all_gather(shared_gate_vec, "dp", axis=0, tiled=True),
        lax.all_gather(shared_w_gate, "dp", axis=0, tiled=True),
        lax.all_gather(shared_w_up, "dp", axis=0, tiled=True),
        lax.all_gather(shared_w_down, "dp", axis=0, tiled=True),
        lax.all_gather(expert_w_gate, "dp", axis=1, tiled=True),
        lax.all_gather(expert_w_up, "dp", axis=1, tiled=True),
        lax.all_gather(expert_w_down, "dp", axis=2, tiled=True),
    )
    (
        gain_one,
        query_w,
        key_w,
        value_w,
        out_w,
        gain_two,
        router_full,
        gate_vec,
        sh_gate,
        sh_up,
        sh_down,
        ex_gate,
        ex_up,
        ex_down,
    ) = fetched
    sh_gate, sh_up, sh_down = (
        lax.all_gather(sh_gate, "experts", axis=1, tiled=True),
        lax.all_gather(sh_up, "experts", axis=1, tiled=True),
        lax.all_gather(sh_down, "experts", axis=0, tiled=True),
    )
    tokens_here = hidden.shape[1]
    model_width = hidden.shape[2]
    x_rows = hidden[0].astype(jnp.float32)
    cot_rows = cotangent[0].astype(jnp.float32)
    inv_one = lax.rsqrt(jnp.mean(x_rows * x_rows, axis=1, keepdims=True) + EPS)
    g_one = gain_one.astype(jnp.float32)
    normed_one = (x_rows * inv_one * g_one).astype(jnp.bfloat16)
    queries = jnp.dot(normed_one, query_w, preferred_element_type=jnp.float32).astype(jnp.bfloat16)
    keys_own = jnp.dot(normed_one, key_w, preferred_element_type=jnp.float32).astype(jnp.bfloat16)
    values_own = jnp.dot(normed_one, value_w, preferred_element_type=jnp.float32).astype(
        jnp.bfloat16
    )
    own_codes = jnp.where(padding[0] > 0, segments[0] + 1, 0)
    code_parts = jnp.stack([own_codes // 64, own_codes % 64]).astype(jnp.bfloat16)
    keys_all, values_all, parts_all = (
        lax.all_gather(keys_own, "context", axis=0, tiled=True),
        lax.all_gather(values_own, "context", axis=0, tiled=True),
        lax.all_gather(code_parts, "context", axis=1, tiled=True),
    )
    key_codes = parts_all[0].astype(jnp.int32) * 64 + parts_all[1].astype(jnp.int32)
    seq_total = keys_all.shape[0]
    query_pos = lax.axis_index("context") * tokens_here + jnp.arange(tokens_here, dtype=jnp.int32)
    key_pos = jnp.arange(seq_total, dtype=jnp.int32)
    same_doc = key_codes[None, :] == (segments[0] + 1)[:, None]
    allowed = (key_pos[None, :] <= query_pos[:, None]) & (
        same_doc | (key_pos[None, :] == query_pos[:, None])
    )
    scale_factor = HEAD_DIM ** (-0.5)

    def to_heads(rows_in):
        return rows_in.reshape(rows_in.shape[0], HEADS, HEAD_DIM).transpose(1, 0, 2)

    def from_heads(heads_in):
        return heads_in.transpose(1, 0, 2).reshape(heads_in.shape[1], model_width)

    head_q = to_heads(queries)
    head_k = to_heads(keys_all)
    head_v = to_heads(values_all)
    head_out, log_total = lax.map(
        partial(attend_head, allowed=allowed, scale_factor=scale_factor), (head_q, head_k, head_v)
    )
    attended = from_heads(head_out)
    residual = x_rows + jnp.dot(attended, out_w, preferred_element_type=jnp.float32)
    inv_two = lax.rsqrt(jnp.mean(residual * residual, axis=1, keepdims=True) + EPS)
    g_two = gain_two.astype(jnp.float32)
    normed_two = (residual * inv_two * g_two).astype(jnp.bfloat16)
    router_logits = jnp.dot(normed_two, router_full, preferred_element_type=jnp.float32)
    router_exp = jnp.exp(router_logits - jnp.max(router_logits, axis=1, keepdims=True))
    router_probs = router_exp / jnp.sum(router_exp, axis=1, keepdims=True)
    route_gates = jnp.take_along_axis(router_probs, routes[0], axis=1)
    shared_gate = jax.nn.sigmoid(jnp.dot(normed_two, gate_vec, preferred_element_type=jnp.float32))
    shared_scaled = (shared_gate[:, None] * cot_rows).astype(jnp.bfloat16)
    rows_group, grads_group = (normed_two, shared_scaled)
    gate_pre = jnp.dot(rows_group, sh_gate, preferred_element_type=jnp.float32)
    up_pre = jnp.dot(rows_group, sh_up, preferred_element_type=jnp.float32)
    gate_act = gate_pre * jax.nn.sigmoid(gate_pre)
    shared_hidden = (gate_act * up_pre).astype(jnp.bfloat16)
    shared_part = jnp.dot(shared_hidden, sh_down, preferred_element_type=jnp.float32)
    experts_all = router_full.shape[1]
    capacity = (9 * tokens_here * TOP + 8 * experts_all - 1) // (8 * experts_all)
    priority = (order[0, 0][:, None] * TOP + jnp.arange(TOP, dtype=jnp.int32)[None, :]).reshape(-1)
    flat_routes = routes[0].reshape(-1)
    slot_index = block_slots(flat_routes, priority, experts_all)
    kept_rows = slot_index < capacity
    target = flat_routes * capacity + jnp.minimum(slot_index, capacity - 1)
    row_gates = route_gates.reshape(-1)
    cot_repeated = jnp.repeat(cot_rows, TOP, axis=0)
    source_rows = jnp.repeat(normed_two, TOP, axis=0)
    source_grads = (cot_repeated * row_gates[:, None]).astype(jnp.bfloat16)
    empty_slots = jnp.zeros((experts_all * capacity, model_width), jnp.bfloat16)
    send_rows = empty_slots.at[target].add(
        jnp.where(kept_rows[:, None], source_rows, jnp.zeros_like(source_rows))
    )
    send_grads = empty_slots.at[target].add(
        jnp.where(kept_rows[:, None], source_grads, jnp.zeros_like(source_grads))
    )
    recv_rows, recv_grads = (
        lax.all_to_all(
            send_rows.reshape(experts_all, capacity, model_width),
            ("experts", "context"),
            split_axis=0,
            concat_axis=0,
            tiled=True,
        ),
        lax.all_to_all(
            send_grads.reshape(experts_all, capacity, model_width),
            ("experts", "context"),
            split_axis=0,
            concat_axis=0,
            tiled=True,
        ),
    )
    local_count = ex_gate.shape[0]
    sources = experts_all // local_count

    def to_local(buffer_in):
        return (
            buffer_in.reshape(sources, local_count, capacity, model_width)
            .transpose(1, 0, 2, 3)
            .reshape(local_count, sources * capacity, model_width)
        )

    def to_owner(buffer_in):
        return (
            buffer_in.reshape(local_count, sources, capacity, model_width)
            .transpose(1, 0, 2, 3)
            .reshape(experts_all, capacity, model_width)
        )

    expert_rows = to_local(recv_rows)
    expert_grads_in = to_local(recv_grads)
    gate_e = jnp.einsum("erd,edf->erf", expert_rows, ex_gate, preferred_element_type=jnp.float32)
    up_e = jnp.einsum("erd,edf->erf", expert_rows, ex_up, preferred_element_type=jnp.float32)
    act_e = gate_e * jax.nn.sigmoid(gate_e)
    hidden_e = (act_e * up_e).astype(jnp.bfloat16)
    result_e = jnp.einsum(
        "erf,efd->erd", hidden_e, ex_down, preferred_element_type=jnp.float32
    ).astype(jnp.bfloat16)
    returned = lax.all_to_all(
        to_owner(result_e), ("experts", "context"), split_axis=0, concat_axis=0, tiled=True
    )
    picked = returned.reshape(experts_all * capacity, model_width)[target]
    picked = jnp.where(kept_rows[:, None], picked, jnp.zeros_like(picked)).astype(jnp.float32)
    routed = jnp.sum((picked * row_gates[:, None]).reshape(tokens_here, TOP, model_width), axis=1)
    output = (residual + shared_gate[:, None] * shared_part + routed).astype(jnp.bfloat16)
    gate_grads = jnp.sum(picked * cot_repeated, axis=1).reshape(tokens_here, TOP)
    hidden_grad_e = jnp.einsum(
        "erd,efd->erf", expert_grads_in, ex_down, preferred_element_type=jnp.float32
    )
    gate_grad_e = (hidden_grad_e * up_e * silu_grad(gate_e)).astype(jnp.bfloat16)
    up_grad_e = (hidden_grad_e * act_e).astype(jnp.bfloat16)
    grad_ex_down = jnp.einsum(
        "erf,erd->efd", hidden_e, expert_grads_in, preferred_element_type=jnp.float32
    )
    grad_ex_gate = jnp.einsum(
        "erd,erf->edf", expert_rows, gate_grad_e, preferred_element_type=jnp.float32
    )
    grad_ex_up = jnp.einsum(
        "erd,erf->edf", expert_rows, up_grad_e, preferred_element_type=jnp.float32
    )
    expert_sums = (
        lax.psum_scatter(grad_ex_gate, "dp", scatter_dimension=1, tiled=True),
        lax.psum_scatter(grad_ex_up, "dp", scatter_dimension=1, tiled=True),
        lax.psum_scatter(grad_ex_down, "dp", scatter_dimension=2, tiled=True),
    )
    rows_grad_e = jnp.einsum(
        "erf,edf->erd", gate_grad_e, ex_gate, preferred_element_type=jnp.float32
    )
    rows_grad_e = (
        rows_grad_e
        + jnp.einsum("erf,edf->erd", up_grad_e, ex_up, preferred_element_type=jnp.float32)
    ).astype(jnp.bfloat16)
    returned_grads = lax.all_to_all(
        to_owner(rows_grad_e), ("experts", "context"), split_axis=0, concat_axis=0, tiled=True
    )
    routed_grad = returned_grads.reshape(experts_all * capacity, model_width)[target]
    routed_grad = jnp.where(kept_rows[:, None], routed_grad, jnp.zeros_like(routed_grad)).astype(
        jnp.float32
    )
    norm_grad = jnp.sum(routed_grad.reshape(tokens_here, TOP, model_width), axis=1)
    choose = (
        routes[0][:, :, None] == jnp.arange(experts_all, dtype=jnp.int32)[None, None, :]
    ).astype(jnp.float32)
    probs_grad = jnp.einsum("tk,tke->te", gate_grads, choose)
    logit_grad = (
        router_probs * (probs_grad - jnp.sum(router_probs * probs_grad, axis=1, keepdims=True))
    ).astype(jnp.bfloat16)
    grad_router = jnp.dot(normed_two.T, logit_grad, preferred_element_type=jnp.float32)
    gate_logit_grad = (
        jnp.sum(cot_rows * shared_part, axis=1) * shared_gate * (1.0 - shared_gate)
    ).astype(jnp.bfloat16)
    grad_gate_vec = jnp.dot(gate_logit_grad, normed_two, preferred_element_type=jnp.float32)
    norm_grad = norm_grad + jnp.dot(logit_grad, router_full.T, preferred_element_type=jnp.float32)
    norm_grad = (
        norm_grad
        + gate_logit_grad.astype(jnp.float32)[:, None] * gate_vec.astype(jnp.float32)[None, :]
    )
    shared_hgrad = jnp.dot(grads_group, sh_down.T, preferred_element_type=jnp.float32)
    gate_grad_s = (shared_hgrad * up_pre * silu_grad(gate_pre)).astype(jnp.bfloat16)
    up_grad_s = (shared_hgrad * gate_act).astype(jnp.bfloat16)
    shared_rows_grad = jnp.dot(gate_grad_s, sh_gate.T, preferred_element_type=jnp.float32)
    shared_rows_grad = shared_rows_grad + jnp.dot(
        up_grad_s, sh_up.T, preferred_element_type=jnp.float32
    )
    groups = lax.axis_size("experts")
    parts_cd = lax.axis_size(("context", "dp"))
    rows_count = rows_group.shape[0]
    arr_gate = jnp.einsum(
        "td,tes->eds",
        rows_group,
        gate_grad_s.reshape(rows_count, groups, -1),
        preferred_element_type=jnp.float32,
    ).reshape(groups * model_width, -1)
    arr_up = jnp.einsum(
        "td,tes->eds",
        rows_group,
        up_grad_s.reshape(rows_count, groups, -1),
        preferred_element_type=jnp.float32,
    ).reshape(groups * model_width, -1)
    arr_down = jnp.einsum(
        "tes,tcd->ecsd",
        shared_hidden.reshape(rows_count, groups, -1),
        grads_group.reshape(rows_count, parts_cd, -1),
        preferred_element_type=jnp.float32,
    ).reshape(-1, model_width // parts_cd)
    sums_gate, sums_up, sums_down = (
        lax.psum_scatter(arr_gate, ("experts", "context", "dp"), scatter_dimension=0, tiled=True),
        lax.psum_scatter(arr_up, ("experts", "context", "dp"), scatter_dimension=0, tiled=True),
        lax.psum_scatter(arr_down, ("experts", "context", "dp"), scatter_dimension=0, tiled=True),
    )
    norm_grad = norm_grad + shared_rows_grad
    residual_grad, grad_gain_two = norm_back(residual, inv_two, g_two, norm_grad)
    residual_grad = residual_grad + cot_rows
    low_residual = residual_grad.astype(jnp.bfloat16)
    grad_out_w = jnp.dot(attended.T, low_residual, preferred_element_type=jnp.float32)
    attended_grad = jnp.dot(low_residual, out_w.T, preferred_element_type=jnp.float32).astype(
        jnp.bfloat16
    )
    head_q_grad, head_k_grad, head_v_grad = lax.map(
        partial(attend_back, allowed=allowed, scale_factor=scale_factor),
        (head_q, head_k, head_v, to_heads(attended_grad), log_total),
    )
    key_sum, value_sum = (
        lax.psum_scatter(from_heads(head_k_grad), "context", scatter_dimension=0, tiled=True),
        lax.psum_scatter(from_heads(head_v_grad), "context", scatter_dimension=0, tiled=True),
    )
    query_low = from_heads(head_q_grad).astype(jnp.bfloat16)
    key_low = key_sum.astype(jnp.bfloat16)
    value_low = value_sum.astype(jnp.bfloat16)
    grad_query = jnp.dot(normed_one.T, query_low, preferred_element_type=jnp.float32)
    grad_key = jnp.dot(normed_one.T, key_low, preferred_element_type=jnp.float32)
    grad_value = jnp.dot(normed_one.T, value_low, preferred_element_type=jnp.float32)
    normed_grad = jnp.dot(query_low, query_w.T, preferred_element_type=jnp.float32)
    normed_grad = normed_grad + jnp.dot(key_low, key_w.T, preferred_element_type=jnp.float32)
    normed_grad = normed_grad + jnp.dot(value_low, value_w.T, preferred_element_type=jnp.float32)
    input_part, grad_gain_one = norm_back(x_rows, inv_one, g_one, normed_grad)
    input_grad = (residual_grad + input_part).astype(jnp.bfloat16)
    dense = (
        lax.psum_scatter(
            grad_gain_one, ("experts", "context", "dp"), scatter_dimension=0, tiled=True
        ),
        lax.psum_scatter(grad_query, ("experts", "context", "dp"), scatter_dimension=0, tiled=True),
        lax.psum_scatter(grad_key, ("experts", "context", "dp"), scatter_dimension=0, tiled=True),
        lax.psum_scatter(grad_value, ("experts", "context", "dp"), scatter_dimension=0, tiled=True),
        lax.psum_scatter(grad_out_w, ("experts", "context", "dp"), scatter_dimension=0, tiled=True),
        lax.psum_scatter(
            grad_gain_two, ("experts", "context", "dp"), scatter_dimension=0, tiled=True
        ),
        lax.psum_scatter(
            grad_router, ("experts", "context", "dp"), scatter_dimension=0, tiled=True
        ),
        lax.psum_scatter(
            grad_gate_vec, ("experts", "context", "dp"), scatter_dimension=0, tiled=True
        ),
    )
    return (
        output[None],
        input_grad[None],
        dense[0],
        dense[1],
        dense[2],
        dense[3],
        dense[4],
        dense[5],
        dense[6],
        dense[7],
        sums_gate,
        sums_up,
        sums_down,
        expert_sums[0],
        expert_sums[1],
        expert_sums[2],
    )


def solution(mesh):
    in_specs = (
        P(("experts", "dp"), "context", None),
        P(("experts", "dp"), "context", None),
        P(("experts", "dp"), "context"),
        P(("experts", "dp"), "context"),
        P(("experts", "dp"), "context", None),
        P(("experts", "dp"), "context", None),
        P("dp"),
        P("dp", None),
        P("dp", None),
        P("dp", None),
        P("dp", None),
        P("dp"),
        P("dp", None),
        P("dp"),
        P("dp", "experts"),
        P("dp", "experts"),
        P(("experts", "dp"), None),
        P(("experts", "context"), "dp", None),
        P(("experts", "context"), "dp", None),
        P(("experts", "context"), None, "dp"),
    )
    out_specs = (
        P(("experts", "dp"), "context", None),
        P(("experts", "dp"), "context", None),
        P(("experts", "context", "dp")),
        P(("experts", "context", "dp"), None),
        P(("experts", "context", "dp"), None),
        P(("experts", "context", "dp"), None),
        P(("experts", "context", "dp"), None),
        P(("experts", "context", "dp")),
        P(("experts", "context", "dp"), None),
        P(("experts", "context", "dp")),
        P(("context", "dp"), "experts"),
        P(("context", "dp"), "experts"),
        P("experts", ("context", "dp")),
        P(("experts", "context"), "dp", None),
        P(("experts", "context"), "dp", None),
        P(("experts", "context"), None, "dp"),
    )
    return jax.shard_map(local, mesh=mesh, in_specs=in_specs, out_specs=out_specs, check_vma=False)
```

profile of v0, /device:TPU:0, one launch (start us, length us, event | category | flops | bytes accessed | tf_op | source)
XLA Modules:
  0.0 7616.5 jit_solution(16089052434070606743)
XLA Ops:
  25.3 136.7 %all-gather.21.cloned.1.call-done = bf16[2048,2048]{1,0:T(8,128)(2,1)} async-done(((bf16[512,2048]{1,0:T(8,128)(2,1)}), bf16[2048,2048]{1,0:T(8,128)(2,1)}) %all-gather.21.cloned.1.call-update) | async-done | bytes 8388624 | tf_op jit(solution)/shard_map/all_gather | solution.py:92
  171.3 140.2 %all-gather.25.cloned.1.call-done = bf16[2048,2048]{1,0:T(8,128)(2,1)} async-done(((bf16[512,2048]{1,0:T(8,128)(2,1)}), bf16[2048,2048]{1,0:T(8,128)(2,1)}) %all-gather.25.cloned.1.call-update) | async-done | bytes 8388624 | tf_op jit(solution)/shard_map/all_gather | solution.py:93
  324.1 93.9 %all-gather.31.cloned.1.call-done = bf16[2048,1408]{1,0:T(8,128)(2,1)} async-done(((bf16[512,1408]{1,0:T(8,128)(2,1)}), bf16[2048,1408]{1,0:T(8,128)(2,1)}) %all-gather.31.cloned.1.call-update) | async-done | bytes 5767184 | tf_op jit(solution)/shard_map/all_gather | solution.py:98
  450.0 74.5 all-gather.35.cloned.1.call-done
  524.5 149.4 %all-gather.19.cloned.1.call-done = bf16[2048,2048]{1,0:T(8,128)(2,1)} async-done(((bf16[512,2048]{1,0:T(8,128)(2,1)}), bf16[2048,2048]{1,0:T(8,128)(2,1)}) %all-gather.19.cloned.1.call-update) | async-done | bytes 8388624 | tf_op jit(solution)/shard_map/all_gather | solution.py:91
  710.0 85.1 %while.28 = (s32[]{:T(128)}, bf16[16,512,128]{1,2,0:T(8,128)(2,1)}, f32[16,512,1]{1,2,0:T(1,128)}, bf16[16,512,128]{2,1,0:T(8,128)(2,1)}, bf16[16,1024,128]{2,1,...) while((s32[]{:T(128)}, bf16[16,512,128]{1,2,0:T(8,128)(2,1)}, ...), condition=%wide.region_4.5_spmd.clone, body=%wide.region_1.4_spmd.clone.sunk | while | flops 275316224 | bytes 7631993 | solution.py:164
  795.1 62.1 all-gather.29.cloned.1.call-done
  963.7 67.8 all-to-all-done
  1093.4 83.4 %all-gather.47.cloned.1.call-done = bf16[1,1408,2048]{2,1,0:T(8,128)(2,1)} async-done(((bf16[1,1408,512]{2,1,0:T(8,128)(2,1)}), bf16[1,1408,2048]{2,1,0:T(8,128)(2,1)}) %all-gather.47.cloned.1.call-update) | async-done | bytes 5767184 | tf_op jit(solution)/shard_map/all_gather | solution.py:103
  1202.1 81.2 %all-gather.39.cloned.1.call-done = bf16[1408,2048]{1,0:T(8,128)(2,1)} async-done(((bf16[352,2048]{1,0:T(8,128)(2,1)}), bf16[1408,2048]{1,0:T(8,128)(2,1)}) %all-gather.39.cloned.1.call-update) | async-done | bytes 5767184 | tf_op jit(solution)/shard_map/all_gather | solution.py:100
  1445.3 153.7 %all-to-all-done.2 = bf16[8,288,2048]{2,1,0:T(8,128)(2,1)} async-done(((bf16[8,288,2048]{2,1,0:T(8,128)(2,1)}), bf16[8,288,2048]{2,1,0:T(8,128)(2,1)}, u32[]{:S(2)}, u32[]{:S(2)}) %all-to-all-start.2) | async-done | bytes 9437216 | tf_op jit(solution)/shard_map/all_to_all | solution.py:210
  1697.4 209.0 %all-gather.37.cloned.1.call-done = bf16[2048,5632]{1,0:T(8,128)(2,1)} async-done(((bf16[2048,1408]{1,0:T(8,128)(2,1)}), bf16[2048,5632]{1,0:T(8,128)(2,1)}) %all-gather.37.cloned.1.call-update) | async-done | bytes 23068688 | tf_op jit(solution)/shard_map/all_gather | solution.py:123
  1932.9 185.7 %all-gather.41.cloned.1.call-done = bf16[5632,2048]{1,0:T(8,128)(2,1)} async-done(((bf16[1408,2048]{1,0:T(8,128)(2,1)}), bf16[5632,2048]{1,0:T(8,128)(2,1)}) %all-gather.41.cloned.1.call-update) | async-done | bytes 23068688 | tf_op jit(solution)/shard_map/all_gather | solution.py:124
  2292.9 158.4 %while.29 = (s32[]{:T(128)}, bf16[16,512,128]{1,2,0:T(8,128)(2,1)}, f32[16,1024,128]{1,2,0:T(8,128)}, f32[16,1024,128]{1,2,0:T(8,128)}, bf16[16,512,128]{2,1,0:T...) while((s32[]{:T(128)}, bf16[16,512,128]{1,2,0:T(8,128)(2,1)}, ...), condition=%wide.region_22.23_spmd.clone, body=%wide.region_20.22_spmd.clone.sunk | while | flops 678952448 | bytes 18373768 | solution.py:344
  2676.4 46.4 copy.86
  2889.8 132.2 %reduce-scatter.36.cloned.1.call-done = f32[1,512,1408]{2,1,0:T(8,128)} async-done(((f32[1,2048,1408]{2,1,0:T(8,128)}), f32[1,512,1408]{2,1,0:T(8,128)}) %reduce-scatter.36.cloned.1.call-update) | async-done | bytes 2883600 | tf_op jit(solution)/shard_map/reduce_scatter | solution.py:268
  3021.9 199.1 %reduce-scatter.38.cloned.1.call-done = f32[1,1408,512]{2,1,0:T(8,128)} async-done(((f32[1,1408,2048]{2,1,0:T(8,128)}), f32[1,1408,512]{2,1,0:T(8,128)}) %reduce-scatter.38.cloned.1.call-update) | async-done | bytes 2883600 | tf_op jit(solution)/shard_map/reduce_scatter | solution.py:269
  3221.0 368.3 %reduce-scatter.20.cloned.1.call-done = f32[64,2048]{1,0:T(8,128)} async-done(((f32[2048,2048]{1,0:T(8,128)}), f32[64,2048]{1,0:T(8,128)}) %reduce-scatter.20.cloned.1.call-update) | async-done | bytes 524304 | tf_op jit(solution)/shard_map/reduce_scatter | solution.py:367
  3589.2 365.2 %reduce-scatter.26.cloned.1.call-done = f32[64,2048]{1,0:T(8,128)} async-done(((f32[2048,2048]{1,0:T(8,128)}), f32[64,2048]{1,0:T(8,128)}) %reduce-scatter.26.cloned.1.call-update) | async-done | bytes 524304 | tf_op jit(solution)/shard_map/reduce_scatter | solution.py:370
  3954.4 365.0 %reduce-scatter.22.cloned.1.call-done = f32[64,2048]{1,0:T(8,128)} async-done(((f32[2048,2048]{1,0:T(8,128)}), f32[64,2048]{1,0:T(8,128)}) %reduce-scatter.22.cloned.1.call-update) | async-done | bytes 524304 | tf_op jit(solution)/shard_map/reduce_scatter | solution.py:368
  4319.4 365.2 %reduce-scatter.24.cloned.1.call-done = f32[64,2048]{1,0:T(8,128)} async-done(((f32[2048,2048]{1,0:T(8,128)}), f32[64,2048]{1,0:T(8,128)}) %reduce-scatter.24.cloned.1.call-update) | async-done | bytes 524304 | tf_op jit(solution)/shard_map/reduce_scatter | solution.py:369
  4684.6 973.2 %reduce-scatter.28.cloned.1.call-done = f32[256,1408]{1,0:T(8,128)} async-done(((f32[8192,1408]{1,0:T(8,128)}), f32[256,1408]{1,0:T(8,128)}) %reduce-scatter.28.cloned.1.call-update) | async-done | bytes 1441808 | tf_op jit(solution)/shard_map/reduce_scatter | solution.py:332
  5657.8 975.6 %reduce-scatter.30.cloned.1.call-done = f32[256,1408]{1,0:T(8,128)} async-done(((f32[8192,1408]{1,0:T(8,128)}), f32[256,1408]{1,0:T(8,128)}) %reduce-scatter.30.cloned.1.call-update) | async-done | bytes 1441808 | tf_op jit(solution)/shard_map/reduce_scatter | solution.py:333
  6633.4 975.8 %reduce-scatter.32.cloned.1.call-done = f32[1408,256]{1,0:T(8,128)} async-done(((f32[45056,256]{1,0:T(8,128)}), f32[1408,256]{1,0:T(8,128)}) %reduce-scatter.32.cloned.1.call-update) | async-done | bytes 1441808 | tf_op jit(solution)/shard_map/reduce_scatter | solution.py:334
  (543 shorter events, 1396.9 us)
Async XLA Ops:
  9.4 515.0 %all-gather.35.cloned.1.call-start = ((), (), s32[]{:S(2)}) async-start(), calls=%async_computation.25 | async-start | bytes 7208960 | tf_op jit(solution)/shard_map/all_gather | solution.py:99
  10.0 663.8 %all-gather.19.cloned.1.call-start = ((), (), s32[]{:S(2)}) async-start(), calls=%async_computation.17 | async-start | bytes 10485760 | tf_op jit(solution)/shard_map/all_gather | solution.py:91
  10.6 677.2 %all-gather.23.cloned.1.call-start = ((), (), s32[]{:S(2)}) async-start(), calls=%async_computation.19 | async-start | bytes 6291456 | tf_op jit(solution)/shard_map/all_gather | solution.py:141
  171.2 533.5 %all-gather.27.cloned.1.call-start = ((), (), s32[]{:S(2)}) async-start(), calls=%async_computation.21 | async-start | bytes 6291456 | tf_op jit(solution)/shard_map/all_gather | solution.py:142
  320.7 536.5 %all-gather.29.cloned.1.call-start = ((), (), s32[]{:S(2)}) async-start(), calls=%async_computation.22 | async-start | bytes 10485760 | tf_op jit(solution)/shard_map/all_gather | solution.py:94
  321.4 642.3 %all-gather.43.cloned.1.call-start = ((), (), s32[]{:S(2)}) async-start(), calls=%async_computation.29 | async-start | bytes 7208960 | tf_op jit(solution)/shard_map/all_gather | solution.py:101
  322.1 748.0 %all-gather.45.cloned.1.call-start = ((), (), s32[]{:S(2)}) async-start(), calls=%async_computation.30 | async-start | bytes 7208960 | tf_op jit(solution)/shard_map/all_gather | solution.py:102
  322.8 854.0 %all-gather.47.cloned.1.call-start = ((), (), s32[]{:S(2)}) async-start(), calls=%async_computation.31 | async-start | bytes 7208960 | tf_op jit(solution)/shard_map/all_gather | solution.py:103
  323.5 959.7 %all-gather.39.cloned.1.call-start = ((), (), s32[]{:S(2)}) async-start(), calls=%async_computation.27 | async-start | bytes 7208960 | tf_op jit(solution)/shard_map/all_gather | solution.py:100
  324.1 1354.2 %all-gather.33.cloned.1.call-start = ((), (), s32[]{:S(2)}) async-start(), calls=%async_computation.24 | async-start | bytes 28835840 | tf_op jit(solution)/shard_map/all_gather | solution.py:122
  418.0 1488.4 %all-gather.37.cloned.1.call-start = ((), (), s32[]{:S(2)}) async-start(), calls=%async_computation.26 | async-start | bytes 28835840 | tf_op jit(solution)/shard_map/all_gather | solution.py:123
  1202.0 916.6 %all-gather.41.cloned.1.call-start = ((), (), s32[]{:S(2)}) async-start(), calls=%async_computation.28 | async-start | bytes 28835840 | tf_op jit(solution)/shard_map/all_gather | solution.py:124
  1672.9 530.1 %all-to-all-start.3 = ((bf16[8,288,2048]{2,1,0:T(8,128)(2,1)}), bf16[8,288,2048]{2,1,0:T(8,128)(2,1)}, u32[]{:S(2)}, u32[]{:S(2)}) async-start(bf16[8,288,2048]{2,1,0:T(8,128)(2,1)} %bitcast.347), calls=%async_computation.3 | async-start | bytes 18874368 | tf_op jit(solution)/shard_map/all_to_all | solution.py:278
  1678.2 866.1 %reduce-scatter.16.cloned.1.call-start = ((), (), s32[]{:S(2)}) async-start(), calls=%async_computation.32 | async-start | bytes 12582912 | tf_op jit(solution)/shard_map/reduce_scatter | solution.py:349
  2454.7 435.0 %reduce-scatter.34.cloned.1.call-start = ((), (), s32[]{:S(2)}) async-start(), calls=%async_computation.41 | async-start | bytes 14417920 | tf_op jit(solution)/shard_map/reduce_scatter | solution.py:267
  2476.2 545.8 %reduce-scatter.36.cloned.1.call-start = ((), (), s32[]{:S(2)}) async-start(), calls=%async_computation.42 | async-start | bytes 14417920 | tf_op jit(solution)/shard_map/reduce_scatter | solution.py:268
  2497.8 723.2 %reduce-scatter.38.cloned.1.call-start = ((), (), s32[]{:S(2)}) async-start(), calls=%async_computation.43 | async-start | bytes 14417920 | tf_op jit(solution)/shard_map/reduce_scatter | solution.py:269
  2517.4 1071.9 %reduce-scatter.20.cloned.1.call-start = ((), (), s32[]{:S(2)}) async-start(), calls=%async_computation.34 | async-start | bytes 17301504 | tf_op jit(solution)/shard_map/reduce_scatter | solution.py:367
  2530.8 1423.6 %reduce-scatter.26.cloned.1.call-start = ((), (), s32[]{:S(2)}) async-start(), calls=%async_computation.37 | async-start | bytes 17301504 | tf_op jit(solution)/shard_map/reduce_scatter | solution.py:370
  2544.1 1775.3 %reduce-scatter.22.cloned.1.call-start = ((), (), s32[]{:S(2)}) async-start(), calls=%async_computation.35 | async-start | bytes 17301504 | tf_op jit(solution)/shard_map/reduce_scatter | solution.py:368
  2557.9 2126.7 %reduce-scatter.24.cloned.1.call-start = ((), (), s32[]{:S(2)}) async-start(), calls=%async_computation.36 | async-start | bytes 17301504 | tf_op jit(solution)/shard_map/reduce_scatter | solution.py:369
  2571.3 3086.4 %reduce-scatter.28.cloned.1.call-start = ((), (), s32[]{:S(2)}) async-start(), calls=%async_computation.38 | async-start | bytes 47579136 | tf_op jit(solution)/shard_map/reduce_scatter | solution.py:332
  2647.1 3986.3 %reduce-scatter.30.cloned.1.call-start = ((), (), s32[]{:S(2)}) async-start(), calls=%async_computation.39 | async-start | bytes 47579136 | tf_op jit(solution)/shard_map/reduce_scatter | solution.py:333
  2722.8 4886.3 %reduce-scatter.32.cloned.1.call-start = ((), (), s32[]{:S(2)}) async-start(), calls=%async_computation.40 | async-start | bytes 47579136 | tf_op jit(solution)/shard_map/reduce_scatter | solution.py:334
  (65 other events, 5998.2 us)
Sparse Core Ops, SparseCore 0:
  9.6 152.3 all-gather.20
  163.5 147.8 all-gather.24
  313.0 104.9 all-gather.30
  419.4 104.9 all-gather.34
  525.9 147.9 all-gather.18
  706.3 150.7 all-gather.28
  858.7 104.9 all-gather.42
  965.1 104.9 all-gather.44
  1071.7 104.9 all-gather.46
  1178.2 104.9 all-gather.38
  1285.1 289.8 all-gather.32
  1576.7 329.6 all-gather.36
  1908.1 210.4 all-gather.40
  2490.8 136.5 reduce-scatter.39
  2630.4 191.5 reduce-scatter.33
  2824.9 196.9 reduce-scatter.35
  3025.0 195.9 reduce-scatter.37
  3224.0 365.2 reduce-scatter.19
  3592.2 362.1 reduce-scatter.25
  3957.2 362.1 reduce-scatter.21
  4322.4 362.1 reduce-scatter.23
  4687.4 970.2 reduce-scatter.27
  5660.6 972.7 reduce-scatter.29
  6636.4 972.7 reduce-scatter.31
  (4 shorter events, 61.4 us)
where the time goes:
time: 7630 us; the launch traced here: 7620 us
  waiting for transfers between devices  6230 us (82%)
  matrix products  736 us (10%)
  local copies, waits for them, and re-layouts  353 us (5%)
  other arithmetic  154 us (2%)
  blocking collectives  99.1 us (1%)
    reduce_scatter x1, waiting for transfers between devices, local(): lax.psum_scatter(arr_down, ('experts', 'context', 'dp'), scatter_dimensio...  976 us
    reduce_scatter x1, waiting for transfers between devices, local(): lax.psum_scatter(arr_up, ('experts', 'context', 'dp'), scatter_dimension=...  976 us
    reduce_scatter x1, waiting for transfers between devices, local(): lax.psum_scatter(arr_gate, ('experts', 'context', 'dp'), scatter_dimensio...  973 us
    reduce_scatter x1, waiting for transfers between devices, local(): lax.psum_scatter(grad_query, ('experts', 'context', 'dp'), scatter_dimens...  368 us
    reduce_scatter x1, waiting for transfers between devices, local(): lax.psum_scatter(grad_value, ('experts', 'context', 'dp'), scatter_dimens...  365 us
    reduce_scatter x1, waiting for transfers between devices, local(): lax.psum_scatter(grad_out_w, ('experts', 'context', 'dp'), scatter_dimens...  365 us
    reduce_scatter x1, waiting for transfers between devices, local(): lax.psum_scatter(grad_key, ('experts', 'context', 'dp'), scatter_dimensio...  365 us
    all_gather x1, waiting for transfers between devices, local(): lax.all_gather(sh_up, 'experts', axis=1, tiled=True)  209 us
  transfers between devices with their start and end apart: 32, of which 25 were waited for; matrix products, arithmetic and copies ran while one was open for 13% of the time, Pallas kernels for 0%

commit v1 on v0

--- a/solution.py
+++ b/solution.py
@@ -3,6 +3,8 @@
 import jax
 import jax.numpy as jnp
 from jax import lax
+from jax.experimental import pallas as pl
+from jax.experimental.pallas import tpu as pltpu
 from jax.sharding import PartitionSpec as P
 
 HEADS = 16
@@ -64,7 +66,7 @@
     return (query_grad, key_grad, value_grad)
 
 
-def local(
+def local_general(
     hidden,
     cotangent,
     segments,
@@ -397,6 +399,437 @@
         expert_sums[2],
     )
 
+PLANE = ("experts", "context")
+
+
+def attention_probs(q_blk, k_part, q_code, k_code, first_row, scale_factor):
+    scores = lax.dot_general(
+        q_blk, k_part, (((1,), (1,)), ((), ())), preferred_element_type=jnp.float32
+    )
+    row = first_row + lax.broadcasted_iota(jnp.int32, scores.shape, 0)
+    col = lax.broadcasted_iota(jnp.int32, scores.shape, 1)
+    allowed = ((col < row) & (k_code == q_code)) | (col == row)
+    logits = jnp.where(allowed, scores * scale_factor, NEG)
+    exp_scores = jnp.exp(logits - jnp.max(logits, axis=1, keepdims=True))
+    return exp_scores * (1.0 / jnp.sum(exp_scores, axis=1, keepdims=True))
+
+
+def attend_kernel(heads, step, qkv_ref, q_code_ref, k_code_ref, out_ref):
+    seq_len = qkv_ref.shape[0]
+    width = heads * HEAD_DIM
+    for head in range(heads):
+        at = head * HEAD_DIM
+        for first in range(0, seq_len, step):
+            upto = first + step
+            probs = attention_probs(
+                qkv_ref[first:upto, at : at + HEAD_DIM],
+                qkv_ref[0:upto, width + at : width + at + HEAD_DIM],
+                q_code_ref[first:upto, :],
+                k_code_ref[0, :, 0:upto],
+                first,
+                HEAD_DIM**-0.5,
+            )
+            out_ref[first:upto, at : at + HEAD_DIM] = jnp.dot(
+                probs.astype(jnp.bfloat16),
+                qkv_ref[0:upto, 2 * width + at : 2 * width + at + HEAD_DIM],
+                preferred_element_type=jnp.float32,
+            ).astype(jnp.bfloat16)
+
+
+def attend_back_kernel(
+    heads, step, qkv_ref, grad_ref, q_code_ref, k_code_ref, out_ref, key_acc, value_acc
+):
+    seq_len = qkv_ref.shape[0]
+    width = heads * HEAD_DIM
+    for head in range(heads):
+        at = head * HEAD_DIM
+        key_at, value_at = width + at, 2 * width + at
+        key_acc[...] = jnp.zeros_like(key_acc)
+        value_acc[...] = jnp.zeros_like(value_acc)
+        for first in range(0, seq_len, step):
+            upto = first + step
+            q_blk = qkv_ref[first:upto, at : at + HEAD_DIM]
+            k_part = qkv_ref[0:upto, key_at : key_at + HEAD_DIM]
+            v_part = qkv_ref[0:upto, value_at : value_at + HEAD_DIM]
+            g_blk = grad_ref[first:upto, at : at + HEAD_DIM]
+            probs = attention_probs(
+                q_blk,
+                k_part,
+                q_code_ref[first:upto, :],
+                k_code_ref[0, :, 0:upto],
+                first,
+                HEAD_DIM**-0.5,
+            )
+            prob_grad = lax.dot_general(
+                g_blk, v_part, (((1,), (1,)), ((), ())), preferred_element_type=jnp.float32
+            )
+            inner = jnp.sum(probs * prob_grad, axis=1, keepdims=True)
+            score_grad = (probs * (prob_grad - inner) * HEAD_DIM**-0.5).astype(jnp.bfloat16)
+            out_ref[first:upto, at : at + HEAD_DIM] = jnp.dot(
+                score_grad, k_part, preferred_element_type=jnp.float32
+            ).astype(jnp.bfloat16)
+            key_acc[0:upto, :] += lax.dot_general(
+                score_grad, q_blk, (((0,), (0,)), ((), ())), preferred_element_type=jnp.float32
+            )
+            value_acc[0:upto, :] += lax.dot_general(
+                probs.astype(jnp.bfloat16),
+                g_blk,
+                (((0,), (0,)), ((), ())),
+                preferred_element_type=jnp.float32,
+            )
+        out_ref[:, key_at : key_at + HEAD_DIM] = key_acc[...].astype(jnp.bfloat16)
+        out_ref[:, value_at : value_at + HEAD_DIM] = value_acc[...].astype(jnp.bfloat16)
+
+
+def attention_call(qkv, grads, q_codes, k_codes, seq_len):
+    rows, triple = qkv.shape
+    width = triple // 3
+    heads = width // HEAD_DIM
+    step = min(256, seq_len)
+    specs = [pl.BlockSpec((seq_len, triple), lambda s: (s, 0))]
+    operands = [qkv]
+    if grads is not None:
+        specs.append(pl.BlockSpec((seq_len, width), lambda s: (s, 0)))
+        operands.append(grads)
+    specs += [
+        pl.BlockSpec((seq_len, 1), lambda s: (s, 0)),
+        pl.BlockSpec((1, 1, seq_len), lambda s: (s, 0, 0)),
+    ]
+    operands += [q_codes, k_codes]
+    out_width = width if grads is None else triple
+    body = attend_kernel if grads is None else attend_back_kernel
+    passes = 2 if grads is None else 5
+    area = rows * seq_len * heads
+    return pl.pallas_call(
+        partial(body, heads, step),
+        grid=(rows // seq_len,),
+        in_specs=specs,
+        out_specs=pl.BlockSpec((seq_len, out_width), lambda s: (s, 0)),
+        out_shape=jax.ShapeDtypeStruct((rows, out_width), jnp.bfloat16),
+        scratch_shapes=[]
+        if grads is None
+        else [pltpu.VMEM((seq_len, HEAD_DIM), jnp.float32)] * 2,
+        compiler_params=pltpu.CompilerParams(vmem_limit_bytes=48 * 2**20),
+        cost_estimate=pl.CostEstimate(
+            flops=2 * passes * area * HEAD_DIM,
+            bytes_accessed=2 * rows * (triple + out_width),
+            transcendentals=area,
+        ),
+    )(*operands)
+
+
+def mm(left, right, dims=((1,), (0,))):
+    return lax.dot_general(left, right, (dims, ((), ())), preferred_element_type=jnp.float32)
+
+
+def low(values):
+    return values.astype(jnp.bfloat16)
+
+
+def local_plane(
+    hidden,
+    cotangent,
+    segments,
+    padding,
+    routes,
+    order,
+    norm1_gain,
+    w_query,
+    w_key,
+    w_value,
+    w_out,
+    norm2_gain,
+    router,
+    shared_gate_vec,
+    shared_w_gate,
+    shared_w_up,
+    shared_w_down,
+    expert_w_gate,
+    expert_w_up,
+    expert_w_down,
+):
+    plane = lax.axis_size(PLANE)
+    groups = lax.axis_size("experts")
+    halves = lax.axis_size("context")
+    depth = lax.axis_size("dp")
+    me = lax.axis_index(PLANE)
+    core = lax.axis_index("context")
+    tokens, width = hidden.shape[1], hidden.shape[2]
+    all_tokens = plane * tokens
+    seq_len = halves * tokens
+    experts_all = router.shape[1]
+    head_cols = width // plane
+    shard = width // depth
+
+    small = jnp.concatenate(
+        [
+            norm1_gain[None],
+            norm2_gain[None],
+            shared_gate_vec[None],
+            jnp.zeros((5, shard), jnp.bfloat16),
+            router.T,
+        ]
+    )
+    small = lax.all_gather(small, "dp", axis=0, tiled=False)
+    small = small.transpose(1, 0, 2).reshape(-1, width)
+    g_one = small[0].astype(jnp.float32)
+    g_two = small[1].astype(jnp.float32)
+    gate_vec = small[2]
+    router_t = small[8:]
+    token_info = jnp.concatenate(
+        [segments + 1, jnp.where(padding > 0, segments + 1, 0), order[0], routes[0].T]
+    )
+    info_rows = token_info.shape[0]
+    token_info = jnp.concatenate([token_info, jnp.zeros((8 - info_rows, tokens), jnp.int32)])
+    info_all = lax.all_gather(token_info, PLANE, axis=0, tiled=False)
+
+    hidden_all = lax.all_gather(hidden[0], PLANE, axis=0, tiled=True)
+    w_qkv_part = jnp.concatenate(
+        [
+            lax.dynamic_slice(w, (0, me * head_cols), (shard, head_cols))
+            for w in (w_query, w_key, w_value)
+        ],
+        axis=1,
+    )
+    w_qkv = lax.all_gather(w_qkv_part, "dp", axis=0, tiled=True)
+    out_rows = shard // plane
+    w_out_part = lax.dynamic_slice(w_out, (me * out_rows, 0), (out_rows, width))
+    w_out_part = lax.all_gather(w_out_part, "dp", axis=0, tiled=False)
+    w_out_full = lax.all_gather(w_out_part, PLANE, axis=0, tiled=False)
+    w_out_full = w_out_full.transpose(1, 0, 2, 3).reshape(width, width)
+
+    def normed(values, gain):
+        values = values.astype(jnp.float32)
+        inv = lax.rsqrt(jnp.mean(values * values, axis=1, keepdims=True) + EPS)
+        return values, inv, low(values * inv * gain)
+
+    _, _, n1_all = normed(hidden_all, g_one)
+    x_rows, inv_one, _ = normed(hidden[0], g_one)
+    cot_rows = cotangent[0].astype(jnp.float32)
+    qkv = low(mm(n1_all, w_qkv))
+    q_codes = info_all[:, 0].reshape(all_tokens, 1)
+    k_codes = info_all[:, 1].reshape(all_tokens // seq_len, 1, seq_len)
+    attended_cols = attention_call(qkv, None, q_codes, k_codes, seq_len)
+
+    def to_tokens(cols):
+        got = lax.all_to_all(
+            cols.reshape(plane, tokens, head_cols), PLANE, split_axis=0, concat_axis=0, tiled=True
+        )
+        return got.transpose(1, 0, 2).reshape(tokens, width)
+
+    def to_columns(rows_in):
+        send = rows_in.reshape(tokens, plane, head_cols).transpose(1, 0, 2)
+        got = lax.all_to_all(send, PLANE, split_axis=0, concat_axis=0, tiled=True)
+        return got.reshape(all_tokens, head_cols)
+
+    attended = to_tokens(attended_cols)
+    residual = x_rows + mm(attended, w_out_full)
+    residual, inv_two, n2 = normed(residual, g_two)
+
+    n2_all = lax.all_gather(n2, PLANE, axis=0, tiled=True)
+    cot_all = lax.all_gather(cotangent[0], PLANE, axis=0, tiled=True)
+    units = shared_w_gate.shape[1]
+    part = units // (depth * halves)
+    pick = lambda w: lax.dynamic_index_in_dim(
+        w.reshape(w.shape[0], depth, halves, part), core, axis=2, keepdims=False
+    ).reshape(w.shape[0], depth * part)
+    sh_gate = lax.all_gather(pick(shared_w_gate), "dp", axis=0, tiled=True)
+    sh_up = lax.all_gather(pick(shared_w_up), "dp", axis=0, tiled=True)
+    sh_down = lax.all_gather(
+        lax.dynamic_slice(shared_w_down, (core * part, 0), (part, width)), "dp", axis=0, tiled=True
+    )
+    ex_gate = lax.all_gather(expert_w_gate[0], "dp", axis=0, tiled=True)
+    ex_up = lax.all_gather(expert_w_up[0], "dp", axis=0, tiled=True)
+    ex_down = lax.all_gather(expert_w_down[0], "dp", axis=1, tiled=True)
+
+    def router_of(rows_in):
+        z = mm(rows_in, router_t, ((1,), (1,)))
+        e = jnp.exp(z - jnp.max(z, axis=1, keepdims=True))
+        return e / jnp.sum(e, axis=1, keepdims=True)
+
+    def shared_gate_of(rows_in):
+        return jax.nn.sigmoid(mm(rows_in, gate_vec[:, None]))
+
+    probs_all = router_of(n2_all)
+    sg_all = shared_gate_of(n2_all)
+    expert_gate = lax.dynamic_slice(probs_all, (0, me), (all_tokens, 1))
+
+    capacity = (9 * tokens * TOP + 8 * experts_all - 1) // (8 * experts_all)
+    order_all = info_all[:, 2]
+    routed_here = jnp.any(info_all[:, 3 : 3 + TOP] == me, axis=1)
+    earlier = (order_all[:, None, :] < order_all[:, :, None]) & routed_here[:, None, :]
+    slots = jnp.sum(earlier.astype(jnp.int32), axis=2)
+    slots = jnp.where(routed_here, slots, capacity)
+    chosen = slots[:, None, :] == jnp.arange(capacity, dtype=jnp.int32)[None, :, None]
+    onehot = chosen.astype(jnp.bfloat16)
+
+    def rows_of(values):
+        got = jnp.einsum(
+            "bst,btd->bsd",
+            onehot,
+            values.reshape(plane, tokens, width),
+            preferred_element_type=jnp.float32,
+        )
+        return got.reshape(plane * capacity, width)
+
+    def back_to_tokens(values):
+        got = jnp.einsum(
+            "bst,bsd->btd",
+            onehot,
+            values.reshape(plane, capacity, width),
+            preferred_element_type=jnp.float32,
+        )
+        return got.reshape(all_tokens, width)
+
+    slot_gates = jnp.sum(
+        jnp.where(chosen, expert_gate.reshape(plane, 1, tokens), 0.0), axis=2
+    ).reshape(plane * capacity, 1)
+    expert_rows = low(rows_of(n2_all))
+    row_cots = low(rows_of(cot_all))
+    row_grads = low(row_cots.astype(jnp.float32) * slot_gates)
+
+    shared_grads = low(sg_all * cot_all.astype(jnp.float32))
+    gate_pre = mm(n2_all, sh_gate)
+    up_pre = mm(n2_all, sh_up)
+    gate_act = gate_pre * jax.nn.sigmoid(gate_pre)
+    shared_hidden = low(gate_act * up_pre)
+    shared_part = mm(shared_hidden, sh_down)
+    cot_dot_shared = jnp.sum(shared_part * cot_all.astype(jnp.float32), axis=1)
+    shared_hgrad = mm(shared_grads, sh_down, ((1,), (1,)))
+    gate_grad_s = low(shared_hgrad * up_pre * silu_grad(gate_pre))
+    up_grad_s = low(shared_hgrad * gate_act)
+
+    def shared_scatter(grad):
+        halved = lax.all_to_all(
+            low(grad).reshape(halves, width // halves, depth * part),
+            "context",
+            split_axis=0,
+            concat_axis=0,
+            tiled=True,
+        )
+        rows_out = width // (halves * depth)
+        halved = (
+            halved.reshape(halves, depth, rows_out, depth * part)
+            .transpose(1, 2, 0, 3)
+            .reshape(depth * rows_out, units)
+        )
+        total = lax.psum_scatter(halved, "dp", scatter_dimension=0, tiled=True)
+        total = total.reshape(rows_out, halves, depth, part).transpose(0, 2, 1, 3)
+        return total.reshape(rows_out, units).astype(jnp.float32)
+
+    grad_sh_gate = shared_scatter(mm(n2_all, gate_grad_s, ((0,), (0,))))
+    grad_sh_up = shared_scatter(mm(n2_all, up_grad_s, ((0,), (0,))))
+    grad_sh_down = shared_scatter(mm(shared_grads, shared_hidden, ((0,), (0,)))).T
+
+    gate_e = mm(expert_rows, ex_gate)
+    up_e = mm(expert_rows, ex_up)
+    act_e = gate_e * jax.nn.sigmoid(gate_e)
+    hidden_e = low(act_e * up_e)
+    result_e = low(mm(hidden_e, ex_down))
+    row_dots = jnp.sum(result_e.astype(jnp.float32) * row_cots.astype(jnp.float32), axis=1)
+    gate_dots = jnp.sum(
+        jnp.where(chosen, row_dots.reshape(plane, capacity, 1), 0.0), axis=1
+    )
+    hgrad_e = mm(row_grads, ex_down, ((1,), (1,)))
+    gate_grad_e = low(hgrad_e * up_e * silu_grad(gate_e))
+    up_grad_e = low(hgrad_e * act_e)
+
+    def expert_scatter(grad, dim):
+        return lax.psum_scatter(low(grad), "dp", scatter_dimension=dim, tiled=True).astype(
+            jnp.float32
+        )[None]
+
+    grad_ex_down = expert_scatter(mm(hidden_e, row_grads, ((0,), (0,))), 1)
+    grad_ex_gate = expert_scatter(mm(expert_rows, gate_grad_e, ((0,), (0,))), 0)
+    grad_ex_up = expert_scatter(mm(expert_rows, up_grad_e, ((0,), (0,))), 0)
+    rows_grad = low(
+        mm(gate_grad_e, ex_gate, ((1,), (1,))) + mm(up_grad_e, ex_up, ((1,), (1,)))
+    )
+
+    out_part = low(sg_all * shared_part + expert_gate * back_to_tokens(result_e))
+    out_sum = lax.psum_scatter(out_part, PLANE, scatter_dimension=0, tiled=True)
+    output = low(residual + out_sum.astype(jnp.float32))
+    n2_grad_part = low(
+        mm(gate_grad_s, sh_gate, ((1,), (1,)))
+        + mm(up_grad_s, sh_up, ((1,), (1,)))
+        + back_to_tokens(rows_grad)
+    )
+    n2_grad = lax.psum_scatter(n2_grad_part, PLANE, scatter_dimension=0, tiled=True).astype(
+        jnp.float32
+    )
+
+    dots = jnp.stack([gate_dots, cot_dot_shared.reshape(plane, tokens)], axis=1)
+    dots = lax.all_to_all(dots, PLANE, split_axis=0, concat_axis=0, tiled=True)
+    probs_grad = dots[:, 0].T
+    probs = router_of(n2)
+    sg = shared_gate_of(n2)
+    logit_grad = low(probs * (probs_grad - jnp.sum(probs * probs_grad, axis=1, keepdims=True)))
+    sg_logit_grad = low(jnp.sum(dots[:, 1], axis=0)[:, None] * sg * (1.0 - sg))
+    small_grads = mm(n2, jnp.concatenate([logit_grad, sg_logit_grad], axis=1), ((0,), (0,)))
+    n2_grad = (
+        n2_grad
+        + mm(logit_grad, router_t)
+        + sg_logit_grad.astype(jnp.float32) * gate_vec.astype(jnp.float32)[None]
+    )
+    residual_grad, grad_gain_two = norm_back(residual, inv_two, g_two, n2_grad)
+    residual_grad = residual_grad + cot_rows
+    low_residual = low(residual_grad)
+
+    grad_out = low(mm(attended, low_residual, ((0,), (0,))))
+    grad_out = lax.psum_scatter(grad_out, PLANE, scatter_dimension=0, tiled=True)
+    grad_out = lax.psum_scatter(grad_out, "dp", scatter_dimension=0, tiled=True).astype(jnp.float32)
+    attended_grad = to_columns(low(mm(low_residual, w_out_full, ((1,), (1,)))))
+    qkv_grad = attention_call(qkv, attended_grad, q_codes, k_codes, seq_len)
+    n1_grad = low(mm(qkv_grad, w_qkv, ((1,), (1,))))
+    n1_grad = lax.psum_scatter(n1_grad, PLANE, scatter_dimension=0, tiled=True).astype(jnp.float32)
+    grad_qkv = low(mm(n1_all, qkv_grad, ((0,), (0,))))
+    fine = shard // plane
+    grad_qkv = (
+        grad_qkv.reshape(plane, depth, fine, 3 * head_cols)
+        .transpose(1, 0, 2, 3)
+        .reshape(width, 3 * head_cols)
+    )
+    grad_qkv = lax.psum_scatter(grad_qkv, "dp", scatter_dimension=0, tiled=True)
+    grad_qkv = lax.all_to_all(
+        grad_qkv.reshape(plane, fine, 3 * head_cols),
+        PLANE,
+        split_axis=0,
+        concat_axis=0,
+        tiled=True,
+    )
+    grad_qkv = (
+        grad_qkv.reshape(plane, fine, 3, head_cols)
+        .transpose(2, 1, 0, 3)
+        .reshape(3, fine, width)
+        .astype(jnp.float32)
+    )
+    input_part, grad_gain_one = norm_back(x_rows, inv_one, g_one, n1_grad)
+    input_grad = low(residual_grad + input_part)
+    small_grads = jnp.concatenate(
+        [small_grads, grad_gain_two[:, None], grad_gain_one[:, None]], axis=1
+    )
+    small_grads = lax.psum_scatter(
+        small_grads, ("experts", "context", "dp"), scatter_dimension=0, tiled=True
+    )
+    return (
+        output[None],
+        input_grad[None],
+        small_grads[:, experts_all + 2],
+        grad_qkv[0],
+        grad_qkv[1],
+        grad_qkv[2],
+        grad_out,
+        small_grads[:, experts_all + 1],
+        small_grads[:, :experts_all],
+        small_grads[:, experts_all],
+        grad_sh_gate,
+        grad_sh_up,
+        grad_sh_down,
+        grad_ex_gate,
+        grad_ex_up,
+        grad_ex_down,
+    )
+
 
 def solution(mesh):
     in_specs = (
@@ -439,4 +872,13 @@
         P(("experts", "context"), "dp", None),
         P(("experts", "context"), None, "dp"),
     )
-    return jax.shard_map(local, mesh=mesh, in_specs=in_specs, out_specs=out_specs, check_vma=False)
+    plane = mesh.shape["experts"] * mesh.shape["context"]
+
+    def run(*args):
+        one_each = args[12].shape[1] == plane and HEADS % plane == 0
+        local = local_plane if one_each else local_general
+        return jax.shard_map(
+            local, mesh=mesh, in_specs=in_specs, out_specs=out_specs, check_vma=False
+        )(*args)
+
+    return run

time: 7630 us -> 2230 us (0.29)
  waiting for transfers between devices: 6230 us -> 1320 us
  local copies, waits for them, and re-layouts: 353 us -> 89 us
  matrix products: 736 us -> 589 us
  other arithmetic: 154 us -> 61.6 us
    reduce_scatter x12, waiting for transfers between devices: 4720 us -> 611 us  [the longest x3 263 us: expert_scatter(): lax.psum_scatter(low(grad), 'dp', scatter_dimension=dim, tiled=True)]
    all_gather x15 -> x12, waiting for transfers between devices: 1290 us -> 562 us  [the longest x1 85.8 us: local_plane(): ex_up = lax.all_gather(expert_w_up[0], 'dp', axis=0, tiled=True)]
    all_to_all x4 -> x3, waiting for transfers between devices: 221 us -> 17.3 us  [the longest x1 12.2 us: to_tokens(): lax.all_to_all(cols.reshape(plane, tokens, head_cols), PLANE, split_axis=...]
    dot_general x147 -> x34, matrix products: 734 us -> 589 us  [the longest x30 518 us: mm(): lax.dot_general(left, right, (dims, ((), ())), preferred_element_type=jnp...]
    transpose x5 -> x2, local copies, waits for them, and re-layouts: 149 us -> 9.6 us  [the longest x1 8.36 us: local_plane(): w_out_full = w_out_full.transpose(1, 0, 2, 3).reshape(width, width)]
    unnamed x29 -> x26, waiting for transfers between devices: 7.05 us -> 134 us
    gather x9 -> x0, local copies, waits for them, and re-layouts: 87.4 us -> none  [the longest x2 34.6 us: local(): returned_grads.reshape(experts_all * capacity, model_width)[target]]
  transfers between devices with their start and end apart: 32 -> 28, of which waited for: 25 -> 21; matrix products, arithmetic and copies ran while one was open for 13% -> 28% of each run, Pallas kernels for 0% -> 2%
where the time goes in v1:
time: 2230 us; the launch traced here: 2220 us
  waiting for transfers between devices  1320 us (59%)
  matrix products  589 us (26%)
  local copies, waits for them, and re-layouts  89 us (4%)
  blocking collectives  73.3 us (3%)
  other arithmetic  61.6 us (3%)
  Pallas kernels  49.9 us (2%)
    dot_general x30, matrix products, mm(): lax.dot_general(left, right, (dims, ((), ())), preferred_element_type=jnp...  518 us
    reduce_scatter x3, waiting for transfers between devices, expert_scatter(): lax.psum_scatter(low(grad), 'dp', scatter_dimension=dim, tiled=True)  263 us
    unnamed x26, waiting for transfers between devices  134 us
    reduce_scatter x1, waiting for transfers between devices, local_plane(): lax.psum_scatter(n1_grad, PLANE, scatter_dimension=0, tiled=True)  116 us
    reduce_scatter x1, waiting for transfers between devices, local_plane(): out_sum = lax.psum_scatter(out_part, PLANE, scatter_dimension=0, tiled=True)  113 us
    all_gather x1, waiting for transfers between devices, local_plane(): ex_up = lax.all_gather(expert_w_up[0], 'dp', axis=0, tiled=True)  85.8 us
    all_gather x1, waiting for transfers between devices, local_plane(): ex_down = lax.all_gather(expert_w_down[0], 'dp', axis=1, tiled=True)  83.4 us
    all_gather x1, waiting for transfers between devices, local_plane(): n2_all = lax.all_gather(n2, PLANE, axis=0, tiled=True)  78.9 us
  transfers between devices with their start and end apart: 28, of which 21 were waited for; matrix products, arithmetic and copies ran while one was open for 28% of the time, Pallas kernels for 2%

profile of v1, /device:TPU:0, one launch (start us, length us, event | category | flops | bytes accessed | tf_op | source)
XLA Modules:
  0.0 2216.7 jit_solution(12307370139648967447)
XLA Ops:
  13.4 27.5 %all-gather.34.cloned.1.call-done = bf16[256,2048]{1,0:T(8,128)(2,1)} async-done(((bf16[64,2048]{1,0:T(8,128)(2,1)}), bf16[256,2048]{1,0:T(8,128)(2,1)}) %all-gather.34.cloned.1.call-update) | async-done | bytes 1048592 | tf_op jit(solution)/shard_map/all_gather | solution.py:597
  66.4 66.4 %all-gather.32.cloned.1.call-done = bf16[1,4096,2048]{2,1,0:T(8,128)(2,1)} async-done(((bf16[1,512,2048]{2,1,0:T(8,128)(2,1)}), bf16[1,4096,2048]{2,1,0:T(8,128)(2,1)}) %all-gather.32.cloned.1.call-update) | async-done | bytes 16777232 | tf_op jit(solution)/shard_map/all_gather | solution.py:586
  139.9 58.5 %all-gather.22.cloned.1.call-done = bf16[2048,768]{1,0:T(8,128)(2,1)} async-done(((bf16[512,768]{1,0:T(8,128)(2,1)}), bf16[2048,768]{1,0:T(8,128)(2,1)}) %all-gather.22.cloned.1.call-update) | async-done | bytes 3145744 | tf_op jit(solution)/shard_map/all_gather | solution.py:594
  303.6 50.6 %all-gather.44.cloned.1.call-done = bf16[1,4096,2048]{2,1,0:T(8,128)(2,1)} async-done(((bf16[1,512,2048]{2,1,0:T(8,128)(2,1)}), bf16[1,4096,2048]{2,1,0:T(8,128)(2,1)}) %all-gather.44.cloned.1.call-update) | async-done | bytes 16777232 | tf_op jit(solution)/shard_map/all_gather | solution.py:630
  367.5 78.9 %all-gather.24.cloned.1.call-done = bf16[4096,2048]{1,0:T(8,128)(2,1)} async-done(((bf16[512,2048]{1,0:T(8,128)(2,1)}), bf16[4096,2048]{1,0:T(8,128)(2,1)}) %all-gather.24.cloned.1.call-update) | async-done | bytes 16777232 | tf_op jit(solution)/shard_map/all_gather | solution.py:629
  477.9 76.8 %all-gather.38.cloned.1.call-done = bf16[1,2048,1408]{2,1,0:T(8,128)(2,1)} async-done(((bf16[1,512,1408]{2,1,0:T(8,128)(2,1)}), bf16[1,2048,1408]{2,1,0:T(8,128)(2,1)}) %all-gather.38.cloned.1.call-update) | async-done | bytes 5767184 | tf_op jit(solution)/shard_map/all_gather | solution.py:641
  575.5 85.8 %all-gather.40.cloned.1.call-done = bf16[1,2048,1408]{2,1,0:T(8,128)(2,1)} async-done(((bf16[1,512,1408]{2,1,0:T(8,128)(2,1)}), bf16[1,2048,1408]{2,1,0:T(8,128)(2,1)}) %all-gather.40.cloned.1.call-update) | async-done | bytes 5767184 | tf_op jit(solution)/shard_map/all_gather | solution.py:642
  684.6 83.4 %all-gather.42.cloned.1.call-done = bf16[1,1408,2048]{2,1,0:T(8,128)(2,1)} async-done(((bf16[1,1408,512]{2,1,0:T(8,128)(2,1)}), bf16[1,1408,2048]{2,1,0:T(8,128)(2,1)}) %all-gather.42.cloned.1.call-update) | async-done | bytes 5767184 | tf_op jit(solution)/shard_map/all_gather | solution.py:643
  800.3 27.1 %all-gather.28.cloned.1.call-done = bf16[2048,704]{0,1:T(8,128)(2,1)} async-done(((bf16[512,704]{0,1:T(8,128)(2,1)}), bf16[2048,704]{0,1:T(8,128)(2,1)}) %all-gather.28.cloned.1.call-update) | async-done | bytes 2883600 | tf_op jit(solution)/shard_map/all_gather | solution.py:637
  846.3 28.3 %multiply_convert_fusion = (bf16[2304,1408]{1,0:T(8,128)(2,1)}, bf16[2304,1408]{1,0:T(8,128)(2,1)}) fusion(f32[2304,1408]{1,0:T(8,128)} %fusion.24, f32[2304,1408]{1,0:T(8,128)} %get-tuple-element.125, bf16[2304,2048]{1,0:T(8,128)(2,1)} %fusion.8, bf16[1,1408,2048]{2,1,0:T(8,128)(2,1)} %all-gather.42.cloned.1.call-done), kind=kOutput, calls=%fused_computation.20 | convolution fusion | flops 13329727488 | bytes 54132736 | tf_op jit(solution)/shard_map/dot_general | solution.py:522
  956.1 27.1 %multiply_convert_fusion.3 = (bf16[4096,704]{0,1:T(8,128)(2,1)}, bf16[4096,704]{0,1:T(8,128)(2,1)}, bf16[4096,704]{0,1:T(8,128)(2,1)}) fusion(f32[4096,704]{0,1:T(8,128)} %fusion.71, f32[4096,704]{0,1:T(8,128)} %fusion.72, bf16[704,2048]{1,0:T(8,128)(2,1)} %all-gather.30.cloned.1.call-done, bf16[1,4096,2048]{2,1,0:T(8,128)(2,1)} %all-gather.44.cloned.1.call-done, ...), kind=kOutput, calls=%fused_computation.25 | convolution fusion | flops 11879579648 | bytes 60047360 | tf_op jit(solution)/shard_map/dot_general | solution.py:522
  1005.2 34.9 %fusion.5 = bf16[4096,2048]{1,0:T(8,128)(2,1)} fusion(f32[8,512,2048]{2,1,0:T(8,128)} %fusion.30, f32[4096,2048]{1,0:T(8,128)} %fusion.73, bf16[4096,704]{0,1:T(8,128)(2,1)} %get-tuple-element.96, bf16[2048,704]{0,1:T(8,128)(2,1)} %all-gather.28.cloned.1.call-done), kind=kOutput, calls=%fused_computation.10 | convolution fusion | flops 11836325888 | bytes 92536832 | tf_op jit(solution)/shard_map/dot_general | solution.py:522
  1040.2 25.4 %fusion.31 = f32[8,512,2048]{2,1,0:T(8,128)} fusion(bf16[8,288,2048]{2,1,0:T(8,128)(2,1)} %bitcast.287, s32[8,512]{1,0:T(8,128)S(1)} %broadcast_select_fusion), kind=kOutput, calls=%fused_computation.63 | convolution fusion | flops 4833017856 | bytes 43008000 | tf_op jit(solution)/shard_map/bst,bsd->btd/dot_general | solution.py:676
  1065.7 30.9 %fusion.4 = (f32[4096]{0:T(1024)S(1)}, bf16[4096,2048]{1,0:T(8,128)(2,1)}) fusion(bf16[1,4096,2048]{2,1,0:T(8,128)(2,1)} %all-gather.44.cloned.1.call-done, f32[8,512,2048]{2,1,0:T(8,128)} %fusion.31, f32[4096]{0:T(1024)S(1)} %bitcast.341, f32[4096]{0:T(1024)S(1)} %copy-done.30, bf16[4096,704]{0,1:T(8,128)(2,1)} %get-tuple-element.98, ...), kind=kOutput, calls=%fused_computation.8 | convolution fusion | flops 11869876224 | bytes 75808768 | tf_op jit(solution)/shard_map/dot_general | solution.py:522
  1112.6 43.1 %reduce-scatter.18.cloned.1.call-done = bf16[512,2048]{1,0:T(8,128)(2,1)} async-done(((bf16[4096,2048]{1,0:T(8,128)(2,1)}), bf16[512,2048]{1,0:T(8,128)(2,1)}) %reduce-scatter.18.cloned.1.call-update) | async-done | bytes 2097168 | tf_op jit(solution)/shard_map/reduce_scatter | solution.py:757
  1162.0 113.1 %reduce-scatter.16.cloned.1.call-done = bf16[512,2048]{1,0:T(8,128)(2,1)} async-done(((bf16[4096,2048]{1,0:T(8,128)(2,1)}), bf16[512,2048]{1,0:T(8,128)(2,1)}) %reduce-scatter.16.cloned.1.call-update) | async-done | bytes 2097168 | tf_op jit(solution)/shard_map/reduce_scatter | solution.py:750
  1428.4 29.2 %all_to_all.38 = bf16[8,512,256]{2,1,0:T(8,128)(2,1)S(1)} all-to-all(bf16[8,512,256]{2,1,0:T(8,128)(2,1)S(1)} %bitcast.292), channel_id=1, replica_groups=mesh['experts'=4,'context'=2,'dp'=4] {'experts','context'}, dimensions={0} | all-to-all | bytes 4194304 | tf_op jit(solution)/shard_map/all_to_all | solution.py:622
  1457.6 30.5 %shard_map.316 = bf16[4096,768]{1,0:T(8,128)(2,1)} custom-call(bf16[4096,768]{1,0:T(8,128)(2,1)} %convolution_convert_fusion.6.qkv_ref, bf16[4096,256]{1,0:T(8,128)(2,1)S(1)} %bitcast.272, s32[4096,1]{1,0:T(8,128)S(1)} %copy.145.q_code_ref, s32[4,1,1024]{2,1,0:T(1,128)S(1)} %bitcast.275), custom_call_target="tpu_custom_call" | custom-call | flops 10737418240 | bytes 12582912 | tf_op jit(solution)/shard_map/pallas_call | solution.py:503
  1584.4 59.8 %reduce-scatter.38.cloned.1.call-done = bf16[1408,512]{1,0:T(8,128)(2,1)} async-done(((bf16[1408,2048]{1,0:T(8,128)(2,1)}), bf16[1408,512]{1,0:T(8,128)(2,1)}) %reduce-scatter.38.cloned.1.call-update) | async-done | bytes 1441808 | tf_op jit(solution)/shard_map/reduce_scatter | solution.py:738
  1647.6 59.7 %reduce-scatter.22.cloned.1.call-done = bf16[512,768]{1,0:T(8,128)(2,1)} async-done(((bf16[2048,768]{1,0:T(8,128)(2,1)}), bf16[512,768]{1,0:T(8,128)(2,1)}) %reduce-scatter.22.cloned.1.call-update) | async-done | bytes 786448 | tf_op jit(solution)/shard_map/reduce_scatter | solution.py:792
  1711.0 101.0 %reduce-scatter.36.cloned.1.call-done = bf16[512,1408]{1,0:T(8,128)(2,1)} async-done(((bf16[2048,1408]{1,0:T(8,128)(2,1)}), bf16[512,1408]{1,0:T(8,128)(2,1)}) %reduce-scatter.36.cloned.1.call-update) | async-done | bytes 1441808 | tf_op jit(solution)/shard_map/reduce_scatter | solution.py:738
  1815.1 102.1 %reduce-scatter.34.cloned.1.call-done = bf16[512,1408]{1,0:T(8,128)(2,1)} async-done(((bf16[2048,1408]{1,0:T(8,128)(2,1)}), bf16[512,1408]{1,0:T(8,128)(2,1)}) %reduce-scatter.34.cloned.1.call-update) | async-done | bytes 1441808 | tf_op jit(solution)/shard_map/reduce_scatter | solution.py:738
  1949.1 116.3 %reduce-scatter.20.cloned.1.call-done = bf16[512,2048]{1,0:T(8,128)(2,1)} async-done(((bf16[4096,2048]{1,0:T(8,128)(2,1)}), bf16[512,2048]{1,0:T(8,128)(2,1)}) %reduce-scatter.20.cloned.1.call-update) | async-done | bytes 2097168 | tf_op jit(solution)/shard_map/reduce_scatter | solution.py:784
  2076.1 129.7 %reduce-scatter.40.cloned.1.call-done = f32[64,11]{1,0:T(8,128)} async-done(((f32[2048,11]{1,0:T(8,128)}), f32[64,11]{1,0:T(8,128)}) %reduce-scatter.40.cloned.1.call-update) | async-done | bytes 2832
  (287 shorter events, 715.4 us)
Async XLA Ops:
  10.3 188.1 %all-gather.22.cloned.1.call-start = ((), (), s32[]{:S(2)}) async-start(), calls=%async_computation.20 | async-start | bytes 3932160 | tf_op jit(solution)/shard_map/all_gather | solution.py:594
  13.3 240.8 %all-gather.36.cloned.1.call-start = ((), (), s32[]{:S(2)}) async-start(), calls=%async_computation.39 | async-start | bytes 9437184 | tf_op jit(solution)/shard_map/all_gather | solution.py:598
  40.9 313.3 %all-gather.44.cloned.1.call-start = ((), (), s32[]{:S(2)}) async-start(), calls=%async_computation.43 | async-start | bytes 18874368 | tf_op jit(solution)/shard_map/all_gather | solution.py:630
  247.2 199.2 %all-gather.24.cloned.1.call-start = ((), (), s32[]{:S(2)}) async-start(), calls=%async_computation.21 | async-start | bytes 18874368 | tf_op jit(solution)/shard_map/all_gather | solution.py:629
  288.7 266.0 %all-gather.38.cloned.1.call-start = ((), (), s32[]{:S(2)}) async-start(), calls=%async_computation.40 | async-start | bytes 7208960 | tf_op jit(solution)/shard_map/all_gather | solution.py:641
  289.5 371.9 %all-gather.40.cloned.1.call-start = ((), (), s32[]{:S(2)}) async-start(), calls=%async_computation.41 | async-start | bytes 7208960 | tf_op jit(solution)/shard_map/all_gather | solution.py:642
  290.2 477.7 %all-gather.42.cloned.1.call-start = ((), (), s32[]{:S(2)}) async-start(), calls=%async_computation.42 | async-start | bytes 7208960 | tf_op jit(solution)/shard_map/all_gather | solution.py:643
  291.0 536.4 %all-gather.28.cloned.1.call-start = ((), (), s32[]{:S(2)}) async-start(), calls=%async_computation.23 | async-start | bytes 3604480 | tf_op jit(solution)/shard_map/all_gather | solution.py:637
  293.6 643.4 %all-gather.26.cloned.1.call-start = ((), (), s32[]{:S(2)}) async-start(), calls=%async_computation.22 | async-start | bytes 3604480 | tf_op jit(solution)/shard_map/all_gather | solution.py:636
  296.3 659.8 %all-gather.30.cloned.1.call-start = ((), (), s32[]{:S(2)}) async-start(), calls=%async_computation.24 | async-start | bytes 3604480 | tf_op jit(solution)/shard_map/all_gather | solution.py:638
  298.5 857.2 %reduce-scatter.18.cloned.1.call-start = ((), (), s32[]{:S(2)}) async-start(), calls=%async_computation.26 | async-start | bytes 18874368 | tf_op jit(solution)/shard_map/reduce_scatter | solution.py:757
  1040.1 235.0 %reduce-scatter.16.cloned.1.call-start = ((), (), s32[]{:S(2)}) async-start(), calls=%async_computation.25 | async-start | bytes 18874368 | tf_op jit(solution)/shard_map/reduce_scatter | solution.py:750
  1106.8 444.6 %reduce-scatter.24.cloned.1.call-start = ((), (), s32[]{:S(2)}) async-start(), calls=%async_computation.29 | async-start | bytes 9437184 | tf_op jit(solution)/shard_map/reduce_scatter | solution.py:779
  1292.0 284.2 %reduce-scatter.28.cloned.1.call-start = ((), (), s32[]{:S(2)}) async-start(), calls=%async_computation.31 | async-start | bytes 3604480 | tf_op jit(solution)/shard_map/reduce_scatter | solution.py:716
  1327.4 251.6 %reduce-scatter.30.cloned.1.call-start = ((), (), s32[]{:S(2)}) async-start(), calls=%async_computation.32 | async-start | bytes 3604480 | tf_op jit(solution)/shard_map/reduce_scatter | solution.py:716
  1363.2 218.7 %reduce-scatter.32.cloned.1.call-start = ((), (), s32[]{:S(2)}) async-start(), calls=%async_computation.33 | async-start | bytes 3604480 | tf_op jit(solution)/shard_map/reduce_scatter | solution.py:716
  1398.9 245.3 %reduce-scatter.38.cloned.1.call-start = ((), (), s32[]{:S(2)}) async-start(), calls=%async_computation.36 | async-start | bytes 7208960 | tf_op jit(solution)/shard_map/reduce_scatter | solution.py:738
  1418.9 288.3 %reduce-scatter.22.cloned.1.call-start = ((), (), s32[]{:S(2)}) async-start(), calls=%async_computation.28 | async-start | bytes 3932160 | tf_op jit(solution)/shard_map/reduce_scatter | solution.py:792
  1510.3 301.7 %reduce-scatter.36.cloned.1.call-start = ((), (), s32[]{:S(2)}) async-start(), calls=%async_computation.35 | async-start | bytes 7208960 | tf_op jit(solution)/shard_map/reduce_scatter | solution.py:738
  1530.6 386.6 %reduce-scatter.34.cloned.1.call-start = ((), (), s32[]{:S(2)}) async-start(), calls=%async_computation.34 | async-start | bytes 7208960 | tf_op jit(solution)/shard_map/reduce_scatter | solution.py:738
  1551.4 395.9 %reduce-scatter.26.cloned.1.call-start = ((), (), s32[]{:S(2)}) async-start(), calls=%async_computation.30 | async-start | bytes 1310720 | tf_op jit(solution)/shard_map/reduce_scatter | solution.py:780
  1552.1 513.3 %reduce-scatter.20.cloned.1.call-start = ((), (), s32[]{:S(2)}) async-start(), calls=%async_computation.27 | async-start | bytes 18874368 | tf_op jit(solution)/shard_map/reduce_scatter | solution.py:784
  1707.3 213.1 %all-to-all-start.3 = ((bf16[8,64,768]{2,1,0:T(8,128)(2,1)}), bf16[8,64,768]{2,1,0:T(8,128)(2,1)S(1)}, u32[]{:S(2)}, u32[]{:S(2)}) async-start(bf16[8,64,768]{2,1,0:T(8,128)(2,1)} %bitcast.310), calls=%async_computation.7 | async-start | bytes 1572864 | tf_op jit(solution)/shard_map/all_to_all | solution.py:793
  1710.9 494.9 %reduce-scatter.40.cloned.1.call-start = ((), (), s32[]{:S(2)}) async-start(), calls=%async_computation.44 | async-start | bytes 1081344
  (48 other events, 2714.7 us)
Sparse Core Ops, SparseCore 0:
  10.3 30.6 all-gather.33
  42.8 89.8 all-gather.31
  134.9 63.4 all-gather.21
  200.2 53.9 all-gather.35
  255.9 98.2 all-gather.43
  356.5 89.8 all-gather.23
  448.0 106.6 all-gather.37
  556.3 104.9 all-gather.39
  662.9 104.9 all-gather.41
  769.9 57.3 all-gather.27
  829.5 57.8 all-gather.25
  889.4 57.8 all-gather.29
  1040.2 115.3 reduce-scatter.17
  1159.1 115.9 reduce-scatter.15
  1292.1 71.2 reduce-scatter.23
  1366.2 56.1 reduce-scatter.27
  1425.3 56.0 reduce-scatter.29
  1483.6 56.0 reduce-scatter.31
  1542.1 102.1 reduce-scatter.37
  1646.5 60.7 reduce-scatter.21
  1709.7 102.2 reduce-scatter.35
  1814.4 102.7 reduce-scatter.33
  1950.7 114.6 reduce-scatter.19
  2070.1 135.6 reduce-scatter.39
  (1 shorter events, 27.6 us)

commit v2 on v1

--- a/solution.py
+++ b/solution.py
@@ -7,6 +7,8 @@
 from jax.experimental.pallas import tpu as pltpu
 from jax.sharding import PartitionSpec as P
 
+EXP, CTX, DP = "experts", "context", "dp"
+PLANE = (EXP, CTX)
 HEADS = 16
 HEAD_DIM = 128
 TOP = 4
@@ -89,20 +91,20 @@
     expert_w_down,
 ):
     fetched = (
-        lax.all_gather(norm1_gain, "dp", axis=0, tiled=True),
-        lax.all_gather(w_query, "dp", axis=0, tiled=True),
-        lax.all_gather(w_key, "dp", axis=0, tiled=True),
-        lax.all_gather(w_value, "dp", axis=0, tiled=True),
-        lax.all_gather(w_out, "dp", axis=0, tiled=True),
-        lax.all_gather(norm2_gain, "dp", axis=0, tiled=True),
-        lax.all_gather(router, "dp", axis=0, tiled=True),
-        lax.all_gather(shared_gate_vec, "dp", axis=0, tiled=True),
-        lax.all_gather(shared_w_gate, "dp", axis=0, tiled=True),
-        lax.all_gather(shared_w_up, "dp", axis=0, tiled=True),
-        lax.all_gather(shared_w_down, "dp", axis=0, tiled=True),
-        lax.all_gather(expert_w_gate, "dp", axis=1, tiled=True),
-        lax.all_gather(expert_w_up, "dp", axis=1, tiled=True),
-        lax.all_gather(expert_w_down, "dp", axis=2, tiled=True),
+        lax.all_gather(norm1_gain, DP, axis=0, tiled=True),
+        lax.all_gather(w_query, DP, axis=0, tiled=True),
+        lax.all_gather(w_key, DP, axis=0, tiled=True),
+        lax.all_gather(w_value, DP, axis=0, tiled=True),
+        lax.all_gather(w_out, DP, axis=0, tiled=True),
+        lax.all_gather(norm2_gain, DP, axis=0, tiled=True),
+        lax.all_gather(router, DP, axis=0, tiled=True),
+        lax.all_gather(shared_gate_vec, DP, axis=0, tiled=True),
+        lax.all_gather(shared_w_gate, DP, axis=0, tiled=True),
+        lax.all_gather(shared_w_up, DP, axis=0, tiled=True),
+        lax.all_gather(shared_w_down, DP, axis=0, tiled=True),
+        lax.all_gather(expert_w_gate, DP, axis=1, tiled=True),
+        lax.all_gather(expert_w_up, DP, axis=1, tiled=True),
+        lax.all_gather(expert_w_down, DP, axis=2, tiled=True),
     )
     (
         gain_one,
@@ -121,9 +123,9 @@
         ex_down,
     ) = fetched
     sh_gate, sh_up, sh_down = (
-        lax.all_gather(sh_gate, "experts", axis=1, tiled=True),
-        lax.all_gather(sh_up, "experts", axis=1, tiled=True),
-        lax.all_gather(sh_down, "experts", axis=0, tiled=True),
+        lax.all_gather(sh_gate, EXP, axis=1, tiled=True),
+        lax.all_gather(sh_up, EXP, axis=1, tiled=True),
+        lax.all_gather(sh_down, EXP, axis=0, tiled=True),
     )
     tokens_here = hidden.shape[1]
     model_width = hidden.shape[2]
@@ -140,13 +142,13 @@
     own_codes = jnp.where(padding[0] > 0, segments[0] + 1, 0)
     code_parts = jnp.stack([own_codes // 64, own_codes % 64]).astype(jnp.bfloat16)
     keys_all, values_all, parts_all = (
-        lax.all_gather(keys_own, "context", axis=0, tiled=True),
-        lax.all_gather(values_own, "context", axis=0, tiled=True),
-        lax.all_gather(code_parts, "context", axis=1, tiled=True),
+        lax.all_gather(keys_own, CTX, axis=0, tiled=True),
+        lax.all_gather(values_own, CTX, axis=0, tiled=True),
+        lax.all_gather(code_parts, CTX, axis=1, tiled=True),
     )
     key_codes = parts_all[0].astype(jnp.int32) * 64 + parts_all[1].astype(jnp.int32)
     seq_total = keys_all.shape[0]
-    query_pos = lax.axis_index("context") * tokens_here + jnp.arange(tokens_here, dtype=jnp.int32)
+    query_pos = lax.axis_index(CTX) * tokens_here + jnp.arange(tokens_here, dtype=jnp.int32)
     key_pos = jnp.arange(seq_total, dtype=jnp.int32)
     same_doc = key_codes[None, :] == (segments[0] + 1)[:, None]
     allowed = (key_pos[None, :] <= query_pos[:, None]) & (
@@ -204,14 +206,14 @@
     recv_rows, recv_grads = (
         lax.all_to_all(
             send_rows.reshape(experts_all, capacity, model_width),
-            ("experts", "context"),
+            (EXP, CTX),
             split_axis=0,
             concat_axis=0,
             tiled=True,
         ),
         lax.all_to_all(
             send_grads.reshape(experts_all, capacity, model_width),
-            ("experts", "context"),
+            (EXP, CTX),
             split_axis=0,
             concat_axis=0,
             tiled=True,
@@ -244,7 +246,7 @@
         "erf,efd->erd", hidden_e, ex_down, preferred_element_type=jnp.float32
     ).astype(jnp.bfloat16)
     returned = lax.all_to_all(
-        to_owner(result_e), ("experts", "context"), split_axis=0, concat_axis=0, tiled=True
+        to_owner(result_e), (EXP, CTX), split_axis=0, concat_axis=0, tiled=True
     )
     picked = returned.reshape(experts_all * capacity, model_width)[target]
     picked = jnp.where(kept_rows[:, None], picked, jnp.zeros_like(picked)).astype(jnp.float32)
@@ -266,9 +268,9 @@
         "erd,erf->edf", expert_rows, up_grad_e, preferred_element_type=jnp.float32
     )
     expert_sums = (
-        lax.psum_scatter(grad_ex_gate, "dp", scatter_dimension=1, tiled=True),
-        lax.psum_scatter(grad_ex_up, "dp", scatter_dimension=1, tiled=True),
-        lax.psum_scatter(grad_ex_down, "dp", scatter_dimension=2, tiled=True),
+        lax.psum_scatter(grad_ex_gate, DP, scatter_dimension=1, tiled=True),
+        lax.psum_scatter(grad_ex_up, DP, scatter_dimension=1, tiled=True),
+        lax.psum_scatter(grad_ex_down, DP, scatter_dimension=2, tiled=True),
     )
     rows_grad_e = jnp.einsum(
         "erf,edf->erd", gate_grad_e, ex_gate, preferred_element_type=jnp.float32
@@ -278,7 +280,7 @@
         + jnp.einsum("erf,edf->erd", up_grad_e, ex_up, preferred_element_type=jnp.float32)
     ).astype(jnp.bfloat16)
     returned_grads = lax.all_to_all(
-        to_owner(rows_grad_e), ("experts", "context"), split_axis=0, concat_axis=0, tiled=True
+        to_owner(rows_grad_e), (EXP, CTX), split_axis=0, concat_axis=0, tiled=True
     )
     routed_grad = returned_grads.reshape(experts_all * capacity, model_width)[target]
     routed_grad = jnp.where(kept_rows[:, None], routed_grad, jnp.zeros_like(routed_grad)).astype(
@@ -309,8 +311,8 @@
     shared_rows_grad = shared_rows_grad + jnp.dot(
         up_grad_s, sh_up.T, preferred_element_type=jnp.float32
     )
-    groups = lax.axis_size("experts")
-    parts_cd = lax.axis_size(("context", "dp"))
+    groups = lax.axis_size(EXP)
+    parts_cd = lax.axis_size((CTX, DP))
     rows_count = rows_group.shape[0]
     arr_gate = jnp.einsum(
         "td,tes->eds",
@@ -331,9 +333,9 @@
         preferred_element_type=jnp.float32,
     ).reshape(-1, model_width // parts_cd)
     sums_gate, sums_up, sums_down = (
-        lax.psum_scatter(arr_gate, ("experts", "context", "dp"), scatter_dimension=0, tiled=True),
-        lax.psum_scatter(arr_up, ("experts", "context", "dp"), scatter_dimension=0, tiled=True),
-        lax.psum_scatter(arr_down, ("experts", "context", "dp"), scatter_dimension=0, tiled=True),
+        lax.psum_scatter(arr_gate, (EXP, CTX, DP), scatter_dimension=0, tiled=True),
+        lax.psum_scatter(arr_up, (EXP, CTX, DP), scatter_dimension=0, tiled=True),
+        lax.psum_scatter(arr_down, (EXP, CTX, DP), scatter_dimension=0, tiled=True),
     )
     norm_grad = norm_grad + shared_rows_grad
     residual_grad, grad_gain_two = norm_back(residual, inv_two, g_two, norm_grad)
@@ -348,8 +350,8 @@
         (head_q, head_k, head_v, to_heads(attended_grad), log_total),
     )
     key_sum, value_sum = (
-        lax.psum_scatter(from_heads(head_k_grad), "context", scatter_dimension=0, tiled=True),
-        lax.psum_scatter(from_heads(head_v_grad), "context", scatter_dimension=0, tiled=True),
+        lax.psum_scatter(from_heads(head_k_grad), CTX, scatter_dimension=0, tiled=True),
+        lax.psum_scatter(from_heads(head_v_grad), CTX, scatter_dimension=0, tiled=True),
     )
     query_low = from_heads(head_q_grad).astype(jnp.bfloat16)
     key_low = key_sum.astype(jnp.bfloat16)
@@ -364,20 +366,20 @@
     input_grad = (residual_grad + input_part).astype(jnp.bfloat16)
     dense = (
         lax.psum_scatter(
-            grad_gain_one, ("experts", "context", "dp"), scatter_dimension=0, tiled=True
+            grad_gain_one, (EXP, CTX, DP), scatter_dimension=0, tiled=True
         ),
-        lax.psum_scatter(grad_query, ("experts", "context", "dp"), scatter_dimension=0, tiled=True),
-        lax.psum_scatter(grad_key, ("experts", "context", "dp"), scatter_dimension=0, tiled=True),
-        lax.psum_scatter(grad_value, ("experts", "context", "dp"), scatter_dimension=0, tiled=True),
-        lax.psum_scatter(grad_out_w, ("experts", "context", "dp"), scatter_dimension=0, tiled=True),
+        lax.psum_scatter(grad_query, (EXP, CTX, DP), scatter_dimension=0, tiled=True),
+        lax.psum_scatter(grad_key, (EXP, CTX, DP), scatter_dimension=0, tiled=True),
+        lax.psum_scatter(grad_value, (EXP, CTX, DP), scatter_dimension=0, tiled=True),
+        lax.psum_scatter(grad_out_w, (EXP, CTX, DP), scatter_dimension=0, tiled=True),
         lax.psum_scatter(
-            grad_gain_two, ("experts", "context", "dp"), scatter_dimension=0, tiled=True
+            grad_gain_two, (EXP, CTX, DP), scatter_dimension=0, tiled=True
         ),
         lax.psum_scatter(
-            grad_router, ("experts", "context", "dp"), scatter_dimension=0, tiled=True
+            grad_router, (EXP, CTX, DP), scatter_dimension=0, tiled=True
         ),
         lax.psum_scatter(
-            grad_gate_vec, ("experts", "context", "dp"), scatter_dimension=0, tiled=True
+            grad_gate_vec, (EXP, CTX, DP), scatter_dimension=0, tiled=True
         ),
     )
     return (
@@ -398,9 +400,6 @@
         expert_sums[1],
         expert_sums[2],
     )
-
-PLANE = ("experts", "context")
-
 
 def attention_probs(q_blk, k_part, q_code, k_code, first_row, scale_factor):
     scores = lax.dot_general(
@@ -518,6 +517,268 @@
     )(*operands)
 
 
+MESH_ID = pl.DeviceIdType.MESH
+
+
+def other_in_pair(index, bit):
+    return index + bit - 2 * bit * (lax.div(index, bit) % 2)
+
+
+def plane_places():
+    at = lax.axis_index(EXP)
+    core = lax.axis_index(CTX)
+    across, along = other_in_pair(at, 1), other_in_pair(at, 2)
+    return at, core, across, along, other_in_pair(along, 1)
+
+
+def greet(across, along, core):
+    barrier = pltpu.get_barrier_semaphore()
+    for target in ({EXP: across}, {EXP: along}, {CTX: 1 - core}):
+        pl.semaphore_signal(barrier, inc=1, device_id=target, device_id_type=MESH_ID)
+    pl.semaphore_wait(barrier, 3)
+
+
+def plane_gather_kernel(with_info, relative, *refs):
+    if with_info:
+        own_ref, info_ref, all_ref, info_all_ref, send_sem, recv_sem, local_sem = refs
+    else:
+        own_ref, all_ref, send_sem, recv_sem, local_sem = refs
+    at, core, across, along, far = plane_places()
+    rows = own_ref.shape[0]
+    half = rows // 2
+    top, bottom, whole = pl.ds(0, half), pl.ds(half, half), pl.ds(0, rows)
+    greet(across, along, core)
+    started = []
+    twin_id = {CTX: 1 - core}
+
+    def slot_of(place, shift, for_twin):
+        if relative:
+            return shift + 4 * for_twin
+        return place * 2 + core
+
+    def send(number, src, dst, target):
+        copy = pltpu.make_async_remote_copy(
+            src_ref=src,
+            dst_ref=dst,
+            send_sem=send_sem.at[number],
+            recv_sem=recv_sem.at[number],
+            device_id=target,
+            device_id_type=MESH_ID,
+        )
+        copy.start()
+        started.append(copy)
+        return copy
+
+    def piece(place, shift, part, for_twin=0):
+        return all_ref.at[slot_of(place, shift, for_twin), part]
+
+    x_top = send(0, own_ref.at[top], piece(at, 1, top), {EXP: across})
+    y_bottom = send(1, own_ref.at[bottom], piece(at, 2, bottom), {EXP: along})
+    x_bottom = send(2, own_ref.at[bottom], piece(at, 1, bottom), {EXP: across})
+    y_top = send(3, own_ref.at[top], piece(at, 2, top), {EXP: along})
+    twins = [send(4, own_ref, piece(at, 0, whole, 1), twin_id)]
+    heres = [pltpu.make_async_copy(own_ref, piece(at, 0, whole), local_sem.at[0])]
+    heres[0].start()
+    if with_info:
+        info_at = lambda place: info_all_ref.at[place * 2 + core]
+        heres.append(pltpu.make_async_copy(info_ref, info_at(at), local_sem.at[1]))
+        heres[1].start()
+        info_x = send(13, info_ref, info_at(at), {EXP: across})
+        info_y = send(14, info_ref, info_at(at), {EXP: along})
+        twins.append(send(15, info_ref, info_at(at), twin_id))
+        info_x.wait_recv()
+        info_far = send(16, info_at(across), info_at(across), {EXP: along})
+        twins.append(send(17, info_at(across), info_at(across), twin_id))
+        info_y.wait_recv()
+        twins.append(send(18, info_at(along), info_at(along), twin_id))
+        info_far.wait_recv()
+        twins.append(send(19, info_at(far), info_at(far), twin_id))
+
+    def hand_on(number, place, shift, part):
+        src = piece(place, shift, part)
+        twins.append(send(number, src, piece(place, shift, part, 1), twin_id))
+
+    x_top.wait_recv()
+    far_top = send(5, piece(across, 1, top), piece(across, 3, top), {EXP: along})
+    hand_on(6, across, 1, top)
+    y_bottom.wait_recv()
+    far_bottom = send(7, piece(along, 2, bottom), piece(along, 3, bottom), {EXP: across})
+    hand_on(8, along, 2, bottom)
+    x_bottom.wait_recv()
+    hand_on(9, across, 1, bottom)
+    y_top.wait_recv()
+    hand_on(10, along, 2, top)
+    far_top.wait_recv()
+    hand_on(11, far, 3, top)
+    far_bottom.wait_recv()
+    hand_on(12, far, 3, bottom)
+    for copy in twins:
+        copy.wait_recv()
+    for copy in started:
+        copy.wait_send()
+    for copy in heres:
+        copy.wait()
+
+
+def plane_gather(own, info, relative, number):
+    plane = lax.axis_size(PLANE)
+    operands = [own] if info is None else [own, info]
+    outs = [jax.ShapeDtypeStruct((plane, *v.shape), v.dtype) for v in operands]
+    anywhere = pl.BlockSpec(memory_space=pl.ANY)
+    return pl.pallas_call(
+        partial(plane_gather_kernel, info is not None, relative),
+        out_shape=outs,
+        in_specs=[anywhere] * len(operands),
+        out_specs=[anywhere] * len(operands),
+        scratch_shapes=[
+            pltpu.SemaphoreType.DMA((20,)),
+            pltpu.SemaphoreType.DMA((20,)),
+            pltpu.SemaphoreType.DMA((2,)),
+        ],
+        compiler_params=pltpu.CompilerParams(collective_id=number, has_side_effects=True),
+        cost_estimate=pl.CostEstimate(
+            flops=0, bytes_accessed=100 * own.size, transcendentals=0
+        ),
+    )(*operands)
+
+
+def plane_scatter_kernel(
+    relative,
+    part_ref,
+    out_ref,
+    own,
+    twin_got,
+    x_got,
+    y_got,
+    x_last,
+    y_last,
+    send_sem,
+    recv_sem,
+    local_sem,
+):
+    at, core, across, along, far = plane_places()
+    rows = part_ref.shape[1]
+    half = rows // 2
+    step = 64
+    greet(across, along, core)
+    started = []
+
+    def send(number, src, dst, target):
+        copy = pltpu.make_async_remote_copy(
+            src_ref=src,
+            dst_ref=dst,
+            send_sem=send_sem.at[number],
+            recv_sem=recv_sem.at[number],
+            device_id=target,
+            device_id_type=MESH_ID,
+        )
+        copy.start()
+        started.append(copy)
+        return copy
+
+    twins, heres = [], []
+    for j, (label, shift) in enumerate(((far, 3), (across, 1), (along, 2), (at, 0))):
+        theirs = shift + 4 if relative else label * 2 + 1 - core
+        ours = shift if relative else label * 2 + core
+        twins.append(send(j, part_ref.at[theirs], twin_got.at[j], {CTX: 1 - core}))
+        here = pltpu.make_async_copy(part_ref.at[ours], own.at[j], local_sem.at[j])
+        here.start()
+        heres.append(here)
+
+    def add_rows(target, t_first, count, source, s_first):
+        @pl.loop(0, count // step)
+        def _(i):
+            into = pl.ds(pl.multiple_of(t_first + i * step, step), step)
+            take = pl.ds(pl.multiple_of(s_first + i * step, step), step)
+            total = target[into].astype(jnp.float32) + source[take].astype(jnp.float32)
+            target[into] = total.astype(target.dtype)
+
+    top, bottom = pl.ds(0, half), pl.ds(half, half)
+    x_sent, y_sent = [], []
+    for j in range(4):
+        twins[j].wait_recv()
+        heres[j].wait()
+        add_rows(own.at[j], 0, rows, twin_got.at[j], 0)
+        if j < 2:
+            x_sent.append(send(4 + j, own.at[j, top], x_got.at[j], {EXP: across}))
+        if j == 0 or j == 2:
+            y_sent.append(send(6 + j // 2, own.at[j, bottom], y_got.at[j // 2], {EXP: along}))
+    x_sent[0].wait_recv()
+    add_rows(own.at[2], 0, half, x_got.at[0], 0)
+    last_y = send(8, own.at[2, top], y_last, {EXP: along})
+    y_sent[0].wait_recv()
+    add_rows(own.at[1], half, half, y_got.at[0], 0)
+    last_x = send(9, own.at[1, bottom], x_last, {EXP: across})
+
+    def finish(first, near, later):
+        @pl.loop(0, half // step)
+        def _(i):
+            take = pl.ds(pl.multiple_of(i * step, step), step)
+            into = pl.ds(pl.multiple_of(first + i * step, step), step)
+            out_ref[into] = (
+                own[3, into].astype(jnp.float32)
+                + near[1, take].astype(jnp.float32)
+                + later[take].astype(jnp.float32)
+            ).astype(out_ref.dtype)
+
+    x_sent[1].wait_recv()
+    last_y.wait_recv()
+    finish(0, x_got, y_last)
+    y_sent[1].wait_recv()
+    last_x.wait_recv()
+    finish(half, y_got, x_last)
+    for copy in started:
+        copy.wait_send()
+
+
+def plane_scatter(parts, relative, number, out_type):
+    plane, rows, cols = parts.shape
+    half = rows // 2
+    vmem = lambda *shape: pltpu.VMEM(shape, parts.dtype)
+    return pl.pallas_call(
+        partial(plane_scatter_kernel, relative),
+        out_shape=jax.ShapeDtypeStruct((rows, cols), out_type),
+        in_specs=[pl.BlockSpec(memory_space=pl.ANY)],
+        out_specs=pl.BlockSpec(memory_space=pltpu.VMEM),
+        scratch_shapes=[
+            vmem(4, rows, cols),
+            vmem(4, rows, cols),
+            vmem(2, half, cols),
+            vmem(2, half, cols),
+            vmem(half, cols),
+            vmem(half, cols),
+            pltpu.SemaphoreType.DMA((10,)),
+            pltpu.SemaphoreType.DMA((10,)),
+            pltpu.SemaphoreType.DMA((4,)),
+        ],
+        compiler_params=pltpu.CompilerParams(
+            collective_id=number, has_side_effects=True, vmem_limit_bytes=44 * 2**20
+        ),
+        cost_estimate=pl.CostEstimate(
+            flops=0, bytes_accessed=100 * rows * cols, transcendentals=0
+        ),
+    )(parts)
+
+
+def swap(values, bits):
+    return lax.ppermute(values, EXP, [(i, i ^ bits) for i in range(4)])
+
+
+def twin(values):
+    return lax.ppermute(values, CTX, [(0, 1), (1, 0)])
+
+
+def hop_sum(ours, theirs):
+    got = twin(theirs)
+    sums = [
+        low(ours[k].astype(jnp.float32) + got[k].astype(jnp.float32)) for k in range(4)
+    ]
+    total = sums[0].astype(jnp.float32)
+    for k in (1, 2, 3):
+        total = total + swap(sums[k], k).astype(jnp.float32)
+    return total
+
+
 def mm(left, right, dims=((1,), (0,))):
     return lax.dot_general(left, right, (dims, ((), ())), preferred_element_type=jnp.float32)
 
@@ -549,11 +810,11 @@
     expert_w_down,
 ):
     plane = lax.axis_size(PLANE)
-    groups = lax.axis_size("experts")
-    halves = lax.axis_size("context")
-    depth = lax.axis_size("dp")
+    groups = lax.axis_size(EXP)
+    halves = lax.axis_size(CTX)
+    depth = lax.axis_size(DP)
     me = lax.axis_index(PLANE)
-    core = lax.axis_index("context")
+    core = lax.axis_index(CTX)
     tokens, width = hidden.shape[1], hidden.shape[2]
     all_tokens = plane * tokens
     seq_len = halves * tokens
@@ -561,42 +822,51 @@
     head_cols = width // plane
     shard = width // depth
 
-    small = jnp.concatenate(
-        [
-            norm1_gain[None],
-            norm2_gain[None],
-            shared_gate_vec[None],
-            jnp.zeros((5, shard), jnp.bfloat16),
-            router.T,
-        ]
-    )
-    small = lax.all_gather(small, "dp", axis=0, tiled=False)
-    small = small.transpose(1, 0, 2).reshape(-1, width)
-    g_one = small[0].astype(jnp.float32)
-    g_two = small[1].astype(jnp.float32)
-    gate_vec = small[2]
-    router_t = small[8:]
     token_info = jnp.concatenate(
         [segments + 1, jnp.where(padding > 0, segments + 1, 0), order[0], routes[0].T]
     )
     info_rows = token_info.shape[0]
     token_info = jnp.concatenate([token_info, jnp.zeros((8 - info_rows, tokens), jnp.int32)])
-    info_all = lax.all_gather(token_info, PLANE, axis=0, tiled=False)
-
-    hidden_all = lax.all_gather(hidden[0], PLANE, axis=0, tiled=True)
+
+    hidden_all, info_all = plane_gather(hidden[0], token_info, False, 0)
+    hidden_all = hidden_all.reshape(all_tokens, width)
+    place = lax.axis_index(EXP)
+    away = [(place ^ k) * 2 + (core ^ j) for j in (0, 1) for k in range(4)]
+    away = jnp.stack(away)
+    cot_own, _ = lax.optimization_barrier((cotangent[0], info_all))
+    cot_near = jnp.stack([cot_own, swap(cot_own, 1), swap(cot_own, 2), swap(cot_own, 3)])
+    cot_all = jnp.concatenate([cot_near, twin(cot_near)]).reshape(all_tokens, width)
     w_qkv_part = jnp.concatenate(
         [
             lax.dynamic_slice(w, (0, me * head_cols), (shard, head_cols))
             for w in (w_query, w_key, w_value)
-        ],
+        ]
+        + [router, norm1_gain[:, None], norm2_gain[:, None], shared_gate_vec[:, None]]
+        + [jnp.zeros((shard, 128 - experts_all - 3), jnp.bfloat16)],
         axis=1,
     )
-    w_qkv = lax.all_gather(w_qkv_part, "dp", axis=0, tiled=True)
+    w_qkv = lax.all_gather(w_qkv_part, DP, axis=0, tiled=True)
+    small = w_qkv[:, 3 * head_cols :].T
+    w_qkv = w_qkv[:, : 3 * head_cols]
+    router_t = small[:experts_all]
+    g_one = small[experts_all].astype(jnp.float32)
+    g_two = small[experts_all + 1].astype(jnp.float32)
+    gate_vec = small[experts_all + 2]
     out_rows = shard // plane
     w_out_part = lax.dynamic_slice(w_out, (me * out_rows, 0), (out_rows, width))
-    w_out_part = lax.all_gather(w_out_part, "dp", axis=0, tiled=False)
-    w_out_full = lax.all_gather(w_out_part, PLANE, axis=0, tiled=False)
-    w_out_full = w_out_full.transpose(1, 0, 2, 3).reshape(width, width)
+    w_out_part = lax.all_gather(w_out_part, DP, axis=0, tiled=False)
+    pieces = [w_out_part] + [swap(w_out_part, k) for k in (1, 2, 3)]
+    w_out_near = jnp.zeros((depth, groups, 1, out_rows, width), jnp.bfloat16)
+    for k in range(4):
+        w_out_near = lax.dynamic_update_slice(
+            w_out_near, pieces[k][:, None, None], (0, place ^ k, 0, 0, 0)
+        )
+    w_out_far = twin(w_out_near)
+    w_out_full = jnp.where(
+        core == 0,
+        jnp.concatenate([w_out_near, w_out_far], axis=2),
+        jnp.concatenate([w_out_far, w_out_near], axis=2),
+    ).reshape(width, width)
 
     def normed(values, gain):
         values = values.astype(jnp.float32)
@@ -626,37 +896,37 @@
     residual = x_rows + mm(attended, w_out_full)
     residual, inv_two, n2 = normed(residual, g_two)
 
-    n2_all = lax.all_gather(n2, PLANE, axis=0, tiled=True)
-    cot_all = lax.all_gather(cotangent[0], PLANE, axis=0, tiled=True)
+    n2, cot_all = lax.optimization_barrier((n2, cot_all))
+    n2_all = plane_gather(n2, None, True, 2)[0].reshape(all_tokens, width)
     units = shared_w_gate.shape[1]
     part = units // (depth * halves)
     pick = lambda w: lax.dynamic_index_in_dim(
         w.reshape(w.shape[0], depth, halves, part), core, axis=2, keepdims=False
     ).reshape(w.shape[0], depth * part)
-    sh_gate = lax.all_gather(pick(shared_w_gate), "dp", axis=0, tiled=True)
-    sh_up = lax.all_gather(pick(shared_w_up), "dp", axis=0, tiled=True)
+    sh_gate = lax.all_gather(pick(shared_w_gate), DP, axis=0, tiled=True)
+    sh_up = lax.all_gather(pick(shared_w_up), DP, axis=0, tiled=True)
     sh_down = lax.all_gather(
-        lax.dynamic_slice(shared_w_down, (core * part, 0), (part, width)), "dp", axis=0, tiled=True
-    )
-    ex_gate = lax.all_gather(expert_w_gate[0], "dp", axis=0, tiled=True)
-    ex_up = lax.all_gather(expert_w_up[0], "dp", axis=0, tiled=True)
-    ex_down = lax.all_gather(expert_w_down[0], "dp", axis=1, tiled=True)
-
-    def router_of(rows_in):
-        z = mm(rows_in, router_t, ((1,), (1,)))
+        lax.dynamic_slice(shared_w_down, (core * part, 0), (part, width)), DP, axis=0, tiled=True
+    )
+    ex_gate = lax.all_gather(expert_w_gate[0], DP, axis=0, tiled=True)
+    ex_up = lax.all_gather(expert_w_up[0], DP, axis=0, tiled=True)
+    ex_down = lax.all_gather(expert_w_down[0], DP, axis=1, tiled=True)
+
+    small_w = jnp.concatenate([router_t, gate_vec[None]])
+
+    def gates_of(rows_in):
+        both = mm(rows_in, small_w, ((1,), (1,)))
+        z = both[:, :experts_all]
         e = jnp.exp(z - jnp.max(z, axis=1, keepdims=True))
-        return e / jnp.sum(e, axis=1, keepdims=True)
-
-    def shared_gate_of(rows_in):
-        return jax.nn.sigmoid(mm(rows_in, gate_vec[:, None]))
-
-    probs_all = router_of(n2_all)
-    sg_all = shared_gate_of(n2_all)
+        return e / jnp.sum(e, axis=1, keepdims=True), jax.nn.sigmoid(both[:, experts_all:])
+
+    probs_all, sg_all = gates_of(n2_all)
     expert_gate = lax.dynamic_slice(probs_all, (0, me), (all_tokens, 1))
 
     capacity = (9 * tokens * TOP + 8 * experts_all - 1) // (8 * experts_all)
-    order_all = info_all[:, 2]
-    routed_here = jnp.any(info_all[:, 3 : 3 + TOP] == me, axis=1)
+    info_away = info_all[away]
+    order_all = info_away[:, 2]
+    routed_here = jnp.any(info_away[:, 3 : 3 + TOP] == me, axis=1)
     earlier = (order_all[:, None, :] < order_all[:, :, None]) & routed_here[:, None, :]
     slots = jnp.sum(earlier.astype(jnp.int32), axis=2)
     slots = jnp.where(routed_here, slots, capacity)
@@ -664,19 +934,19 @@
     onehot = chosen.astype(jnp.bfloat16)
 
     def rows_of(values):
-        got = jnp.einsum(
-            "bst,btd->bsd",
+        got = lax.dot_general(
             onehot,
             values.reshape(plane, tokens, width),
+            (((2,), (1,)), ((0,), (0,))),
             preferred_element_type=jnp.float32,
         )
         return got.reshape(plane * capacity, width)
 
     def back_to_tokens(values):
-        got = jnp.einsum(
-            "bst,bsd->btd",
+        got = lax.dot_general(
             onehot,
             values.reshape(plane, capacity, width),
+            (((1,), (1,)), ((0,), (0,))),
             preferred_element_type=jnp.float32,
         )
         return got.reshape(all_tokens, width)
@@ -699,27 +969,24 @@
     gate_grad_s = low(shared_hgrad * up_pre * silu_grad(gate_pre))
     up_grad_s = low(shared_hgrad * gate_act)
 
+    rows_out = width // (halves * depth)
+
+    def own_units(grad):
+        grad = low(grad).reshape(depth * part, halves, depth, rows_out).transpose(2, 0, 1, 3)
+        return grad.reshape(depth * depth * part, halves * rows_out)
+
     def shared_scatter(grad):
-        halved = lax.all_to_all(
-            low(grad).reshape(halves, width // halves, depth * part),
-            "context",
-            split_axis=0,
-            concat_axis=0,
-            tiled=True,
-        )
-        rows_out = width // (halves * depth)
-        halved = (
-            halved.reshape(halves, depth, rows_out, depth * part)
-            .transpose(1, 2, 0, 3)
-            .reshape(depth * rows_out, units)
-        )
-        total = lax.psum_scatter(halved, "dp", scatter_dimension=0, tiled=True)
-        total = total.reshape(rows_out, halves, depth, part).transpose(0, 2, 1, 3)
-        return total.reshape(rows_out, units).astype(jnp.float32)
-
-    grad_sh_gate = shared_scatter(mm(n2_all, gate_grad_s, ((0,), (0,))))
-    grad_sh_up = shared_scatter(mm(n2_all, up_grad_s, ((0,), (0,))))
-    grad_sh_down = shared_scatter(mm(shared_grads, shared_hidden, ((0,), (0,)))).T
+        total = lax.psum_scatter(grad, DP, scatter_dimension=0, tiled=True)
+        total = total.reshape(depth * part, halves, rows_out)
+        keep = lax.dynamic_index_in_dim(total, core, axis=1, keepdims=False)
+        give = lax.dynamic_index_in_dim(total, 1 - core, axis=1, keepdims=False)
+        both = jnp.stack([keep, twin(give)]).reshape(halves, depth, part, rows_out)
+        both = jnp.where(core == 0, both, both[::-1]).transpose(1, 0, 2, 3)
+        return both.reshape(units, rows_out).astype(jnp.float32)
+
+    grad_sh_gate = own_units(mm(gate_grad_s, n2_all, ((0,), (0,))))
+    grad_sh_up = own_units(mm(up_grad_s, n2_all, ((0,), (0,))))
+    grad_sh_down = own_units(mm(shared_hidden, shared_grads, ((0,), (0,))))
 
     gate_e = mm(expert_rows, ex_gate)
     up_e = mm(expert_rows, ex_up)
@@ -735,34 +1002,39 @@
     up_grad_e = low(hgrad_e * act_e)
 
     def expert_scatter(grad, dim):
-        return lax.psum_scatter(low(grad), "dp", scatter_dimension=dim, tiled=True).astype(
+        return lax.psum_scatter(grad, DP, scatter_dimension=dim, tiled=True).astype(
             jnp.float32
         )[None]
 
-    grad_ex_down = expert_scatter(mm(hidden_e, row_grads, ((0,), (0,))), 1)
-    grad_ex_gate = expert_scatter(mm(expert_rows, gate_grad_e, ((0,), (0,))), 0)
-    grad_ex_up = expert_scatter(mm(expert_rows, up_grad_e, ((0,), (0,))), 0)
+    grad_ex_down = low(mm(hidden_e, row_grads, ((0,), (0,))))
+    grad_ex_gate = low(mm(expert_rows, gate_grad_e, ((0,), (0,))))
+    grad_ex_up = low(mm(expert_rows, up_grad_e, ((0,), (0,))))
     rows_grad = low(
         mm(gate_grad_e, ex_gate, ((1,), (1,))) + mm(up_grad_e, ex_up, ((1,), (1,)))
     )
 
     out_part = low(sg_all * shared_part + expert_gate * back_to_tokens(result_e))
-    out_sum = lax.psum_scatter(out_part, PLANE, scatter_dimension=0, tiled=True)
-    output = low(residual + out_sum.astype(jnp.float32))
+    out_part = out_part.reshape(plane, tokens, width)
+    output = low(residual + hop_sum(out_part[:4], out_part[4:]))
     n2_grad_part = low(
         mm(gate_grad_s, sh_gate, ((1,), (1,)))
         + mm(up_grad_s, sh_up, ((1,), (1,)))
         + back_to_tokens(rows_grad)
     )
-    n2_grad = lax.psum_scatter(n2_grad_part, PLANE, scatter_dimension=0, tiled=True).astype(
-        jnp.float32
-    )
+    grads = (grad_sh_gate, grad_sh_up, grad_sh_down, grad_ex_down, grad_ex_gate, grad_ex_up)
+    n2_grad_part, grads = lax.optimization_barrier((n2_grad_part, grads))
+    grad_sh_gate, grad_sh_up, grad_sh_down = [shared_scatter(v) for v in grads[:3]]
+    grad_sh_gate, grad_sh_up = grad_sh_gate.T, grad_sh_up.T
+    grad_ex_down = expert_scatter(grads[3], 1)
+    grad_ex_gate, grad_ex_up = [expert_scatter(v, 0) for v in grads[4:]]
+    n2_grad = plane_scatter(n2_grad_part.reshape(plane, tokens, width), True, 3, jnp.float32)
 
     dots = jnp.stack([gate_dots, cot_dot_shared.reshape(plane, tokens)], axis=1)
+    back = jnp.arange(plane, dtype=jnp.int32) ^ me
+    dots = dots[(back // 2) + 4 * (back % 2)]
     dots = lax.all_to_all(dots, PLANE, split_axis=0, concat_axis=0, tiled=True)
     probs_grad = dots[:, 0].T
-    probs = router_of(n2)
-    sg = shared_gate_of(n2)
+    probs, sg = gates_of(n2)
     logit_grad = low(probs * (probs_grad - jnp.sum(probs * probs_grad, axis=1, keepdims=True)))
     sg_logit_grad = low(jnp.sum(dots[:, 1], axis=0)[:, None] * sg * (1.0 - sg))
     small_grads = mm(n2, jnp.concatenate([logit_grad, sg_logit_grad], axis=1), ((0,), (0,)))
@@ -775,13 +1047,32 @@
     residual_grad = residual_grad + cot_rows
     low_residual = low(residual_grad)
 
+    small_grads = jnp.concatenate([small_grads, grad_gain_two[:, None]], axis=1).T
+    small_grads = jnp.pad(small_grads, ((0, 14 - experts_all), (0, 0)))
+    small_grads = small_grads.reshape(16, plane, width // plane).transpose(1, 0, 2)
+    small_grads = jnp.sum(
+        lax.all_to_all(small_grads, PLANE, split_axis=0, concat_axis=0, tiled=True), axis=0
+    )
+    small_grads = small_grads.reshape(16, depth, shard // plane).transpose(1, 0, 2)
+    small_grads = jnp.sum(
+        lax.all_to_all(small_grads, DP, split_axis=0, concat_axis=0, tiled=True), axis=0
+    )
     grad_out = low(mm(attended, low_residual, ((0,), (0,))))
-    grad_out = lax.psum_scatter(grad_out, PLANE, scatter_dimension=0, tiled=True)
-    grad_out = lax.psum_scatter(grad_out, "dp", scatter_dimension=0, tiled=True).astype(jnp.float32)
+    grad_out = grad_out.reshape(groups, halves, width // plane, width)
+    block_of = lambda k, c: lax.dynamic_slice(
+        grad_out, (place ^ k, c, 0, 0), (1, 1, width // plane, width)
+    )[0, 0]
+    grad_out = low(
+        hop_sum(
+            [block_of(k, core) for k in range(4)],
+            jnp.stack([block_of(k, 1 - core) for k in range(4)]),
+        )
+    )
+    grad_out = lax.psum_scatter(grad_out, DP, scatter_dimension=0, tiled=True).astype(jnp.float32)
     attended_grad = to_columns(low(mm(low_residual, w_out_full, ((1,), (1,)))))
     qkv_grad = attention_call(qkv, attended_grad, q_codes, k_codes, seq_len)
     n1_grad = low(mm(qkv_grad, w_qkv, ((1,), (1,))))
-    n1_grad = lax.psum_scatter(n1_grad, PLANE, scatter_dimension=0, tiled=True).astype(jnp.float32)
+    n1_grad = plane_scatter(n1_grad.reshape(plane, tokens, width), False, 1, jnp.float32)
     grad_qkv = low(mm(n1_all, qkv_grad, ((0,), (0,))))
     fine = shard // plane
     grad_qkv = (
@@ -789,7 +1080,21 @@
         .transpose(1, 0, 2, 3)
         .reshape(width, 3 * head_cols)
     )
-    grad_qkv = lax.psum_scatter(grad_qkv, "dp", scatter_dimension=0, tiled=True)
+    grad_qkv = lax.psum_scatter(grad_qkv, DP, scatter_dimension=0, tiled=True)
+    w_rows = (
+        w_qkv.reshape(plane, depth, fine, 3 * head_cols)
+        .transpose(1, 0, 2, 3)
+        .reshape(depth, plane * fine, 3 * head_cols)
+    )
+    w_rows = lax.dynamic_index_in_dim(w_rows, lax.axis_index(DP), axis=0, keepdims=False)
+    gain_dots = jnp.sum(grad_qkv.astype(jnp.float32) * w_rows.astype(jnp.float32), axis=1)
+    gain_dots = lax.all_to_all(
+        gain_dots.reshape(plane, 1, fine), PLANE, split_axis=0, concat_axis=0, tiled=True
+    )
+    my_gain = lax.dynamic_slice(
+        g_one, ((me * depth + lax.axis_index(DP)) * fine,), (fine,)
+    )
+    grad_gain_one = jnp.sum(gain_dots[:, 0], axis=0) / my_gain
     grad_qkv = lax.all_to_all(
         grad_qkv.reshape(plane, fine, 3 * head_cols),
         PLANE,
@@ -803,25 +1108,19 @@
         .reshape(3, fine, width)
         .astype(jnp.float32)
     )
-    input_part, grad_gain_one = norm_back(x_rows, inv_one, g_one, n1_grad)
+    input_part, _ = norm_back(x_rows, inv_one, g_one, n1_grad)
     input_grad = low(residual_grad + input_part)
-    small_grads = jnp.concatenate(
-        [small_grads, grad_gain_two[:, None], grad_gain_one[:, None]], axis=1
-    )
-    small_grads = lax.psum_scatter(
-        small_grads, ("experts", "context", "dp"), scatter_dimension=0, tiled=True
-    )
     return (
         output[None],
         input_grad[None],
-        small_grads[:, experts_all + 2],
+        grad_gain_one,
         grad_qkv[0],
         grad_qkv[1],
         grad_qkv[2],
         grad_out,
-        small_grads[:, experts_all + 1],
-        small_grads[:, :experts_all],
-        small_grads[:, experts_all],
+        small_grads[experts_all + 1],
+        small_grads[:experts_all].T,
+        small_grads[experts_all],
         grad_sh_gate,
         grad_sh_up,
         grad_sh_down,
@@ -833,49 +1132,50 @@
 
 def solution(mesh):
     in_specs = (
-        P(("experts", "dp"), "context", None),
-        P(("experts", "dp"), "context", None),
-        P(("experts", "dp"), "context"),
-        P(("experts", "dp"), "context"),
-        P(("experts", "dp"), "context", None),
-        P(("experts", "dp"), "context", None),
-        P("dp"),
-        P("dp", None),
-        P("dp", None),
-        P("dp", None),
-        P("dp", None),
-        P("dp"),
-        P("dp", None),
-        P("dp"),
-        P("dp", "experts"),
-        P("dp", "experts"),
-        P(("experts", "dp"), None),
-        P(("experts", "context"), "dp", None),
-        P(("experts", "context"), "dp", None),
-        P(("experts", "context"), None, "dp"),
+        P((EXP, DP), CTX, None),
+        P((EXP, DP), CTX, None),
+        P((EXP, DP), CTX),
+        P((EXP, DP), CTX),
+        P((EXP, DP), CTX, None),
+        P((EXP, DP), CTX, None),
+        P(DP),
+        P(DP, None),
+        P(DP, None),
+        P(DP, None),
+        P(DP, None),
+        P(DP),
+        P(DP, None),
+        P(DP),
+        P(DP, EXP),
+        P(DP, EXP),
+        P((EXP, DP), None),
+        P((EXP, CTX), DP, None),
+        P((EXP, CTX), DP, None),
+        P((EXP, CTX), None, DP),
     )
     out_specs = (
-        P(("experts", "dp"), "context", None),
-        P(("experts", "dp"), "context", None),
-        P(("experts", "context", "dp")),
-        P(("experts", "context", "dp"), None),
-        P(("experts", "context", "dp"), None),
-        P(("experts", "context", "dp"), None),
-        P(("experts", "context", "dp"), None),
-        P(("experts", "context", "dp")),
-        P(("experts", "context", "dp"), None),
-        P(("experts", "context", "dp")),
-        P(("context", "dp"), "experts"),
-        P(("context", "dp"), "experts"),
-        P("experts", ("context", "dp")),
-        P(("experts", "context"), "dp", None),
-        P(("experts", "context"), "dp", None),
-        P(("experts", "context"), None, "dp"),
-    )
-    plane = mesh.shape["experts"] * mesh.shape["context"]
+        P((EXP, DP), CTX, None),
+        P((EXP, DP), CTX, None),
+        P((EXP, CTX, DP)),
+        P((EXP, CTX, DP), None),
+        P((EXP, CTX, DP), None),
+        P((EXP, CTX, DP), None),
+        P((EXP, CTX, DP), None),
+        P((EXP, CTX, DP)),
+        P((EXP, CTX, DP), None),
+        P((EXP, CTX, DP)),
+        P((CTX, DP), EXP),
+        P((CTX, DP), EXP),
+        P(EXP, (CTX, DP)),
+        P((EXP, CTX), DP, None),
+        P((EXP, CTX), DP, None),
+        P((EXP, CTX), None, DP),
+    )
+    plane = mesh.shape[EXP] * mesh.shape[CTX]
 
     def run(*args):
-        one_each = args[12].shape[1] == plane and HEADS % plane == 0
+        square = mesh.shape[EXP] == 4 and mesh.shape[CTX] == 2
+        one_each = square and args[12].shape[1] == plane
         local = local_plane if one_each else local_general
         return jax.shard_map(
             local, mesh=mesh, in_specs=in_specs, out_specs=out_specs, check_vma=False

time: 2230 us -> 1560 us (0.70)
  waiting for transfers between devices: 1320 us -> 223 us
  Pallas kernels: 49.9 us -> 441 us
  blocking collectives: 73.3 us -> 7.92 us
  local copies, waits for them, and re-layouts: 89 us -> 152 us
  other arithmetic: 61.6 us -> 113 us
  starting transfers between devices: 13.8 us -> 40.8 us
  matrix products: 589 us -> 566 us
    all_gather x11 -> x7, waiting for transfers between devices: 562 us -> 0.03 us  [the longest x1 0.02 us: local_plane(): ex_down = lax.all_gather(expert_w_down[0], DP, axis=1, tiled=True)]
    reduce_scatter x12 -> x8, waiting for transfers between devices: 611 us -> 81.2 us  [the longest x3 81.1 us: expert_scatter(): lax.psum_scatter(grad, DP, scatter_dimension=dim, tiled=True)]
    pallas_call x0 -> x4, Pallas kernels: none -> 390 us  [the longest x2 235 us: plane_scatter(): pl.pallas_call(partial(plane_scatter_kernel, relative), out_shape=jax.Sha...]
    unnamed x26 -> x16, waiting for transfers between devices: 134 us -> 3.64 us
    ppermute x0 -> x19, waiting for transfers between devices: none -> 104 us  [the longest x12 95.8 us: swap(): return lax.ppermute(values, EXP, [(i, i ^ bits) for i in range(4)])]
    all_to_all x4 -> x1, blocking collectives: 50.7 us -> 7.92 us  [local_plane(): lax.all_to_all(small_grads, PLANE, split_axis=0, concat_axis=0, tiled=True)]
    convert_element_type x3 -> x7, other arithmetic: 10.7 us -> 42.5 us  [low(): return values.astype(jnp.bfloat16)]
    all_gather x2 -> x0, blocking collectives: 22.6 us -> none  [the longest x1 13.1 us: local_plane(): small = lax.all_gather(small, 'dp', axis=0, tiled=False)]
  transfers between devices with their start and end apart: 28 -> 41, of which waited for: 21 -> 12; matrix products, arithmetic and copies ran while one was open for 28% -> 36% of each run, Pallas kernels for 2% -> 28%
where the time goes in v2:
time: 1560 us
  matrix products  566 us (36%)
  Pallas kernels  441 us (28%)
  waiting for transfers between devices  223 us (14%)
  local copies, waits for them, and re-layouts  152 us (10%)
  other arithmetic  113 us (7%)
  starting transfers between devices  40.8 us (3%)
  between operations  15.7 us (1%)
    dot_general x28, matrix products, mm(): lax.dot_general(left, right, (dims, ((), ())), preferred_element_type=jnp...  501 us
    pallas_call x2, Pallas kernels, plane_scatter(): pl.pallas_call(partial(plane_scatter_kernel, relative), out_shape=jax.Sha...  235 us
    pallas_call x2, Pallas kernels, plane_gather(): pl.pallas_call(partial(plane_gather_kernel, info is not None, relative),...  156 us
    ppermute x12, waiting for transfers between devices, swap(): return lax.ppermute(values, EXP, [(i, i ^ bits) for i in range(4)])  95.8 us
    reduce_scatter x3, waiting for transfers between devices, expert_scatter(): lax.psum_scatter(grad, DP, scatter_dimension=dim, tiled=True)  81.1 us
    pallas_call x2, Pallas kernels, attention_call(): pl.pallas_call(partial(body, heads, step), grid=(rows // seq_len,), in_sp...  50.5 us
    convert_element_type x7, other arithmetic, low(): return values.astype(jnp.bfloat16)  42.5 us
    unnamed x121, local copies, waits for them, and re-layouts  42.4 us
  transfers between devices with their start and end apart: 41, of which 12 were waited for; matrix products, arithmetic and copies ran while one was open for 36% of the time, Pallas kernels for 28%

profile of v2, /device:TPU:0, one launch (start us, length us, event | category | flops | bytes accessed | tf_op | source)
XLA Modules:
  0.0 1559.0 jit_solution(3600142500565642182)
XLA Ops:
  24.7 81.1 %shard_map.315 = (bf16[8,512,2048]{2,1,0:T(8,128)(2,1)}, s32[8,8,512]{2,1,0:T(8,128)}) custom-call(bf16[512,2048]{1,0:T(8,128)(2,1)} %bitcast.342, s32[8,512]{1,0:T(8,128)} %concatenate.47.refs_1_), custom_call_target="tpu_custom_call" | custom-call | bytes 104857600 | tf_op jit(solution)/shard_map/pallas_call | solution.py:628
  131.7 22.8 %collective-permute-done.4 = bf16[512,2048]{1,0:T(8,128)(2,1)} collective-permute-done((bf16[512,2048]{1,0:T(8,128)(2,1)}, bf16[512,2048]{1,0:T(8,128)(2,1)}, u32[]{:S(2)}, u32[]{:S(2)}) %collective-permute-start.4) | collective-permute-done | bytes 2097184 | tf_op jit(solution)/shard_map/ppermute | solution.py:764
  156.0 43.7 %collective-permute-done.5 = bf16[512,2048]{1,0:T(8,128)(2,1)} collective-permute-done((bf16[512,2048]{1,0:T(8,128)(2,1)}, bf16[512,2048]{1,0:T(8,128)(2,1)}, u32[]{:S(2)}, u32[]{:S(2)}) %collective-permute-start.5) | collective-permute-done | bytes 2097184 | tf_op jit(solution)/shard_map/ppermute | solution.py:764
  224.0 20.8 %collective-permute-done.2 = bf16[4,64,2048]{2,1,0:T(8,128)(2,1)S(1)} collective-permute-done((bf16[4,64,2048]{2,1,0:T(8,128)(2,1)S(1)}, bf16[4,64,2048]{2,1,0:T(8,128)(2,1)S(1)}, u32[]{:S(2)}, u32[]{:S(2)}) %collective-permute-start.2) | collective-permute-done | bytes 1048608 | tf_op jit(solution)/shard_map/ppermute | solution.py:764
  282.3 19.9 %shard_map.316 = bf16[4096,256]{1,0:T(8,128)(2,1)S(1)} custom-call(bf16[4096,768]{1,0:T(8,128)(2,1)} %convolution_convert_fusion.6.qkv_ref, s32[4096,1]{1,0:T(8,128)S(1)} %copy.203.q_code_ref, s32[4,1,1024]{2,1,0:T(1,128)S(1)} %bitcast.334), custom_call_target="tpu_custom_call" | custom-call | flops 4294967296 | bytes 8388608 | tf_op jit(solution)/shard_map/pallas_call | solution.py:502
  360.6 74.5 %shard_map.317 = bf16[8,512,2048]{2,1,0:T(8,128)(2,1)} custom-call(bf16[512,2048]{1,0:T(8,128)(2,1)} %multiply_convert_fusion.6.refs_0_), custom_call_target="tpu_custom_call" | custom-call | bytes 104857600 | tf_op jit(solution)/shard_map/pallas_call | solution.py:628
  474.0 20.9 %fusion.23 = f32[2304,1408]{1,0:T(8,128)} fusion(bf16[2304,2048]{1,0:T(8,128)(2,1)} %bitcast.414, bf16[1,2048,1408]{2,1,0:T(8,128)(2,1)} %all-gather.23.cloned.1.call-done), kind=kOutput, calls=%fused_computation.54 | convolution fusion | flops 13287555072 | bytes 28180480 | tf_op jit(solution)/shard_map/dot_general | solution.py:783
  494.9 23.6 %multiply_convert_fusion.2 = (bf16[2304,1408]{1,0:T(8,128)(2,1)}, f32[2304,1408]{1,0:T(8,128)}) fusion(f32[2304,1408]{1,0:T(8,128)} %fusion.23, bf16[2304,2048]{1,0:T(8,128)(2,1)} %bitcast.415, bf16[1,2048,1408]{2,1,0:T(8,128)(2,1)} %all-gather.25.cloned.1.call-done), kind=kOutput, calls=%fused_computation.23 | convolution fusion | flops 13307019264 | bytes 47644672 | tf_op jit(solution)/shard_map/dot_general | solution.py:783
  518.6 21.3 %fusion.8 = (f32[2304]{0:T(1024)S(1)}, bf16[2304,2048]{1,0:T(8,128)(2,1)}) fusion(bf16[8,288,2048]{2,1,0:T(8,128)(2,1)} %convolution_convert_fusion.7, bf16[2304,1408]{1,0:T(8,128)(2,1)} %get-tuple-element.211, bf16[1,1408,2048]{2,1,0:T(8,128)(2,1)} %all-gather.27.cloned.1.call-done), kind=kOutput, calls=%fused_computation.18 | convolution fusion | flops 13311145984 | bytes 31138816 | tf_op jit(solution)/shard_map/dot_general | solution.py:783
  550.7 19.9 %convolution_convert_fusion.5 = bf16[1408,2048]{1,0:T(8,128)(2,1)} fusion(bf16[2304,1408]{1,0:T(8,128)(2,1)} %get-tuple-element.211, bf16[2304,2048]{1,0:T(8,128)(2,1)} %fusion.7), kind=kOutput, calls=%fused_computation.38 | convolution fusion | flops 13290438656 | bytes 21692416 | tf_op jit(solution)/shard_map/dot_general | solution.py:783
  570.5 28.0 %multiply_convert_fusion = (bf16[2304,1408]{1,0:T(8,128)(2,1)}, bf16[2304,1408]{1,0:T(8,128)(2,1)}) fusion(f32[2304,1408]{1,0:T(8,128)} %fusion.23, f32[2304,1408]{1,0:T(8,128)} %get-tuple-element.212, bf16[2304,2048]{1,0:T(8,128)(2,1)} %fusion.7, bf16[1,1408,2048]{2,1,0:T(8,128)(2,1)} %all-gather.27.cloned.1.call-done), kind=kOutput, calls=%fused_computation.21 | convolution fusion | flops 13329727488 | bytes 54132736 | tf_op jit(solution)/shard_map/dot_general | solution.py:783
  598.6 20.4 %convolution_convert_fusion.3 = bf16[2048,1408]{1,0:T(8,128)(2,1)} fusion(bf16[2304,2048]{1,0:T(8,128)(2,1)} %bitcast.416, bf16[2304,1408]{1,0:T(8,128)(2,1)} %get-tuple-element.169), kind=kOutput, calls=%fused_computation.36 | convolution fusion | flops 13290438656 | bytes 21692416 | tf_op jit(solution)/shard_map/dot_general | solution.py:783
  658.2 20.3 %convolution_convert_fusion.4 = bf16[2048,1408]{1,0:T(8,128)(2,1)} fusion(bf16[2304,2048]{1,0:T(8,128)(2,1)} %bitcast.417, bf16[2304,1408]{1,0:T(8,128)(2,1)} %get-tuple-element.170), kind=kOutput, calls=%fused_computation.37 | convolution fusion | flops 13290438656 | bytes 21692416 | tf_op jit(solution)/shard_map/dot_general | solution.py:783
  678.5 27.4 %multiply_convert_fusion.3 = (bf16[4096,704]{0,1:T(8,128)(2,1)}, bf16[4096,704]{0,1:T(8,128)(2,1)}, bf16[4096,704]{0,1:T(8,128)(2,1)}) fusion(f32[4096,704]{0,1:T(8,128)} %fusion.84, f32[4096,704]{0,1:T(8,128)} %fusion.85, bf16[704,2048]{1,0:T(8,128)(2,1)} %all-gather.19.cloned.1.call-done, bf16[4096,2048]{1,0:T(8,128)(2,1)} %bitcast.394, ...), kind=kOutput, calls=%fused_computation.26 | convolution fusion | flops 11879579648 | bytes 60047360 | tf_op jit(solution)/shard_map/dot_general | solution.py:783
  801.4 20.8 %fusion.21 = f32[2304,2048]{1,0:T(8,128)} fusion(bf16[2304,1408]{1,0:T(8,128)(2,1)} %get-tuple-element.170, bf16[1,2048,1408]{2,1,0:T(8,128)(2,1)} %all-gather.23.cloned.1.call-done), kind=kOutput, calls=%fused_computation.52 | convolution fusion | flops 13287555072 | bytes 31129600 | tf_op jit(solution)/shard_map/dot_general | solution.py:783
  822.2 21.9 %add_convert_fusion = bf16[2304,2048]{1,0:T(8,128)(2,1)} fusion(f32[2304,2048]{1,0:T(8,128)} %fusion.21, bf16[2304,1408]{1,0:T(8,128)(2,1)} %get-tuple-element.169, bf16[1,2048,1408]{2,1,0:T(8,128)(2,1)S(1)} %bitcast.413), kind=kOutput, calls=%fused_computation.19 | convolution fusion | flops 13296992256 | bytes 40566784 | tf_op jit(solution)/shard_map/dot_general | solution.py:783
  863.3 20.0 %fusion.86 = f32[4096,2048]{1,0:T(8,128)} fusion(bf16[4096,704]{0,1:T(8,128)(2,1)} %get-tuple-element.175, bf16[2048,704]{0,1:T(8,128)(2,1)S(1)} %copy-done.43), kind=kOutput, calls=%fused_computation.237 | convolution fusion | flops 11811160064 | bytes 42205184 | tf_op jit(solution)/shard_map/dot_general | solution.py:783
  883.3 34.8 %fusion.2 = bf16[4096,2048]{1,0:T(8,128)(2,1)} fusion(f32[8,512,2048]{2,1,0:T(8,128)} %fusion.25, f32[4096,2048]{1,0:T(8,128)} %fusion.86, bf16[4096,704]{0,1:T(8,128)(2,1)} %get-tuple-element.174, bf16[2048,704]{0,1:T(8,128)(2,1)} %all-gather.17.cloned.1.call-done), kind=kOutput, calls=%fused_computation.7 | convolution fusion | flops 11836325888 | bytes 92536832 | tf_op jit(solution)/shard_map/dot_general | solution.py:783
  939.9 31.1 %fusion.1 = (f32[4096]{0:T(1024)S(1)}, bf16[4096,2048]{1,0:T(8,128)(2,1)}) fusion(bf16[4096,2048]{1,0:T(8,128)(2,1)} %bitcast.396, f32[8,512,2048]{2,1,0:T(8,128)} %fusion.26, f32[4096]{0:T(1024)S(1)} %bitcast.406, f32[4096]{0:T(1024)S(1)} %bitcast.405, bf16[4096,704]{0,1:T(8,128)(2,1)} %get-tuple-element.176, ...), kind=kOutput, calls=%fused_computation.5 | convolution fusion | flops 11869876224 | bytes 75808768 | tf_op jit(solution)/shard_map/dot_general | solution.py:783
  1004.8 158.0 %shard_map.318 = f32[512,2048]{1,0:T(8,128)S(1)} custom-call(bf16[8,512,2048]{2,1,0:T(8,128)(2,1)} %bitcast.343), custom_call_target="tpu_custom_call" | custom-call | bytes 104857600 | tf_op jit(solution)/shard_map/pallas_call | solution.py:738
  1215.3 30.6 %shard_map.319 = bf16[4096,768]{1,0:T(8,128)(2,1)} custom-call(bf16[4096,768]{1,0:T(8,128)(2,1)} %convolution_convert_fusion.6.qkv_ref, bf16[4096,256]{1,0:T(8,128)(2,1)} %bitcast.70.grad_ref, s32[4096,1]{1,0:T(8,128)S(1)} %copy.203.q_code_ref, s32[4,1,1024]{2,1,0:T(1,128)S(1)} %bitcast.335), custom_call_target="tpu_custom_call" | custom-call | flops 10737418240 | bytes 12582912 | tf_op jit(solution)/shard_map/pallas_call | solution.py:502
  1325.7 81.1 %reduce-scatter.19.cloned.1.call-done = bf16[512,1408]{1,0:T(8,128)(2,1)} async-done(((bf16[2048,1408]{1,0:T(8,128)(2,1)}), bf16[512,1408]{1,0:T(8,128)(2,1)}) %reduce-scatter.19.cloned.1.call-update) | async-done | bytes 1441808 | tf_op jit(solution)/shard_map/reduce_scatter | solution.py:1005
  1414.5 20.8 %convolution_convert_fusion = bf16[4096,2048]{1,0:T(8,128)(2,1)} fusion(bf16[4096,768]{1,0:T(8,128)(2,1)} %shard_map.319, bf16[2048,896]{1,0:T(8,128)(2,1)} %all-gather.13.cloned.1.call-done), kind=kOutput, calls=%fused_computation.20 | convolution fusion | flops 12893290496 | bytes 26214400 | tf_op jit(solution)/shard_map/dot_general | solution.py:783
  1435.3 76.8 %shard_map.320 = f32[512,2048]{1,0:T(8,128)S(1)} custom-call(bf16[8,512,2048]{2,1,0:T(8,128)(2,1)} %bitcast.344), custom_call_target="tpu_custom_call" | custom-call | bytes 104857600 | tf_op jit(solution)/shard_map/pallas_call | solution.py:738
  (362 shorter events, 602.8 us)
Async XLA Ops:
  7.2 117.7 %all-gather.21.cloned.1.call-start = ((), (), s32[]{:S(2)}) async-start(), calls=%async_computation.27 | async-start | bytes 1310720 | tf_op jit(solution)/shard_map/all_gather | solution.py:857
  9.5 236.3 %all-gather.13.cloned.1.call-start = ((), (), s32[]{:S(2)}) async-start(), calls=%async_computation.15 | async-start | bytes 4587520 | tf_op jit(solution)/shard_map/all_gather | solution.py:848
  17.5 456.4 %all-gather.23.cloned.1.call-start = ((), (), s32[]{:S(2)}) async-start(), calls=%async_computation.28 | async-start | bytes 7208960 | tf_op jit(solution)/shard_map/all_gather | solution.py:911
  18.3 476.6 %all-gather.25.cloned.1.call-start = ((), (), s32[]{:S(2)}) async-start(), calls=%async_computation.29 | async-start | bytes 7208960 | tf_op jit(solution)/shard_map/all_gather | solution.py:912
  18.9 499.7 %all-gather.27.cloned.1.call-start = ((), (), s32[]{:S(2)}) async-start(), calls=%async_computation.30 | async-start | bytes 7208960 | tf_op jit(solution)/shard_map/all_gather | solution.py:913
  19.5 599.5 %all-gather.15.cloned.1.call-start = ((), (), s32[]{:S(2)}) async-start(), calls=%async_computation.16 | async-start | bytes 3604480 | tf_op jit(solution)/shard_map/all_gather | solution.py:906
  21.2 616.7 %all-gather.17.cloned.1.call-start = ((), (), s32[]{:S(2)}) async-start(), calls=%async_computation.17 | async-start | bytes 3604480 | tf_op jit(solution)/shard_map/all_gather | solution.py:907
  23.9 654.6 %all-gather.19.cloned.1.call-start = ((), (), s32[]{:S(2)}) async-start(), calls=%async_computation.18 | async-start | bytes 3604480 | tf_op jit(solution)/shard_map/all_gather | solution.py:908
  124.9 97.0 %collective-permute-start = (bf16[4,64,2048]{2,1,0:T(8,128)(2,1)}, bf16[4,64,2048]{2,1,0:T(8,128)(2,1)S(1)}, u32[]{:S(2)}, u32[]{:S(2)}) collective-permute-start(bf16[4,64,2048]{2,1,0:T(8,128)(2,1)} %bitcast.382), channel_id=1, source_target_pairs={{0,8},{8,0},{16,24},{24,16},{1,9},{9,1},{17,25},{25,17},{2,10},{10... | collective-permute-start | bytes 3145736 | tf_op jit(solution)/shard_map/ppermute | solution.py:764
  125.3 97.6 %collective-permute-start.1 = (bf16[4,64,2048]{2,1,0:T(8,128)(2,1)}, bf16[4,64,2048]{2,1,0:T(8,128)(2,1)S(1)}, u32[]{:S(2)}, u32[]{:S(2)}) collective-permute-start(bf16[4,64,2048]{2,1,0:T(8,128)(2,1)} %bitcast.383), channel_id=1, source_target_pairs={{0,16},{8,24},{16,0},{24,8},{1,17},{9,25},{17,1},{25,9},{2,18},{10... | collective-permute-start | bytes 3145736 | tf_op jit(solution)/shard_map/ppermute | solution.py:764
  207.6 144.6 %collective-permute-start.7 = (bf16[4,512,2048]{2,1,0:T(8,128)(2,1)}, bf16[4,512,2048]{2,1,0:T(8,128)(2,1)}, u32[]{:S(2)}, u32[]{:S(2)}) collective-permute-start(bf16[4,512,2048]{2,1,0:T(8,128)(2,1)} %pad_maximum_fusion), channel_id=1, source_target_pairs={{0,4},{4,0},{1,5},{5,1},{2,6},{6,2},{3,7},{7,3},{8,12},{12,8},{9,1... | collective-permute-start | bytes 25165832 | tf_op jit(solution)/shard_map/ppermute | solution.py:768
  311.8 977.8 %reduce-scatter.17.cloned.1.call-start = ((), (), s32[]{:S(2)}) async-start(), calls=%async_computation.23 | async-start | bytes 3604480 | tf_op jit(solution)/shard_map/reduce_scatter | solution.py:979
  918.1 376.1 %reduce-scatter.15.cloned.1.call-start = ((), (), s32[]{:S(2)}) async-start(), calls=%async_computation.22 | async-start | bytes 3604480 | tf_op jit(solution)/shard_map/reduce_scatter | solution.py:979
  918.7 379.8 %reduce-scatter.13.cloned.1.call-start = ((), (), s32[]{:S(2)}) async-start(), calls=%async_computation.21 | async-start | bytes 3604480 | tf_op jit(solution)/shard_map/reduce_scatter | solution.py:979
  919.5 391.8 %reduce-scatter.23.cloned.1.call-start = ((), (), s32[]{:S(2)}) async-start(), calls=%async_computation.26 | async-start | bytes 7208960 | tf_op jit(solution)/shard_map/reduce_scatter | solution.py:1005
  920.0 402.6 %reduce-scatter.21.cloned.1.call-start = ((), (), s32[]{:S(2)}) async-start(), calls=%async_computation.25 | async-start | bytes 7208960 | tf_op jit(solution)/shard_map/reduce_scatter | solution.py:1005
  939.2 467.6 %reduce-scatter.19.cloned.1.call-start = ((), (), s32[]{:S(2)}) async-start(), calls=%async_computation.24 | async-start | bytes 7208960 | tf_op jit(solution)/shard_map/reduce_scatter | solution.py:1005
  981.4 183.4 %all-to-all-start.1 = ((f32[8,2,512]{2,1,0:T(2,128)}), f32[8,2,512]{2,1,0:T(2,128)S(1)}, u32[]{:S(2)}, u32[]{:S(2)}) async-start(f32[8,2,512]{2,1,0:T(2,128)} %gather_fusion.1), calls=%async_computation.1 | async-start | bytes 65536 | tf_op jit(solution)/shard_map/all_to_all | solution.py:1035
  1000.5 169.3 %collective-permute-start.10 = (bf16[512,2048]{1,0:T(8,128)(2,1)}, bf16[512,2048]{1,0:T(8,128)(2,1)}, u32[]{:S(2)}, u32[]{:S(2)}) collective-permute-start(bf16[512,2048]{1,0:T(8,128)(2,1)} %get-tuple-element.173), channel_id=1, source_target_pairs={{0,16},{8,24},{16,0},{24,8},{1,17},{9,25},{17,1},{25,9},{2,18},{10... | collective-permute-start | bytes 6291464 | tf_op jit(solution)/shard_map/ppermute | solution.py:764
  1001.7 168.1 %collective-permute-start.11 = (bf16[512,2048]{1,0:T(8,128)(2,1)}, bf16[512,2048]{1,0:T(8,128)(2,1)}, u32[]{:S(2)}, u32[]{:S(2)}) collective-permute-start(bf16[512,2048]{1,0:T(8,128)(2,1)} %get-tuple-element.172), channel_id=1, source_target_pairs={{0,24},{8,16},{16,8},{24,0},{1,25},{9,17},{17,9},{25,1},{2,26},{10... | collective-permute-start | bytes 6291464 | tf_op jit(solution)/shard_map/ppermute | solution.py:764
  1003.2 166.7 %collective-permute-start.9 = (bf16[512,2048]{1,0:T(8,128)(2,1)}, bf16[512,2048]{1,0:T(8,128)(2,1)}, u32[]{:S(2)}, u32[]{:S(2)}) collective-permute-start(bf16[512,2048]{1,0:T(8,128)(2,1)} %get-tuple-element.171), channel_id=1, source_target_pairs={{0,8},{8,0},{16,24},{24,16},{1,9},{9,1},{17,25},{25,17},{2,10},{10... | collective-permute-start | bytes 6291464 | tf_op jit(solution)/shard_map/ppermute | solution.py:764
  1188.7 326.4 %reduce-scatter.9.cloned.1.call-start = ((), (), s32[]{:S(2)}) async-start(), calls=%async_computation.19 | async-start | bytes 3932160 | tf_op jit(solution)/shard_map/reduce_scatter | solution.py:1083
  1201.0 113.8 %collective-permute-start.12 = (bf16[4,256,2048]{2,1,0:T(8,128)(2,1)}, bf16[4,256,2048]{2,1,0:T(8,128)(2,1)}, u32[]{:S(2)}, u32[]{:S(2)}) collective-permute-start(bf16[4,256,2048]{2,1,0:T(8,128)(2,1)} %pad_maximum_fusion.1), channel_id=1, source_target_pairs={{0,4},{4,0},{1,5},{5,1},{2,6},{6,2},{3,7},{7,3},{8,12},{12,8},{9,1... | collective-permute-start | bytes 12582920 | tf_op jit(solution)/shard_map/ppermute | solution.py:768
  1281.7 253.3 %reduce-scatter.11.cloned.1.call-start = ((), (), s32[]{:S(2)}) async-start(), calls=%async_computation.20 | async-start | bytes 1310720 | tf_op jit(solution)/shard_map/reduce_scatter | solution.py:1071
  (66 other events, 2907.3 us)
Sparse Core Ops, SparseCore 0:
  10.2 30.6 all-gather.20
  43.0 71.5 all-gather.12
  116.2 105.3 all-gather.22
  223.0 104.9 all-gather.24
  329.5 104.9 all-gather.26
  436.5 57.3 all-gather.14
  496.1 57.8 all-gather.16
  556.1 57.8 all-gather.18
  918.2 56.1 reduce-scatter.16
  977.2 56.0 reduce-scatter.14
  1036.2 56.0 reduce-scatter.12
  1094.4 102.0 reduce-scatter.22
  1198.8 103.0 reduce-scatter.20
  1304.0 102.7 reduce-scatter.18
  1409.0 60.7 reduce-scatter.8
  1472.0 27.1 reduce-scatter.10

commit v3 on v2

--- a/solution.py
+++ b/solution.py
@@ -760,6 +760,10 @@
     )(parts)
 
 
+def after(values, others):
+    return lax.optimization_barrier((values, others))[0]
+
+
 def swap(values, bits):
     return lax.ppermute(values, EXP, [(i, i ^ bits) for i in range(4)])
 
@@ -768,14 +772,15 @@
     return lax.ppermute(values, CTX, [(0, 1), (1, 0)])
 
 
-def hop_sum(ours, theirs):
+def twin_sums(ours, theirs):
     got = twin(theirs)
-    sums = [
-        low(ours[k].astype(jnp.float32) + got[k].astype(jnp.float32)) for k in range(4)
-    ]
+    return [low(ours[k].astype(jnp.float32) + got[k].astype(jnp.float32)) for k in range(4)]
+
+
+def hop_sum(sums, later):
     total = sums[0].astype(jnp.float32)
     for k in (1, 2, 3):
-        total = total + swap(sums[k], k).astype(jnp.float32)
+        total = total + after(swap(sums[k], k), later).astype(jnp.float32)
     return total
 
 
@@ -833,9 +838,6 @@
     place = lax.axis_index(EXP)
     away = [(place ^ k) * 2 + (core ^ j) for j in (0, 1) for k in range(4)]
     away = jnp.stack(away)
-    cot_own, _ = lax.optimization_barrier((cotangent[0], info_all))
-    cot_near = jnp.stack([cot_own, swap(cot_own, 1), swap(cot_own, 2), swap(cot_own, 3)])
-    cot_all = jnp.concatenate([cot_near, twin(cot_near)]).reshape(all_tokens, width)
     w_qkv_part = jnp.concatenate(
         [
             lax.dynamic_slice(w, (0, me * head_cols), (shard, head_cols))
@@ -855,7 +857,20 @@
     out_rows = shard // plane
     w_out_part = lax.dynamic_slice(w_out, (me * out_rows, 0), (out_rows, width))
     w_out_part = lax.all_gather(w_out_part, DP, axis=0, tiled=False)
-    pieces = [w_out_part] + [swap(w_out_part, k) for k in (1, 2, 3)]
+    w_out_part = after(w_out_part, info_all)
+    w_out_got = [swap(w_out_part, k) for k in (1, 2, 3)]
+
+    def normed(values, gain):
+        values = values.astype(jnp.float32)
+        inv = lax.rsqrt(jnp.mean(values * values, axis=1, keepdims=True) + EPS)
+        return values, inv, low(values * inv * gain)
+
+    _, _, n1_all = normed(hidden_all, g_one)
+    qkv = low(mm(n1_all, w_qkv))
+    q_codes = info_all[:, 0].reshape(all_tokens, 1)
+    k_codes = info_all[:, 1].reshape(all_tokens // seq_len, 1, seq_len)
+    attended_cols = attention_call(qkv, None, q_codes, k_codes, seq_len)
+    pieces = [w_out_part] + [after(v, qkv) for v in w_out_got]
     w_out_near = jnp.zeros((depth, groups, 1, out_rows, width), jnp.bfloat16)
     for k in range(4):
         w_out_near = lax.dynamic_update_slice(
@@ -868,18 +883,8 @@
         jnp.concatenate([w_out_far, w_out_near], axis=2),
     ).reshape(width, width)
 
-    def normed(values, gain):
-        values = values.astype(jnp.float32)
-        inv = lax.rsqrt(jnp.mean(values * values, axis=1, keepdims=True) + EPS)
-        return values, inv, low(values * inv * gain)
-
-    _, _, n1_all = normed(hidden_all, g_one)
     x_rows, inv_one, _ = normed(hidden[0], g_one)
     cot_rows = cotangent[0].astype(jnp.float32)
-    qkv = low(mm(n1_all, w_qkv))
-    q_codes = info_all[:, 0].reshape(all_tokens, 1)
-    k_codes = info_all[:, 1].reshape(all_tokens // seq_len, 1, seq_len)
-    attended_cols = attention_call(qkv, None, q_codes, k_codes, seq_len)
 
     def to_tokens(cols):
         got = lax.all_to_all(
@@ -896,8 +901,6 @@
     residual = x_rows + mm(attended, w_out_full)
     residual, inv_two, n2 = normed(residual, g_two)
 
-    n2, cot_all = lax.optimization_barrier((n2, cot_all))
-    n2_all = plane_gather(n2, None, True, 2)[0].reshape(all_tokens, width)
     units = shared_w_gate.shape[1]
     part = units // (depth * halves)
     pick = lambda w: lax.dynamic_index_in_dim(
@@ -908,9 +911,13 @@
     sh_down = lax.all_gather(
         lax.dynamic_slice(shared_w_down, (core * part, 0), (part, width)), DP, axis=0, tiled=True
     )
-    ex_gate = lax.all_gather(expert_w_gate[0], DP, axis=0, tiled=True)
-    ex_up = lax.all_gather(expert_w_up[0], DP, axis=0, tiled=True)
-    ex_down = lax.all_gather(expert_w_down[0], DP, axis=1, tiled=True)
+    n2 = after(n2, (sh_gate, sh_up))
+    n2_all = plane_gather(n2, None, True, 2)[0].reshape(all_tokens, width)
+    cot_own = after(cotangent[0], n2_all)
+    cot_got = [swap(cot_own, k) for k in (1, 2, 3)]
+    ex_gate = lax.all_gather(after(expert_w_gate[0], info_all), DP, axis=0, tiled=True)
+    ex_up = lax.all_gather(after(expert_w_up[0], info_all), DP, axis=0, tiled=True)
+    ex_down = lax.all_gather(after(expert_w_down[0], info_all), DP, axis=1, tiled=True)
 
     small_w = jnp.concatenate([router_t, gate_vec[None]])
 
@@ -955,6 +962,12 @@
         jnp.where(chosen, expert_gate.reshape(plane, 1, tokens), 0.0), axis=2
     ).reshape(plane * capacity, 1)
     expert_rows = low(rows_of(n2_all))
+    gate_e = mm(expert_rows, ex_gate)
+    up_e = mm(expert_rows, ex_up)
+    act_e = gate_e * jax.nn.sigmoid(gate_e)
+    hidden_e = low(act_e * up_e)
+    cot_near = jnp.concatenate([cot_own] + [after(v, hidden_e) for v in cot_got])
+    cot_all = jnp.concatenate([cot_near, twin(cot_near)])
     row_cots = low(rows_of(cot_all))
     row_grads = low(row_cots.astype(jnp.float32) * slot_gates)
 
@@ -972,12 +985,17 @@
     rows_out = width // (halves * depth)
 
     def own_units(grad):
-        grad = low(grad).reshape(depth * part, halves, depth, rows_out).transpose(2, 0, 1, 3)
-        return grad.reshape(depth * depth * part, halves * rows_out)
+        grad = low(grad)
+        cut = lambda c, z: grad[:, (c * depth + z) * rows_out : (c * depth + z + 1) * rows_out]
+        return jnp.concatenate(
+            [
+                jnp.concatenate([cut(c, z) for c in range(halves)], axis=1)
+                for z in range(depth)
+            ]
+        )
 
     def shared_scatter(grad):
-        total = lax.psum_scatter(grad, DP, scatter_dimension=0, tiled=True)
-        total = total.reshape(depth * part, halves, rows_out)
+        total = grad.reshape(depth * part, halves, rows_out)
         keep = lax.dynamic_index_in_dim(total, core, axis=1, keepdims=False)
         give = lax.dynamic_index_in_dim(total, 1 - core, axis=1, keepdims=False)
         both = jnp.stack([keep, twin(give)]).reshape(halves, depth, part, rows_out)
@@ -988,10 +1006,6 @@
     grad_sh_up = own_units(mm(up_grad_s, n2_all, ((0,), (0,))))
     grad_sh_down = own_units(mm(shared_hidden, shared_grads, ((0,), (0,))))
 
-    gate_e = mm(expert_rows, ex_gate)
-    up_e = mm(expert_rows, ex_up)
-    act_e = gate_e * jax.nn.sigmoid(gate_e)
-    hidden_e = low(act_e * up_e)
     result_e = low(mm(hidden_e, ex_down))
     row_dots = jnp.sum(result_e.astype(jnp.float32) * row_cots.astype(jnp.float32), axis=1)
     gate_dots = jnp.sum(
@@ -1000,11 +1014,6 @@
     hgrad_e = mm(row_grads, ex_down, ((1,), (1,)))
     gate_grad_e = low(hgrad_e * up_e * silu_grad(gate_e))
     up_grad_e = low(hgrad_e * act_e)
-
-    def expert_scatter(grad, dim):
-        return lax.psum_scatter(grad, DP, scatter_dimension=dim, tiled=True).astype(
-            jnp.float32
-        )[None]
 
     grad_ex_down = low(mm(hidden_e, row_grads, ((0,), (0,))))
     grad_ex_gate = low(mm(expert_rows, gate_grad_e, ((0,), (0,))))
@@ -1014,19 +1023,18 @@
     )
 
     out_part = low(sg_all * shared_part + expert_gate * back_to_tokens(result_e))
-    out_part = out_part.reshape(plane, tokens, width)
-    output = low(residual + hop_sum(out_part[:4], out_part[4:]))
     n2_grad_part = low(
         mm(gate_grad_s, sh_gate, ((1,), (1,)))
         + mm(up_grad_s, sh_up, ((1,), (1,)))
         + back_to_tokens(rows_grad)
     )
     grads = (grad_sh_gate, grad_sh_up, grad_sh_down, grad_ex_down, grad_ex_gate, grad_ex_up)
-    n2_grad_part, grads = lax.optimization_barrier((n2_grad_part, grads))
-    grad_sh_gate, grad_sh_up, grad_sh_down = [shared_scatter(v) for v in grads[:3]]
-    grad_sh_gate, grad_sh_up = grad_sh_gate.T, grad_sh_up.T
-    grad_ex_down = expert_scatter(grads[3], 1)
-    grad_ex_gate, grad_ex_up = [expert_scatter(v, 0) for v in grads[4:]]
+    grads_made = grads
+    grads = [
+        lax.psum_scatter(v, DP, scatter_dimension=dim, tiled=True)
+        for v, dim in zip(grads, (0, 0, 0, 1, 0, 0))
+    ]
+    n2_grad_part = after(n2_grad_part, (grads_made, out_part, grads[:3]))
     n2_grad = plane_scatter(n2_grad_part.reshape(plane, tokens, width), True, 3, jnp.float32)
 
     dots = jnp.stack([gate_dots, cot_dot_shared.reshape(plane, tokens)], axis=1)
@@ -1062,18 +1070,26 @@
     block_of = lambda k, c: lax.dynamic_slice(
         grad_out, (place ^ k, c, 0, 0), (1, 1, width // plane, width)
     )[0, 0]
-    grad_out = low(
-        hop_sum(
-            [block_of(k, core) for k in range(4)],
-            jnp.stack([block_of(k, 1 - core) for k in range(4)]),
-        )
-    )
-    grad_out = lax.psum_scatter(grad_out, DP, scatter_dimension=0, tiled=True).astype(jnp.float32)
     attended_grad = to_columns(low(mm(low_residual, w_out_full, ((1,), (1,)))))
+    out_part = after(out_part, n2_grad).reshape(plane, tokens, width)
+    out_sums = twin_sums(out_part[:4], out_part[4:])
+    attended_grad = after(attended_grad, (out_sums, grads[3]))
     qkv_grad = attention_call(qkv, attended_grad, q_codes, k_codes, seq_len)
+    out_grad_sums = twin_sums(
+        [block_of(k, core) for k in range(4)],
+        jnp.stack([block_of(k, 1 - core) for k in range(4)]),
+    )
+    grad_qkv = low(mm(n1_all, qkv_grad, ((0,), (0,))))
     n1_grad = low(mm(qkv_grad, w_qkv, ((1,), (1,))))
+    grad_out = low(hop_sum(out_grad_sums, n1_grad))
+    grad_out = lax.psum_scatter(grad_out, DP, scatter_dimension=0, tiled=True)
+    n1_grad = after(n1_grad, (grad_qkv, out_grad_sums, grads[4]))
     n1_grad = plane_scatter(n1_grad.reshape(plane, tokens, width), False, 1, jnp.float32)
-    grad_qkv = low(mm(n1_all, qkv_grad, ((0,), (0,))))
+    output = low(residual + hop_sum(out_sums, n1_grad))
+    grad_sh_gate, grad_sh_up, grad_sh_down = [
+        shared_scatter(after(v, n1_grad)) for v in grads[:3]
+    ]
+    grad_sh_gate, grad_sh_up = grad_sh_gate.T, grad_sh_up.T
     fine = shard // plane
     grad_qkv = (
         grad_qkv.reshape(plane, depth, fine, 3 * head_cols)
@@ -1108,6 +1124,10 @@
         .reshape(3, fine, width)
         .astype(jnp.float32)
     )
+    grad_out = after(grad_out, n1_grad).astype(jnp.float32)
+    grad_ex_down, grad_ex_gate, grad_ex_up = [
+        after(v, n1_grad).astype(jnp.float32)[None] for v in grads[3:]
+    ]
     input_part, _ = norm_back(x_rows, inv_one, g_one, n1_grad)
     input_grad = low(residual_grad + input_part)
     return (

time: 1560 us -> 1440 us (0.923)
  waiting for transfers between devices: 223 us -> 120 us
  other arithmetic: 113 us -> 172 us
  local copies, waits for them, and re-layouts: 152 us -> 108 us
  Pallas kernels: 441 us -> 405 us
    all_gather x3, waiting for transfers between devices: 0.02 us -> 94.7 us  [the longest x1 85.5 us: local_plane(): lax.all_gather(after(expert_w_up[0], info_all), DP, axis=0, tiled=True)]
    ppermute x12, waiting for transfers between devices: 95.8 us -> 4.26 us  [swap(): return lax.ppermute(values, EXP, [(i, i ^ bits) for i in range(4)])]
    reduce_scatter x7, waiting for transfers between devices: 81.2 us -> 2.52 us  [the longest x1 2.46 us: local_plane(): grad_out = lax.psum_scatter(grad_out, DP, scatter_dimension=0, tiled=True)]
    concatenate x0 -> x4, other arithmetic: none -> 57.1 us  [the longest x3 49.3 us: own_units(): jnp.concatenate([jnp.concatenate([cut(c, z) for c in range(halves)], axis...]
    reshape x9 -> x3, local copies, waits for them, and re-layouts: 40.3 us -> 2.45 us  [shared_scatter(): total = grad.reshape(depth * part, halves, rows_out)]
    pallas_call x2, Pallas kernels: 235 us -> 200 us  [plane_scatter(): pl.pallas_call(partial(plane_scatter_kernel, relative), out_shape=jax.Sha...]
    unnamed x121 -> x116, local copies, waits for them, and re-layouts: 42.4 us -> 31.9 us
  transfers between devices with their start and end apart: 41 -> 41, of which waited for: 12 -> 7; matrix products, arithmetic and copies ran while one was open for 36% -> 58% of each run, Pallas kernels for 28% -> 28%
where the time goes in v3:
time: 1440 us
  matrix products  567 us (39%)
  Pallas kernels  405 us (28%)
  other arithmetic  172 us (12%)
  waiting for transfers between devices  120 us (8%)
  local copies, waits for them, and re-layouts  108 us (8%)
  starting transfers between devices  39.8 us (3%)
  between operations  15.5 us (1%)
    dot_general x28, matrix products, mm(): lax.dot_general(left, right, (dims, ((), ())), preferred_element_type=jnp...  502 us
    pallas_call x2, Pallas kernels, plane_scatter(): pl.pallas_call(partial(plane_scatter_kernel, relative), out_shape=jax.Sha...  200 us
    pallas_call x2, Pallas kernels, plane_gather(): pl.pallas_call(partial(plane_gather_kernel, info is not None, relative),...  155 us
    all_gather x1, waiting for transfers between devices, local_plane(): lax.all_gather(after(expert_w_up[0], info_all), DP, axis=0, tiled=True)  85.5 us
    pallas_call x2, Pallas kernels, attention_call(): pl.pallas_call(partial(body, heads, step), grid=(rows // seq_len,), in_sp...  50.3 us
    concatenate x3, other arithmetic, own_units(): jnp.concatenate([jnp.concatenate([cut(c, z) for c in range(halves)], axis...  49.3 us
    convert_element_type x7, other arithmetic, low(): return values.astype(jnp.bfloat16)  48.6 us
    dot_general x2, matrix products, back_to_tokens(): lax.dot_general(onehot, values.reshape(plane, capacity, width), (((1,), (...  38.4 us
  transfers between devices with their start and end apart: 41, of which 7 were waited for; matrix products, arithmetic and copies ran while one was open for 58% of the time, Pallas kernels for 28%

profile of v3, /device:TPU:0, one launch (start us, length us, event | category | flops | bytes accessed | tf_op | source)
XLA Modules:
  0.0 1435.3 jit_solution(6451554834362873977)
XLA Ops:
  22.8 81.0 %shard_map.315 = (bf16[8,512,2048]{2,1,0:T(8,128)(2,1)}, s32[8,8,512]{2,1,0:T(8,128)}) custom-call(bf16[512,2048]{1,0:T(8,128)(2,1)} %bitcast.316, s32[8,512]{1,0:T(8,128)} %concatenate.95.refs_1_), custom_call_target="tpu_custom_call" | custom-call | bytes 104857600 | tf_op jit(solution)/shard_map/pallas_call | solution.py:628
  169.3 19.6 %shard_map.316 = bf16[4096,256]{1,0:T(8,128)(2,1)S(1)} custom-call(bf16[4096,768]{1,0:T(8,128)(2,1)} %convolution_convert_fusion.6.qkv_ref, s32[4096,1]{1,0:T(8,128)S(1)} %copy.212.q_code_ref, s32[4,1,1024]{2,1,0:T(1,128)S(1)} %bitcast.306), custom_call_target="tpu_custom_call" | custom-call | flops 4294967296 | bytes 8388608 | tf_op jit(solution)/shard_map/pallas_call | solution.py:502
  241.2 74.1 %shard_map.317 = bf16[8,512,2048]{2,1,0:T(8,128)(2,1)} custom-call(bf16[512,2048]{1,0:T(8,128)(2,1)} %multiply_convert_fusion.6.refs_0_), custom_call_target="tpu_custom_call" | custom-call | bytes 104857600 | tf_op jit(solution)/shard_map/pallas_call | solution.py:628
  341.3 21.0 %fusion.80 = f32[2304,1408]{1,0:T(8,128)} fusion(bf16[2304,2048]{1,0:T(8,128)(2,1)} %bitcast.383, bf16[2048,1408]{1,0:T(8,128)(2,1)} %all-gather.18.cloned.1.call-done), kind=kOutput, calls=%fused_computation.233 | convolution fusion | flops 13287555072 | bytes 28180480 | tf_op jit(solution)/shard_map/dot_general | solution.py:788
  362.3 85.5 %all-gather.20.cloned.1.call-done = bf16[2048,1408]{1,0:T(8,128)(2,1)} async-done(((bf16[512,1408]{1,0:T(8,128)(2,1)}), bf16[2048,1408]{1,0:T(8,128)(2,1)}) %all-gather.20.cloned.1.call-update) | async-done | bytes 5767184 | tf_op jit(solution)/shard_map/all_gather | solution.py:919
  447.8 23.4 %multiply_convert_fusion.2 = (bf16[2304,1408]{1,0:T(8,128)(2,1)}, f32[2304,1408]{1,0:T(8,128)}) fusion(f32[2304,1408]{1,0:T(8,128)} %fusion.80, bf16[2304,2048]{1,0:T(8,128)(2,1)} %bitcast.384, bf16[2048,1408]{1,0:T(8,128)(2,1)} %all-gather.20.cloned.1.call-done), kind=kOutput, calls=%fused_computation.23 | convolution fusion | flops 13307019264 | bytes 47644672 | tf_op jit(solution)/shard_map/dot_general | solution.py:788
  542.2 27.2 %multiply_convert_fusion.3 = (bf16[4096,704]{0,1:T(8,128)(2,1)}, bf16[4096,704]{0,1:T(8,128)(2,1)}, bf16[4096,704]{0,1:T(8,128)(2,1)}) fusion(f32[4096,704]{0,1:T(8,128)} %fusion.78, f32[4096,704]{0,1:T(8,128)} %fusion.79, bf16[704,2048]{1,0:T(8,128)(2,1)} %all-gather.16.cloned.1.call-done, bf16[4096,2048]{1,0:T(8,128)(2,1)} %constant_dynamic-update-slice_fusion, ...), kind=kOutput, calls=%fused_computation.26 | convolution fusion | flops 11879579648 | bytes 60047360 | tf_op jit(solution)/shard_map/dot_general | solution.py:788
  690.3 21.7 %fusion.8 = (f32[2304]{0:T(1024)S(1)}, bf16[2304,2048]{1,0:T(8,128)(2,1)}) fusion(bf16[8,288,2048]{2,1,0:T(8,128)(2,1)} %convolution_convert_fusion.7, bf16[2304,1408]{1,0:T(8,128)(2,1)} %get-tuple-element.258, bf16[1408,2048]{1,0:T(8,128)(2,1)} %all-gather.22.cloned.1.call-done), kind=kOutput, calls=%fused_computation.18 | convolution fusion | flops 13311145984 | bytes 31138816 | tf_op jit(solution)/shard_map/dot_general | solution.py:788
  712.0 19.2 %fusion.16 = f32[8,512,2048]{2,1,0:T(8,128)} fusion(bf16[8,288,2048]{2,1,0:T(8,128)(2,1)} %bitcast.327, s32[8,512]{1,0:T(8,128)S(1)} %copy-done.16), kind=kOutput, calls=%fused_computation.52 | convolution fusion | flops 4833017856 | bytes 43008000 | tf_op jit(solution)/shard_map/dot_general | solution.py:953
  741.9 20.0 %convolution_convert_fusion.5 = bf16[1408,2048]{1,0:T(8,128)(2,1)} fusion(bf16[2304,1408]{1,0:T(8,128)(2,1)} %get-tuple-element.258, bf16[2304,2048]{1,0:T(8,128)(2,1)} %fusion.7), kind=kOutput, calls=%fused_computation.38 | convolution fusion | flops 13290438656 | bytes 21692416 | tf_op jit(solution)/shard_map/dot_general | solution.py:788
  761.9 31.2 %fusion.1 = (f32[4096]{0:T(1024)S(1)}, bf16[4096,2048]{1,0:T(8,128)(2,1)}) fusion(bf16[4096,2048]{1,0:T(8,128)(2,1)} %constant_dynamic-update-slice_fusion, f32[8,512,2048]{2,1,0:T(8,128)} %fusion.16, f32[4096]{0:T(1024)S(1)} %bitcast.377, f32[4096]{0:T(1024)S(1)} %bitcast.376, bf16[4096,704]{0,1:T(8,128)(2,1)} %get-tuple-element.201, ...), kind=kOutput, calls=%fused_computation.5 | convolution fusion | flops 11869876224 | bytes 75808768 | tf_op jit(solution)/shard_map/dot_general | solution.py:788
  798.4 28.3 %multiply_convert_fusion = (bf16[2304,1408]{1,0:T(8,128)(2,1)}, bf16[2304,1408]{1,0:T(8,128)(2,1)}) fusion(f32[2304,1408]{1,0:T(8,128)} %fusion.80, f32[2304,1408]{1,0:T(8,128)} %get-tuple-element.259, bf16[2304,2048]{1,0:T(8,128)(2,1)} %fusion.7, bf16[1408,2048]{1,0:T(8,128)(2,1)} %all-gather.22.cloned.1.call-done), kind=kOutput, calls=%fused_computation.21 | convolution fusion | flops 13329727488 | bytes 54132736 | tf_op jit(solution)/shard_map/dot_general | solution.py:788
  826.7 20.3 %convolution_convert_fusion.4 = bf16[2048,1408]{1,0:T(8,128)(2,1)} fusion(bf16[2304,2048]{1,0:T(8,128)(2,1)} %bitcast.385, bf16[2304,1408]{1,0:T(8,128)(2,1)} %get-tuple-element.194), kind=kOutput, calls=%fused_computation.37 | convolution fusion | flops 13290438656 | bytes 21692416 | tf_op jit(solution)/shard_map/dot_general | solution.py:788
  847.0 21.3 %fusion.82 = f32[2304,2048]{1,0:T(8,128)} fusion(bf16[2304,1408]{1,0:T(8,128)(2,1)} %get-tuple-element.194, bf16[2048,1408]{1,0:T(8,128)(2,1)} %all-gather.18.cloned.1.call-done), kind=kOutput, calls=%fused_computation.235 | convolution fusion | flops 13287555072 | bytes 31129600 | tf_op jit(solution)/shard_map/dot_general | solution.py:788
  868.3 19.9 %fusion.81 = f32[4096,2048]{1,0:T(8,128)} fusion(bf16[4096,704]{0,1:T(8,128)(2,1)} %get-tuple-element.200, bf16[2048,704]{0,1:T(8,128)(2,1)S(1)} %copy-done.42), kind=kOutput, calls=%fused_computation.234 | convolution fusion | flops 11811160064 | bytes 42205184 | tf_op jit(solution)/shard_map/dot_general | solution.py:788
  888.2 22.0 %add_convert_fusion = bf16[2304,2048]{1,0:T(8,128)(2,1)} fusion(f32[2304,2048]{1,0:T(8,128)} %fusion.82, bf16[2304,1408]{1,0:T(8,128)(2,1)} %get-tuple-element.193, bf16[2048,1408]{1,0:T(8,128)(2,1)} %all-gather.20.cloned.1.call-done), kind=kOutput, calls=%fused_computation.19 | convolution fusion | flops 13296992256 | bytes 40566784 | tf_op jit(solution)/shard_map/dot_general | solution.py:788
  910.2 19.3 %fusion.15 = f32[8,512,2048]{2,1,0:T(8,128)} fusion(bf16[8,288,2048]{2,1,0:T(8,128)(2,1)} %bitcast.326, s32[8,512]{1,0:T(8,128)S(1)} %copy-done.17), kind=kOutput, calls=%fused_computation.51 | convolution fusion | flops 4833017856 | bytes 43008000 | tf_op jit(solution)/shard_map/dot_general | solution.py:953
  929.5 34.9 %fusion.2 = bf16[4096,2048]{1,0:T(8,128)(2,1)} fusion(f32[8,512,2048]{2,1,0:T(8,128)} %fusion.15, f32[4096,2048]{1,0:T(8,128)} %fusion.81, bf16[4096,704]{0,1:T(8,128)(2,1)} %get-tuple-element.199, bf16[2048,704]{0,1:T(8,128)(2,1)} %all-gather.14.cloned.1.call-done), kind=kOutput, calls=%fused_computation.7 | convolution fusion | flops 11836325888 | bytes 92536832 | tf_op jit(solution)/shard_map/dot_general | solution.py:788
  964.3 20.3 %convolution_convert_fusion.3 = bf16[2048,1408]{1,0:T(8,128)(2,1)} fusion(bf16[2304,2048]{1,0:T(8,128)(2,1)} %bitcast.386, bf16[2304,1408]{1,0:T(8,128)(2,1)} %get-tuple-element.193), kind=kOutput, calls=%fused_computation.36 | convolution fusion | flops 13290438656 | bytes 21692416 | tf_op jit(solution)/shard_map/dot_general | solution.py:788
  985.8 77.6 %shard_map.318 = f32[512,2048]{1,0:T(8,128)S(1)} custom-call(bf16[8,512,2048]{2,1,0:T(8,128)(2,1)} %bitcast.322), custom_call_target="tpu_custom_call" | custom-call | bytes 104857600 | tf_op jit(solution)/shard_map/pallas_call | solution.py:738
  1153.8 30.7 %shard_map.319 = bf16[4096,768]{1,0:T(8,128)(2,1)} custom-call(bf16[4096,768]{1,0:T(8,128)(2,1)} %convolution_convert_fusion.6.qkv_ref, bf16[4096,256]{1,0:T(8,128)(2,1)} %bitcast.60.grad_ref, s32[4096,1]{1,0:T(8,128)S(1)} %copy.212.q_code_ref, s32[4,1,1024]{2,1,0:T(1,128)S(1)} %bitcast.307), custom_call_target="tpu_custom_call" | custom-call | flops 10737418240 | bytes 12582912 | tf_op jit(solution)/shard_map/pallas_call | solution.py:502
  1184.6 19.1 %convolution_convert_fusion.9 = bf16[2048,768]{1,0:T(8,128)(2,1)S(1)} fusion(bf16[4096,2048]{1,0:T(8,128)(2,1)} %fusion.6, bf16[4096,768]{1,0:T(8,128)(2,1)} %shard_map.319), kind=kOutput, calls=%fused_computation.75 | convolution fusion | flops 12886474752 | bytes 26214400 | tf_op jit(solution)/shard_map/dot_general | solution.py:788
  1205.6 20.3 %convolution_convert_fusion = bf16[4096,2048]{1,0:T(8,128)(2,1)} fusion(bf16[4096,768]{1,0:T(8,128)(2,1)} %shard_map.319, bf16[2048,896]{1,0:T(8,128)(2,1)} %all-gather.10.cloned.1.call-done), kind=kOutput, calls=%fused_computation.20 | convolution fusion | flops 12893290496 | bytes 26214400 | tf_op jit(solution)/shard_map/dot_general | solution.py:788
  1230.5 122.2 %shard_map.320 = f32[512,2048]{1,0:T(8,128)S(1)} custom-call(bf16[8,512,2048]{2,1,0:T(8,128)(2,1)} %bitcast.323), custom_call_target="tpu_custom_call" | custom-call | bytes 104857600 | tf_op jit(solution)/shard_map/pallas_call | solution.py:738
  (357 shorter events, 539.9 us)
Async XLA Ops:
  7.2 106.1 %all-gather.24.cloned.1.call-start = ((), (), s32[]{:S(2)}) async-start(), calls=%async_computation.30 | async-start | bytes 1310720 | tf_op jit(solution)/shard_map/all_gather | solution.py:859
  9.5 112.2 %all-gather.10.cloned.1.call-start = ((), (), s32[]{:S(2)}) async-start(), calls=%async_computation.15 | async-start | bytes 4587520 | tf_op jit(solution)/shard_map/all_gather | solution.py:850
  17.5 223.7 %all-gather.12.cloned.1.call-start = ((), (), s32[]{:S(2)}) async-start(), calls=%async_computation.16 | async-start | bytes 3604480 | tf_op jit(solution)/shard_map/all_gather | solution.py:909
  19.3 221.9 %all-gather.14.cloned.1.call-start = ((), (), s32[]{:S(2)}) async-start(), calls=%async_computation.17 | async-start | bytes 3604480 | tf_op jit(solution)/shard_map/all_gather | solution.py:910
  22.1 319.2 %all-gather.18.cloned.1.call-start = ((), (), s32[]{:S(2)}) async-start(), calls=%async_computation.19 | async-start | bytes 7208960 | tf_op jit(solution)/shard_map/all_gather | solution.py:918
  103.9 343.9 %all-gather.20.cloned.1.call-start = ((), (), s32[]{:S(2)}) async-start(), calls=%async_computation.20 | async-start | bytes 7208960 | tf_op jit(solution)/shard_map/all_gather | solution.py:919
  104.4 437.7 %all-gather.16.cloned.1.call-start = ((), (), s32[]{:S(2)}) async-start(), calls=%async_computation.18 | async-start | bytes 3604480 | tf_op jit(solution)/shard_map/all_gather | solution.py:911
  105.4 584.8 %all-gather.22.cloned.1.call-start = ((), (), s32[]{:S(2)}) async-start(), calls=%async_computation.21 | async-start | bytes 7208960 | tf_op jit(solution)/shard_map/all_gather | solution.py:920
  198.5 787.2 %reduce-scatter.11.cloned.1.call-start = ((), (), s32[]{:S(2)}) async-start(), calls=%async_computation.23 | async-start | bytes 3604480 | tf_op jit(solution)/shard_map/reduce_scatter | solution.py:1034
  315.4 155.8 %collective-permute-start.6 = (bf16[512,2048]{1,0:T(8,128)(2,1)}, bf16[512,2048]{1,0:T(8,128)(2,1)}, u32[]{:S(2)}, u32[]{:S(2)}) collective-permute-start(bf16[512,2048]{1,0:T(8,128)(2,1)} %bitcast.317), channel_id=1, source_target_pairs={{0,24},{8,16},{16,8},{24,0},{1,25},{9,17},{17,9},{25,1},{2,26},{10... | collective-permute-start | bytes 6291464 | tf_op jit(solution)/shard_map/ppermute | solution.py:768
  316.9 154.3 %collective-permute-start.5 = (bf16[512,2048]{1,0:T(8,128)(2,1)}, bf16[512,2048]{1,0:T(8,128)(2,1)}, u32[]{:S(2)}, u32[]{:S(2)}) collective-permute-start(bf16[512,2048]{1,0:T(8,128)(2,1)} %bitcast.318), channel_id=1, source_target_pairs={{0,16},{8,24},{16,0},{24,8},{1,17},{9,25},{17,1},{25,9},{2,18},{10... | collective-permute-start | bytes 6291464 | tf_op jit(solution)/shard_map/ppermute | solution.py:768
  318.2 153.0 %collective-permute-start.4 = (bf16[512,2048]{1,0:T(8,128)(2,1)}, bf16[512,2048]{1,0:T(8,128)(2,1)}, u32[]{:S(2)}, u32[]{:S(2)}) collective-permute-start(bf16[512,2048]{1,0:T(8,128)(2,1)} %bitcast.319), channel_id=1, source_target_pairs={{0,8},{8,0},{16,24},{24,16},{1,9},{9,1},{17,25},{25,17},{2,10},{10... | collective-permute-start | bytes 6291464 | tf_op jit(solution)/shard_map/ppermute | solution.py:768
  603.6 382.2 %reduce-scatter.9.cloned.1.call-start = ((), (), s32[]{:S(2)}) async-start(), calls=%async_computation.22 | async-start | bytes 3604480 | tf_op jit(solution)/shard_map/reduce_scatter | solution.py:1034
  642.2 343.6 %reduce-scatter.13.cloned.1.call-start = ((), (), s32[]{:S(2)}) async-start(), calls=%async_computation.24 | async-start | bytes 3604480 | tf_op jit(solution)/shard_map/reduce_scatter | solution.py:1034
  690.2 463.6 %reduce-scatter.15.cloned.1.call-start = ((), (), s32[]{:S(2)}) async-start(), calls=%async_computation.25 | async-start | bytes 7208960 | tf_op jit(solution)/shard_map/reduce_scatter | solution.py:1034
  794.4 190.3 %all-to-all-start.1 = ((f32[8,2,512]{2,1,0:T(2,128)}), f32[8,2,512]{2,1,0:T(2,128)}, u32[]{:S(2)}, u32[]{:S(2)}) async-start(f32[8,2,512]{2,1,0:T(2,128)} %gather_fusion.1), calls=%async_computation.4 | async-start | bytes 65536 | tf_op jit(solution)/shard_map/all_to_all | solution.py:1043
  798.4 432.1 %reduce-scatter.17.cloned.1.call-start = ((), (), s32[]{:S(2)}) async-start(), calls=%async_computation.26 | async-start | bytes 7208960 | tf_op jit(solution)/shard_map/reduce_scatter | solution.py:1034
  846.9 507.7 %reduce-scatter.23.cloned.1.call-start = ((), (), s32[]{:S(2)}) async-start(), calls=%async_computation.29 | async-start | bytes 7208960 | tf_op jit(solution)/shard_map/reduce_scatter | solution.py:1034
  1123.7 257.0 %reduce-scatter.19.cloned.1.call-start = ((), (), s32[]{:S(2)}) async-start(), calls=%async_computation.27 | async-start | bytes 3932160 | tf_op jit(solution)/shard_map/reduce_scatter | solution.py:1099
  1137.0 89.0 %collective-permute-start.13 = (bf16[256,2048]{1,0:T(8,128)(2,1)S(1)}, bf16[256,2048]{1,0:T(8,128)(2,1)}, u32[]{:S(2)}, u32[]{:S(2)}) collective-permute-start(bf16[256,2048]{1,0:T(8,128)(2,1)S(1)} %get-tuple-element.202), channel_id=1, source_target_pairs={{0,8},{8,0},{16,24},{24,16},{1,9},{9,1},{17,25},{25,17},{2,10},{10... | collective-permute-start | bytes 3145736 | tf_op jit(solution)/shard_map/ppermute | solution.py:768
  1150.5 246.9 %collective-permute-start.11 = (bf16[512,2048]{1,0:T(8,128)(2,1)}, bf16[512,2048]{1,0:T(8,128)(2,1)}, u32[]{:S(2)}, u32[]{:S(2)}) collective-permute-start(bf16[512,2048]{1,0:T(8,128)(2,1)} %get-tuple-element.195), channel_id=1, source_target_pairs={{0,16},{8,24},{16,0},{24,8},{1,17},{9,25},{17,1},{25,9},{2,18},{10... | collective-permute-start | bytes 6291464 | tf_op jit(solution)/shard_map/ppermute | solution.py:768
  1152.4 245.0 %collective-permute-start.12 = (bf16[512,2048]{1,0:T(8,128)(2,1)}, bf16[512,2048]{1,0:T(8,128)(2,1)}, u32[]{:S(2)}, u32[]{:S(2)}) collective-permute-start(bf16[512,2048]{1,0:T(8,128)(2,1)} %get-tuple-element.196), channel_id=1, source_target_pairs={{0,24},{8,16},{16,8},{24,0},{1,25},{9,17},{17,9},{25,1},{2,26},{10... | collective-permute-start | bytes 6291464 | tf_op jit(solution)/shard_map/ppermute | solution.py:768
  1205.6 194.3 %reduce-scatter.21.cloned.1.call-start = ((), (), s32[]{:S(2)}) async-start(), calls=%async_computation.28 | async-start | bytes 1310720 | tf_op jit(solution)/shard_map/reduce_scatter | solution.py:1085
  1225.9 171.5 %collective-permute-start.9 = (bf16[512,2048]{1,0:T(8,128)(2,1)}, bf16[512,2048]{1,0:T(8,128)(2,1)}, u32[]{:S(2)}, u32[]{:S(2)}) collective-permute-start(bf16[512,2048]{1,0:T(8,128)(2,1)} %get-tuple-element.197), channel_id=1, source_target_pairs={{0,8},{8,0},{16,24},{24,16},{1,9},{9,1},{17,25},{25,17},{2,10},{10... | collective-permute-start | bytes 6291464 | tf_op jit(solution)/shard_map/ppermute | solution.py:768
  (65 other events, 2058.7 us)
Sparse Core Ops, SparseCore 0:
  10.2 30.6 all-gather.23
  43.0 71.5 all-gather.9
  116.8 57.7 all-gather.11
  176.6 57.8 all-gather.13
  235.9 105.4 all-gather.17
  342.8 104.9 all-gather.19
  450.0 57.4 all-gather.15
  509.0 105.3 all-gather.21
  617.3 54.4 reduce-scatter.10
  674.5 56.0 reduce-scatter.8
  733.5 56.0 reduce-scatter.12
  791.7 102.0 reduce-scatter.14
  896.2 102.7 reduce-scatter.16
  1077.2 100.5 reduce-scatter.22
  1205.7 60.7 reduce-scatter.18
  1372.3 27.4 reduce-scatter.20

commit v4 on v3

--- a/solution.py
+++ b/solution.py
@@ -637,25 +637,19 @@
         ],
         compiler_params=pltpu.CompilerParams(collective_id=number, has_side_effects=True),
         cost_estimate=pl.CostEstimate(
-            flops=0, bytes_accessed=100 * own.size, transcendentals=0
+            flops=0, bytes_accessed=own.size, transcendentals=0
         ),
     )(*operands)
 
 
-def plane_scatter_kernel(
-    relative,
-    part_ref,
-    out_ref,
-    own,
-    twin_got,
-    x_got,
-    y_got,
-    x_last,
-    y_last,
-    send_sem,
-    recv_sem,
-    local_sem,
-):
+def plane_scatter_kernel(relative, with_extra, *refs):
+    if with_extra:
+        part_ref, extra_ref, out_ref, *refs = refs
+        extra_out, refs = refs[:4], refs[4:]
+        extra_own, extra_got, extra_sems, refs = refs[0], refs[1], refs[2:5], refs[5:]
+    else:
+        part_ref, out_ref, *refs = refs
+    own, twin_got, x_got, y_got, x_last, y_last, send_sem, recv_sem, local_sem = refs
     at, core, across, along, far = plane_places()
     rows = part_ref.shape[1]
     half = rows // 2
@@ -703,6 +697,30 @@
             x_sent.append(send(4 + j, own.at[j, top], x_got.at[j], {EXP: across}))
         if j == 0 or j == 2:
             y_sent.append(send(6 + j // 2, own.at[j, bottom], y_got.at[j // 2], {EXP: along}))
+    if with_extra:
+        extra_here, extra_twin, extra_done = [], [], []
+        for k in range(4):
+            copy = pltpu.make_async_remote_copy(
+                src_ref=extra_ref.at[k + 4],
+                dst_ref=extra_got.at[k],
+                send_sem=extra_sems[0].at[k],
+                recv_sem=extra_sems[1].at[k],
+                device_id={CTX: 1 - core},
+                device_id_type=MESH_ID,
+            )
+            copy.start()
+            started.append(copy)
+            extra_twin.append(copy)
+            here = pltpu.make_async_copy(extra_ref.at[k], extra_own.at[k], extra_sems[2].at[k])
+            here.start()
+            extra_here.append(here)
+        for k in range(4):
+            extra_twin[k].wait_recv()
+            extra_here[k].wait()
+            add_rows(extra_own.at[k], 0, rows, extra_got.at[k], 0)
+            here = pltpu.make_async_copy(extra_own.at[k], extra_out[k], extra_sems[2].at[k])
+            here.start()
+            extra_done.append(here)
     x_sent[0].wait_recv()
     add_rows(own.at[2], 0, half, x_got.at[0], 0)
     last_y = send(8, own.at[2, top], y_last, {EXP: along})
@@ -727,20 +745,34 @@
     y_sent[1].wait_recv()
     last_x.wait_recv()
     finish(half, y_got, x_last)
+    if with_extra:
+        for copy in extra_done:
+            copy.wait()
     for copy in started:
         copy.wait_send()
 
 
-def plane_scatter(parts, relative, number, out_type):
+def plane_scatter(parts, relative, number, out_type, extra=None):
     plane, rows, cols = parts.shape
+    operands, extra_scratch = [parts], []
+    out_shape = [jax.ShapeDtypeStruct((rows, cols), out_type)]
+    out_specs = [pl.BlockSpec(memory_space=pltpu.VMEM)]
+    anywhere = pl.BlockSpec(memory_space=pl.ANY)
+    if extra is not None:
+        operands.append(extra)
+        out_shape += [jax.ShapeDtypeStruct((rows, cols), extra.dtype)] * 4
+        out_specs += [anywhere] * 4
+        extra_scratch = [pltpu.VMEM((4, rows, cols), extra.dtype)] * 2
+        extra_scratch += [pltpu.SemaphoreType.DMA((4,))] * 3
     half = rows // 2
     vmem = lambda *shape: pltpu.VMEM(shape, parts.dtype)
     return pl.pallas_call(
-        partial(plane_scatter_kernel, relative),
-        out_shape=jax.ShapeDtypeStruct((rows, cols), out_type),
-        in_specs=[pl.BlockSpec(memory_space=pl.ANY)],
-        out_specs=pl.BlockSpec(memory_space=pltpu.VMEM),
-        scratch_shapes=[
+        partial(plane_scatter_kernel, relative, extra is not None),
+        out_shape=out_shape,
+        in_specs=[anywhere] * len(operands),
+        out_specs=out_specs,
+        scratch_shapes=extra_scratch
+        + [
             vmem(4, rows, cols),
             vmem(4, rows, cols),
             vmem(2, half, cols),
@@ -752,12 +784,14 @@
             pltpu.SemaphoreType.DMA((4,)),
         ],
         compiler_params=pltpu.CompilerParams(
-            collective_id=number, has_side_effects=True, vmem_limit_bytes=44 * 2**20
+            collective_id=number,
+            has_side_effects=True,
+            vmem_limit_bytes=(36 if extra is None else 54) * 2**20,
         ),
         cost_estimate=pl.CostEstimate(
-            flops=0, bytes_accessed=100 * rows * cols, transcendentals=0
+            flops=0, bytes_accessed=rows * cols, transcendentals=0
         ),
-    )(parts)
+    )(*operands)
 
 
 def after(values, others):
@@ -962,6 +996,11 @@
         jnp.where(chosen, expert_gate.reshape(plane, 1, tokens), 0.0), axis=2
     ).reshape(plane * capacity, 1)
     expert_rows = low(rows_of(n2_all))
+    gate_pre = mm(n2_all, sh_gate)
+    up_pre = mm(n2_all, sh_up)
+    gate_act = gate_pre * jax.nn.sigmoid(gate_pre)
+    shared_hidden = low(gate_act * up_pre)
+    expert_rows = after(expert_rows, (shared_hidden, sh_down))
     gate_e = mm(expert_rows, ex_gate)
     up_e = mm(expert_rows, ex_up)
     act_e = gate_e * jax.nn.sigmoid(gate_e)
@@ -972,10 +1011,6 @@
     row_grads = low(row_cots.astype(jnp.float32) * slot_gates)
 
     shared_grads = low(sg_all * cot_all.astype(jnp.float32))
-    gate_pre = mm(n2_all, sh_gate)
-    up_pre = mm(n2_all, sh_up)
-    gate_act = gate_pre * jax.nn.sigmoid(gate_pre)
-    shared_hidden = low(gate_act * up_pre)
     shared_part = mm(shared_hidden, sh_down)
     cot_dot_shared = jnp.sum(shared_part * cot_all.astype(jnp.float32), axis=1)
     shared_hgrad = mm(shared_grads, sh_down, ((1,), (1,)))
@@ -984,27 +1019,16 @@
 
     rows_out = width // (halves * depth)
 
-    def own_units(grad):
-        grad = low(grad)
-        cut = lambda c, z: grad[:, (c * depth + z) * rows_out : (c * depth + z + 1) * rows_out]
-        return jnp.concatenate(
-            [
-                jnp.concatenate([cut(c, z) for c in range(halves)], axis=1)
-                for z in range(depth)
-            ]
-        )
-
-    def shared_scatter(grad):
-        total = grad.reshape(depth * part, halves, rows_out)
-        keep = lax.dynamic_index_in_dim(total, core, axis=1, keepdims=False)
-        give = lax.dynamic_index_in_dim(total, 1 - core, axis=1, keepdims=False)
-        both = jnp.stack([keep, twin(give)]).reshape(halves, depth, part, rows_out)
-        both = jnp.where(core == 0, both, both[::-1]).transpose(1, 0, 2, 3)
+    def shared_scatter(first, second):
+        keep = jnp.where(core == 0, first, second)
+        got = twin(jnp.where(core == 0, second, first))
+        both = jnp.where(core == 0, jnp.stack([keep, got]), jnp.stack([got, keep]))
+        both = both.reshape(halves, depth, part, rows_out).transpose(1, 0, 2, 3)
         return both.reshape(units, rows_out).astype(jnp.float32)
 
-    grad_sh_gate = own_units(mm(gate_grad_s, n2_all, ((0,), (0,))))
-    grad_sh_up = own_units(mm(up_grad_s, n2_all, ((0,), (0,))))
-    grad_sh_down = own_units(mm(shared_hidden, shared_grads, ((0,), (0,))))
+    grad_sh_gate = low(mm(gate_grad_s, n2_all, ((0,), (0,))))
+    grad_sh_up = low(mm(up_grad_s, n2_all, ((0,), (0,))))
+    grad_sh_down = low(mm(shared_hidden, shared_grads, ((0,), (0,))))
 
     result_e = low(mm(hidden_e, ex_down))
     row_dots = jnp.sum(result_e.astype(jnp.float32) * row_cots.astype(jnp.float32), axis=1)
@@ -1018,6 +1042,15 @@
     grad_ex_down = low(mm(hidden_e, row_grads, ((0,), (0,))))
     grad_ex_gate = low(mm(expert_rows, gate_grad_e, ((0,), (0,))))
     grad_ex_up = low(mm(expert_rows, up_grad_e, ((0,), (0,))))
+    scatter = lambda v, dim: lax.psum_scatter(v, DP, scatter_dimension=dim, tiled=True)
+    side = width // halves
+    shared_sums = [
+        [scatter(v[:, c * side : (c + 1) * side], 1) for c in range(halves)]
+        for v in (grad_sh_gate, grad_sh_up, grad_sh_down)
+    ]
+    grads_made = (grad_ex_down, grad_ex_gate, grad_ex_up)
+    grads = [scatter(v, dim) for v, dim in zip(grads_made, (1, 0, 0))]
+    result_e, gate_grad_s = after((result_e, gate_grad_s), grads_made)
     rows_grad = low(
         mm(gate_grad_e, ex_gate, ((1,), (1,))) + mm(up_grad_e, ex_up, ((1,), (1,)))
     )
@@ -1028,14 +1061,14 @@
         + mm(up_grad_s, sh_up, ((1,), (1,)))
         + back_to_tokens(rows_grad)
     )
-    grads = (grad_sh_gate, grad_sh_up, grad_sh_down, grad_ex_down, grad_ex_gate, grad_ex_up)
-    grads_made = grads
-    grads = [
-        lax.psum_scatter(v, DP, scatter_dimension=dim, tiled=True)
-        for v, dim in zip(grads, (0, 0, 0, 1, 0, 0))
-    ]
-    n2_grad_part = after(n2_grad_part, (grads_made, out_part, grads[:3]))
-    n2_grad = plane_scatter(n2_grad_part.reshape(plane, tokens, width), True, 3, jnp.float32)
+    n2_grad_part = after(n2_grad_part, (out_part, shared_sums))
+    n2_grad, *out_sums = plane_scatter(
+        n2_grad_part.reshape(plane, tokens, width),
+        True,
+        3,
+        jnp.float32,
+        out_part.reshape(plane, tokens, width),
+    )
 
     dots = jnp.stack([gate_dots, cot_dot_shared.reshape(plane, tokens)], axis=1)
     back = jnp.arange(plane, dtype=jnp.int32) ^ me
@@ -1071,23 +1104,21 @@
         grad_out, (place ^ k, c, 0, 0), (1, 1, width // plane, width)
     )[0, 0]
     attended_grad = to_columns(low(mm(low_residual, w_out_full, ((1,), (1,)))))
-    out_part = after(out_part, n2_grad).reshape(plane, tokens, width)
-    out_sums = twin_sums(out_part[:4], out_part[4:])
-    attended_grad = after(attended_grad, (out_sums, grads[3]))
-    qkv_grad = attention_call(qkv, attended_grad, q_codes, k_codes, seq_len)
     out_grad_sums = twin_sums(
         [block_of(k, core) for k in range(4)],
         jnp.stack([block_of(k, 1 - core) for k in range(4)]),
     )
+    attended_grad = after(attended_grad, (out_grad_sums, grads[0]))
+    qkv_grad = attention_call(qkv, attended_grad, q_codes, k_codes, seq_len)
     grad_qkv = low(mm(n1_all, qkv_grad, ((0,), (0,))))
     n1_grad = low(mm(qkv_grad, w_qkv, ((1,), (1,))))
-    grad_out = low(hop_sum(out_grad_sums, n1_grad))
+    grad_out = low(hop_sum(out_grad_sums, (n1_grad, grad_qkv)))
+    n1_grad = after(n1_grad, (grad_qkv, grad_out, grads[1]))
     grad_out = lax.psum_scatter(grad_out, DP, scatter_dimension=0, tiled=True)
-    n1_grad = after(n1_grad, (grad_qkv, out_grad_sums, grads[4]))
-    n1_grad = plane_scatter(n1_grad.reshape(plane, tokens, width), False, 1, jnp.float32)
+    n1_grad = plane_scatter(n1_grad.reshape(plane, tokens, width), False, 1, jnp.float32)[0]
     output = low(residual + hop_sum(out_sums, n1_grad))
     grad_sh_gate, grad_sh_up, grad_sh_down = [
-        shared_scatter(after(v, n1_grad)) for v in grads[:3]
+        shared_scatter(*after(v, n1_grad)) for v in shared_sums
     ]
     grad_sh_gate, grad_sh_up = grad_sh_gate.T, grad_sh_up.T
     fine = shard // plane
@@ -1126,7 +1157,7 @@
     )
     grad_out = after(grad_out, n1_grad).astype(jnp.float32)
     grad_ex_down, grad_ex_gate, grad_ex_up = [
-        after(v, n1_grad).astype(jnp.float32)[None] for v in grads[3:]
+        after(v, n1_grad).astype(jnp.float32)[None] for v in grads
     ]
     input_part, _ = norm_back(x_rows, inv_one, g_one, n1_grad)
     input_grad = low(residual_grad + input_part)

time: 1440 us -> 1540 us (1.069)
  waiting for transfers between devices: 120 us -> 276 us
  other arithmetic: 172 us -> 125 us
  Pallas kernels: 405 us -> 360 us
  local copies, waits for them, and re-layouts: 108 us -> 127 us
  blocking collectives: 7.92 us -> 24.3 us
    ppermute x12, waiting for transfers between devices: 4.26 us -> 98.4 us  [swap(): return lax.ppermute(values, EXP, [(i, i ^ bits) for i in range(4)])]
    concatenate x3 -> x0, other arithmetic: 49.3 us -> none  [own_units(): jnp.concatenate([jnp.concatenate([cut(c, z) for c in range(halves)], axis...]
    pallas_call x2, Pallas kernels: 200 us -> 154 us  [plane_scatter(): pl.pallas_call(partial(plane_scatter_kernel, relative, extra is not None)...]
    all_gather x1, waiting for transfers between devices: 0.02 us -> 26.3 us  [local_plane(): lax.all_gather(after(expert_w_down[0], info_all), DP, axis=1, tiled=True)]
    all_gather x1, waiting for transfers between devices: 9.26 us -> 31.1 us  [local_plane(): lax.all_gather(after(expert_w_gate[0], info_all), DP, axis=0, tiled=True)]
    all_to_all x1, waiting for transfers between devices: 0.01 us -> 19.9 us  [to_columns(): got = lax.all_to_all(send, PLANE, split_axis=0, concat_axis=0, tiled=True)]
    convert_element_type x7 -> x6, other arithmetic: 48.6 us -> 30.7 us  [low(): return values.astype(jnp.bfloat16)]
    convert_element_type x1, local copies, waits for them, and re-layouts: 1.23 us -> 18.8 us  [local_plane(): row_grads = low(row_cots.astype(jnp.float32) * slot_gates)]
  transfers between devices with their start and end apart: 41 -> 43, of which waited for: 7 -> 10; matrix products, arithmetic and copies ran while one was open for 58% -> 52% of each run, Pallas kernels for 28% -> 23%
where the time goes in v4:
time: 1540 us; the launch traced here: 1530 us
  matrix products  567 us (37%)
  Pallas kernels  360 us (23%)
  waiting for transfers between devices  276 us (18%)
  local copies, waits for them, and re-layouts  127 us (8%)
  other arithmetic  125 us (8%)
  starting transfers between devices  40.1 us (3%)
  blocking collectives  24.3 us (2%)
  between operations  15.4 us (1%)
    dot_general x28, matrix products, mm(): lax.dot_general(left, right, (dims, ((), ())), preferred_element_type=jnp...  502 us
    pallas_call x2, Pallas kernels, plane_gather(): pl.pallas_call(partial(plane_gather_kernel, info is not None, relative),...  155 us
    pallas_call x2, Pallas kernels, plane_scatter(): pl.pallas_call(partial(plane_scatter_kernel, relative, extra is not None)...  154 us
    ppermute x12, waiting for transfers between devices, swap(): return lax.ppermute(values, EXP, [(i, i ^ bits) for i in range(4)])  98.4 us
    all_gather x1, waiting for transfers between devices, local_plane(): lax.all_gather(after(expert_w_up[0], info_all), DP, axis=0, tiled=True)  85.8 us
    pallas_call x2, Pallas kernels, attention_call(): pl.pallas_call(partial(body, heads, step), grid=(rows // seq_len,), in_sp...  50.3 us
    dot_general x2, matrix products, back_to_tokens(): lax.dot_general(onehot, values.reshape(plane, capacity, width), (((1,), (...  38.6 us
    all_gather x1, waiting for transfers between devices, local_plane(): lax.all_gather(after(expert_w_gate[0], info_all), DP, axis=0, tiled=True)  31.1 us
  transfers between devices with their start and end apart: 43, of which 10 were waited for; matrix products, arithmetic and copies ran while one was open for 52% of the time, Pallas kernels for 23%

profile of v4, /device:TPU:0, one launch (start us, length us, event | category | flops | bytes accessed | tf_op | source)
XLA Modules:
  0.0 1534.8 jit_solution(2713450467468366515)
XLA Ops:
  23.8 81.0 %shard_map.315 = (bf16[8,512,2048]{2,1,0:T(8,128)(2,1)}, s32[8,8,512]{2,1,0:T(8,128)}) custom-call(bf16[512,2048]{1,0:T(8,128)(2,1)} %bitcast.303, s32[8,512]{1,0:T(8,128)} %concatenate.53.refs_1_), custom_call_target="tpu_custom_call" | custom-call | bytes 1048576 | tf_op jit(solution)/shard_map/pallas_call | solution.py:628
  237.5 74.1 %shard_map.317 = bf16[8,512,2048]{2,1,0:T(8,128)(2,1)} custom-call(bf16[512,2048]{1,0:T(8,128)(2,1)} %multiply_convert_fusion.7.refs_0_), custom_call_target="tpu_custom_call" | custom-call | bytes 1048576 | tf_op jit(solution)/shard_map/pallas_call | solution.py:628
  347.9 22.3 %multiply_convert_fusion.6 = (bf16[4096,704]{0,1:T(8,128)(2,1)}, f32[4096,704]{0,1:T(8,128)}) fusion(f32[4096,704]{0,1:T(8,128)} %fusion.74, bf16[4096,2048]{1,0:T(8,128)(2,1)} %bitcast.297, bf16[2048,704]{0,1:T(8,128)(2,1)} %all-gather.14.cloned.1.call-done), kind=kOutput, calls=%fused_computation.26 | convolution fusion | flops 11828461568 | bytes 48496640 | tf_op jit(solution)/shard_map/dot_general | solution.py:822
  370.2 31.1 %all-gather.18.cloned.1.call-done = bf16[2048,1408]{1,0:T(8,128)(2,1)} async-done(((bf16[512,1408]{1,0:T(8,128)(2,1)}), bf16[2048,1408]{1,0:T(8,128)(2,1)}) %all-gather.18.cloned.1.call-update) | async-done | bytes 5767184 | tf_op jit(solution)/shard_map/all_gather | solution.py:952
  401.2 20.9 %fusion.75 = f32[2304,1408]{1,0:T(8,128)} fusion(bf16[2304,2048]{1,0:T(8,128)(2,1)} %bitcast.366, bf16[2048,1408]{1,0:T(8,128)(2,1)} %all-gather.18.cloned.1.call-done), kind=kOutput, calls=%fused_computation.210 | convolution fusion | flops 13287555072 | bytes 28180480 | tf_op jit(solution)/shard_map/dot_general | solution.py:822
  422.1 85.8 %all-gather.20.cloned.1.call-done = bf16[2048,1408]{1,0:T(8,128)(2,1)} async-done(((bf16[512,1408]{1,0:T(8,128)(2,1)}), bf16[2048,1408]{1,0:T(8,128)(2,1)}) %all-gather.20.cloned.1.call-update) | async-done | bytes 5767184 | tf_op jit(solution)/shard_map/all_gather | solution.py:953
  507.9 23.6 %multiply_convert_fusion.3 = (bf16[2304,1408]{1,0:T(8,128)(2,1)}, f32[2304,1408]{1,0:T(8,128)}) fusion(f32[2304,1408]{1,0:T(8,128)} %fusion.75, bf16[2304,2048]{1,0:T(8,128)(2,1)} %bitcast.367, bf16[2048,1408]{1,0:T(8,128)(2,1)} %all-gather.20.cloned.1.call-done), kind=kOutput, calls=%fused_computation.21 | convolution fusion | flops 13307019264 | bytes 47644672 | tf_op jit(solution)/shard_map/dot_general | solution.py:822
  571.1 24.8 %multiply_convert_fusion.4 = (bf16[4096,704]{0,1:T(8,128)(2,1)}, bf16[4096,704]{0,1:T(8,128)(2,1)}) fusion(f32[4096,704]{0,1:T(8,128)} %fusion.74, f32[4096,704]{0,1:T(8,128)} %get-tuple-element.255, bf16[704,2048]{1,0:T(8,128)(2,1)S(1)} %copy-done.53, bf16[4096,2048]{1,0:T(8,128)(2,1)} %constant_dynamic-update-slice_fusion, f32[4096]{0:T(1024)S(1)} %bitcast.357), kind=kOutput, calls=%fused_computation.24 | convolution fusion | flops 11873812480 | bytes 54280192 | tf_op jit(solution)/shard_map/dot_general | solution.py:822
  617.1 26.3 %all-gather.22.cloned.1.call-done = bf16[1408,2048]{1,0:T(8,128)(2,1)} async-done(((bf16[1408,512]{1,0:T(8,128)(2,1)}), bf16[1408,2048]{1,0:T(8,128)(2,1)}) %all-gather.22.cloned.1.call-update) | async-done | bytes 5767184 | tf_op jit(solution)/shard_map/all_gather | solution.py:954
  643.4 20.8 %convolution_convert_fusion.1 = bf16[2304,2048]{0,1:T(8,128)(2,1)} fusion(bf16[2304,1408]{1,0:T(8,128)(2,1)} %get-tuple-element.256, bf16[1408,2048]{1,0:T(8,128)(2,1)} %all-gather.22.cloned.1.call-done), kind=kOutput, calls=%fused_computation.29 | convolution fusion | flops 13292273664 | bytes 21692416 | tf_op jit(solution)/shard_map/dot_general | solution.py:822
  789.2 28.7 %multiply_convert_fusion.1 = (bf16[2304,1408]{1,0:T(8,128)(2,1)}, bf16[2304,1408]{1,0:T(8,128)(2,1)}) fusion(f32[2304,1408]{1,0:T(8,128)} %fusion.75, f32[2304,1408]{1,0:T(8,128)} %get-tuple-element.257, bf16[2304,2048]{1,0:T(8,128)(2,1)} %multiply_convert_fusion, bf16[1408,2048]{1,0:T(8,128)(2,1)} %all-gather.22.cloned.1.call-done), kind=kOutput, calls=%fused_computation.19 | convolution fusion | flops 13329727488 | bytes 54132736 | tf_op jit(solution)/shard_map/dot_general | solution.py:822
  817.9 20.2 %convolution_convert_fusion.4 = bf16[2048,1408]{1,0:T(8,128)(2,1)} fusion(bf16[2304,2048]{1,0:T(8,128)(2,1)} %bitcast.368, bf16[2304,1408]{1,0:T(8,128)(2,1)} %get-tuple-element.212), kind=kOutput, calls=%fused_computation.36 | convolution fusion | flops 13290438656 | bytes 21692416 | tf_op jit(solution)/shard_map/dot_general | solution.py:822
  842.4 20.4 %convolution_convert_fusion.3 = bf16[2048,1408]{1,0:T(8,128)(2,1)} fusion(bf16[2304,2048]{1,0:T(8,128)(2,1)} %bitcast.369, bf16[2304,1408]{1,0:T(8,128)(2,1)} %get-tuple-element.211), kind=kOutput, calls=%fused_computation.35 | convolution fusion | flops 13290438656 | bytes 21692416 | tf_op jit(solution)/shard_map/dot_general | solution.py:822
  894.8 30.0 %fusion.1 = (f32[4096]{0:T(1024)S(1)}, bf16[4096,2048]{1,0:T(8,128)(2,1)}) fusion(bf16[4096,2048]{1,0:T(8,128)(2,1)} %constant_dynamic-update-slice_fusion, f32[8,512,2048]{2,1,0:T(8,128)} %fusion.13, f32[4096]{0:T(1024)S(1)} %bitcast.360, f32[4096]{0:T(1024)S(1)} %bitcast.359, bf16[4096,704]{0,1:T(8,128)(2,1)} %get-tuple-element.254, ...), kind=kOutput, calls=%fused_computation.5 | convolution fusion | flops 11869876224 | bytes 75808768 | tf_op jit(solution)/shard_map/dot_general | solution.py:822
  930.1 20.7 %fusion.77 = f32[2304,2048]{1,0:T(8,128)} fusion(bf16[2304,1408]{1,0:T(8,128)(2,1)} %get-tuple-element.212, bf16[2048,1408]{1,0:T(8,128)(2,1)} %all-gather.18.cloned.1.call-done), kind=kOutput, calls=%fused_computation.212 | convolution fusion | flops 13287555072 | bytes 31129600 | tf_op jit(solution)/shard_map/dot_general | solution.py:822
  950.8 22.4 %add_convert_fusion = bf16[2304,2048]{1,0:T(8,128)(2,1)} fusion(f32[2304,2048]{1,0:T(8,128)} %fusion.77, bf16[2304,1408]{1,0:T(8,128)(2,1)} %get-tuple-element.211, bf16[2048,1408]{1,0:T(8,128)(2,1)} %all-gather.20.cloned.1.call-done), kind=kOutput, calls=%fused_computation.16 | convolution fusion | flops 13296992256 | bytes 40566784 | tf_op jit(solution)/shard_map/dot_general | solution.py:822
  992.6 20.3 %fusion.76 = f32[4096,2048]{1,0:T(8,128)} fusion(bf16[4096,704]{0,1:T(8,128)(2,1)} %get-tuple-element.72, bf16[2048,704]{0,1:T(8,128)(2,1)S(1)} %copy-done.52), kind=kOutput, calls=%fused_computation.211 | convolution fusion | flops 11811160064 | bytes 42205184 | tf_op jit(solution)/shard_map/dot_general | solution.py:822
  1013.0 35.3 %fusion.4 = bf16[4096,2048]{1,0:T(8,128)(2,1)} fusion(f32[8,512,2048]{2,1,0:T(8,128)} %fusion.14, f32[4096,2048]{1,0:T(8,128)} %fusion.76, bf16[4096,704]{0,1:T(8,128)(2,1)} %get-tuple-element.213, bf16[2048,704]{0,1:T(8,128)(2,1)} %all-gather.14.cloned.1.call-done), kind=kOutput, calls=%fused_computation.10 | convolution fusion | flops 11836325888 | bytes 92536832 | tf_op jit(solution)/shard_map/dot_general | solution.py:822
  1048.6 80.0 %shard_map.318 = (f32[512,2048]{1,0:T(8,128)}, bf16[512,2048]{1,0:T(8,128)(2,1)}, bf16[512,2048]{1,0:T(8,128)(2,1)}, bf16[512,2048]{1,0:T(8,128)(2,1)}, bf16[512,2048]{1,0:T(8,128)(2,1)}) custom-call(bf16[8,512,2048]{2,1,0:T(8,128)(2,1)} %bitcast.311, bf16[8,512,2048]{2,1,0:T(8,128)(2,1)} %bitcast.310), custom_call_target="tpu_custom_call" | custom-call | bytes 1048576 | tf_op jit(solution)/shard_map/pallas_call | solution.py:769
  1187.7 30.9 %shard_map.319 = bf16[4096,768]{1,0:T(8,128)(2,1)} custom-call(bf16[4096,768]{1,0:T(8,128)(2,1)} %convolution_convert_fusion.6.qkv_ref, bf16[4096,256]{1,0:T(8,128)(2,1)} %bitcast.58.grad_ref, s32[4096,1]{1,0:T(8,128)S(1)} %copy.229.q_code_ref, s32[4,1,1024]{2,1,0:T(1,128)S(1)} %bitcast.295), custom_call_target="tpu_custom_call" | custom-call | flops 10737418240 | bytes 12582912 | tf_op jit(solution)/shard_map/pallas_call | solution.py:502
  1240.8 24.3 %all_to_all.35 = f32[8,16,256]{2,1,0:T(8,128)S(1)} all-to-all(f32[8,16,256]{2,1,0:T(8,128)S(1)} %bitcast.350), channel_id=1, replica_groups=mesh['experts'=4,'context'=2,'dp'=4] {'experts','context'}, dimensions={0} | all-to-all | bytes 262144 | tf_op jit(solution)/shard_map/all_to_all | solution.py:1095
  1283.3 20.5 %convolution_convert_fusion = bf16[4096,2048]{1,0:T(8,128)(2,1)} fusion(bf16[4096,768]{1,0:T(8,128)(2,1)} %shard_map.319, bf16[2048,896]{1,0:T(8,128)(2,1)} %all-gather.10.cloned.1.call-done), kind=kOutput, calls=%fused_computation.18 | convolution fusion | flops 12893290496 | bytes 26214400 | tf_op jit(solution)/shard_map/dot_general | solution.py:822
  1303.8 88.0 %collective-permute-done.11 = bf16[256,2048]{1,0:T(8,128)(2,1)S(1)} collective-permute-done((bf16[256,2048]{1,0:T(8,128)(2,1)}, bf16[256,2048]{1,0:T(8,128)(2,1)S(1)}, u32[]{:S(2)}, u32[]{:S(2)}) %collective-permute-start.11) | collective-permute-done | bytes 1048608 | tf_op jit(solution)/shard_map/ppermute | solution.py:802
  1394.8 74.3 %shard_map.320 = f32[512,2048]{1,0:T(8,128)S(1)} custom-call(bf16[8,512,2048]{2,1,0:T(8,128)(2,1)} %bitcast.309), custom_call_target="tpu_custom_call" | custom-call | bytes 1048576 | tf_op jit(solution)/shard_map/pallas_call | solution.py:769
  (368 shorter events, 592.8 us)
Async XLA Ops:
  17.5 220.0 %all-gather.12.cloned.1.call-start = ((), (), s32[]{:S(2)}) async-start(), calls=%async_computation.19 | async-start | bytes 3604480 | tf_op jit(solution)/shard_map/all_gather | solution.py:943
  19.3 218.2 %all-gather.14.cloned.1.call-start = ((), (), s32[]{:S(2)}) async-start(), calls=%async_computation.20 | async-start | bytes 3604480 | tf_op jit(solution)/shard_map/all_gather | solution.py:944
  22.0 348.1 %all-gather.16.cloned.1.call-start = ((), (), s32[]{:S(2)}) async-start(), calls=%async_computation.21 | async-start | bytes 3604480 | tf_op jit(solution)/shard_map/all_gather | solution.py:945
  23.0 378.2 %all-gather.18.cloned.1.call-start = ((), (), s32[]{:S(2)}) async-start(), calls=%async_computation.22 | async-start | bytes 7208960 | tf_op jit(solution)/shard_map/all_gather | solution.py:952
  104.8 403.1 %all-gather.20.cloned.1.call-start = ((), (), s32[]{:S(2)}) async-start(), calls=%async_computation.23 | async-start | bytes 7208960 | tf_op jit(solution)/shard_map/all_gather | solution.py:953
  197.4 446.1 %all-gather.22.cloned.1.call-start = ((), (), s32[]{:S(2)}) async-start(), calls=%async_computation.24 | async-start | bytes 7208960 | tf_op jit(solution)/shard_map/all_gather | solution.py:954
  311.6 219.8 %collective-permute-start.6 = (bf16[512,2048]{1,0:T(8,128)(2,1)}, bf16[512,2048]{1,0:T(8,128)(2,1)}, u32[]{:S(2)}, u32[]{:S(2)}) collective-permute-start(bf16[512,2048]{1,0:T(8,128)(2,1)} %bitcast.304), channel_id=1, source_target_pairs={{0,24},{8,16},{16,8},{24,0},{1,25},{9,17},{17,9},{25,1},{2,26},{10... | collective-permute-start | bytes 6291464 | tf_op jit(solution)/shard_map/ppermute | solution.py:802
  313.2 218.3 %collective-permute-start.5 = (bf16[512,2048]{1,0:T(8,128)(2,1)}, bf16[512,2048]{1,0:T(8,128)(2,1)}, u32[]{:S(2)}, u32[]{:S(2)}) collective-permute-start(bf16[512,2048]{1,0:T(8,128)(2,1)} %bitcast.305), channel_id=1, source_target_pairs={{0,16},{8,24},{16,0},{24,8},{1,17},{9,25},{17,1},{25,9},{2,18},{10... | collective-permute-start | bytes 6291464 | tf_op jit(solution)/shard_map/ppermute | solution.py:802
  314.5 217.0 %collective-permute-start.4 = (bf16[512,2048]{1,0:T(8,128)(2,1)}, bf16[512,2048]{1,0:T(8,128)(2,1)}, u32[]{:S(2)}, u32[]{:S(2)}) collective-permute-start(bf16[512,2048]{1,0:T(8,128)(2,1)} %bitcast.306), channel_id=1, source_target_pairs={{0,8},{8,0},{16,24},{24,16},{1,9},{9,1},{17,25},{25,17},{2,10},{10... | collective-permute-start | bytes 6291464 | tf_op jit(solution)/shard_map/ppermute | solution.py:802
  538.1 510.2 %reduce-scatter.18.cloned.1.call-start = ((), (), s32[]{:S(2)}) async-start(), calls=%async_computation.28 | async-start | bytes 1802240 | tf_op jit(solution)/shard_map/reduce_scatter | solution.py:1045
  615.2 433.2 %reduce-scatter.16.cloned.1.call-start = ((), (), s32[]{:S(2)}) async-start(), calls=%async_computation.27 | async-start | bytes 1802240 | tf_op jit(solution)/shard_map/reduce_scatter | solution.py:1045
  664.2 384.2 %reduce-scatter.14.cloned.1.call-start = ((), (), s32[]{:S(2)}) async-start(), calls=%async_computation.26 | async-start | bytes 1802240 | tf_op jit(solution)/shard_map/reduce_scatter | solution.py:1045
  683.5 364.9 %reduce-scatter.12.cloned.1.call-start = ((), (), s32[]{:S(2)}) async-start(), calls=%async_computation.25 | async-start | bytes 1802240 | tf_op jit(solution)/shard_map/reduce_scatter | solution.py:1045
  728.6 319.8 %reduce-scatter.22.cloned.1.call-start = ((), (), s32[]{:S(2)}) async-start(), calls=%async_computation.30 | async-start | bytes 1802240 | tf_op jit(solution)/shard_map/reduce_scatter | solution.py:1045
  748.2 300.3 %reduce-scatter.20.cloned.1.call-start = ((), (), s32[]{:S(2)}) async-start(), calls=%async_computation.29 | async-start | bytes 1802240 | tf_op jit(solution)/shard_map/reduce_scatter | solution.py:1045
  769.2 418.4 %reduce-scatter.24.cloned.1.call-start = ((), (), s32[]{:S(2)}) async-start(), calls=%async_computation.31 | async-start | bytes 7208960 | tf_op jit(solution)/shard_map/reduce_scatter | solution.py:1045
  789.1 605.6 %reduce-scatter.26.cloned.1.call-start = ((), (), s32[]{:S(2)}) async-start(), calls=%async_computation.32 | async-start | bytes 7208960 | tf_op jit(solution)/shard_map/reduce_scatter | solution.py:1045
  838.1 651.9 %reduce-scatter.32.cloned.1.call-start = ((), (), s32[]{:S(2)}) async-start(), calls=%async_computation.35 | async-start | bytes 7208960 | tf_op jit(solution)/shard_map/reduce_scatter | solution.py:1045
  926.2 122.0 %all-to-all-start.1 = ((f32[8,2,512]{2,1,0:T(2,128)}), f32[8,2,512]{2,1,0:T(2,128)S(1)}, u32[]{:S(2)}, u32[]{:S(2)}) async-start(f32[8,2,512]{2,1,0:T(2,128)} %gather_fusion.1), calls=%async_computation.7 | async-start | bytes 65536 | tf_op jit(solution)/shard_map/all_to_all | solution.py:1076
  1161.0 330.5 %reduce-scatter.28.cloned.1.call-start = ((), (), s32[]{:S(2)}) async-start(), calls=%async_computation.33 | async-start | bytes 3932160 | tf_op jit(solution)/shard_map/reduce_scatter | solution.py:1130
  1269.2 246.2 %reduce-scatter.30.cloned.1.call-start = ((), (), s32[]{:S(2)}) async-start(), calls=%async_computation.34 | async-start | bytes 1310720 | tf_op jit(solution)/shard_map/reduce_scatter | solution.py:1117
  1273.9 195.2 %collective-permute-start.8 = (bf16[512,2048]{1,0:T(8,128)(2,1)}, bf16[512,2048]{1,0:T(8,128)(2,1)}, u32[]{:S(2)}, u32[]{:S(2)}) collective-permute-start(bf16[512,2048]{1,0:T(8,128)(2,1)} %get-tuple-element.76), channel_id=1, source_target_pairs={{0,8},{8,0},{16,24},{24,16},{1,9},{9,1},{17,25},{25,17},{2,10},{10... | collective-permute-start | bytes 6291464 | tf_op jit(solution)/shard_map/ppermute | solution.py:802
  1276.7 192.4 %collective-permute-start.13 = (bf16[512,2048]{1,0:T(8,128)(2,1)}, bf16[512,2048]{1,0:T(8,128)(2,1)}, u32[]{:S(2)}, u32[]{:S(2)}) collective-permute-start(bf16[512,2048]{1,0:T(8,128)(2,1)} %get-tuple-element.84), channel_id=1, source_target_pairs={{0,16},{8,24},{16,0},{24,8},{1,17},{9,25},{17,1},{25,9},{2,18},{10... | collective-permute-start | bytes 6291464 | tf_op jit(solution)/shard_map/ppermute | solution.py:802
  1277.4 191.8 %collective-permute-start.14 = (bf16[512,2048]{1,0:T(8,128)(2,1)}, bf16[512,2048]{1,0:T(8,128)(2,1)}, u32[]{:S(2)}, u32[]{:S(2)}) collective-permute-start(bf16[512,2048]{1,0:T(8,128)(2,1)} %get-tuple-element.86), channel_id=1, source_target_pairs={{0,24},{8,16},{16,8},{24,0},{1,25},{9,17},{17,9},{25,1},{2,26},{10... | collective-permute-start | bytes 6291464 | tf_op jit(solution)/shard_map/ppermute | solution.py:802
  (77 other events, 2226.4 us)
Sparse Core Ops, SparseCore 0:
  10.2 30.6 all-gather.23
  43.0 71.5 all-gather.9
  116.8 57.7 all-gather.11
  176.6 57.8 all-gather.13
  236.4 57.8 all-gather.15
  295.8 105.3 all-gather.17
  402.8 104.9 all-gather.19
  538.3 105.1 all-gather.21
  646.3 31.5 reduce-scatter.17
  680.6 32.1 reduce-scatter.15
  715.7 32.1 reduce-scatter.13
  750.6 32.1 reduce-scatter.11
  785.6 32.1 reduce-scatter.21
  820.5 32.1 reduce-scatter.19
  854.9 101.1 reduce-scatter.23
  958.2 102.7 reduce-scatter.25
  1063.1 102.7 reduce-scatter.31
  1239.8 56.8 reduce-scatter.27
  1472.2 28.1 reduce-scatter.29

commit v5 on v4

--- a/solution.py
+++ b/solution.py
@@ -794,6 +794,193 @@
     )(*operands)
 
 
+def chosen_rows(slots, capacity):
+    lanes = lax.broadcasted_iota(jnp.int32, (slots.shape[0], capacity), 1)
+    return (slots == lanes).astype(jnp.bfloat16)
+
+
+def output_kernel(
+    half,
+    hidden_ref,
+    down_ref,
+    rows_ref,
+    slot_ref,
+    sg_ref,
+    gate_ref,
+    cot_ref,
+    near_ref,
+    dots_ref,
+    given,
+    got,
+    send_sem,
+    recv_sem,
+):
+    step_at = pl.program_id(0)
+    is_far = step_at < half
+    slot = lax.rem(step_at, half)
+    twin_id = {CTX: 1 - lax.axis_index(CTX)}
+
+    @pl.when(step_at == 0)
+    def _():
+        barrier = pltpu.get_barrier_semaphore()
+        pl.semaphore_signal(barrier, inc=1, device_id=twin_id, device_id_type=MESH_ID)
+        pl.semaphore_wait(barrier, 1)
+
+    def block_copy(k):
+        return pltpu.make_async_remote_copy(
+            src_ref=given.at[k],
+            dst_ref=got.at[k],
+            send_sem=send_sem.at[k],
+            recv_sem=recv_sem.at[k],
+            device_id=twin_id,
+            device_id_type=MESH_ID,
+        )
+
+    @pl.when(jnp.logical_not(is_far))
+    def _():
+        block_copy(slot).wait_recv()
+
+    chosen = chosen_rows(slot_ref[...], rows_ref.shape[1])
+    width = down_ref.shape[1]
+    step = 512
+    gate_dot, shared_dot = 0.0, 0.0
+    for first in range(0, width, step):
+        cols = pl.ds(first, step)
+        shared = mm(hidden_ref[...], down_ref[:, cols], ((0,), (0,)))
+        picked = mm(chosen, rows_ref[0, :, cols])
+        cot = cot_ref[:, cols].astype(jnp.float32)
+        gate_dot += jnp.sum(picked * cot, axis=1, keepdims=True)
+        shared_dot += jnp.sum(shared * cot, axis=1, keepdims=True)
+        total = sg_ref[...] * shared + gate_ref[...] * picked
+
+        @pl.when(is_far)
+        def _():
+            given[slot, :, cols] = low(total)
+
+        @pl.when(jnp.logical_not(is_far))
+        def _():
+            near_ref[0, :, cols] = low(total + got[slot, :, cols].astype(jnp.float32))
+
+    lanes = lax.broadcasted_iota(jnp.int32, dots_ref.shape, 1)
+    dots_ref[...] = jnp.where(lanes == 0, gate_dot, jnp.where(lanes == 1, shared_dot, 0.0))
+
+    @pl.when(is_far)
+    def _():
+        block_copy(slot).start()
+
+    @pl.when(step_at == 2 * half - 1)
+    def _():
+        for k in range(half):
+            block_copy(k).wait_send()
+
+
+def output_parts(hidden, down, rows, slots, sg, gates, cot):
+    blocks, capacity, width = rows.shape
+    units, count = hidden.shape
+    tokens, half = count // blocks, blocks // 2
+    at = lambda i: lax.rem(i + half, blocks)
+    column = pl.BlockSpec((tokens, 1), lambda i: (at(i), 0))
+    return pl.pallas_call(
+        partial(output_kernel, half),
+        grid=(blocks,),
+        in_specs=[
+            pl.BlockSpec((units, tokens), lambda i: (0, at(i))),
+            pl.BlockSpec((units, width), lambda i: (0, 0)),
+            pl.BlockSpec((1, capacity, width), lambda i: (at(i), 0, 0)),
+            column,
+            column,
+            column,
+            pl.BlockSpec((tokens, width), lambda i: (at(i), 0)),
+        ],
+        out_specs=[
+            pl.BlockSpec((1, tokens, width), lambda i: (jnp.maximum(i - half, 0), 0, 0)),
+            pl.BlockSpec((tokens, 128), lambda i: (at(i), 0)),
+        ],
+        out_shape=[
+            jax.ShapeDtypeStruct((half, tokens, width), jnp.bfloat16),
+            jax.ShapeDtypeStruct((count, 128), jnp.float32),
+        ],
+        scratch_shapes=[
+            pltpu.VMEM((half, tokens, width), jnp.bfloat16),
+            pltpu.VMEM((half, tokens, width), jnp.bfloat16),
+            pltpu.SemaphoreType.DMA((half,)),
+            pltpu.SemaphoreType.DMA((half,)),
+        ],
+        compiler_params=pltpu.CompilerParams(
+            collective_id=4, has_side_effects=True, vmem_limit_bytes=56 * 2**20
+        ),
+        cost_estimate=pl.CostEstimate(
+            flops=2 * count * width * (units + capacity),
+            bytes_accessed=6 * count * width,
+            transcendentals=0,
+        ),
+    )(hidden, down, rows, slots, sg, gates, cot)
+
+
+def n2_grad_kernel(dgate_ref, dup_ref, gate_ref, up_ref, rows_ref, slot_ref, out_ref):
+    chosen = chosen_rows(slot_ref[...], rows_ref.shape[1])
+    step = 512
+    for first in range(0, gate_ref.shape[1], step):
+        cols = pl.ds(first, step)
+        total = mm(dgate_ref[...], gate_ref[:, cols], ((0,), (0,)))
+        total += mm(dup_ref[...], up_ref[:, cols], ((0,), (0,)))
+        out_ref[0, :, cols] = low(total + mm(chosen, rows_ref[0, :, cols]))
+
+
+def n2_grad_parts(dgate, dup, gate_w, up_w, rows, slots):
+    blocks, capacity, width = rows.shape
+    units, count = dgate.shape
+    tokens = count // blocks
+    by_units = pl.BlockSpec((units, tokens), lambda i: (0, i))
+    whole = pl.BlockSpec((units, width), lambda i: (0, 0))
+    return pl.pallas_call(
+        n2_grad_kernel,
+        grid=(blocks,),
+        in_specs=[
+            by_units,
+            by_units,
+            whole,
+            whole,
+            pl.BlockSpec((1, capacity, width), lambda i: (i, 0, 0)),
+            pl.BlockSpec((tokens, 1), lambda i: (i, 0)),
+        ],
+        out_specs=pl.BlockSpec((1, tokens, width), lambda i: (i, 0, 0)),
+        out_shape=jax.ShapeDtypeStruct((blocks, tokens, width), jnp.bfloat16),
+        compiler_params=pltpu.CompilerParams(vmem_limit_bytes=48 * 2**20),
+        cost_estimate=pl.CostEstimate(
+            flops=2 * count * width * (2 * units + capacity),
+            bytes_accessed=4 * count * width,
+            transcendentals=0,
+        ),
+    )(dgate, dup, gate_w, up_w, rows, slots)
+
+
+def unit_grad_kernel(left_ref, right_ref, out_ref):
+    out_ref[0] = low(mm(left_ref[...], right_ref[...]))
+
+
+def unit_grads(left, right, depth, halves):
+    units, count = left.shape
+    width = right.shape[1]
+    cols = width // (depth * halves)
+    return pl.pallas_call(
+        unit_grad_kernel,
+        grid=(depth * halves,),
+        in_specs=[
+            pl.BlockSpec((units, count), lambda i: (0, 0)),
+            pl.BlockSpec((count, cols), lambda i: (0, i)),
+        ],
+        out_specs=pl.BlockSpec((1, units, cols), lambda i: (lax.rem(i, depth), 0, i // depth)),
+        out_shape=jax.ShapeDtypeStruct((depth, units, halves * cols), jnp.bfloat16),
+        compiler_params=pltpu.CompilerParams(vmem_limit_bytes=48 * 2**20),
+        cost_estimate=pl.CostEstimate(
+            flops=2 * units * count * width,
+            bytes_accessed=2 * (units * count + count * width + units * width),
+            transcendentals=0,
+        ),
+    )(left, right)
+
+
 def after(values, others):
     return lax.optimization_barrier((values, others))[0]
 
@@ -811,11 +998,12 @@
     return [low(ours[k].astype(jnp.float32) + got[k].astype(jnp.float32)) for k in range(4)]
 
 
-def hop_sum(sums, later):
-    total = sums[0].astype(jnp.float32)
-    for k in (1, 2, 3):
-        total = total + after(swap(sums[k], k), later).astype(jnp.float32)
-    return total
+def hops(sums):
+    return [sums[0]] + [swap(sums[k], k) for k in (1, 2, 3)]
+
+
+def sum_up(parts):
+    return sum(v.astype(jnp.float32) for v in parts)
 
 
 def mm(left, right, dims=((1,), (0,))):
@@ -942,6 +1130,7 @@
     ).reshape(w.shape[0], depth * part)
     sh_gate = lax.all_gather(pick(shared_w_gate), DP, axis=0, tiled=True)
     sh_up = lax.all_gather(pick(shared_w_up), DP, axis=0, tiled=True)
+    sh_gate_t, sh_up_t = sh_gate.T, sh_up.T
     sh_down = lax.all_gather(
         lax.dynamic_slice(shared_w_down, (core * part, 0), (part, width)), DP, axis=0, tiled=True
     )
@@ -983,21 +1172,12 @@
         )
         return got.reshape(plane * capacity, width)
 
-    def back_to_tokens(values):
-        got = lax.dot_general(
-            onehot,
-            values.reshape(plane, capacity, width),
-            (((1,), (1,)), ((0,), (0,))),
-            preferred_element_type=jnp.float32,
-        )
-        return got.reshape(all_tokens, width)
-
     slot_gates = jnp.sum(
         jnp.where(chosen, expert_gate.reshape(plane, 1, tokens), 0.0), axis=2
     ).reshape(plane * capacity, 1)
     expert_rows = low(rows_of(n2_all))
-    gate_pre = mm(n2_all, sh_gate)
-    up_pre = mm(n2_all, sh_up)
+    gate_pre = mm(sh_gate_t, n2_all, ((1,), (1,)))
+    up_pre = mm(sh_up_t, n2_all, ((1,), (1,)))
     gate_act = gate_pre * jax.nn.sigmoid(gate_pre)
     shared_hidden = low(gate_act * up_pre)
     expert_rows = after(expert_rows, (shared_hidden, sh_down))
@@ -1005,36 +1185,37 @@
     up_e = mm(expert_rows, ex_up)
     act_e = gate_e * jax.nn.sigmoid(gate_e)
     hidden_e = low(act_e * up_e)
-    cot_near = jnp.concatenate([cot_own] + [after(v, hidden_e) for v in cot_got])
+    cot_near = jnp.concatenate([cot_own] + [after(v, gate_e) for v in cot_got])
     cot_all = jnp.concatenate([cot_near, twin(cot_near)])
     row_cots = low(rows_of(cot_all))
     row_grads = low(row_cots.astype(jnp.float32) * slot_gates)
 
     shared_grads = low(sg_all * cot_all.astype(jnp.float32))
-    shared_part = mm(shared_hidden, sh_down)
-    cot_dot_shared = jnp.sum(shared_part * cot_all.astype(jnp.float32), axis=1)
-    shared_hgrad = mm(shared_grads, sh_down, ((1,), (1,)))
+    shared_hgrad = mm(sh_down, shared_grads, ((1,), (1,)))
     gate_grad_s = low(shared_hgrad * up_pre * silu_grad(gate_pre))
     up_grad_s = low(shared_hgrad * gate_act)
-
     rows_out = width // (halves * depth)
 
-    def shared_scatter(first, second):
+    def shared_scatter(total):
+        first, second = total[:, :rows_out], total[:, rows_out:]
         keep = jnp.where(core == 0, first, second)
         got = twin(jnp.where(core == 0, second, first))
         both = jnp.where(core == 0, jnp.stack([keep, got]), jnp.stack([got, keep]))
         both = both.reshape(halves, depth, part, rows_out).transpose(1, 0, 2, 3)
         return both.reshape(units, rows_out).astype(jnp.float32)
 
-    grad_sh_gate = low(mm(gate_grad_s, n2_all, ((0,), (0,))))
-    grad_sh_up = low(mm(up_grad_s, n2_all, ((0,), (0,))))
-    grad_sh_down = low(mm(shared_hidden, shared_grads, ((0,), (0,))))
-
+    scatter = lambda v, dim: lax.psum_scatter(v, DP, scatter_dimension=dim, tiled=True)
+    shared_sums = [
+        scatter(
+            unit_grads(left, right, depth, halves).reshape(depth * depth * part, -1), 0
+        )
+        for left, right in (
+            (shared_hidden, shared_grads),
+            (gate_grad_s, n2_all),
+            (up_grad_s, n2_all),
+        )
+    ]
     result_e = low(mm(hidden_e, ex_down))
-    row_dots = jnp.sum(result_e.astype(jnp.float32) * row_cots.astype(jnp.float32), axis=1)
-    gate_dots = jnp.sum(
-        jnp.where(chosen, row_dots.reshape(plane, capacity, 1), 0.0), axis=1
-    )
     hgrad_e = mm(row_grads, ex_down, ((1,), (1,)))
     gate_grad_e = low(hgrad_e * up_e * silu_grad(gate_e))
     up_grad_e = low(hgrad_e * act_e)
@@ -1042,35 +1223,37 @@
     grad_ex_down = low(mm(hidden_e, row_grads, ((0,), (0,))))
     grad_ex_gate = low(mm(expert_rows, gate_grad_e, ((0,), (0,))))
     grad_ex_up = low(mm(expert_rows, up_grad_e, ((0,), (0,))))
-    scatter = lambda v, dim: lax.psum_scatter(v, DP, scatter_dimension=dim, tiled=True)
-    side = width // halves
-    shared_sums = [
-        [scatter(v[:, c * side : (c + 1) * side], 1) for c in range(halves)]
-        for v in (grad_sh_gate, grad_sh_up, grad_sh_down)
-    ]
     grads_made = (grad_ex_down, grad_ex_gate, grad_ex_up)
     grads = [scatter(v, dim) for v, dim in zip(grads_made, (1, 0, 0))]
-    result_e, gate_grad_s = after((result_e, gate_grad_s), grads_made)
+    slots = slots.reshape(all_tokens, 1)
+    out_near, dots = output_parts(
+        shared_hidden,
+        sh_down,
+        result_e.reshape(plane, capacity, width),
+        after(slots, grads_made),
+        sg_all,
+        expert_gate,
+        cot_all,
+    )
+    out_sums = [out_near[k] for k in range(4)]
     rows_grad = low(
         mm(gate_grad_e, ex_gate, ((1,), (1,))) + mm(up_grad_e, ex_up, ((1,), (1,)))
     )
 
-    out_part = low(sg_all * shared_part + expert_gate * back_to_tokens(result_e))
-    n2_grad_part = low(
-        mm(gate_grad_s, sh_gate, ((1,), (1,)))
-        + mm(up_grad_s, sh_up, ((1,), (1,)))
-        + back_to_tokens(rows_grad)
-    )
-    n2_grad_part = after(n2_grad_part, (out_part, shared_sums))
-    n2_grad, *out_sums = plane_scatter(
-        n2_grad_part.reshape(plane, tokens, width),
-        True,
-        3,
-        jnp.float32,
-        out_part.reshape(plane, tokens, width),
-    )
-
-    dots = jnp.stack([gate_dots, cot_dot_shared.reshape(plane, tokens)], axis=1)
+    n2_grad_part = n2_grad_parts(
+        gate_grad_s,
+        up_grad_s,
+        sh_gate_t,
+        sh_up_t,
+        rows_grad.reshape(plane, capacity, width),
+        after(slots, out_sums),
+    )
+    out_got = hops(out_sums)
+    n2_grad_part, out_got, _ = lax.optimization_barrier((n2_grad_part, out_got, shared_sums))
+    output = low(residual + sum_up(out_got))
+    n2_grad = plane_scatter(n2_grad_part, True, 3, jnp.float32)[0]
+
+    dots = dots.reshape(plane, tokens, 128)[:, :, :2].transpose(0, 2, 1)
     back = jnp.arange(plane, dtype=jnp.int32) ^ me
     dots = dots[(back // 2) + 4 * (back % 2)]
     dots = lax.all_to_all(dots, PLANE, split_axis=0, concat_axis=0, tiled=True)
@@ -1112,13 +1295,13 @@
     qkv_grad = attention_call(qkv, attended_grad, q_codes, k_codes, seq_len)
     grad_qkv = low(mm(n1_all, qkv_grad, ((0,), (0,))))
     n1_grad = low(mm(qkv_grad, w_qkv, ((1,), (1,))))
-    grad_out = low(hop_sum(out_grad_sums, (n1_grad, grad_qkv)))
+    out_grad_got = hops(out_grad_sums)
+    grad_out = low(sum_up(after(out_grad_got, (n1_grad, grad_qkv))))
     n1_grad = after(n1_grad, (grad_qkv, grad_out, grads[1]))
     grad_out = lax.psum_scatter(grad_out, DP, scatter_dimension=0, tiled=True)
     n1_grad = plane_scatter(n1_grad.reshape(plane, tokens, width), False, 1, jnp.float32)[0]
-    output = low(residual + hop_sum(out_sums, n1_grad))
-    grad_sh_gate, grad_sh_up, grad_sh_down = [
-        shared_scatter(*after(v, n1_grad)) for v in shared_sums
+    grad_sh_down, grad_sh_gate, grad_sh_up = [
+        shared_scatter(after(v, n1_grad)) for v in shared_sums
     ]
     grad_sh_gate, grad_sh_up = grad_sh_gate.T, grad_sh_up.T
     fine = shard // plane

time: 1540 us -> 1290 us (0.84)
  matrix products: 567 us -> 388 us
  waiting for transfers between devices: 276 us -> 107 us
  Pallas kernels: 360 us -> 498 us
  local copies, waits for them, and re-layouts: 127 us -> 104 us
  blocking collectives: 24.3 us -> 7.92 us
    pallas_call x0 -> x5, Pallas kernels: none -> 141 us  [the longest x3 52.9 us: unit_grads(): pl.pallas_call(unit_grad_kernel, grid=(depth * halves,), in_specs=[pl.Blo...]
    dot_general x28 -> x22, matrix products: 502 us -> 361 us  [mm(): lax.dot_general(left, right, (dims, ((), ())), preferred_element_type=jnp...]
    all_gather x1, waiting for transfers between devices: 85.8 us -> 6.79 us  [local_plane(): lax.all_gather(after(expert_w_up[0], info_all), DP, axis=0, tiled=True)]
    ppermute x12, waiting for transfers between devices: 98.4 us -> 36.9 us  [swap(): return lax.ppermute(values, EXP, [(i, i ^ bits) for i in range(4)])]
    dot_general x2 -> x0, matrix products: 38.6 us -> none  [back_to_tokens(): lax.dot_general(onehot, values.reshape(plane, capacity, width), (((1,), (...]
    all_gather x1, waiting for transfers between devices: 26.3 us -> 0.02 us  [local_plane(): lax.all_gather(after(expert_w_down[0], info_all), DP, axis=1, tiled=True)]
    convert_element_type x1 -> x0, local copies, waits for them, and re-layouts: 18.8 us -> none  [local_plane(): row_grads = low(row_cots.astype(jnp.float32) * slot_gates)]
    all_to_all x1, blocking collectives: 24.3 us -> 7.92 us  [local_plane(): lax.all_to_all(small_grads, PLANE, split_axis=0, concat_axis=0, tiled=True)]
  transfers between devices with their start and end apart: 43 -> 40, of which waited for: 10 -> 12; matrix products, arithmetic and copies ran while one was open for 52% -> 46% of each run, Pallas kernels for 23% -> 39%
where the time goes in v5:
time: 1290 us; the launch traced here: 1280 us
  Pallas kernels  498 us (39%)
  matrix products  388 us (30%)
  other arithmetic  123 us (10%)
  waiting for transfers between devices  107 us (8%)
  local copies, waits for them, and re-layouts  104 us (8%)
  starting transfers between devices  38.5 us (3%)
  between operations  15.2 us (1%)
    dot_general x22, matrix products, mm(): lax.dot_general(left, right, (dims, ((), ())), preferred_element_type=jnp...  361 us
    pallas_call x2, Pallas kernels, plane_gather(): pl.pallas_call(partial(plane_gather_kernel, info is not None, relative),...  155 us
    pallas_call x2, Pallas kernels, plane_scatter(): pl.pallas_call(partial(plane_scatter_kernel, relative, extra is not None)...  152 us
    pallas_call x3, Pallas kernels, unit_grads(): pl.pallas_call(unit_grad_kernel, grid=(depth * halves,), in_specs=[pl.Blo...  52.9 us
    pallas_call x2, Pallas kernels, attention_call(): pl.pallas_call(partial(body, heads, step), grid=(rows // seq_len,), in_sp...  50.3 us
    pallas_call x1, Pallas kernels, output_parts(): pl.pallas_call(partial(output_kernel, half), grid=(blocks,), in_specs=[pl...  46.8 us
    convert_element_type x7, other arithmetic, low(): return values.astype(jnp.bfloat16)  44.6 us
    pallas_call x1, Pallas kernels, n2_grad_parts(): pl.pallas_call(n2_grad_kernel, grid=(blocks,), in_specs=[by_units, by_uni...  41.1 us
  transfers between devices with their start and end apart: 40, of which 12 were waited for; matrix products, arithmetic and copies ran while one was open for 46% of the time, Pallas kernels for 39%

profile of v5, /device:TPU:0, one launch (start us, length us, event | category | flops | bytes accessed | tf_op | source)
XLA Modules:
  0.0 1281.8 jit_solution(4586147153859795595)
XLA Ops:
  23.8 81.0 %shard_map.315 = (bf16[8,512,2048]{2,1,0:T(8,128)(2,1)}, s32[8,8,512]{2,1,0:T(8,128)}) custom-call(bf16[512,2048]{1,0:T(8,128)(2,1)} %bitcast.270, s32[8,512]{1,0:T(8,128)} %concatenate.53.refs_1_), custom_call_target="tpu_custom_call" | custom-call | bytes 1048576 | tf_op jit(solution)/shard_map/pallas_call | solution.py:628
  169.3 19.4 %shard_map.316 = bf16[4096,256]{1,0:T(8,128)(2,1)S(1)} custom-call(bf16[4096,768]{1,0:T(8,128)(2,1)} %convolution_convert_fusion.6.qkv_ref, s32[4096,1]{1,0:T(8,128)S(1)} %copy.197.q_code_ref, s32[4,1,1024]{2,1,0:T(1,128)S(1)} %bitcast.266), custom_call_target="tpu_custom_call" | custom-call | flops 4294967296 | bytes 8388608 | tf_op jit(solution)/shard_map/pallas_call | solution.py:502
  238.7 74.1 %shard_map.317 = bf16[8,512,2048]{2,1,0:T(8,128)(2,1)} custom-call(bf16[512,2048]{1,0:T(8,128)(2,1)} %multiply_convert_fusion.7.refs_0_), custom_call_target="tpu_custom_call" | custom-call | bytes 1048576 | tf_op jit(solution)/shard_map/pallas_call | solution.py:628
  335.5 24.1 %multiply_convert_fusion.6 = (bf16[704,4096]{1,0:T(8,128)(2,1)}, f32[704,4096]{1,0:T(8,128)}) fusion(f32[704,4096]{1,0:T(8,128)} %fusion.60, bf16[2048,704]{0,1:T(8,128)(2,1)S(1)} %copy-done.48, bf16[4096,2048]{1,0:T(8,128)(2,1)} %bitcast.278), kind=kOutput, calls=%fused_computation.18 | convolution fusion | flops 11828461568 | bytes 48496640 | tf_op jit(solution)/shard_map/dot_general | solution.py:1010
  372.8 28.4 %all-gather.18.cloned.1.call-done = bf16[2048,1408]{1,0:T(8,128)(2,1)} async-done(((bf16[512,1408]{1,0:T(8,128)(2,1)}), bf16[2048,1408]{1,0:T(8,128)(2,1)}) %all-gather.18.cloned.1.call-update) | async-done | bytes 5767184 | tf_op jit(solution)/shard_map/all_gather | solution.py:1141
  401.2 21.0 %fusion.61 = f32[2304,1408]{1,0:T(8,128)} fusion(bf16[2304,2048]{1,0:T(8,128)(2,1)} %bitcast.336, bf16[2048,1408]{1,0:T(8,128)(2,1)} %all-gather.18.cloned.1.call-done), kind=kOutput, calls=%fused_computation.194 | convolution fusion | flops 13287555072 | bytes 28180480 | tf_op jit(solution)/shard_map/dot_general | solution.py:1010
  494.9 25.4 %multiply_convert_fusion.4 = (bf16[704,4096]{1,0:T(8,128)(2,1)}, bf16[704,4096]{1,0:T(8,128)(2,1)}) fusion(f32[704,4096]{1,0:T(8,128)} %fusion.60, f32[704,4096]{1,0:T(8,128)} %get-tuple-element.247, bf16[704,2048]{1,0:T(8,128)(2,1)} %all-gather.12.cloned.1.call-done.down_ref, bf16[4096,2048]{1,0:T(8,128)(2,1)} %multiply_convert_fusion.right_ref), kind=kOutput, calls=%fused_computation.16 | convolution fusion | flops 11848646656 | bytes 54263808 | tf_op jit(solution)/shard_map/dot_general | solution.py:1010
  586.3 21.3 %fusion.62 = f32[2304,1408]{1,0:T(8,128)} fusion(bf16[2304,2048]{1,0:T(8,128)(2,1)} %fusion.2, bf16[1408,2048]{1,0:T(8,128)(2,1)} %all-gather.20.cloned.1.call-done), kind=kOutput, calls=%fused_computation.195 | convolution fusion | flops 13287555072 | bytes 28180480 | tf_op jit(solution)/shard_map/dot_general | solution.py:1010
  614.4 29.7 %multiply_convert_fusion.1 = (bf16[2304,1408]{1,0:T(8,128)(2,1)}, bf16[2304,1408]{1,0:T(8,128)(2,1)}, bf16[2304,1408]{1,0:T(8,128)(2,1)}) fusion(f32[2304,1408]{1,0:T(8,128)} %fusion.61, f32[2304,1408]{1,0:T(8,128)} %fusion.62, bf16[2304,2048]{1,0:T(8,128)(2,1)} %bitcast.337, bf16[2048,1408]{1,0:T(8,128)(2,1)} %all-gather.22.cloned.1.call-done), kind=kOutput, calls=%fused_computation.11 | convolution fusion | flops 13336215552 | bytes 60620800 | tf_op jit(solution)/shard_map/dot_general | solution.py:1010
  644.1 20.0 %convolution_convert_fusion.5 = bf16[1408,2048]{1,0:T(8,128)(2,1)} fusion(bf16[2304,1408]{1,0:T(8,128)(2,1)} %get-tuple-element.202, bf16[2304,2048]{1,0:T(8,128)(2,1)} %fusion.2), kind=kOutput, calls=%fused_computation.28 | convolution fusion | flops 13290438656 | bytes 21692416 | tf_op jit(solution)/shard_map/dot_general | solution.py:1010
  664.2 20.4 %convolution_convert_fusion.4 = bf16[2048,1408]{1,0:T(8,128)(2,1)} fusion(bf16[2304,2048]{1,0:T(8,128)(2,1)} %bitcast.338, bf16[2304,1408]{1,0:T(8,128)(2,1)} %get-tuple-element.203), kind=kOutput, calls=%fused_computation.27 | convolution fusion | flops 13290438656 | bytes 21692416 | tf_op jit(solution)/shard_map/dot_general | solution.py:1010
  687.7 20.2 %convolution_convert_fusion.3 = bf16[2048,1408]{1,0:T(8,128)(2,1)} fusion(bf16[2304,2048]{1,0:T(8,128)(2,1)} %bitcast.339, bf16[2304,1408]{1,0:T(8,128)(2,1)} %get-tuple-element.204), kind=kOutput, calls=%fused_computation.26 | convolution fusion | flops 13290438656 | bytes 21692416 | tf_op jit(solution)/shard_map/dot_general | solution.py:1010
  709.9 20.1 %convolution_convert_fusion.1 = bf16[2304,2048]{1,0:T(8,128)(2,1)} fusion(bf16[2304,1408]{1,0:T(8,128)(2,1)} %get-tuple-element.202, bf16[1408,2048]{1,0:T(8,128)(2,1)} %all-gather.20.cloned.1.call-done), kind=kOutput, calls=%fused_computation.21 | convolution fusion | flops 13292273664 | bytes 21692416 | tf_op jit(solution)/shard_map/dot_general | solution.py:1010
  730.0 46.8 %shard_map.318 = (bf16[4,512,2048]{2,1,0:T(8,128)(2,1)}, f32[4096,128]{1,0:T(8,128)}) custom-call(bf16[704,4096]{1,0:T(8,128)(2,1)} %get-tuple-element.246.hidden_ref.left_ref, bf16[704,2048]{1,0:T(8,128)(2,1)} %all-gather.12.cloned.1.call-done.down_ref, bf16[8,288,2048]{2,1,0:T(8,128)(2,1)} %bitcast.340, s32[4096,1]{1,0:T(8,128)} %copy.208.slot_ref, ...), custom_call_target="tpu_custom_call" | custom-call | flops 16642998272 | bytes 50331648 | tf_op jit(solution)/shard_map/pallas_call | solution.py:883
  795.7 21.8 %fusion.63 = f32[2304,2048]{1,0:T(8,128)} fusion(bf16[2304,1408]{1,0:T(8,128)(2,1)} %get-tuple-element.203, bf16[2048,1408]{1,0:T(8,128)(2,1)} %all-gather.18.cloned.1.call-done), kind=kOutput, calls=%fused_computation.196 | convolution fusion | flops 13287555072 | bytes 31129600 | tf_op jit(solution)/shard_map/dot_general | solution.py:1010
  817.4 22.1 %add_convert_fusion = bf16[2304,2048]{1,0:T(8,128)(2,1)} fusion(f32[2304,2048]{1,0:T(8,128)} %fusion.63, bf16[2304,1408]{1,0:T(8,128)(2,1)} %get-tuple-element.204, bf16[2048,1408]{1,0:T(8,128)(2,1)} %all-gather.22.cloned.1.call-done), kind=kOutput, calls=%fused_computation.9 | convolution fusion | flops 13296992256 | bytes 40566784 | tf_op jit(solution)/shard_map/dot_general | solution.py:1010
  839.5 41.1 %shard_map.319.refs_0_ = bf16[8,512,2048]{2,1,0:T(8,128)(2,1)} custom-call(bf16[704,4096]{1,0:T(8,128)(2,1)} %get-tuple-element.206.dgate_ref.left_ref, bf16[704,4096]{1,0:T(8,128)(2,1)} %get-tuple-element.205.dup_ref.left_ref, bf16[704,2048]{1,0:T(8,128)(2,1)S(1)} %bitcast.268, bf16[704,2048]{1,0:T(8,128)(2,1)} %bitcast.335, ...), custom_call_target="tpu_custom_call" | custom-call | flops 28454158336 | bytes 33554432 | tf_op jit(solution)/shard_map/pallas_call | solution.py:936
  884.8 76.2 %shard_map.323 = f32[512,2048]{1,0:T(8,128)S(1)} custom-call(bf16[8,512,2048]{2,1,0:T(8,128)(2,1)} %shard_map.319.refs_0_), custom_call_target="tpu_custom_call" | custom-call | bytes 1048576 | tf_op jit(solution)/shard_map/pallas_call | solution.py:769
  1003.8 19.8 %all-to-all-done.2 = bf16[8,512,256]{2,1,0:T(8,128)(2,1)} async-done(((bf16[8,512,256]{2,1,0:T(8,128)(2,1)}), bf16[8,512,256]{2,1,0:T(8,128)(2,1)}, u32[]{:S(2)}, u32[]{:S(2)}) %all-to-all-start.2) | async-done | bytes 2097184 | tf_op jit(solution)/shard_map/all_to_all | solution.py:1119
  1023.6 30.9 %shard_map.324 = bf16[4096,768]{1,0:T(8,128)(2,1)} custom-call(bf16[4096,768]{1,0:T(8,128)(2,1)} %convolution_convert_fusion.6.qkv_ref, bf16[4096,256]{1,0:T(8,128)(2,1)} %bitcast.62.grad_ref, s32[4096,1]{1,0:T(8,128)S(1)} %copy.197.q_code_ref, s32[4,1,1024]{2,1,0:T(1,128)S(1)} %bitcast.267), custom_call_target="tpu_custom_call" | custom-call | flops 10737418240 | bytes 12582912 | tf_op jit(solution)/shard_map/pallas_call | solution.py:502
  1054.5 19.2 %convolution_convert_fusion.9 = bf16[2048,768]{1,0:T(8,128)(2,1)S(1)} fusion(bf16[4096,2048]{1,0:T(8,128)(2,1)} %copy-done.18, bf16[4096,768]{1,0:T(8,128)(2,1)} %shard_map.324), kind=kOutput, calls=%fused_computation.52 | convolution fusion | flops 12886474752 | bytes 26214400 | tf_op jit(solution)/shard_map/dot_general | solution.py:1010
  1100.5 20.6 %convolution_convert_fusion = bf16[4096,2048]{1,0:T(8,128)(2,1)} fusion(bf16[4096,768]{1,0:T(8,128)(2,1)} %shard_map.324, bf16[2048,896]{1,0:T(8,128)(2,1)} %all-gather.10.cloned.1.call-done), kind=kOutput, calls=%fused_computation.10 | convolution fusion | flops 12893290496 | bytes 26214400 | tf_op jit(solution)/shard_map/dot_general | solution.py:1010
  1123.3 22.0 %collective-permute-done.13 = bf16[256,2048]{1,0:T(8,128)(2,1)S(1)} collective-permute-done((bf16[256,2048]{1,0:T(8,128)(2,1)}, bf16[256,2048]{1,0:T(8,128)(2,1)S(1)}, u32[]{:S(2)}, u32[]{:S(2)}) %collective-permute-start.13) | collective-permute-done | bytes 1048608 | tf_op jit(solution)/shard_map/ppermute | solution.py:989
  1147.0 76.1 %shard_map.325 = f32[512,2048]{1,0:T(8,128)S(1)} custom-call(bf16[8,512,2048]{2,1,0:T(8,128)(2,1)} %bitcast.276), custom_call_target="tpu_custom_call" | custom-call | bytes 1048576 | tf_op jit(solution)/shard_map/pallas_call | solution.py:769
  (338 shorter events, 465.1 us)
Async XLA Ops:
  7.2 105.0 %all-gather.24.cloned.1.call-start = ((), (), s32[]{:S(2)}) async-start(), calls=%async_computation.30 | async-start | bytes 1310720 | tf_op jit(solution)/shard_map/all_gather | solution.py:1081
  9.5 109.9 %all-gather.10.cloned.1.call-start = ((), (), s32[]{:S(2)}) async-start(), calls=%async_computation.15 | async-start | bytes 4587520 | tf_op jit(solution)/shard_map/all_gather | solution.py:1072
  17.5 221.1 %all-gather.14.cloned.1.call-start = ((), (), s32[]{:S(2)}) async-start(), calls=%async_computation.17 | async-start | bytes 3604480 | tf_op jit(solution)/shard_map/all_gather | solution.py:1131
  19.3 219.4 %all-gather.16.cloned.1.call-start = ((), (), s32[]{:S(2)}) async-start(), calls=%async_computation.18 | async-start | bytes 3604480 | tf_op jit(solution)/shard_map/all_gather | solution.py:1132
  22.0 350.8 %all-gather.12.cloned.1.call-start = ((), (), s32[]{:S(2)}) async-start(), calls=%async_computation.16 | async-start | bytes 3604480 | tf_op jit(solution)/shard_map/all_gather | solution.py:1134
  23.0 378.2 %all-gather.18.cloned.1.call-start = ((), (), s32[]{:S(2)}) async-start(), calls=%async_computation.19 | async-start | bytes 7208960 | tf_op jit(solution)/shard_map/all_gather | solution.py:1141
  104.7 481.6 %all-gather.20.cloned.1.call-start = ((), (), s32[]{:S(2)}) async-start(), calls=%async_computation.20 | async-start | bytes 7208960 | tf_op jit(solution)/shard_map/all_gather | solution.py:1143
  198.5 415.9 %all-gather.22.cloned.1.call-start = ((), (), s32[]{:S(2)}) async-start(), calls=%async_computation.21 | async-start | bytes 7208960 | tf_op jit(solution)/shard_map/all_gather | solution.py:1142
  312.8 109.4 %collective-permute-start.4 = (bf16[512,2048]{1,0:T(8,128)(2,1)}, bf16[512,2048]{1,0:T(8,128)(2,1)}, u32[]{:S(2)}, u32[]{:S(2)}) collective-permute-start(bf16[512,2048]{1,0:T(8,128)(2,1)} %bitcast.271), channel_id=1, source_target_pairs={{0,8},{8,0},{16,24},{24,16},{1,9},{9,1},{17,25},{25,17},{2,10},{10... | collective-permute-start | bytes 6291464 | tf_op jit(solution)/shard_map/ppermute | solution.py:989
  314.2 108.0 %collective-permute-start.5 = (bf16[512,2048]{1,0:T(8,128)(2,1)}, bf16[512,2048]{1,0:T(8,128)(2,1)}, u32[]{:S(2)}, u32[]{:S(2)}) collective-permute-start(bf16[512,2048]{1,0:T(8,128)(2,1)} %bitcast.272), channel_id=1, source_target_pairs={{0,16},{8,24},{16,0},{24,8},{1,17},{9,25},{17,1},{25,9},{2,18},{10... | collective-permute-start | bytes 6291464 | tf_op jit(solution)/shard_map/ppermute | solution.py:989
  314.9 107.3 %collective-permute-start.6 = (bf16[512,2048]{1,0:T(8,128)(2,1)}, bf16[512,2048]{1,0:T(8,128)(2,1)}, u32[]{:S(2)}, u32[]{:S(2)}) collective-permute-start(bf16[512,2048]{1,0:T(8,128)(2,1)} %bitcast.273), channel_id=1, source_target_pairs={{0,24},{8,16},{16,8},{24,0},{1,25},{9,17},{17,9},{25,1},{2,26},{10... | collective-permute-start | bytes 6291464 | tf_op jit(solution)/shard_map/ppermute | solution.py:989
  429.0 455.8 %reduce-scatter.9.cloned.1.call-start = ((), (), s32[]{:S(2)}) async-start(), calls=%async_computation.22 | async-start | bytes 3604480 | tf_op jit(solution)/shard_map/reduce_scatter | solution.py:1207
  494.9 389.9 %reduce-scatter.11.cloned.1.call-start = ((), (), s32[]{:S(2)}) async-start(), calls=%async_computation.23 | async-start | bytes 3604480 | tf_op jit(solution)/shard_map/reduce_scatter | solution.py:1207
  537.9 346.8 %reduce-scatter.13.cloned.1.call-start = ((), (), s32[]{:S(2)}) async-start(), calls=%async_computation.24 | async-start | bytes 3604480 | tf_op jit(solution)/shard_map/reduce_scatter | solution.py:1207
  586.3 437.3 %reduce-scatter.15.cloned.1.call-start = ((), (), s32[]{:S(2)}) async-start(), calls=%async_computation.25 | async-start | bytes 7208960 | tf_op jit(solution)/shard_map/reduce_scatter | solution.py:1207
  664.2 482.8 %reduce-scatter.17.cloned.1.call-start = ((), (), s32[]{:S(2)}) async-start(), calls=%async_computation.26 | async-start | bytes 7208960 | tf_op jit(solution)/shard_map/reduce_scatter | solution.py:1207
  780.4 100.3 %all-to-all-start.1 = ((f32[8,2,512]{2,1,0:T(2,128)}), f32[8,2,512]{2,1,0:T(2,128)S(1)}, u32[]{:S(2)}, u32[]{:S(2)}) async-start(f32[8,2,512]{2,1,0:T(2,128)} %gather_fusion.1), calls=%async_computation.4 | async-start | bytes 65536 | tf_op jit(solution)/shard_map/all_to_all | solution.py:1259
  784.0 454.2 %reduce-scatter.23.cloned.1.call-start = ((), (), s32[]{:S(2)}) async-start(), calls=%async_computation.29 | async-start | bytes 7208960 | tf_op jit(solution)/shard_map/reduce_scatter | solution.py:1207
  790.2 93.4 %collective-permute-start.8 = (bf16[512,2048]{1,0:T(8,128)(2,1)}, bf16[512,2048]{1,0:T(8,128)(2,1)}, u32[]{:S(2)}, u32[]{:S(2)}) collective-permute-start(bf16[512,2048]{1,0:T(8,128)(2,1)} %get-tuple-element.217), channel_id=1, source_target_pairs={{0,8},{8,0},{16,24},{24,16},{1,9},{9,1},{17,25},{25,17},{2,10},{10... | collective-permute-start | bytes 6291464 | tf_op jit(solution)/shard_map/ppermute | solution.py:989
  792.1 92.6 %collective-permute-start.9 = (bf16[512,2048]{1,0:T(8,128)(2,1)}, bf16[512,2048]{1,0:T(8,128)(2,1)}, u32[]{:S(2)}, u32[]{:S(2)}) collective-permute-start(bf16[512,2048]{1,0:T(8,128)(2,1)} %get-tuple-element.216), channel_id=1, source_target_pairs={{0,16},{8,24},{16,0},{24,8},{1,17},{9,25},{17,1},{25,9},{2,18},{10... | collective-permute-start | bytes 6291464 | tf_op jit(solution)/shard_map/ppermute | solution.py:989
  793.6 91.2 %collective-permute-start.10 = (bf16[512,2048]{1,0:T(8,128)(2,1)}, bf16[512,2048]{1,0:T(8,128)(2,1)}, u32[]{:S(2)}, u32[]{:S(2)}) collective-permute-start(bf16[512,2048]{1,0:T(8,128)(2,1)} %get-tuple-element.215), channel_id=1, source_target_pairs={{0,24},{8,16},{16,8},{24,0},{1,25},{9,17},{17,9},{25,1},{2,26},{10... | collective-permute-start | bytes 6291464 | tf_op jit(solution)/shard_map/ppermute | solution.py:989
  996.9 241.2 %reduce-scatter.19.cloned.1.call-start = ((), (), s32[]{:S(2)}) async-start(), calls=%async_computation.27 | async-start | bytes 3932160 | tf_op jit(solution)/shard_map/reduce_scatter | solution.py:1313
  1088.7 173.5 %reduce-scatter.21.cloned.1.call-start = ((), (), s32[]{:S(2)}) async-start(), calls=%async_computation.28 | async-start | bytes 1310720 | tf_op jit(solution)/shard_map/reduce_scatter | solution.py:1301
  1097.7 47.6 %collective-permute-start.13 = (bf16[256,2048]{1,0:T(8,128)(2,1)}, bf16[256,2048]{1,0:T(8,128)(2,1)S(1)}, u32[]{:S(2)}, u32[]{:S(2)}) collective-permute-start(bf16[256,2048]{1,0:T(8,128)(2,1)} %get-tuple-element.208), channel_id=1, source_target_pairs={{0,16},{8,24},{16,0},{24,8},{1,17},{9,25},{17,1},{25,9},{2,18},{10... | collective-permute-start | bytes 3145736 | tf_op jit(solution)/shard_map/ppermute | solution.py:989
  (67 other events, 1541.6 us)
Sparse Core Ops, SparseCore 0:
  10.2 30.6 all-gather.23
  43.0 71.5 all-gather.9
  116.8 57.7 all-gather.13
  176.6 57.8 all-gather.15
  236.5 57.8 all-gather.11
  295.8 105.3 all-gather.17
  402.8 104.9 all-gather.19
  509.4 104.9 all-gather.21
  617.3 54.4 reduce-scatter.8
  674.5 56.0 reduce-scatter.10
  733.5 56.0 reduce-scatter.12
  791.7 102.1 reduce-scatter.14
  896.2 102.7 reduce-scatter.16
  1001.1 103.0 reduce-scatter.22
  1106.4 60.7 reduce-scatter.18
  1226.8 26.7 reduce-scatter.20

commit v6 on v5

--- a/solution.py
+++ b/solution.py
@@ -794,6 +794,41 @@
     )(*operands)
 
 
+def norm_qkv_kernel(hidden_ref, gain_ref, w_ref, norm_ref, qkv_ref):
+    values = hidden_ref[...].astype(jnp.float32)
+    inv = lax.rsqrt(jnp.mean(values * values, axis=1, keepdims=True) + EPS)
+    norm_ref[...] = low(values * inv * gain_ref[...])
+    qkv_ref[...] = low(mm(norm_ref[...], w_ref[...]))
+
+
+def norm_qkv(hidden, gain, w, block):
+    rows, width = hidden.shape
+    cols = w.shape[1]
+    return pl.pallas_call(
+        norm_qkv_kernel,
+        grid=(rows // block,),
+        in_specs=[
+            pl.BlockSpec((block, width), lambda i: (i, 0)),
+            pl.BlockSpec((1, width), lambda i: (0, 0)),
+            pl.BlockSpec((width, cols), lambda i: (0, 0)),
+        ],
+        out_specs=[
+            pl.BlockSpec((block, width), lambda i: (i, 0)),
+            pl.BlockSpec((block, cols), lambda i: (i, 0)),
+        ],
+        out_shape=[
+            jax.ShapeDtypeStruct((rows, width), jnp.bfloat16),
+            jax.ShapeDtypeStruct((rows, cols), jnp.bfloat16),
+        ],
+        compiler_params=pltpu.CompilerParams(vmem_limit_bytes=48 * 2**20),
+        cost_estimate=pl.CostEstimate(
+            flops=2 * rows * width * cols,
+            bytes_accessed=4 * rows * width,
+            transcendentals=0,
+        ),
+    )(hidden, gain, w)
+
+
 def chosen_rows(slots, capacity):
     lanes = lax.broadcasted_iota(jnp.int32, (slots.shape[0], capacity), 1)
     return (slots == lanes).astype(jnp.bfloat16)
@@ -836,37 +871,44 @@
             device_id_type=MESH_ID,
         )
 
+    def make(store):
+        chosen = chosen_rows(slot_ref[...], rows_ref.shape[1])
+        hidden = hidden_ref[...].T
+        tokens, width = cot_ref.shape
+        step, lanes = 512, 128
+        gate_dot = jnp.zeros((tokens, lanes), jnp.float32)
+        shared_dot = jnp.zeros((tokens, lanes), jnp.float32)
+        for first in range(0, width, step):
+            cols = pl.ds(first, step)
+            shared = mm(hidden, down_ref[:, cols])
+            picked = mm(chosen, rows_ref[0, :, cols])
+            cot = cot_ref[:, cols].astype(jnp.float32)
+            gate_part, shared_part = picked * cot, shared * cot
+            for at in range(0, step, lanes):
+                gate_dot += gate_part[:, at : at + lanes]
+                shared_dot += shared_part[:, at : at + lanes]
+            store(cols, sg_ref[...] * shared + gate_ref[...] * picked)
+        lane = lax.broadcasted_iota(jnp.int32, dots_ref.shape, 1)
+        gate_dot = jnp.sum(gate_dot, axis=1, keepdims=True)
+        shared_dot = jnp.sum(shared_dot, axis=1, keepdims=True)
+        dots_ref[...] = jnp.where(lane == 0, gate_dot, jnp.where(lane == 1, shared_dot, 0.0))
+
+    @pl.when(is_far)
+    def _():
+        def store(cols, total):
+            given[slot, :, cols] = low(total)
+
+        make(store)
+        block_copy(slot).start()
+
     @pl.when(jnp.logical_not(is_far))
     def _():
         block_copy(slot).wait_recv()
 
-    chosen = chosen_rows(slot_ref[...], rows_ref.shape[1])
-    width = down_ref.shape[1]
-    step = 512
-    gate_dot, shared_dot = 0.0, 0.0
-    for first in range(0, width, step):
-        cols = pl.ds(first, step)
-        shared = mm(hidden_ref[...], down_ref[:, cols], ((0,), (0,)))
-        picked = mm(chosen, rows_ref[0, :, cols])
-        cot = cot_ref[:, cols].astype(jnp.float32)
-        gate_dot += jnp.sum(picked * cot, axis=1, keepdims=True)
-        shared_dot += jnp.sum(shared * cot, axis=1, keepdims=True)
-        total = sg_ref[...] * shared + gate_ref[...] * picked
-
-        @pl.when(is_far)
-        def _():
-            given[slot, :, cols] = low(total)
-
-        @pl.when(jnp.logical_not(is_far))
-        def _():
+        def store(cols, total):
             near_ref[0, :, cols] = low(total + got[slot, :, cols].astype(jnp.float32))
 
-    lanes = lax.broadcasted_iota(jnp.int32, dots_ref.shape, 1)
-    dots_ref[...] = jnp.where(lanes == 0, gate_dot, jnp.where(lanes == 1, shared_dot, 0.0))
-
-    @pl.when(is_far)
-    def _():
-        block_copy(slot).start()
+        make(store)
 
     @pl.when(step_at == 2 * half - 1)
     def _():
@@ -1087,12 +1129,11 @@
         inv = lax.rsqrt(jnp.mean(values * values, axis=1, keepdims=True) + EPS)
         return values, inv, low(values * inv * gain)
 
-    _, _, n1_all = normed(hidden_all, g_one)
-    qkv = low(mm(n1_all, w_qkv))
+    n1_all, qkv = norm_qkv(hidden_all, g_one[None], w_qkv, tokens)
     q_codes = info_all[:, 0].reshape(all_tokens, 1)
     k_codes = info_all[:, 1].reshape(all_tokens // seq_len, 1, seq_len)
     attended_cols = attention_call(qkv, None, q_codes, k_codes, seq_len)
-    pieces = [w_out_part] + [after(v, qkv) for v in w_out_got]
+    pieces = [w_out_part] + [after(v, attended_cols) for v in w_out_got]
     w_out_near = jnp.zeros((depth, groups, 1, out_rows, width), jnp.bfloat16)
     for k in range(4):
         w_out_near = lax.dynamic_update_slice(
@@ -1139,7 +1180,9 @@
     cot_own = after(cotangent[0], n2_all)
     cot_got = [swap(cot_own, k) for k in (1, 2, 3)]
     ex_gate = lax.all_gather(after(expert_w_gate[0], info_all), DP, axis=0, tiled=True)
-    ex_up = lax.all_gather(after(expert_w_up[0], info_all), DP, axis=0, tiled=True)
+    ex_up = jnp.broadcast_to(after(expert_w_up, info_all), (depth, *expert_w_up.shape[1:]))
+    ex_up = lax.all_to_all(ex_up, DP, split_axis=0, concat_axis=0, tiled=True)
+    ex_up = ex_up.reshape(width, -1)
     ex_down = lax.all_gather(after(expert_w_down[0], info_all), DP, axis=1, tiled=True)
 
     small_w = jnp.concatenate([router_t, gate_vec[None]])
@@ -1291,25 +1334,29 @@
         [block_of(k, core) for k in range(4)],
         jnp.stack([block_of(k, 1 - core) for k in range(4)]),
     )
-    attended_grad = after(attended_grad, (out_grad_sums, grads[0]))
-    qkv_grad = attention_call(qkv, attended_grad, q_codes, k_codes, seq_len)
-    grad_qkv = low(mm(n1_all, qkv_grad, ((0,), (0,))))
-    n1_grad = low(mm(qkv_grad, w_qkv, ((1,), (1,))))
-    out_grad_got = hops(out_grad_sums)
-    grad_out = low(sum_up(after(out_grad_got, (n1_grad, grad_qkv))))
-    n1_grad = after(n1_grad, (grad_qkv, grad_out, grads[1]))
-    grad_out = lax.psum_scatter(grad_out, DP, scatter_dimension=0, tiled=True)
-    n1_grad = plane_scatter(n1_grad.reshape(plane, tokens, width), False, 1, jnp.float32)[0]
     grad_sh_down, grad_sh_gate, grad_sh_up = [
-        shared_scatter(after(v, n1_grad)) for v in shared_sums
+        shared_scatter(after(v, low_residual)) for v in shared_sums
     ]
     grad_sh_gate, grad_sh_up = grad_sh_gate.T, grad_sh_up.T
+    attended_grad = after(
+        attended_grad,
+        (out_grad_sums, grads[0], small_grads, grad_sh_down, grad_sh_gate, grad_sh_up),
+    )
+    qkv_grad = attention_call(qkv, attended_grad, q_codes, k_codes, seq_len)
+    qkv_grad, grad_out = lax.optimization_barrier((qkv_grad, hops(out_grad_sums)))
+    grad_out = low(sum_up(grad_out))
+    grad_qkv = low(mm(n1_all, qkv_grad, ((0,), (0,))))
     fine = shard // plane
     grad_qkv = (
         grad_qkv.reshape(plane, depth, fine, 3 * head_cols)
         .transpose(1, 0, 2, 3)
         .reshape(width, 3 * head_cols)
     )
+    n1_grad = low(mm(after(qkv_grad, grad_qkv), w_qkv, ((1,), (1,))))
+    grad_ex_down, grad_ex_gate = [v.astype(jnp.float32)[None] for v in grads[:2]]
+    n1_grad = after(n1_grad, (grad_qkv, grad_out, grad_ex_down, grad_ex_gate))
+    grad_out = lax.psum_scatter(grad_out, DP, scatter_dimension=0, tiled=True)
+    n1_grad = plane_scatter(n1_grad.reshape(plane, tokens, width), False, 1, jnp.float32)[0]
     grad_qkv = lax.psum_scatter(grad_qkv, DP, scatter_dimension=0, tiled=True)
     w_rows = (
         w_qkv.reshape(plane, depth, fine, 3 * head_cols)
@@ -1339,9 +1386,7 @@
         .astype(jnp.float32)
     )
     grad_out = after(grad_out, n1_grad).astype(jnp.float32)
-    grad_ex_down, grad_ex_gate, grad_ex_up = [
-        after(v, n1_grad).astype(jnp.float32)[None] for v in grads
-    ]
+    grad_ex_up = after(grads[2], n1_grad).astype(jnp.float32)[None]
     input_part, _ = norm_back(x_rows, inv_one, g_one, n1_grad)
     input_grad = low(residual_grad + input_part)
     return (

time: 1290 us -> 1390 us (1.078)
  waiting for transfers between devices: 107 us -> 226 us
  matrix products: 388 us -> 363 us
  other arithmetic: 123 us -> 106 us
    all_to_all x0 -> x1, waiting for transfers between devices: none -> 130 us  [local_plane(): ex_up = lax.all_to_all(ex_up, DP, split_axis=0, concat_axis=0, tiled=True)]
    dot_general x22 -> x21, matrix products: 361 us -> 337 us  [mm(): lax.dot_general(left, right, (dims, ((), ())), preferred_element_type=jnp...]
    ppermute x12, waiting for transfers between devices: 36.9 us -> 13.7 us  [swap(): return lax.ppermute(values, EXP, [(i, i ^ bits) for i in range(4)])]
    all_gather x1, waiting for transfers between devices: 0.01 us -> 22.4 us  [local_plane(): sh_up = lax.all_gather(pick(shared_w_up), DP, axis=0, tiled=True)]
    pallas_call x0 -> x1, Pallas kernels: none -> 21.7 us  [norm_qkv(): pl.pallas_call(norm_qkv_kernel, grid=(rows // block,), in_specs=[pl.Block...]
    all_to_all x1, waiting for transfers between devices: 19.8 us -> 5.56 us  [to_columns(): got = lax.all_to_all(send, PLANE, split_axis=0, concat_axis=0, tiled=True)]
    unnamed x120 -> x131, local copies, waits for them, and re-layouts: 34.2 us -> 38 us
  transfers between devices with their start and end apart: 40 -> 40, of which waited for: 12 -> 9; matrix products, arithmetic and copies ran while one was open for 46% -> 40% of each run, Pallas kernels for 39% -> 37%
where the time goes in v6:
time: 1390 us; the launch traced here: 1380 us
  Pallas kernels  509 us (37%)
  matrix products  363 us (26%)
  waiting for transfers between devices  226 us (16%)
  local copies, waits for them, and re-layouts  110 us (8%)
  other arithmetic  106 us (8%)
  starting transfers between devices  45.8 us (3%)
  between operations  15.5 us (1%)
    dot_general x21, matrix products, mm(): lax.dot_general(left, right, (dims, ((), ())), preferred_element_type=jnp...  337 us
    pallas_call x2, Pallas kernels, plane_gather(): pl.pallas_call(partial(plane_gather_kernel, info is not None, relative),...  157 us
    pallas_call x2, Pallas kernels, plane_scatter(): pl.pallas_call(partial(plane_scatter_kernel, relative, extra is not None)...  153 us
    all_to_all x1, waiting for transfers between devices, local_plane(): ex_up = lax.all_to_all(ex_up, DP, split_axis=0, concat_axis=0, tiled=True)  130 us
    pallas_call x3, Pallas kernels, unit_grads(): pl.pallas_call(unit_grad_kernel, grid=(depth * halves,), in_specs=[pl.Blo...  51.1 us
    pallas_call x2, Pallas kernels, attention_call(): pl.pallas_call(partial(body, heads, step), grid=(rows // seq_len,), in_sp...  50.1 us
    convert_element_type x7, other arithmetic, low(): return values.astype(jnp.bfloat16)  44.4 us
    pallas_call x1, Pallas kernels, n2_grad_parts(): pl.pallas_call(n2_grad_kernel, grid=(blocks,), in_specs=[by_units, by_uni...  41.1 us
  transfers between devices with their start and end apart: 40, of which 9 were waited for; matrix products, arithmetic and copies ran while one was open for 40% of the time, Pallas kernels for 37%

profile of v6, /device:TPU:0, one launch (start us, length us, event | category | flops | bytes accessed | tf_op | source)
XLA Modules:
  0.0 1383.0 jit_solution(3518555974000334073)
XLA Ops:
  23.8 81.0 %shard_map.315 = (bf16[8,512,2048]{2,1,0:T(8,128)(2,1)}, s32[8,8,512]{2,1,0:T(8,128)}) custom-call(bf16[512,2048]{1,0:T(8,128)(2,1)} %bitcast.269, s32[8,512]{1,0:T(8,128)} %concatenate.53.refs_1_), custom_call_target="tpu_custom_call" | custom-call | bytes 1048576 | tf_op jit(solution)/shard_map/pallas_call | solution.py:628
  118.7 21.7 %shard_map.316 = (bf16[4096,2048]{1,0:T(8,128)(2,1)}, bf16[4096,768]{1,0:T(8,128)(2,1)}) custom-call(bf16[4096,2048]{1,0:T(8,128)(2,1)} %bitcast.331, f32[1,2048]{1,0:T(1,128)S(1)} %copy.204.gain_ref, bf16[2048,768]{1,0:T(8,128)(2,1)S(1)} %slice.157.w_ref), custom_call_target="tpu_custom_call" | custom-call | flops 12884901888 | bytes 33554432 | tf_op jit(solution)/shard_map/pallas_call | solution.py:807
  140.5 19.4 %shard_map.317 = bf16[4096,256]{1,0:T(8,128)(2,1)S(1)} custom-call(bf16[4096,768]{1,0:T(8,128)(2,1)} %get-tuple-element.56.qkv_ref, s32[4096,1]{1,0:T(8,128)S(1)} %copy-done.7, s32[4,1,1024]{2,1,0:T(1,128)S(1)} %bitcast.265), custom_call_target="tpu_custom_call" | custom-call | flops 4294967296 | bytes 8388608 | tf_op jit(solution)/shard_map/pallas_call | solution.py:502
  212.0 22.4 %all-gather.15.cloned.1.call-done = bf16[2048,704]{0,1:T(8,128)(2,1)} async-done(((bf16[512,704]{0,1:T(8,128)(2,1)}), bf16[2048,704]{0,1:T(8,128)(2,1)}) %all-gather.15.cloned.1.call-update) | async-done | bytes 2883600 | tf_op jit(solution)/shard_map/all_gather | solution.py:1173
  234.5 75.6 %shard_map.318 = bf16[8,512,2048]{2,1,0:T(8,128)(2,1)} custom-call(bf16[512,2048]{1,0:T(8,128)(2,1)} %multiply_convert_fusion.7.refs_0_), custom_call_target="tpu_custom_call" | custom-call | bytes 1048576 | tf_op jit(solution)/shard_map/pallas_call | solution.py:628
  345.3 22.6 %multiply_convert_fusion.6 = (bf16[704,4096]{1,0:T(8,128)(2,1)}, f32[704,4096]{1,0:T(8,128)}) fusion(f32[704,4096]{1,0:T(8,128)} %fusion.57, bf16[2048,704]{0,1:T(8,128)(2,1)} %all-gather.15.cloned.1.call-done, bf16[4096,2048]{1,0:T(8,128)(2,1)} %bitcast.277), kind=kOutput, calls=%fused_computation.14 | convolution fusion | flops 11828461568 | bytes 48496640 | tf_op jit(solution)/shard_map/dot_general | solution.py:1052
  367.9 33.4 %all-gather.17.cloned.1.call-done = bf16[2048,1408]{1,0:T(8,128)(2,1)} async-done(((bf16[512,1408]{1,0:T(8,128)(2,1)}), bf16[2048,1408]{1,0:T(8,128)(2,1)}) %all-gather.17.cloned.1.call-update) | async-done | bytes 5767184 | tf_op jit(solution)/shard_map/all_gather | solution.py:1182
  401.2 20.8 %fusion.58 = f32[2304,1408]{1,0:T(8,128)} fusion(bf16[2304,2048]{1,0:T(8,128)(2,1)} %bitcast.333, bf16[2048,1408]{1,0:T(8,128)(2,1)} %all-gather.17.cloned.1.call-done), kind=kOutput, calls=%fused_computation.187 | convolution fusion | flops 13287555072 | bytes 28180480 | tf_op jit(solution)/shard_map/dot_general | solution.py:1052
  494.1 25.2 %multiply_convert_fusion.4 = (bf16[704,4096]{1,0:T(8,128)(2,1)}, bf16[704,4096]{1,0:T(8,128)(2,1)}) fusion(f32[704,4096]{1,0:T(8,128)} %fusion.57, f32[704,4096]{1,0:T(8,128)} %get-tuple-element.252, bf16[704,2048]{1,0:T(8,128)(2,1)} %all-gather.11.cloned.1.call-done.down_ref, bf16[4096,2048]{1,0:T(8,128)(2,1)} %multiply_convert_fusion.right_ref), kind=kOutput, calls=%fused_computation.12 | convolution fusion | flops 11848646656 | bytes 54263808 | tf_op jit(solution)/shard_map/dot_general | solution.py:1052
  592.4 20.8 %fusion.59 = f32[2304,1408]{1,0:T(8,128)} fusion(bf16[2304,2048]{1,0:T(8,128)(2,1)} %fusion, bf16[1408,2048]{1,0:T(8,128)(2,1)} %all-gather.19.cloned.1.call-done), kind=kOutput, calls=%fused_computation.188 | convolution fusion | flops 13287555072 | bytes 28180480 | tf_op jit(solution)/shard_map/dot_general | solution.py:1052
  613.3 130.1 %all-to-all-done.1 = bf16[4,512,1408]{2,1,0:T(8,128)(2,1)} async-done(((bf16[4,512,1408]{2,1,0:T(8,128)(2,1)}), bf16[4,512,1408]{2,1,0:T(8,128)(2,1)}, u32[]{:S(2)}, u32[]{:S(2)}) %all-to-all-start.1) | async-done | bytes 5767200 | tf_op jit(solution)/shard_map/all_to_all | solution.py:1184
  743.3 29.8 %multiply_convert_fusion.1 = (bf16[2304,1408]{1,0:T(8,128)(2,1)}, bf16[2304,1408]{1,0:T(8,128)(2,1)}, bf16[2304,1408]{1,0:T(8,128)(2,1)}) fusion(f32[2304,1408]{1,0:T(8,128)} %fusion.58, f32[2304,1408]{1,0:T(8,128)} %fusion.59, bf16[2304,2048]{1,0:T(8,128)(2,1)} %bitcast.334, bf16[2048,1408]{1,0:T(8,128)(2,1)} %bitcast.43), kind=kOutput, calls=%fused_computation.7 | convolution fusion | flops 13336215552 | bytes 60620800 | tf_op jit(solution)/shard_map/dot_general | solution.py:1052
  773.2 19.8 %convolution_convert_fusion.5 = bf16[1408,2048]{1,0:T(8,128)(2,1)} fusion(bf16[2304,1408]{1,0:T(8,128)(2,1)} %get-tuple-element.208, bf16[2304,2048]{1,0:T(8,128)(2,1)} %fusion), kind=kOutput, calls=%fused_computation.24 | convolution fusion | flops 13290438656 | bytes 21692416 | tf_op jit(solution)/shard_map/dot_general | solution.py:1052
  793.1 20.6 %convolution_convert_fusion.4 = bf16[2048,1408]{1,0:T(8,128)(2,1)} fusion(bf16[2304,2048]{1,0:T(8,128)(2,1)} %bitcast.335, bf16[2304,1408]{1,0:T(8,128)(2,1)} %get-tuple-element.209), kind=kOutput, calls=%fused_computation.23 | convolution fusion | flops 13290438656 | bytes 21692416 | tf_op jit(solution)/shard_map/dot_general | solution.py:1052
  816.0 20.2 %convolution_convert_fusion.3 = bf16[2048,1408]{1,0:T(8,128)(2,1)} fusion(bf16[2304,2048]{1,0:T(8,128)(2,1)} %bitcast.336, bf16[2304,1408]{1,0:T(8,128)(2,1)} %get-tuple-element.210), kind=kOutput, calls=%fused_computation.22 | convolution fusion | flops 13290438656 | bytes 21692416 | tf_op jit(solution)/shard_map/dot_general | solution.py:1052
  838.2 20.1 %convolution_convert_fusion.1 = bf16[2304,2048]{1,0:T(8,128)(2,1)} fusion(bf16[2304,1408]{1,0:T(8,128)(2,1)} %get-tuple-element.208, bf16[1408,2048]{1,0:T(8,128)(2,1)} %all-gather.19.cloned.1.call-done), kind=kOutput, calls=%fused_computation.17 | convolution fusion | flops 13292273664 | bytes 21692416 | tf_op jit(solution)/shard_map/dot_general | solution.py:1052
  858.4 35.3 %shard_map.319 = (bf16[4,512,2048]{2,1,0:T(8,128)(2,1)}, f32[4096,128]{1,0:T(8,128)}) custom-call(bf16[704,4096]{1,0:T(8,128)(2,1)} %get-tuple-element.251.hidden_ref.left_ref, bf16[704,2048]{1,0:T(8,128)(2,1)} %all-gather.11.cloned.1.call-done.down_ref, bf16[8,288,2048]{2,1,0:T(8,128)(2,1)} %bitcast.337, s32[4096,1]{1,0:T(8,128)} %copy.216.slot_ref, ...), custom_call_target="tpu_custom_call" | custom-call | flops 16642998272 | bytes 50331648 | tf_op jit(solution)/shard_map/pallas_call | solution.py:925
  911.3 20.7 %fusion.60 = f32[2304,2048]{1,0:T(8,128)} fusion(bf16[2304,1408]{1,0:T(8,128)(2,1)} %get-tuple-element.209, bf16[2048,1408]{1,0:T(8,128)(2,1)} %all-gather.17.cloned.1.call-done), kind=kOutput, calls=%fused_computation.189 | convolution fusion | flops 13287555072 | bytes 31129600 | tf_op jit(solution)/shard_map/dot_general | solution.py:1052
  932.0 22.9 %add_convert_fusion = bf16[2304,2048]{1,0:T(8,128)(2,1)} fusion(f32[2304,2048]{1,0:T(8,128)} %fusion.60, bf16[2304,1408]{1,0:T(8,128)(2,1)} %get-tuple-element.210, bf16[2048,1408]{1,0:T(8,128)(2,1)} %bitcast.43), kind=kOutput, calls=%fused_computation.5 | convolution fusion | flops 13296992256 | bytes 40566784 | tf_op jit(solution)/shard_map/dot_general | solution.py:1052
  954.9 41.1 %shard_map.320.refs_0_ = bf16[8,512,2048]{2,1,0:T(8,128)(2,1)} custom-call(bf16[704,4096]{1,0:T(8,128)(2,1)} %get-tuple-element.212.dgate_ref.left_ref, bf16[704,4096]{1,0:T(8,128)(2,1)} %get-tuple-element.211.dup_ref.left_ref, bf16[704,2048]{1,0:T(8,128)(2,1)S(1)} %bitcast.267, bf16[704,2048]{1,0:T(8,128)(2,1)} %bitcast.332, ...), custom_call_target="tpu_custom_call" | custom-call | flops 28454158336 | bytes 33554432 | tf_op jit(solution)/shard_map/pallas_call | solution.py:978
  999.4 77.1 %shard_map.324 = f32[512,2048]{1,0:T(8,128)S(1)} custom-call(bf16[8,512,2048]{2,1,0:T(8,128)(2,1)} %shard_map.320.refs_0_), custom_call_target="tpu_custom_call" | custom-call | bytes 1048576 | tf_op jit(solution)/shard_map/pallas_call | solution.py:769
  1154.2 30.7 %shard_map.325 = bf16[4096,768]{1,0:T(8,128)(2,1)} custom-call(bf16[4096,768]{1,0:T(8,128)(2,1)} %get-tuple-element.56.qkv_ref, bf16[4096,256]{1,0:T(8,128)(2,1)} %bitcast.63.grad_ref, s32[4096,1]{1,0:T(8,128)S(1)} %copy-done.8, s32[4,1,1024]{2,1,0:T(1,128)S(1)} %bitcast.266), custom_call_target="tpu_custom_call" | custom-call | flops 10737418240 | bytes 12582912 | tf_op jit(solution)/shard_map/pallas_call | solution.py:502
  1198.5 19.2 %convolution_convert_fusion.8 = bf16[2048,768]{1,0:T(8,128)(2,1)S(1)} fusion(bf16[4096,2048]{1,0:T(8,128)(2,1)} %get-tuple-element.85, bf16[4096,768]{1,0:T(8,128)(2,1)} %shard_map.325), kind=kOutput, calls=%fused_computation.47 | convolution fusion | flops 12886474752 | bytes 26214400 | tf_op jit(solution)/shard_map/dot_general | solution.py:1052
  1257.4 75.9 %shard_map.326 = f32[512,2048]{1,0:T(8,128)S(1)} custom-call(bf16[8,512,2048]{2,1,0:T(8,128)(2,1)} %bitcast.275), custom_call_target="tpu_custom_call" | custom-call | bytes 1048576 | tf_op jit(solution)/shard_map/pallas_call | solution.py:769
  (346 shorter events, 461.0 us)
Async XLA Ops:
  7.2 100.5 %all-gather.21.cloned.1.call-start = ((), (), s32[]{:S(2)}) async-start(), calls=%async_computation.30 | async-start | bytes 1310720 | tf_op jit(solution)/shard_map/all_gather | solution.py:1123
  9.5 105.3 %all-gather.9.cloned.1.call-start = ((), (), s32[]{:S(2)}) async-start(), calls=%async_computation.16 | async-start | bytes 4587520 | tf_op jit(solution)/shard_map/all_gather | solution.py:1114
  17.5 194.5 %all-gather.13.cloned.1.call-start = ((), (), s32[]{:S(2)}) async-start(), calls=%async_computation.18 | async-start | bytes 3604480 | tf_op jit(solution)/shard_map/all_gather | solution.py:1172
  19.3 215.2 %all-gather.15.cloned.1.call-start = ((), (), s32[]{:S(2)}) async-start(), calls=%async_computation.19 | async-start | bytes 3604480 | tf_op jit(solution)/shard_map/all_gather | solution.py:1173
  22.0 345.9 %all-gather.11.cloned.1.call-start = ((), (), s32[]{:S(2)}) async-start(), calls=%async_computation.17 | async-start | bytes 3604480 | tf_op jit(solution)/shard_map/all_gather | solution.py:1175
  23.0 378.2 %all-gather.17.cloned.1.call-start = ((), (), s32[]{:S(2)}) async-start(), calls=%async_computation.20 | async-start | bytes 7208960 | tf_op jit(solution)/shard_map/all_gather | solution.py:1182
  173.8 418.6 %all-gather.19.cloned.1.call-start = ((), (), s32[]{:S(2)}) async-start(), calls=%async_computation.21 | async-start | bytes 7208960 | tf_op jit(solution)/shard_map/all_gather | solution.py:1186
  310.1 112.0 %collective-permute-start.6 = (bf16[512,2048]{1,0:T(8,128)(2,1)S(1)}, bf16[512,2048]{1,0:T(8,128)(2,1)}, u32[]{:S(2)}, u32[]{:S(2)}) collective-permute-start(bf16[512,2048]{1,0:T(8,128)(2,1)S(1)} %bitcast.270), channel_id=1, source_target_pairs={{0,24},{8,16},{16,8},{24,0},{1,25},{9,17},{17,9},{25,1},{2,26},{10... | collective-permute-start | bytes 6291464 | tf_op jit(solution)/shard_map/ppermute | solution.py:1031
  311.6 110.4 %collective-permute-start.5 = (bf16[512,2048]{1,0:T(8,128)(2,1)S(1)}, bf16[512,2048]{1,0:T(8,128)(2,1)}, u32[]{:S(2)}, u32[]{:S(2)}) collective-permute-start(bf16[512,2048]{1,0:T(8,128)(2,1)S(1)} %bitcast.271), channel_id=1, source_target_pairs={{0,16},{8,24},{16,0},{24,8},{1,17},{9,25},{17,1},{25,9},{2,18},{10... | collective-permute-start | bytes 6291464 | tf_op jit(solution)/shard_map/ppermute | solution.py:1031
  312.6 109.5 %collective-permute-start.4 = (bf16[512,2048]{1,0:T(8,128)(2,1)S(1)}, bf16[512,2048]{1,0:T(8,128)(2,1)}, u32[]{:S(2)}, u32[]{:S(2)}) collective-permute-start(bf16[512,2048]{1,0:T(8,128)(2,1)S(1)} %bitcast.272), channel_id=1, source_target_pairs={{0,8},{8,0},{16,24},{24,16},{1,9},{9,1},{17,25},{25,17},{2,10},{10... | collective-permute-start | bytes 6291464 | tf_op jit(solution)/shard_map/ppermute | solution.py:1031
  428.8 570.5 %reduce-scatter.9.cloned.1.call-start = ((), (), s32[]{:S(2)}) async-start(), calls=%async_computation.22 | async-start | bytes 3604480 | tf_op jit(solution)/shard_map/reduce_scatter | solution.py:1250
  493.6 505.7 %reduce-scatter.13.cloned.1.call-start = ((), (), s32[]{:S(2)}) async-start(), calls=%async_computation.24 | async-start | bytes 3604480 | tf_op jit(solution)/shard_map/reduce_scatter | solution.py:1250
  540.9 202.5 %all-to-all-start.1 = ((bf16[4,512,1408]{2,1,0:T(8,128)(2,1)}), bf16[4,512,1408]{2,1,0:T(8,128)(2,1)}, u32[]{:S(2)}, u32[]{:S(2)}) async-start(bf16[4,512,1408]{2,1,0:T(8,128)(2,1)} %broadcast_in_dim.117), calls=%async_computation.1 | async-start | bytes 11534336 | tf_op jit(solution)/shard_map/all_to_all | solution.py:1184
  546.1 453.2 %reduce-scatter.11.cloned.1.call-start = ((), (), s32[]{:S(2)}) async-start(), calls=%async_computation.23 | async-start | bytes 3604480 | tf_op jit(solution)/shard_map/reduce_scatter | solution.py:1250
  570.1 584.0 %reduce-scatter.15.cloned.1.call-start = ((), (), s32[]{:S(2)}) async-start(), calls=%async_computation.25 | async-start | bytes 7208960 | tf_op jit(solution)/shard_map/reduce_scatter | solution.py:1250
  793.0 442.0 %reduce-scatter.17.cloned.1.call-start = ((), (), s32[]{:S(2)}) async-start(), calls=%async_computation.26 | async-start | bytes 7208960 | tf_op jit(solution)/shard_map/reduce_scatter | solution.py:1250
  813.8 522.5 %reduce-scatter.23.cloned.1.call-start = ((), (), s32[]{:S(2)}) async-start(), calls=%async_computation.29 | async-start | bytes 7208960 | tf_op jit(solution)/shard_map/reduce_scatter | solution.py:1250
  902.0 97.3 %collective-permute-start.10 = (bf16[512,2048]{1,0:T(8,128)(2,1)}, bf16[512,2048]{1,0:T(8,128)(2,1)}, u32[]{:S(2)}, u32[]{:S(2)}) collective-permute-start(bf16[512,2048]{1,0:T(8,128)(2,1)} %get-tuple-element.221), channel_id=1, source_target_pairs={{0,24},{8,16},{16,8},{24,0},{1,25},{9,17},{17,9},{25,1},{2,26},{10... | collective-permute-start | bytes 6291464 | tf_op jit(solution)/shard_map/ppermute | solution.py:1031
  904.3 94.9 %collective-permute-start.9 = (bf16[512,2048]{1,0:T(8,128)(2,1)}, bf16[512,2048]{1,0:T(8,128)(2,1)}, u32[]{:S(2)}, u32[]{:S(2)}) collective-permute-start(bf16[512,2048]{1,0:T(8,128)(2,1)} %get-tuple-element.222), channel_id=1, source_target_pairs={{0,16},{8,24},{16,0},{24,8},{1,17},{9,25},{17,1},{25,9},{2,18},{10... | collective-permute-start | bytes 6291464 | tf_op jit(solution)/shard_map/ppermute | solution.py:1031
  904.9 94.4 %collective-permute-start.8 = (bf16[512,2048]{1,0:T(8,128)(2,1)}, bf16[512,2048]{1,0:T(8,128)(2,1)}, u32[]{:S(2)}, u32[]{:S(2)}) collective-permute-start(bf16[512,2048]{1,0:T(8,128)(2,1)} %get-tuple-element.223), channel_id=1, source_target_pairs={{0,8},{8,0},{16,24},{24,16},{1,9},{9,1},{17,25},{25,17},{2,10},{10... | collective-permute-start | bytes 6291464 | tf_op jit(solution)/shard_map/ppermute | solution.py:1031
  906.8 89.6 %all-to-all-start.2 = ((f32[8,2,512]{2,1,0:T(2,128)}), f32[8,2,512]{2,1,0:T(2,128)S(1)}, u32[]{:S(2)}, u32[]{:S(2)}) async-start(f32[8,2,512]{2,1,0:T(2,128)} %gather_fusion.1), calls=%async_computation.5 | async-start | bytes 65536 | tf_op jit(solution)/shard_map/all_to_all | solution.py:1302
  1126.9 212.4 %reduce-scatter.19.cloned.1.call-start = ((), (), s32[]{:S(2)}) async-start(), calls=%async_computation.27 | async-start | bytes 3932160 | tf_op jit(solution)/shard_map/reduce_scatter | solution.py:1360
  1145.4 53.1 %collective-permute-start.16 = (bf16[256,2048]{1,0:T(8,128)(2,1)}, bf16[256,2048]{1,0:T(8,128)(2,1)}, u32[]{:S(2)}, u32[]{:S(2)}) collective-permute-start(bf16[256,2048]{1,0:T(8,128)(2,1)} %get-tuple-element.214), channel_id=1, source_target_pairs={{0,16},{8,24},{16,0},{24,8},{1,17},{9,25},{17,1},{25,9},{2,18},{10... | collective-permute-start | bytes 3145736 | tf_op jit(solution)/shard_map/ppermute | solution.py:1031
  1219.5 139.5 %reduce-scatter.21.cloned.1.call-start = ((), (), s32[]{:S(2)}) async-start(), calls=%async_computation.28 | async-start | bytes 1310720 | tf_op jit(solution)/shard_map/reduce_scatter | solution.py:1358
  (73 other events, 1936.9 us)
Sparse Core Ops, SparseCore 0:
  10.2 30.6 all-gather.20
  43.0 71.5 all-gather.8
  116.8 57.7 all-gather.12
  176.6 57.8 all-gather.14
  236.4 57.8 all-gather.10
  295.8 105.3 all-gather.16
  428.9 105.0 all-gather.18
  536.9 104.1 reduce-scatter.8
  644.0 117.5 reduce-scatter.12
  764.3 55.1 reduce-scatter.10
  821.9 102.0 reduce-scatter.14
  926.1 102.7 reduce-scatter.16
  1031.2 103.0 reduce-scatter.22
  1219.6 59.9 reduce-scatter.18
  1281.7 27.1 reduce-scatter.20

commit v7 on v6

--- a/solution.py
+++ b/solution.py
@@ -959,22 +959,151 @@
     )(hidden, down, rows, slots, sg, gates, cot)
 
 
-def n2_grad_kernel(dgate_ref, dup_ref, gate_ref, up_ref, rows_ref, slot_ref, out_ref):
-    chosen = chosen_rows(slot_ref[...], rows_ref.shape[1])
-    step = 512
-    for first in range(0, gate_ref.shape[1], step):
-        cols = pl.ds(first, step)
-        total = mm(dgate_ref[...], gate_ref[:, cols], ((0,), (0,)))
-        total += mm(dup_ref[...], up_ref[:, cols], ((0,), (0,)))
-        out_ref[0, :, cols] = low(total + mm(chosen, rows_ref[0, :, cols]))
-
-
-def n2_grad_parts(dgate, dup, gate_w, up_w, rows, slots):
+def scatter_step(compute, out_ref, scratch):
+    given, total, x_got, y_got, x_last, y_last, send_sem, recv_sem = scratch
+    at, core, across, along, far = plane_places()
+    step_at = pl.program_id(0)
+    row = step_at // 2
+    is_twin = step_at % 2 == 0
+    rows = total.shape[1]
+    half = rows // 2
+    top, bottom = pl.ds(0, half), pl.ds(half, half)
+
+    def copy_of(number, src, dst, target):
+        return pltpu.make_async_remote_copy(
+            src_ref=src,
+            dst_ref=dst,
+            send_sem=send_sem.at[number],
+            recv_sem=recv_sem.at[number],
+            device_id=target,
+            device_id_type=MESH_ID,
+        )
+
+    def twin_copy(k):
+        return copy_of(k, given.at[k % 2], total.at[k], {CTX: 1 - core})
+
+    far_x = copy_of(4, total.at[0, top], x_got.at[0], {EXP: across})
+    far_y = copy_of(5, total.at[0, bottom], y_got.at[0], {EXP: along})
+    own_x = copy_of(6, total.at[1, top], x_got.at[1], {EXP: across})
+    own_y = copy_of(7, total.at[2, bottom], y_got.at[1], {EXP: along})
+    last_y = copy_of(8, total.at[2, top], y_last, {EXP: along})
+    last_x = copy_of(9, total.at[1, bottom], x_last, {EXP: across})
+
+    @pl.when(step_at == 0)
+    def _():
+        greet(across, along, core)
+
+    @pl.when(is_twin)
+    def _():
+        @pl.when(row >= 2)
+        def _():
+            twin_copy(row - 2).wait_send()
+
+        def store(cols, values):
+            given[row % 2, :, cols] = low(values)
+
+        compute(store)
+        twin_copy(row).start()
+
+    @pl.when(jnp.logical_not(is_twin))
+    def _():
+        twin_copy(row).wait_recv()
+
+        def store(cols, values):
+            total[row, :, cols] = low(values + total[row, :, cols].astype(jnp.float32))
+
+        compute(store)
+
+    @pl.when(step_at == 1)
+    def _():
+        far_x.start()
+        far_y.start()
+
+    @pl.when(step_at == 3)
+    def _():
+        own_x.start()
+
+    @pl.when(step_at == 5)
+    def _():
+        own_y.start()
+
+    @pl.when(step_at == 7)
+    def _():
+        def add_half(k, first, got):
+            @pl.loop(0, half // 64)
+            def _(i):
+                take = pl.ds(pl.multiple_of(i * 64, 64), 64)
+                into = pl.ds(pl.multiple_of(first + i * 64, 64), 64)
+                total[k, into] = low(
+                    total[k, into].astype(jnp.float32) + got[0, take].astype(jnp.float32)
+                )
+
+        def finish(first, near, later):
+            @pl.loop(0, half // 64)
+            def _(i):
+                take = pl.ds(pl.multiple_of(i * 64, 64), 64)
+                into = pl.ds(pl.multiple_of(first + i * 64, 64), 64)
+                out_ref[into] = (
+                    total[3, into].astype(jnp.float32)
+                    + near[1, take].astype(jnp.float32)
+                    + later[take].astype(jnp.float32)
+                )
+
+        far_x.wait_recv()
+        add_half(2, 0, x_got)
+        last_y.start()
+        far_y.wait_recv()
+        add_half(1, half, y_got)
+        last_x.start()
+        own_x.wait_recv()
+        last_y.wait_recv()
+        finish(0, x_got, y_last)
+        own_y.wait_recv()
+        last_x.wait_recv()
+        finish(half, y_got, x_last)
+        for copy in (twin_copy(2), twin_copy(3), far_x, far_y, own_x, own_y, last_y, last_x):
+            copy.wait_send()
+
+
+def step_slot(i):
+    row = i // 2
+    shift = jnp.where(row == 0, 3, jnp.where(row == 3, 0, row))
+    return shift + 4 * (1 - i % 2)
+
+
+def scatter_scratch(tokens, width):
+    vmem = lambda *shape: pltpu.VMEM(shape, jnp.bfloat16)
+    return [
+        vmem(2, tokens, width),
+        vmem(4, tokens, width),
+        vmem(2, tokens // 2, width),
+        vmem(2, tokens // 2, width),
+        vmem(tokens // 2, width),
+        vmem(tokens // 2, width),
+        pltpu.SemaphoreType.DMA((10,)),
+        pltpu.SemaphoreType.DMA((10,)),
+    ]
+
+
+def n2_grad_kernel(dgate_ref, dup_ref, gate_ref, up_ref, rows_ref, slot_ref, out_ref, *scratch):
+    def compute(store):
+        chosen = chosen_rows(slot_ref[...], rows_ref.shape[1])
+        dgate, dup = dgate_ref[...].T, dup_ref[...].T
+        step = 512
+        for first in range(0, gate_ref.shape[1], step):
+            cols = pl.ds(first, step)
+            total = mm(dgate, gate_ref[:, cols]) + mm(dup, up_ref[:, cols])
+            store(cols, total + mm(chosen, rows_ref[0, :, cols]))
+
+    scatter_step(compute, out_ref, scratch)
+
+
+def n2_grad_sum(dgate, dup, gate_w, up_w, rows, slots):
     blocks, capacity, width = rows.shape
     units, count = dgate.shape
     tokens = count // blocks
-    by_units = pl.BlockSpec((units, tokens), lambda i: (0, i))
-    whole = pl.BlockSpec((units, width), lambda i: (0, 0))
+    by_units = pl.BlockSpec((units, tokens), lambda i: (0, step_slot(i)))
+    whole = pl.BlockSpec((units, width), lambda i: (0, 0), pipeline_mode=pl.Buffered(1))
     return pl.pallas_call(
         n2_grad_kernel,
         grid=(blocks,),
@@ -983,12 +1112,15 @@
             by_units,
             whole,
             whole,
-            pl.BlockSpec((1, capacity, width), lambda i: (i, 0, 0)),
-            pl.BlockSpec((tokens, 1), lambda i: (i, 0)),
+            pl.BlockSpec((1, capacity, width), lambda i: (step_slot(i), 0, 0)),
+            pl.BlockSpec((tokens, 1), lambda i: (step_slot(i), 0)),
         ],
-        out_specs=pl.BlockSpec((1, tokens, width), lambda i: (i, 0, 0)),
-        out_shape=jax.ShapeDtypeStruct((blocks, tokens, width), jnp.bfloat16),
-        compiler_params=pltpu.CompilerParams(vmem_limit_bytes=48 * 2**20),
+        out_specs=pl.BlockSpec((tokens, width), lambda i: (0, 0)),
+        out_shape=jax.ShapeDtypeStruct((tokens, width), jnp.float32),
+        scratch_shapes=scatter_scratch(tokens, width),
+        compiler_params=pltpu.CompilerParams(
+            collective_id=3, has_side_effects=True, vmem_limit_bytes=56 * 2**20
+        ),
         cost_estimate=pl.CostEstimate(
             flops=2 * count * width * (2 * units + capacity),
             bytes_accessed=4 * count * width,
@@ -1180,9 +1312,7 @@
     cot_own = after(cotangent[0], n2_all)
     cot_got = [swap(cot_own, k) for k in (1, 2, 3)]
     ex_gate = lax.all_gather(after(expert_w_gate[0], info_all), DP, axis=0, tiled=True)
-    ex_up = jnp.broadcast_to(after(expert_w_up, info_all), (depth, *expert_w_up.shape[1:]))
-    ex_up = lax.all_to_all(ex_up, DP, split_axis=0, concat_axis=0, tiled=True)
-    ex_up = ex_up.reshape(width, -1)
+    ex_up = lax.all_gather(after(expert_w_up[0], info_all), DP, axis=0, tiled=True)
     ex_down = lax.all_gather(after(expert_w_down[0], info_all), DP, axis=1, tiled=True)
 
     small_w = jnp.concatenate([router_t, gate_vec[None]])
@@ -1248,15 +1378,20 @@
         return both.reshape(units, rows_out).astype(jnp.float32)
 
     scatter = lambda v, dim: lax.psum_scatter(v, DP, scatter_dimension=dim, tiled=True)
-    shared_sums = [
-        scatter(
-            unit_grads(left, right, depth, halves).reshape(depth * depth * part, -1), 0
-        )
+    level = lax.axis_index(DP)
+    made = [
+        unit_grads(left, right, depth, halves)
         for left, right in (
             (shared_hidden, shared_grads),
             (gate_grad_s, n2_all),
             (up_grad_s, n2_all),
         )
+    ]
+    for_level = lambda k: jnp.concatenate(
+        [lax.dynamic_index_in_dim(v, level ^ k, axis=0, keepdims=False) for v in made]
+    )
+    shared_sums = [for_level(0)] + [
+        lax.ppermute(for_level(k), DP, [(i, i ^ k) for i in range(4)]) for k in (1, 2, 3)
     ]
     result_e = low(mm(hidden_e, ex_down))
     hgrad_e = mm(row_grads, ex_down, ((1,), (1,)))
@@ -1278,23 +1413,20 @@
         expert_gate,
         cot_all,
     )
-    out_sums = [out_near[k] for k in range(4)]
     rows_grad = low(
         mm(gate_grad_e, ex_gate, ((1,), (1,))) + mm(up_grad_e, ex_up, ((1,), (1,)))
     )
 
-    n2_grad_part = n2_grad_parts(
+    n2_grad = n2_grad_sum(
         gate_grad_s,
         up_grad_s,
         sh_gate_t,
         sh_up_t,
         rows_grad.reshape(plane, capacity, width),
-        after(slots, out_sums),
-    )
-    out_got = hops(out_sums)
-    n2_grad_part, out_got, _ = lax.optimization_barrier((n2_grad_part, out_got, shared_sums))
-    output = low(residual + sum_up(out_got))
-    n2_grad = plane_scatter(n2_grad_part, True, 3, jnp.float32)[0]
+        slots,
+    )
+    out_near = after(out_near, n2_grad)
+    out_got = hops([out_near[k] for k in range(4)])
 
     dots = dots.reshape(plane, tokens, 128)[:, :, :2].transpose(0, 2, 1)
     back = jnp.arange(plane, dtype=jnp.int32) ^ me
@@ -1334,8 +1466,9 @@
         [block_of(k, core) for k in range(4)],
         jnp.stack([block_of(k, 1 - core) for k in range(4)]),
     )
+    shared_sums = low(sum_up(after(shared_sums, low_residual)))
     grad_sh_down, grad_sh_gate, grad_sh_up = [
-        shared_scatter(after(v, low_residual)) for v in shared_sums
+        shared_scatter(v) for v in shared_sums.reshape(3, units // halves, -1)
     ]
     grad_sh_gate, grad_sh_up = grad_sh_gate.T, grad_sh_up.T
     attended_grad = after(
@@ -1387,6 +1520,7 @@
     )
     grad_out = after(grad_out, n1_grad).astype(jnp.float32)
     grad_ex_up = after(grads[2], n1_grad).astype(jnp.float32)[None]
+    output = low(residual + sum_up(after(out_got, n1_grad)))
     input_part, _ = norm_back(x_rows, inv_one, g_one, n1_grad)
     input_grad = low(residual_grad + input_part)
     return (
@@ -1453,7 +1587,7 @@
     plane = mesh.shape[EXP] * mesh.shape[CTX]
 
     def run(*args):
-        square = mesh.shape[EXP] == 4 and mesh.shape[CTX] == 2
+        square = mesh.shape[EXP] == 4 and mesh.shape[CTX] == 2 and mesh.shape[DP] == 4
         one_each = square and args[12].shape[1] == plane
         local = local_plane if one_each else local_general
         return jax.shard_map(

time: 1390 us -> 1530 us (1.10)
  waiting for transfers between devices: 226 us -> 328 us
  Pallas kernels: 509 us -> 535 us
  other arithmetic: 106 us -> 124 us
    ppermute x0 -> x3, waiting for transfers between devices: none -> 129 us  [local_plane(): lax.ppermute(for_level(k), DP, [(i, i ^ k) for i in range(4)])]
    all_to_all x1, waiting for transfers between devices: 130 us -> 2.81 us  [local_plane(): lax.all_to_all(small_grads, PLANE, split_axis=0, concat_axis=0, tiled=True)]
    all_gather x0 -> x1, waiting for transfers between devices: none -> 61.8 us  [local_plane(): lax.all_gather(after(expert_w_up[0], info_all), DP, axis=0, tiled=True)]
    pallas_call x1, Pallas kernels: 41.1 us -> 95.5 us  [n2_grad_sum(): pl.pallas_call(n2_grad_kernel, grid=(blocks,), in_specs=[by_units, by_uni...]
    all_gather x1, waiting for transfers between devices: 0.01 us -> 45.5 us  [local_plane(): lax.all_gather(after(expert_w_down[0], info_all), DP, axis=1, tiled=True)]
    pallas_call x2 -> x1, Pallas kernels: 153 us -> 125 us  [plane_scatter(): pl.pallas_call(partial(plane_scatter_kernel, relative, extra is not None)...]
    convert_element_type x7 -> x8, other arithmetic: 44.4 us -> 49.1 us  [low(): return values.astype(jnp.bfloat16)]
    unnamed x131 -> x135, local copies, waits for them, and re-layouts: 38 us -> 33.5 us
  transfers between devices with their start and end apart: 40 -> 41, of which waited for: 9 -> 12; matrix products, arithmetic and copies ran while one was open for 40% -> 35% of each run, Pallas kernels for 37% -> 35%
where the time goes in v7:
time: 1530 us; the launch traced here: 1520 us
  Pallas kernels  535 us (35%)
  matrix products  364 us (24%)
  waiting for transfers between devices  328 us (21%)
  other arithmetic  124 us (8%)
  local copies, waits for them, and re-layouts  109 us (7%)
  starting transfers between devices  46.6 us (3%)
  between operations  15.5 us (1%)
    dot_general x21, matrix products, mm(): lax.dot_general(left, right, (dims, ((), ())), preferred_element_type=jnp...  337 us
    pallas_call x2, Pallas kernels, plane_gather(): pl.pallas_call(partial(plane_gather_kernel, info is not None, relative),...  157 us
    ppermute x3, waiting for transfers between devices, local_plane(): lax.ppermute(for_level(k), DP, [(i, i ^ k) for i in range(4)])  129 us
    pallas_call x1, Pallas kernels, plane_scatter(): pl.pallas_call(partial(plane_scatter_kernel, relative, extra is not None)...  125 us
    pallas_call x1, Pallas kernels, n2_grad_sum(): pl.pallas_call(n2_grad_kernel, grid=(blocks,), in_specs=[by_units, by_uni...  95.5 us
    all_gather x1, waiting for transfers between devices, local_plane(): lax.all_gather(after(expert_w_up[0], info_all), DP, axis=0, tiled=True)  61.8 us
    pallas_call x3, Pallas kernels, unit_grads(): pl.pallas_call(unit_grad_kernel, grid=(depth * halves,), in_specs=[pl.Blo...  51.4 us
    pallas_call x2, Pallas kernels, attention_call(): pl.pallas_call(partial(body, heads, step), grid=(rows // seq_len,), in_sp...  50.1 us
  transfers between devices with their start and end apart: 41, of which 12 were waited for; matrix products, arithmetic and copies ran while one was open for 35% of the time, Pallas kernels for 35%

profile of v7, /device:TPU:0, one launch (start us, length us, event | category | flops | bytes accessed | tf_op | source)
XLA Modules:
  0.0 1522.4 jit_solution(16833883190694730600)
XLA Ops:
  23.7 81.0 %shard_map.315 = (bf16[8,512,2048]{2,1,0:T(8,128)(2,1)}, s32[8,8,512]{2,1,0:T(8,128)}) custom-call(bf16[512,2048]{1,0:T(8,128)(2,1)} %bitcast.285, s32[8,512]{1,0:T(8,128)} %concatenate.65.refs_1_), custom_call_target="tpu_custom_call" | custom-call | bytes 1048576 | tf_op jit(solution)/shard_map/pallas_call | solution.py:628
  118.8 21.7 %shard_map.316 = (bf16[4096,2048]{1,0:T(8,128)(2,1)}, bf16[4096,768]{1,0:T(8,128)(2,1)}) custom-call(bf16[4096,2048]{1,0:T(8,128)(2,1)} %bitcast.348, f32[1,2048]{1,0:T(1,128)S(1)} %copy.192.gain_ref, bf16[2048,768]{1,0:T(8,128)(2,1)S(1)} %slice.166.w_ref), custom_call_target="tpu_custom_call" | custom-call | flops 12884901888 | bytes 33554432 | tf_op jit(solution)/shard_map/pallas_call | solution.py:807
  140.5 19.4 %shard_map.317 = bf16[4096,256]{1,0:T(8,128)(2,1)S(1)} custom-call(bf16[4096,768]{1,0:T(8,128)(2,1)} %get-tuple-element.56.qkv_ref, s32[4096,1]{1,0:T(8,128)S(1)} %copy-done.4, s32[4,1,1024]{2,1,0:T(1,128)S(1)} %bitcast.282), custom_call_target="tpu_custom_call" | custom-call | flops 4294967296 | bytes 8388608 | tf_op jit(solution)/shard_map/pallas_call | solution.py:502
  234.5 75.6 %shard_map.318 = bf16[8,512,2048]{2,1,0:T(8,128)(2,1)} custom-call(bf16[512,2048]{1,0:T(8,128)(2,1)} %multiply_convert_fusion.7.refs_0_), custom_call_target="tpu_custom_call" | custom-call | bytes 1048576 | tf_op jit(solution)/shard_map/pallas_call | solution.py:628
  313.7 19.4 %fusion.55 = f32[704,4096]{1,0:T(8,128)} fusion(bf16[2048,704]{0,1:T(8,128)(2,1)} %all-gather.12.cloned.1.call-done, bf16[4096,2048]{1,0:T(8,128)(2,1)} %bitcast.292), kind=kOutput, calls=%fused_computation.201 | convolution fusion | flops 11811160064 | bytes 31195136 | tf_op jit(solution)/shard_map/dot_general | solution.py:1184
  333.0 23.8 %multiply_convert_fusion.6 = (bf16[704,4096]{1,0:T(8,128)(2,1)}, f32[704,4096]{1,0:T(8,128)}) fusion(f32[704,4096]{1,0:T(8,128)} %fusion.55, bf16[2048,704]{0,1:T(8,128)(2,1)S(1)} %copy-done.51, bf16[4096,2048]{1,0:T(8,128)(2,1)} %bitcast.293), kind=kOutput, calls=%fused_computation.14 | convolution fusion | flops 11828461568 | bytes 48496640 | tf_op jit(solution)/shard_map/dot_general | solution.py:1184
  370.1 31.1 %all-gather.18.cloned.1.call-done = bf16[2048,1408]{1,0:T(8,128)(2,1)} async-done(((bf16[512,1408]{1,0:T(8,128)(2,1)}), bf16[2048,1408]{1,0:T(8,128)(2,1)}) %all-gather.18.cloned.1.call-update) | async-done | bytes 5767184 | tf_op jit(solution)/shard_map/all_gather | solution.py:1314
  401.2 20.7 %fusion.56 = f32[2304,1408]{1,0:T(8,128)} fusion(bf16[2304,2048]{1,0:T(8,128)(2,1)} %bitcast.351, bf16[2048,1408]{1,0:T(8,128)(2,1)} %all-gather.18.cloned.1.call-done), kind=kOutput, calls=%fused_computation.202 | convolution fusion | flops 13287555072 | bytes 28180480 | tf_op jit(solution)/shard_map/dot_general | solution.py:1184
  446.0 61.8 %all-gather.20.cloned.1.call-done = bf16[2048,1408]{1,0:T(8,128)(2,1)} async-done(((bf16[512,1408]{1,0:T(8,128)(2,1)}), bf16[2048,1408]{1,0:T(8,128)(2,1)}) %all-gather.20.cloned.1.call-update) | async-done | bytes 5767184 | tf_op jit(solution)/shard_map/all_gather | solution.py:1315
  507.9 20.7 %fusion.57 = f32[2304,1408]{1,0:T(8,128)} fusion(bf16[2304,2048]{1,0:T(8,128)(2,1)} %bitcast.352, bf16[2048,1408]{1,0:T(8,128)(2,1)} %all-gather.20.cloned.1.call-done), kind=kOutput, calls=%fused_computation.203 | convolution fusion | flops 13287555072 | bytes 28180480 | tf_op jit(solution)/shard_map/dot_general | solution.py:1184
  569.0 45.5 %all-gather.22.cloned.1.call-done = bf16[1408,2048]{1,0:T(8,128)(2,1)} async-done(((bf16[1408,512]{1,0:T(8,128)(2,1)}), bf16[1408,2048]{1,0:T(8,128)(2,1)}) %all-gather.22.cloned.1.call-update) | async-done | bytes 5767184 | tf_op jit(solution)/shard_map/all_gather | solution.py:1316
  614.5 29.5 %multiply_convert_fusion.1 = (bf16[2304,1408]{1,0:T(8,128)(2,1)}, bf16[2304,1408]{1,0:T(8,128)(2,1)}, bf16[2304,1408]{1,0:T(8,128)(2,1)}) fusion(f32[2304,1408]{1,0:T(8,128)} %fusion.56, f32[2304,1408]{1,0:T(8,128)} %fusion.57, bf16[2304,2048]{1,0:T(8,128)(2,1)} %fusion, bf16[1408,2048]{1,0:T(8,128)(2,1)} %all-gather.22.cloned.1.call-done), kind=kOutput, calls=%fused_computation.7 | convolution fusion | flops 13336215552 | bytes 60620800 | tf_op jit(solution)/shard_map/dot_general | solution.py:1184
  644.0 19.9 %convolution_convert_fusion.5 = bf16[1408,2048]{1,0:T(8,128)(2,1)} fusion(bf16[2304,1408]{1,0:T(8,128)(2,1)} %get-tuple-element.209, bf16[2304,2048]{1,0:T(8,128)(2,1)} %fusion), kind=kOutput, calls=%fused_computation.24 | convolution fusion | flops 13290438656 | bytes 21692416 | tf_op jit(solution)/shard_map/dot_general | solution.py:1184
  706.4 25.4 %multiply_convert_fusion.4 = (bf16[704,4096]{1,0:T(8,128)(2,1)}, bf16[704,4096]{1,0:T(8,128)(2,1)}) fusion(f32[704,4096]{1,0:T(8,128)} %fusion.55, f32[704,4096]{1,0:T(8,128)} %get-tuple-element.262, bf16[704,2048]{1,0:T(8,128)(2,1)} %all-gather.16.cloned.1.call-done.down_ref, bf16[4096,2048]{1,0:T(8,128)(2,1)} %multiply_convert_fusion.right_ref), kind=kOutput, calls=%fused_computation.12 | convolution fusion | flops 11848646656 | bytes 54263808 | tf_op jit(solution)/shard_map/dot_general | solution.py:1184
  811.2 20.0 %convolution_convert_fusion.1 = bf16[2304,2048]{1,0:T(8,128)(2,1)} fusion(bf16[2304,1408]{1,0:T(8,128)(2,1)} %get-tuple-element.209, bf16[1408,2048]{1,0:T(8,128)(2,1)} %all-gather.22.cloned.1.call-done), kind=kOutput, calls=%fused_computation.17 | convolution fusion | flops 13292273664 | bytes 21692416 | tf_op jit(solution)/shard_map/dot_general | solution.py:1184
  831.2 35.6 %shard_map.319 = (bf16[4,512,2048]{2,1,0:T(8,128)(2,1)}, f32[4096,128]{1,0:T(8,128)}) custom-call(bf16[704,4096]{1,0:T(8,128)(2,1)} %get-tuple-element.261.hidden_ref.left_ref, bf16[704,2048]{1,0:T(8,128)(2,1)} %all-gather.16.cloned.1.call-done.down_ref, bf16[8,288,2048]{2,1,0:T(8,128)(2,1)} %bitcast.357, s32[4096,1]{1,0:T(8,128)} %copy.204.slot_ref, ...), custom_call_target="tpu_custom_call" | custom-call | flops 16642998272 | bytes 50331648 | tf_op jit(solution)/shard_map/pallas_call | solution.py:925
  874.9 20.9 %fusion.58 = f32[2304,2048]{1,0:T(8,128)} fusion(bf16[2304,1408]{1,0:T(8,128)(2,1)} %get-tuple-element.208, bf16[2048,1408]{1,0:T(8,128)(2,1)} %all-gather.18.cloned.1.call-done), kind=kOutput, calls=%fused_computation.204 | convolution fusion | flops 13287555072 | bytes 31129600 | tf_op jit(solution)/shard_map/dot_general | solution.py:1184
  895.8 22.1 %add_convert_fusion = bf16[2304,2048]{1,0:T(8,128)(2,1)} fusion(f32[2304,2048]{1,0:T(8,128)} %fusion.58, bf16[2304,1408]{1,0:T(8,128)(2,1)} %get-tuple-element.207, bf16[2048,1408]{1,0:T(8,128)(2,1)} %all-gather.20.cloned.1.call-done), kind=kOutput, calls=%fused_computation.5 | convolution fusion | flops 13296992256 | bytes 40566784 | tf_op jit(solution)/shard_map/dot_general | solution.py:1184
  917.9 95.5 %shard_map.320 = f32[512,2048]{1,0:T(8,128)} custom-call(bf16[704,4096]{1,0:T(8,128)(2,1)} %get-tuple-element.211.dgate_ref.left_ref, bf16[704,4096]{1,0:T(8,128)(2,1)} %get-tuple-element.210.dup_ref.left_ref, bf16[704,2048]{1,0:T(8,128)(2,1)} %bitcast.349, bf16[704,2048]{1,0:T(8,128)(2,1)} %bitcast.350, bf16[8,288,2048]{2,1,0:T(8,128)(2,1)} %bitcast.358, ...), custom_call_target="tpu_custom_call" | custom-call | flops 28454158336 | bytes 33554432 | tf_op jit(solution)/shard_map/pallas_call | solution.py:1107
  1064.8 59.2 %collective-permute-done.13 = bf16[2112,512]{1,0:T(8,128)(2,1)} collective-permute-done((bf16[2112,512]{1,0:T(8,128)(2,1)}, bf16[2112,512]{1,0:T(8,128)(2,1)}, u32[]{:S(2)}, u32[]{:S(2)}) %collective-permute-start.13) | collective-permute-done | bytes 2162720 | tf_op jit(solution)/shard_map/ppermute | solution.py:1394
  1124.0 69.6 %collective-permute-done.12 = bf16[2112,512]{1,0:T(8,128)(2,1)} collective-permute-done((bf16[2112,512]{1,0:T(8,128)(2,1)}, bf16[2112,512]{1,0:T(8,128)(2,1)}, u32[]{:S(2)}, u32[]{:S(2)}) %collective-permute-start.12) | collective-permute-done | bytes 2162720 | tf_op jit(solution)/shard_map/ppermute | solution.py:1394
  1225.2 30.7 %shard_map.324 = bf16[4096,768]{1,0:T(8,128)(2,1)} custom-call(bf16[4096,768]{1,0:T(8,128)(2,1)} %get-tuple-element.56.qkv_ref, bf16[4096,256]{1,0:T(8,128)(2,1)} %bitcast.58.grad_ref, s32[4096,1]{1,0:T(8,128)S(1)} %copy-done.5, s32[4,1,1024]{2,1,0:T(1,128)S(1)} %bitcast.283), custom_call_target="tpu_custom_call" | custom-call | flops 10737418240 | bytes 12582912 | tf_op jit(solution)/shard_map/pallas_call | solution.py:502
  1269.6 19.2 %convolution_convert_fusion.8 = bf16[2048,768]{1,0:T(8,128)(2,1)S(1)} fusion(bf16[4096,2048]{1,0:T(8,128)(2,1)} %get-tuple-element.81, bf16[4096,768]{1,0:T(8,128)(2,1)} %shard_map.324), kind=kOutput, calls=%fused_computation.48 | convolution fusion | flops 12886474752 | bytes 26214400 | tf_op jit(solution)/shard_map/dot_general | solution.py:1184
  1339.3 124.7 %shard_map.325 = f32[512,2048]{1,0:T(8,128)S(1)} custom-call(bf16[8,512,2048]{2,1,0:T(8,128)(2,1)} %bitcast.291), custom_call_target="tpu_custom_call" | custom-call | bytes 1048576 | tf_op jit(solution)/shard_map/pallas_call | solution.py:769
  (356 shorter events, 514.0 us)
Async XLA Ops:
  17.5 198.9 %all-gather.12.cloned.1.call-start = ((), (), s32[]{:S(2)}) async-start(), calls=%async_computation.13 | async-start | bytes 3604480 | tf_op jit(solution)/shard_map/all_gather | solution.py:1304
  19.3 215.2 %all-gather.14.cloned.1.call-start = ((), (), s32[]{:S(2)}) async-start(), calls=%async_computation.14 | async-start | bytes 3604480 | tf_op jit(solution)/shard_map/all_gather | solution.py:1305
  22.0 348.1 %all-gather.16.cloned.1.call-start = ((), (), s32[]{:S(2)}) async-start(), calls=%async_computation.15 | async-start | bytes 3604480 | tf_op jit(solution)/shard_map/all_gather | solution.py:1307
  23.0 378.2 %all-gather.18.cloned.1.call-start = ((), (), s32[]{:S(2)}) async-start(), calls=%async_computation.16 | async-start | bytes 7208960 | tf_op jit(solution)/shard_map/all_gather | solution.py:1314
  104.7 403.1 %all-gather.20.cloned.1.call-start = ((), (), s32[]{:S(2)}) async-start(), calls=%async_computation.17 | async-start | bytes 7208960 | tf_op jit(solution)/shard_map/all_gather | solution.py:1315
  173.8 440.6 %all-gather.22.cloned.1.call-start = ((), (), s32[]{:S(2)}) async-start(), calls=%async_computation.18 | async-start | bytes 7208960 | tf_op jit(solution)/shard_map/all_gather | solution.py:1316
  310.1 111.9 %collective-permute-start.6 = (bf16[512,2048]{1,0:T(8,128)(2,1)S(1)}, bf16[512,2048]{1,0:T(8,128)(2,1)}, u32[]{:S(2)}, u32[]{:S(2)}) collective-permute-start(bf16[512,2048]{1,0:T(8,128)(2,1)S(1)} %bitcast.287), channel_id=1, source_target_pairs={{0,24},{8,16},{16,8},{24,0},{1,25},{9,17},{17,9},{25,1},{2,26},{10... | collective-permute-start | bytes 6291464 | tf_op jit(solution)/shard_map/ppermute | solution.py:1163
  311.6 110.3 %collective-permute-start.5 = (bf16[512,2048]{1,0:T(8,128)(2,1)S(1)}, bf16[512,2048]{1,0:T(8,128)(2,1)}, u32[]{:S(2)}, u32[]{:S(2)}) collective-permute-start(bf16[512,2048]{1,0:T(8,128)(2,1)S(1)} %bitcast.288), channel_id=1, source_target_pairs={{0,16},{8,24},{16,0},{24,8},{1,17},{9,25},{17,1},{25,9},{2,18},{10... | collective-permute-start | bytes 6291464 | tf_op jit(solution)/shard_map/ppermute | solution.py:1163
  312.6 109.3 %collective-permute-start.4 = (bf16[512,2048]{1,0:T(8,128)(2,1)S(1)}, bf16[512,2048]{1,0:T(8,128)(2,1)}, u32[]{:S(2)}, u32[]{:S(2)}) collective-permute-start(bf16[512,2048]{1,0:T(8,128)(2,1)S(1)} %bitcast.289), channel_id=1, source_target_pairs={{0,8},{8,0},{16,24},{24,16},{1,9},{9,1},{17,25},{25,17},{2,10},{10... | collective-permute-start | bytes 6291464 | tf_op jit(solution)/shard_map/ppermute | solution.py:1163
  428.5 109.6 %collective-permute-start.7 = (bf16[2048,2048]{1,0:T(8,128)(2,1)}, bf16[2048,2048]{1,0:T(8,128)(2,1)}, u32[]{:S(2)}, u32[]{:S(2)}) collective-permute-start(bf16[2048,2048]{1,0:T(8,128)(2,1)} %pad_maximum_fusion), channel_id=1, source_target_pairs={{0,4},{4,0},{1,5},{5,1},{2,6},{6,2},{3,7},{7,3},{8,12},{12,8},{9,1... | collective-permute-start | bytes 25165832 | tf_op jit(solution)/shard_map/ppermute | solution.py:1167
  428.6 796.6 %reduce-scatter.6.cloned.1.call-start = ((), (), s32[]{:S(2)}) async-start(), calls=%async_computation.19 | async-start | bytes 7208960 | tf_op jit(solution)/shard_map/reduce_scatter | solution.py:1380
  663.9 672.2 %reduce-scatter.8.cloned.1.call-start = ((), (), s32[]{:S(2)}) async-start(), calls=%async_computation.20 | async-start | bytes 7208960 | tf_op jit(solution)/shard_map/reduce_scatter | solution.py:1380
  788.6 276.2 %collective-permute-start.14 = (bf16[2112,512]{1,0:T(8,128)(2,1)}, bf16[2112,512]{1,0:T(8,128)(2,1)}, u32[]{:S(2)}, u32[]{:S(2)}) collective-permute-start(bf16[2112,512]{1,0:T(8,128)(2,1)} %pad_maximum_fusion.5), channel_id=1, source_target_pairs={{0,3},{1,2},{2,1},{3,0},{4,7},{5,6},{6,5},{7,4},{8,11},{9,10},{10,... | collective-permute-start | bytes 6488072 | tf_op jit(solution)/shard_map/ppermute | solution.py:1394
  790.3 333.7 %collective-permute-start.13 = (bf16[2112,512]{1,0:T(8,128)(2,1)}, bf16[2112,512]{1,0:T(8,128)(2,1)}, u32[]{:S(2)}, u32[]{:S(2)}) collective-permute-start(bf16[2112,512]{1,0:T(8,128)(2,1)} %pad_maximum_fusion.4), channel_id=1, source_target_pairs={{0,2},{1,3},{2,0},{3,1},{4,6},{5,7},{6,4},{7,5},{8,10},{9,11},{10,... | collective-permute-start | bytes 6488072 | tf_op jit(solution)/shard_map/ppermute | solution.py:1394
  870.3 143.0 %all-to-all-start.1 = ((f32[8,2,512]{2,1,0:T(2,128)}), f32[8,2,512]{2,1,0:T(2,128)S(1)}, u32[]{:S(2)}, u32[]{:S(2)}) async-start(f32[8,2,512]{2,1,0:T(2,128)} %gather_fusion.1), calls=%async_computation.1 | async-start | bytes 65536 | tf_op jit(solution)/shard_map/all_to_all | solution.py:1434
  874.2 591.8 %reduce-scatter.14.cloned.1.call-start = ((), (), s32[]{:S(2)}) async-start(), calls=%async_computation.23 | async-start | bytes 7208960 | tf_op jit(solution)/shard_map/reduce_scatter | solution.py:1380
  1035.9 172.1 %collective-permute-start.11 = (bf16[4,256,2048]{2,1,0:T(8,128)(2,1)}, bf16[4,256,2048]{2,1,0:T(8,128)(2,1)}, u32[]{:S(2)}, u32[]{:S(2)}) collective-permute-start(bf16[4,256,2048]{2,1,0:T(8,128)(2,1)} %pad_maximum_fusion.1), channel_id=1, source_target_pairs={{0,4},{4,0},{1,5},{5,1},{2,6},{6,2},{3,7},{7,3},{8,12},{12,8},{9,1... | collective-permute-start | bytes 12582920 | tf_op jit(solution)/shard_map/ppermute | solution.py:1167
  1037.6 156.0 %collective-permute-start.12 = (bf16[2112,512]{1,0:T(8,128)(2,1)}, bf16[2112,512]{1,0:T(8,128)(2,1)}, u32[]{:S(2)}, u32[]{:S(2)}) collective-permute-start(bf16[2112,512]{1,0:T(8,128)(2,1)} %pad_maximum_fusion.3), channel_id=1, source_target_pairs={{0,1},{1,0},{2,3},{3,2},{4,5},{5,4},{6,7},{7,6},{8,9},{9,8},{10,11... | collective-permute-start | bytes 6488072 | tf_op jit(solution)/shard_map/ppermute | solution.py:1394
  1051.5 142.1 %all-to-all-start.4 = ((f32[4,1,1024]{2,1,0:T(1,128)}), f32[4,1,1024]{2,1,0:T(1,128)S(1)}, u32[]{:S(2)}, u32[]{:S(2)}) async-start(f32[4,1,1024]{2,1,0:T(1,128)} %reshape.739), calls=%async_computation.5 | async-start | bytes 32768 | tf_op jit(solution)/shard_map/all_to_all | solution.py:1457
  1198.0 280.5 %reduce-scatter.10.cloned.1.call-start = ((), (), s32[]{:S(2)}) async-start(), calls=%async_computation.21 | async-start | bytes 3932160 | tf_op jit(solution)/shard_map/reduce_scatter | solution.py:1493
  1290.7 207.7 %reduce-scatter.12.cloned.1.call-start = ((), (), s32[]{:S(2)}) async-start(), calls=%async_computation.22 | async-start | bytes 1310720 | tf_op jit(solution)/shard_map/reduce_scatter | solution.py:1491
  1302.4 168.6 %collective-permute-start.10 = (bf16[512,2048]{1,0:T(8,128)(2,1)}, bf16[512,2048]{1,0:T(8,128)(2,1)}, u32[]{:S(2)}, u32[]{:S(2)}) collective-permute-start(bf16[512,2048]{1,0:T(8,128)(2,1)} %get-tuple-element.220), channel_id=1, source_target_pairs={{0,24},{8,16},{16,8},{24,0},{1,25},{9,17},{17,9},{25,1},{2,26},{10... | collective-permute-start | bytes 6291464 | tf_op jit(solution)/shard_map/ppermute | solution.py:1163
  1303.0 168.0 %collective-permute-start.8 = (bf16[512,2048]{1,0:T(8,128)(2,1)}, bf16[512,2048]{1,0:T(8,128)(2,1)}, u32[]{:S(2)}, u32[]{:S(2)}) collective-permute-start(bf16[512,2048]{1,0:T(8,128)(2,1)} %get-tuple-element.222), channel_id=1, source_target_pairs={{0,8},{8,0},{16,24},{24,16},{1,9},{9,1},{17,25},{25,17},{2,10},{10... | collective-permute-start | bytes 6291464 | tf_op jit(solution)/shard_map/ppermute | solution.py:1163
  1304.4 166.6 %collective-permute-start.9 = (bf16[512,2048]{1,0:T(8,128)(2,1)}, bf16[512,2048]{1,0:T(8,128)(2,1)}, u32[]{:S(2)}, u32[]{:S(2)}) collective-permute-start(bf16[512,2048]{1,0:T(8,128)(2,1)} %get-tuple-element.221), channel_id=1, source_target_pairs={{0,16},{8,24},{16,0},{24,8},{1,17},{9,25},{17,1},{25,9},{2,18},{10... | collective-permute-start | bytes 6291464 | tf_op jit(solution)/shard_map/ppermute | solution.py:1163
  (76 other events, 2481.4 us)
Sparse Core Ops, SparseCore 0:
  10.2 30.6 all-gather.23
  43.0 71.5 all-gather.9
  116.8 57.7 all-gather.11
  176.6 57.8 all-gather.13
  236.4 57.8 all-gather.15
  295.8 105.3 all-gather.17
  402.8 104.9 all-gather.19
  509.4 104.9 all-gather.21
  664.0 100.4 reduce-scatter.5
  766.7 210.5 reduce-scatter.7
  979.6 208.2 reduce-scatter.13
  1290.8 57.4 reduce-scatter.9
  1466.1 25.9 reduce-scatter.11

commit v8 on v7

--- a/solution.py
+++ b/solution.py
@@ -1129,30 +1129,34 @@
     )(dgate, dup, gate_w, up_w, rows, slots)
 
 
-def unit_grad_kernel(left_ref, right_ref, out_ref):
-    out_ref[0] = low(mm(left_ref[...], right_ref[...]))
-
-
-def unit_grads(left, right, depth, halves):
-    units, count = left.shape
-    width = right.shape[1]
+def unit_grad_kernel(hid_ref, dgate_ref, dup_ref, cot_ref, n2_ref, out_ref):
+    units = hid_ref.shape[0]
+    out_ref[0, :units] = low(mm(hid_ref[...], cot_ref[...]))
+    out_ref[0, units : 2 * units] = low(mm(dgate_ref[...], n2_ref[...]))
+    out_ref[0, 2 * units :] = low(mm(dup_ref[...], n2_ref[...]))
+
+
+def unit_grads(hidden, dgate, dup, cots, n2, depth, halves):
+    units, count = hidden.shape
+    width = n2.shape[1]
     cols = width // (depth * halves)
+    whole = pl.BlockSpec((units, count), lambda i: (0, 0), pipeline_mode=pl.Buffered(1))
+    strip = pl.BlockSpec((count, cols), lambda i: (0, i))
     return pl.pallas_call(
         unit_grad_kernel,
         grid=(depth * halves,),
-        in_specs=[
-            pl.BlockSpec((units, count), lambda i: (0, 0)),
-            pl.BlockSpec((count, cols), lambda i: (0, i)),
-        ],
-        out_specs=pl.BlockSpec((1, units, cols), lambda i: (lax.rem(i, depth), 0, i // depth)),
-        out_shape=jax.ShapeDtypeStruct((depth, units, halves * cols), jnp.bfloat16),
+        in_specs=[whole, whole, whole, strip, strip],
+        out_specs=pl.BlockSpec(
+            (1, 3 * units, cols), lambda i: (lax.rem(i, depth), 0, i // depth)
+        ),
+        out_shape=jax.ShapeDtypeStruct((depth, 3 * units, halves * cols), jnp.bfloat16),
         compiler_params=pltpu.CompilerParams(vmem_limit_bytes=48 * 2**20),
         cost_estimate=pl.CostEstimate(
-            flops=2 * units * count * width,
-            bytes_accessed=2 * (units * count + count * width + units * width),
+            flops=6 * units * count * width,
+            bytes_accessed=2 * (3 * units * count + 2 * count * width + 3 * units * width),
             transcendentals=0,
         ),
-    )(left, right)
+    )(hidden, dgate, dup, cots, n2)
 
 
 def after(values, others):
@@ -1234,25 +1238,26 @@
     place = lax.axis_index(EXP)
     away = [(place ^ k) * 2 + (core ^ j) for j in (0, 1) for k in range(4)]
     away = jnp.stack(away)
+    out_rows = shard // plane
+    w_out_part = lax.dynamic_slice(w_out, (me * out_rows, 0), (out_rows, width))
     w_qkv_part = jnp.concatenate(
         [
             lax.dynamic_slice(w, (0, me * head_cols), (shard, head_cols))
             for w in (w_query, w_key, w_value)
         ]
         + [router, norm1_gain[:, None], norm2_gain[:, None], shared_gate_vec[:, None]]
-        + [jnp.zeros((shard, 128 - experts_all - 3), jnp.bfloat16)],
+        + [jnp.zeros((shard, 128 - experts_all - 3), jnp.bfloat16)]
+        + [w_out_part.reshape(shard, -1)],
         axis=1,
     )
     w_qkv = lax.all_gather(w_qkv_part, DP, axis=0, tiled=True)
-    small = w_qkv[:, 3 * head_cols :].T
+    w_out_part = w_qkv[:, 3 * head_cols + 128 :].reshape(depth, out_rows, width)
+    small = w_qkv[:, 3 * head_cols : 3 * head_cols + 128].T
     w_qkv = w_qkv[:, : 3 * head_cols]
     router_t = small[:experts_all]
     g_one = small[experts_all].astype(jnp.float32)
     g_two = small[experts_all + 1].astype(jnp.float32)
     gate_vec = small[experts_all + 2]
-    out_rows = shard // plane
-    w_out_part = lax.dynamic_slice(w_out, (me * out_rows, 0), (out_rows, width))
-    w_out_part = lax.all_gather(w_out_part, DP, axis=0, tiled=False)
     w_out_part = after(w_out_part, info_all)
     w_out_got = [swap(w_out_part, k) for k in (1, 2, 3)]
 
@@ -1301,13 +1306,13 @@
     pick = lambda w: lax.dynamic_index_in_dim(
         w.reshape(w.shape[0], depth, halves, part), core, axis=2, keepdims=False
     ).reshape(w.shape[0], depth * part)
-    sh_gate = lax.all_gather(pick(shared_w_gate), DP, axis=0, tiled=True)
-    sh_up = lax.all_gather(pick(shared_w_up), DP, axis=0, tiled=True)
-    sh_gate_t, sh_up_t = sh_gate.T, sh_up.T
+    sh_gate_up = jnp.concatenate([pick(shared_w_gate), pick(shared_w_up)], axis=1)
+    sh_gate_up = lax.all_gather(sh_gate_up, DP, axis=0, tiled=True)
+    sh_gate_t, sh_up_t = sh_gate_up[:, : depth * part].T, sh_gate_up[:, depth * part :].T
     sh_down = lax.all_gather(
         lax.dynamic_slice(shared_w_down, (core * part, 0), (part, width)), DP, axis=0, tiled=True
     )
-    n2 = after(n2, (sh_gate, sh_up))
+    n2 = after(n2, sh_gate_up)
     n2_all = plane_gather(n2, None, True, 2)[0].reshape(all_tokens, width)
     cot_own = after(cotangent[0], n2_all)
     cot_got = [swap(cot_own, k) for k in (1, 2, 3)]
@@ -1378,21 +1383,10 @@
         return both.reshape(units, rows_out).astype(jnp.float32)
 
     scatter = lambda v, dim: lax.psum_scatter(v, DP, scatter_dimension=dim, tiled=True)
-    level = lax.axis_index(DP)
-    made = [
-        unit_grads(left, right, depth, halves)
-        for left, right in (
-            (shared_hidden, shared_grads),
-            (gate_grad_s, n2_all),
-            (up_grad_s, n2_all),
-        )
-    ]
-    for_level = lambda k: jnp.concatenate(
-        [lax.dynamic_index_in_dim(v, level ^ k, axis=0, keepdims=False) for v in made]
-    )
-    shared_sums = [for_level(0)] + [
-        lax.ppermute(for_level(k), DP, [(i, i ^ k) for i in range(4)]) for k in (1, 2, 3)
-    ]
+    shared_sums = unit_grads(
+        shared_hidden, gate_grad_s, up_grad_s, shared_grads, n2_all, depth, halves
+    )
+    shared_sums = scatter(shared_sums.reshape(3 * depth * depth * part, -1), 0)
     result_e = low(mm(hidden_e, ex_down))
     hgrad_e = mm(row_grads, ex_down, ((1,), (1,)))
     gate_grad_e = low(hgrad_e * up_e * silu_grad(gate_e))
@@ -1417,6 +1411,8 @@
         mm(gate_grad_e, ex_gate, ((1,), (1,))) + mm(up_grad_e, ex_up, ((1,), (1,)))
     )
 
+    out_got = [swap(out_near[k], k) for k in (1, 2)]
+    slots, out_got, _ = lax.optimization_barrier((slots, out_got, shared_sums))
     n2_grad = n2_grad_sum(
         gate_grad_s,
         up_grad_s,
@@ -1425,8 +1421,7 @@
         rows_grad.reshape(plane, capacity, width),
         slots,
     )
-    out_near = after(out_near, n2_grad)
-    out_got = hops([out_near[k] for k in range(4)])
+    out_far = swap(after(out_near[3], n2_grad), 3)
 
     dots = dots.reshape(plane, tokens, 128)[:, :, :2].transpose(0, 2, 1)
     back = jnp.arange(plane, dtype=jnp.int32) ^ me
@@ -1436,7 +1431,6 @@
     probs, sg = gates_of(n2)
     logit_grad = low(probs * (probs_grad - jnp.sum(probs * probs_grad, axis=1, keepdims=True)))
     sg_logit_grad = low(jnp.sum(dots[:, 1], axis=0)[:, None] * sg * (1.0 - sg))
-    small_grads = mm(n2, jnp.concatenate([logit_grad, sg_logit_grad], axis=1), ((0,), (0,)))
     n2_grad = (
         n2_grad
         + mm(logit_grad, router_t)
@@ -1446,38 +1440,22 @@
     residual_grad = residual_grad + cot_rows
     low_residual = low(residual_grad)
 
-    small_grads = jnp.concatenate([small_grads, grad_gain_two[:, None]], axis=1).T
-    small_grads = jnp.pad(small_grads, ((0, 14 - experts_all), (0, 0)))
-    small_grads = small_grads.reshape(16, plane, width // plane).transpose(1, 0, 2)
-    small_grads = jnp.sum(
-        lax.all_to_all(small_grads, PLANE, split_axis=0, concat_axis=0, tiled=True), axis=0
-    )
-    small_grads = small_grads.reshape(16, depth, shard // plane).transpose(1, 0, 2)
-    small_grads = jnp.sum(
-        lax.all_to_all(small_grads, DP, split_axis=0, concat_axis=0, tiled=True), axis=0
-    )
+    attended_grad = low(mm(low_residual, w_out_full, ((1,), (1,))))
+    low_residual = after(low_residual, attended_grad)
+    out_got = after(out_got, attended_grad)
+    output = residual + out_near[0].astype(jnp.float32) + sum_up(out_got)
+    attended_grad = to_columns(attended_grad)
     grad_out = low(mm(attended, low_residual, ((0,), (0,))))
     grad_out = grad_out.reshape(groups, halves, width // plane, width)
     block_of = lambda k, c: lax.dynamic_slice(
         grad_out, (place ^ k, c, 0, 0), (1, 1, width // plane, width)
     )[0, 0]
-    attended_grad = to_columns(low(mm(low_residual, w_out_full, ((1,), (1,)))))
     out_grad_sums = twin_sums(
         [block_of(k, core) for k in range(4)],
         jnp.stack([block_of(k, 1 - core) for k in range(4)]),
     )
-    shared_sums = low(sum_up(after(shared_sums, low_residual)))
-    grad_sh_down, grad_sh_gate, grad_sh_up = [
-        shared_scatter(v) for v in shared_sums.reshape(3, units // halves, -1)
-    ]
-    grad_sh_gate, grad_sh_up = grad_sh_gate.T, grad_sh_up.T
-    attended_grad = after(
-        attended_grad,
-        (out_grad_sums, grads[0], small_grads, grad_sh_down, grad_sh_gate, grad_sh_up),
-    )
+    attended_grad = after(attended_grad, (out_grad_sums, output, grads[0]))
     qkv_grad = attention_call(qkv, attended_grad, q_codes, k_codes, seq_len)
-    qkv_grad, grad_out = lax.optimization_barrier((qkv_grad, hops(out_grad_sums)))
-    grad_out = low(sum_up(grad_out))
     grad_qkv = low(mm(n1_all, qkv_grad, ((0,), (0,))))
     fine = shard // plane
     grad_qkv = (
@@ -1485,12 +1463,16 @@
         .transpose(1, 0, 2, 3)
         .reshape(width, 3 * head_cols)
     )
-    n1_grad = low(mm(after(qkv_grad, grad_qkv), w_qkv, ((1,), (1,))))
-    grad_ex_down, grad_ex_gate = [v.astype(jnp.float32)[None] for v in grads[:2]]
-    n1_grad = after(n1_grad, (grad_qkv, grad_out, grad_ex_down, grad_ex_gate))
-    grad_out = lax.psum_scatter(grad_out, DP, scatter_dimension=0, tiled=True)
+    qkv_grad, grad_out, _ = lax.optimization_barrier((qkv_grad, hops(out_grad_sums), grad_qkv))
+    grad_out = low(sum_up(grad_out))
+    n1_grad = low(mm(qkv_grad, w_qkv, ((1,), (1,))))
+    n1_grad, out_far, _ = lax.optimization_barrier(
+        (n1_grad, out_far, (grad_qkv, grad_out, grads[1]))
+    )
+    output = low(output + out_far.astype(jnp.float32))
     n1_grad = plane_scatter(n1_grad.reshape(plane, tokens, width), False, 1, jnp.float32)[0]
     grad_qkv = lax.psum_scatter(grad_qkv, DP, scatter_dimension=0, tiled=True)
+    qkv_sum = grad_qkv
     w_rows = (
         w_qkv.reshape(plane, depth, fine, 3 * head_cols)
         .transpose(1, 0, 2, 3)
@@ -1518,9 +1500,29 @@
         .reshape(3, fine, width)
         .astype(jnp.float32)
     )
-    grad_out = after(grad_out, n1_grad).astype(jnp.float32)
-    grad_ex_up = after(grads[2], n1_grad).astype(jnp.float32)[None]
-    output = low(residual + sum_up(after(out_got, n1_grad)))
+    grad_ex_down, grad_ex_gate, grad_ex_up = [
+        v.astype(jnp.float32)[None] for v in after(grads, n1_grad)
+    ]
+    grad_out = scatter(after(grad_out, (n1_grad, qkv_sum)), 0).astype(jnp.float32)
+    shared_sums = after(shared_sums, (n1_grad, qkv_sum))
+    grad_sh_down, grad_sh_gate, grad_sh_up = [
+        shared_scatter(v)
+        for v in shared_sums.reshape(3, units // halves, -1)
+    ]
+    grad_sh_gate, grad_sh_up = grad_sh_gate.T, grad_sh_up.T
+    dz_all = jnp.concatenate([logit_grad, sg_logit_grad], axis=1)
+    dz_all = after(dz_all, (n1_grad, qkv_sum))
+    small_grads = mm(n2, dz_all, ((0,), (0,)))
+    small_grads = jnp.concatenate([small_grads, grad_gain_two[:, None]], axis=1).T
+    small_grads = jnp.pad(small_grads, ((0, 14 - experts_all), (0, 0)))
+    small_grads = small_grads.reshape(16, plane, width // plane).transpose(1, 0, 2)
+    small_grads = jnp.sum(
+        lax.all_to_all(small_grads, PLANE, split_axis=0, concat_axis=0, tiled=True), axis=0
+    )
+    small_grads = small_grads.reshape(16, depth, shard // plane).transpose(1, 0, 2)
+    small_grads = jnp.sum(
+        lax.all_to_all(small_grads, DP, split_axis=0, concat_axis=0, tiled=True), axis=0
+    )
     input_part, _ = norm_back(x_rows, inv_one, g_one, n1_grad)
     input_grad = low(residual_grad + input_part)
     return (

time: 1530 us -> 1250 us (0.82)
  waiting for transfers between devices: 328 us -> 117 us
  Pallas kernels: 535 us -> 476 us
  other arithmetic: 124 us -> 105 us
    ppermute x3 -> x0, waiting for transfers between devices: 129 us -> none  [local_plane(): lax.ppermute(for_level(k), DP, [(i, i ^ k) for i in range(4)])]
    all_gather x1, waiting for transfers between devices: 61.8 us -> 0.01 us  [local_plane(): lax.all_gather(after(expert_w_up[0], info_all), DP, axis=0, tiled=True)]
    pallas_call x1, Pallas kernels: 125 us -> 75.3 us  [plane_scatter(): pl.pallas_call(partial(plane_scatter_kernel, relative, extra is not None)...]
    ppermute x12, waiting for transfers between devices: 13.8 us -> 40.4 us  [swap(): return lax.ppermute(values, EXP, [(i, i ^ bits) for i in range(4)])]
    all_gather x1, waiting for transfers between devices: 45.5 us -> 19.9 us  [local_plane(): lax.all_gather(after(expert_w_down[0], info_all), DP, axis=1, tiled=True)]
    all_gather x3 -> x1, waiting for transfers between devices: 18 us -> 0.01 us  [local_plane(): sh_gate_up = lax.all_gather(sh_gate_up, DP, axis=0, tiled=True)]
    convert_element_type x8 -> x7, other arithmetic: 49.1 us -> 37.6 us  [low(): return values.astype(jnp.bfloat16)]
    pallas_call x3 -> x1, Pallas kernels: 51.4 us -> 44.1 us  [unit_grads(): pl.pallas_call(unit_grad_kernel, grid=(depth * halves,), in_specs=[whole,...]
  transfers between devices with their start and end apart: 41 -> 37, of which waited for: 12 -> 14; matrix products, arithmetic and copies ran while one was open for 35% -> 45% of each run, Pallas kernels for 35% -> 38%
where the time goes in v8:
time: 1250 us; the launch traced here: 1240 us
  Pallas kernels  476 us (38%)
  matrix products  362 us (29%)
  local copies, waits for them, and re-layouts  118 us (9%)
  waiting for transfers between devices  117 us (9%)
  other arithmetic  105 us (8%)
  starting transfers between devices  44.5 us (4%)
  between operations  15.5 us (1%)
    dot_general x21, matrix products, mm(): lax.dot_general(left, right, (dims, ((), ())), preferred_element_type=jnp...  336 us
    pallas_call x2, Pallas kernels, plane_gather(): pl.pallas_call(partial(plane_gather_kernel, info is not None, relative),...  155 us
    pallas_call x1, Pallas kernels, n2_grad_sum(): pl.pallas_call(n2_grad_kernel, grid=(blocks,), in_specs=[by_units, by_uni...  94.1 us
    pallas_call x1, Pallas kernels, plane_scatter(): pl.pallas_call(partial(plane_scatter_kernel, relative, extra is not None)...  75.3 us
    pallas_call x2, Pallas kernels, attention_call(): pl.pallas_call(partial(body, heads, step), grid=(rows // seq_len,), in_sp...  50.5 us
    pallas_call x1, Pallas kernels, unit_grads(): pl.pallas_call(unit_grad_kernel, grid=(depth * halves,), in_specs=[whole,...  44.1 us
    ppermute x12, waiting for transfers between devices, swap(): return lax.ppermute(values, EXP, [(i, i ^ bits) for i in range(4)])  40.4 us
    convert_element_type x7, other arithmetic, low(): return values.astype(jnp.bfloat16)  37.6 us
  transfers between devices with their start and end apart: 37, of which 14 were waited for; matrix products, arithmetic and copies ran while one was open for 45% of the time, Pallas kernels for 38%

profile of v8, /device:TPU:0, one launch (start us, length us, event | category | flops | bytes accessed | tf_op | source)
XLA Modules:
  0.0 1238.0 jit_solution(9005433860740188364)
XLA Ops:
  25.0 81.1 %shard_map.315 = (bf16[8,512,2048]{2,1,0:T(8,128)(2,1)}, s32[8,8,512]{2,1,0:T(8,128)}) custom-call(bf16[512,2048]{1,0:T(8,128)(2,1)} %bitcast.263, s32[8,512]{1,0:T(8,128)} %concatenate.56.refs_1_), custom_call_target="tpu_custom_call" | custom-call | bytes 1048576 | tf_op jit(solution)/shard_map/pallas_call | solution.py:628
  122.2 21.7 %shard_map.316 = (bf16[4096,2048]{1,0:T(8,128)(2,1)}, bf16[4096,768]{1,0:T(8,128)(2,1)}) custom-call(bf16[4096,2048]{1,0:T(8,128)(2,1)} %bitcast.323, f32[1,2048]{1,0:T(1,128)S(1)} %copy.204.gain_ref, bf16[2048,768]{1,0:T(8,128)(2,1)S(1)} %slice.178.w_ref), custom_call_target="tpu_custom_call" | custom-call | flops 12884901888 | bytes 33554432 | tf_op jit(solution)/shard_map/pallas_call | solution.py:807
  220.3 74.1 %shard_map.318 = bf16[8,512,2048]{2,1,0:T(8,128)(2,1)} custom-call(bf16[512,2048]{1,0:T(8,128)(2,1)} %multiply_convert_fusion.7.refs_0_), custom_call_target="tpu_custom_call" | custom-call | bytes 1048576 | tf_op jit(solution)/shard_map/pallas_call | solution.py:628
  311.3 19.5 %fusion.12 = f32[704,4096]{1,0:T(8,128)} fusion(bf16[4096,2048]{1,0:T(8,128)(2,1)} %bitcast.270, bf16[2048,1408]{0,1:T(8,128)(2,1)} %all-gather.9.cloned.1.call-done), kind=kOutput, calls=%fused_computation.55 | convolution fusion | flops 11811160064 | bytes 31195136 | tf_op jit(solution)/shard_map/dot_general | solution.py:1188
  330.8 22.6 %multiply_convert_fusion.6 = (bf16[704,4096]{1,0:T(8,128)(2,1)}, f32[704,4096]{1,0:T(8,128)}) fusion(f32[704,4096]{1,0:T(8,128)} %fusion.12, bf16[4096,2048]{1,0:T(8,128)(2,1)} %bitcast.271, bf16[2048,1408]{0,1:T(8,128)(2,1)} %all-gather.9.cloned.1.call-done), kind=kOutput, calls=%fused_computation.14 | convolution fusion | flops 11828461568 | bytes 48496640 | tf_op jit(solution)/shard_map/dot_general | solution.py:1188
  353.3 31.5 %all-gather.13.cloned.1.call-done = bf16[2048,1408]{1,0:T(8,128)(2,1)} async-done(((bf16[512,1408]{1,0:T(8,128)(2,1)}), bf16[2048,1408]{1,0:T(8,128)(2,1)}) %all-gather.13.cloned.1.call-update) | async-done | bytes 5767184 | tf_op jit(solution)/shard_map/all_gather | solution.py:1319
  384.8 20.8 %fusion.55 = f32[2304,1408]{1,0:T(8,128)} fusion(bf16[2304,2048]{1,0:T(8,128)(2,1)} %bitcast.324, bf16[2048,1408]{1,0:T(8,128)(2,1)} %all-gather.13.cloned.1.call-done), kind=kOutput, calls=%fused_computation.188 | convolution fusion | flops 13287555072 | bytes 28180480 | tf_op jit(solution)/shard_map/dot_general | solution.py:1188
  457.7 25.2 %multiply_convert_fusion.4 = (bf16[704,4096]{1,0:T(8,128)(2,1)}, bf16[704,4096]{1,0:T(8,128)(2,1)}) fusion(f32[704,4096]{1,0:T(8,128)} %fusion.12, f32[704,4096]{1,0:T(8,128)} %get-tuple-element.255, bf16[704,2048]{1,0:T(8,128)(2,1)} %all-gather.11.cloned.1.call-done.down_ref, bf16[4096,2048]{1,0:T(8,128)(2,1)} %multiply_convert_fusion.cot_ref), kind=kOutput, calls=%fused_computation.12 | convolution fusion | flops 11848646656 | bytes 54263808 | tf_op jit(solution)/shard_map/dot_general | solution.py:1188
  485.5 44.1 %shard_map.320 = bf16[4,2112,512]{2,1,0:T(8,128)(2,1)} custom-call(bf16[704,4096]{1,0:T(8,128)(2,1)S(1)} %copy-done.7, bf16[704,4096]{1,0:T(8,128)(2,1)} %get-tuple-element.215.dgate_ref, bf16[704,4096]{1,0:T(8,128)(2,1)} %get-tuple-element.214.dup_ref, bf16[4096,2048]{1,0:T(8,128)(2,1)} %multiply_convert_fusion.cot_ref, bf16[4096,2048]{1,0:T(8,128)(2,1)} %bitcast.273), custom_call_target="tpu_custom_call" | custom-call | flops 35433480192 | bytes 59506688 | tf_op jit(solution)/shard_map/pallas_call | solution.py:1145
  535.0 20.8 %fusion.56 = f32[2304,1408]{1,0:T(8,128)} fusion(bf16[2304,2048]{1,0:T(8,128)(2,1)} %bitcast.325, bf16[2048,1408]{1,0:T(8,128)(2,1)} %all-gather.15.cloned.1.call-done), kind=kOutput, calls=%fused_computation.189 | convolution fusion | flops 13287555072 | bytes 28180480 | tf_op jit(solution)/shard_map/dot_general | solution.py:1188
  577.8 19.9 %all-gather.17.cloned.1.call-done = bf16[1408,2048]{1,0:T(8,128)(2,1)} async-done(((bf16[1408,512]{1,0:T(8,128)(2,1)}), bf16[1408,2048]{1,0:T(8,128)(2,1)}) %all-gather.17.cloned.1.call-update) | async-done | bytes 5767184 | tf_op jit(solution)/shard_map/all_gather | solution.py:1321
  597.7 30.6 %multiply_convert_fusion.1 = (bf16[2304,1408]{1,0:T(8,128)(2,1)}, bf16[2304,1408]{1,0:T(8,128)(2,1)}, bf16[2304,1408]{1,0:T(8,128)(2,1)}) fusion(f32[2304,1408]{1,0:T(8,128)} %fusion.55, f32[2304,1408]{1,0:T(8,128)} %fusion.56, bf16[2304,2048]{1,0:T(8,128)(2,1)} %fusion, bf16[1408,2048]{1,0:T(8,128)(2,1)} %all-gather.17.cloned.1.call-done), kind=kOutput, calls=%fused_computation.7 | convolution fusion | flops 13336215552 | bytes 60620800 | tf_op jit(solution)/shard_map/dot_general | solution.py:1188
  628.4 19.8 %convolution_convert_fusion.5 = bf16[1408,2048]{1,0:T(8,128)(2,1)} fusion(bf16[2304,1408]{1,0:T(8,128)(2,1)} %get-tuple-element.213, bf16[2304,2048]{1,0:T(8,128)(2,1)} %fusion), kind=kOutput, calls=%fused_computation.24 | convolution fusion | flops 13290438656 | bytes 21692416 | tf_op jit(solution)/shard_map/dot_general | solution.py:1188
  648.2 20.4 %convolution_convert_fusion.4 = bf16[2048,1408]{1,0:T(8,128)(2,1)} fusion(bf16[2304,2048]{1,0:T(8,128)(2,1)} %bitcast.326, bf16[2304,1408]{1,0:T(8,128)(2,1)} %get-tuple-element.212), kind=kOutput, calls=%fused_computation.23 | convolution fusion | flops 13290438656 | bytes 21692416 | tf_op jit(solution)/shard_map/dot_general | solution.py:1188
  675.8 20.6 %convolution_convert_fusion.3 = bf16[2048,1408]{1,0:T(8,128)(2,1)} fusion(bf16[2304,2048]{1,0:T(8,128)(2,1)} %bitcast.327, bf16[2304,1408]{1,0:T(8,128)(2,1)} %get-tuple-element.211), kind=kOutput, calls=%fused_computation.22 | convolution fusion | flops 13290438656 | bytes 21692416 | tf_op jit(solution)/shard_map/dot_general | solution.py:1188
  698.4 20.0 %convolution_convert_fusion.1 = bf16[2304,2048]{1,0:T(8,128)(2,1)} fusion(bf16[2304,1408]{1,0:T(8,128)(2,1)} %get-tuple-element.213, bf16[1408,2048]{1,0:T(8,128)(2,1)} %all-gather.17.cloned.1.call-done), kind=kOutput, calls=%fused_computation.17 | convolution fusion | flops 13292273664 | bytes 21692416 | tf_op jit(solution)/shard_map/dot_general | solution.py:1188
  718.4 35.2 %shard_map.319 = (bf16[4,512,2048]{2,1,0:T(8,128)(2,1)}, f32[4096,128]{1,0:T(8,128)}) custom-call(bf16[704,4096]{1,0:T(8,128)(2,1)} %get-tuple-element.254.hidden_ref.hid_ref, bf16[704,2048]{1,0:T(8,128)(2,1)} %all-gather.11.cloned.1.call-done.down_ref, bf16[8,288,2048]{2,1,0:T(8,128)(2,1)} %bitcast.329, s32[4096,1]{1,0:T(8,128)} %copy.216.slot_ref, ...), custom_call_target="tpu_custom_call" | custom-call | flops 16642998272 | bytes 50331648 | tf_op jit(solution)/shard_map/pallas_call | solution.py:925
  770.2 21.1 %fusion.57 = f32[2304,2048]{1,0:T(8,128)} fusion(bf16[2304,1408]{1,0:T(8,128)(2,1)} %get-tuple-element.212, bf16[2048,1408]{1,0:T(8,128)(2,1)} %all-gather.13.cloned.1.call-done), kind=kOutput, calls=%fused_computation.190 | convolution fusion | flops 13287555072 | bytes 31129600 | tf_op jit(solution)/shard_map/dot_general | solution.py:1188
  791.3 22.0 %add_convert_fusion = bf16[2304,2048]{1,0:T(8,128)(2,1)} fusion(f32[2304,2048]{1,0:T(8,128)} %fusion.57, bf16[2304,1408]{1,0:T(8,128)(2,1)} %get-tuple-element.211, bf16[2048,1408]{1,0:T(8,128)(2,1)} %all-gather.15.cloned.1.call-done), kind=kOutput, calls=%fused_computation.5 | convolution fusion | flops 13296992256 | bytes 40566784 | tf_op jit(solution)/shard_map/dot_general | solution.py:1188
  818.5 94.1 %shard_map.321 = f32[512,2048]{1,0:T(8,128)} custom-call(bf16[704,4096]{1,0:T(8,128)(2,1)} %get-tuple-element.215.dgate_ref, bf16[704,4096]{1,0:T(8,128)(2,1)} %get-tuple-element.214.dup_ref, bf16[704,2048]{1,0:T(8,128)(2,1)} %get-tuple-element.228.gate_ref, bf16[704,2048]{1,0:T(8,128)(2,1)} %get-tuple-element.227.up_ref, bf16[8,288,2048]{2,1,0:T(8,128)(2,1)} %bitcast.328, ...), custom_call_target="tpu_custom_call" | custom-call | flops 28454158336 | bytes 33554432 | tf_op jit(solution)/shard_map/pallas_call | solution.py:1107
  970.2 31.1 %shard_map.322 = bf16[4096,768]{1,0:T(8,128)(2,1)} custom-call(bf16[4096,768]{1,0:T(8,128)(2,1)} %get-tuple-element.58.qkv_ref, bf16[4096,256]{1,0:T(8,128)(2,1)} %bitcast.57.grad_ref, s32[4096,1]{1,0:T(8,128)S(1)} %copy-done.6, s32[4,1,1024]{2,1,0:T(1,128)S(1)} %bitcast.261), custom_call_target="tpu_custom_call" | custom-call | flops 10737418240 | bytes 12582912 | tf_op jit(solution)/shard_map/pallas_call | solution.py:502
  1037.4 22.1 %collective-permute-done.13 = bf16[256,2048]{1,0:T(8,128)(2,1)} collective-permute-done((bf16[256,2048]{1,0:T(8,128)(2,1)}, bf16[256,2048]{1,0:T(8,128)(2,1)}, u32[]{:S(2)}, u32[]{:S(2)}) %collective-permute-start.13) | collective-permute-done | bytes 1048608 | tf_op jit(solution)/shard_map/ppermute | solution.py:1167
  1063.2 20.2 %convolution_convert_fusion = bf16[4096,2048]{1,0:T(8,128)(2,1)} fusion(bf16[4096,768]{1,0:T(8,128)(2,1)} %shard_map.322, bf16[2048,1152]{1,0:T(8,128)(2,1)} %all-gather.7.cloned.1.call-done), kind=kOutput, calls=%fused_computation.6 | convolution fusion | flops 12893290496 | bytes 26214400 | tf_op jit(solution)/shard_map/dot_general | solution.py:1188
  1083.4 75.3 %shard_map.323 = f32[512,2048]{1,0:T(8,128)S(1)} custom-call(bf16[8,512,2048]{2,1,0:T(8,128)(2,1)} %bitcast.269), custom_call_target="tpu_custom_call" | custom-call | bytes 1048576 | tf_op jit(solution)/shard_map/pallas_call | solution.py:769
  (336 shorter events, 408.8 us)
Async XLA Ops:
  7.2 103.8 %all-gather.7.cloned.1.call-start = ((), (), s32[]{:S(2)}) async-start(), calls=%async_computation.13 | async-start | bytes 5898240 | tf_op jit(solution)/shard_map/all_gather | solution.py:1253
  18.7 201.6 %all-gather.9.cloned.1.call-start = ((), (), s32[]{:S(2)}) async-start(), calls=%async_computation.14 | async-start | bytes 7208960 | tf_op jit(solution)/shard_map/all_gather | solution.py:1310
  22.6 330.7 %all-gather.11.cloned.1.call-start = ((), (), s32[]{:S(2)}) async-start(), calls=%async_computation.15 | async-start | bytes 3604480 | tf_op jit(solution)/shard_map/all_gather | solution.py:1312
  24.2 360.6 %all-gather.13.cloned.1.call-start = ((), (), s32[]{:S(2)}) async-start(), calls=%async_computation.16 | async-start | bytes 7208960 | tf_op jit(solution)/shard_map/all_gather | solution.py:1319
  106.0 428.9 %all-gather.15.cloned.1.call-start = ((), (), s32[]{:S(2)}) async-start(), calls=%async_computation.17 | async-start | bytes 7208960 | tf_op jit(solution)/shard_map/all_gather | solution.py:1320
  113.6 54.6 %collective-permute-start.2 = (bf16[4,64,2048]{2,1,0:T(8,128)(2,1)}, bf16[4,64,2048]{2,1,0:T(8,128)(2,1)}, u32[]{:S(2)}, u32[]{:S(2)}) collective-permute-start(bf16[4,64,2048]{2,1,0:T(8,128)(2,1)} %reshape.687), channel_id=1, source_target_pairs={{0,24},{8,16},{16,8},{24,0},{1,25},{9,17},{17,9},{25,1},{2,26},{10... | collective-permute-start | bytes 3145736 | tf_op jit(solution)/shard_map/ppermute | solution.py:1167
  116.0 52.2 %collective-permute-start.1 = (bf16[4,64,2048]{2,1,0:T(8,128)(2,1)}, bf16[4,64,2048]{2,1,0:T(8,128)(2,1)}, u32[]{:S(2)}, u32[]{:S(2)}) collective-permute-start(bf16[4,64,2048]{2,1,0:T(8,128)(2,1)} %reshape.687), channel_id=1, source_target_pairs={{0,16},{8,24},{16,0},{24,8},{1,17},{9,25},{17,1},{25,9},{2,18},{10... | collective-permute-start | bytes 3145736 | tf_op jit(solution)/shard_map/ppermute | solution.py:1167
  116.6 51.7 %collective-permute-start = (bf16[4,64,2048]{2,1,0:T(8,128)(2,1)}, bf16[4,64,2048]{2,1,0:T(8,128)(2,1)}, u32[]{:S(2)}, u32[]{:S(2)}) collective-permute-start(bf16[4,64,2048]{2,1,0:T(8,128)(2,1)} %reshape.687), channel_id=1, source_target_pairs={{0,8},{8,0},{16,24},{24,16},{1,9},{9,1},{17,25},{25,17},{2,10},{10... | collective-permute-start | bytes 3145736 | tf_op jit(solution)/shard_map/ppermute | solution.py:1167
  182.2 415.6 %all-gather.17.cloned.1.call-start = ((), (), s32[]{:S(2)}) async-start(), calls=%async_computation.18 | async-start | bytes 7208960 | tf_op jit(solution)/shard_map/all_gather | solution.py:1321
  294.5 111.2 %collective-permute-start.6 = (bf16[512,2048]{1,0:T(8,128)(2,1)S(1)}, bf16[512,2048]{1,0:T(8,128)(2,1)}, u32[]{:S(2)}, u32[]{:S(2)}) collective-permute-start(bf16[512,2048]{1,0:T(8,128)(2,1)S(1)} %bitcast.264), channel_id=1, source_target_pairs={{0,24},{8,16},{16,8},{24,0},{1,25},{9,17},{17,9},{25,1},{2,26},{10... | collective-permute-start | bytes 6291464 | tf_op jit(solution)/shard_map/ppermute | solution.py:1167
  296.0 109.6 %collective-permute-start.5 = (bf16[512,2048]{1,0:T(8,128)(2,1)S(1)}, bf16[512,2048]{1,0:T(8,128)(2,1)}, u32[]{:S(2)}, u32[]{:S(2)}) collective-permute-start(bf16[512,2048]{1,0:T(8,128)(2,1)S(1)} %bitcast.265), channel_id=1, source_target_pairs={{0,16},{8,24},{16,0},{24,8},{1,17},{9,25},{17,1},{25,9},{2,18},{10... | collective-permute-start | bytes 6291464 | tf_op jit(solution)/shard_map/ppermute | solution.py:1167
  297.3 108.3 %collective-permute-start.4 = (bf16[512,2048]{1,0:T(8,128)(2,1)S(1)}, bf16[512,2048]{1,0:T(8,128)(2,1)}, u32[]{:S(2)}, u32[]{:S(2)}) collective-permute-start(bf16[512,2048]{1,0:T(8,128)(2,1)S(1)} %bitcast.266), channel_id=1, source_target_pairs={{0,8},{8,0},{16,24},{24,16},{1,9},{9,1},{17,25},{25,17},{2,10},{10... | collective-permute-start | bytes 6291464 | tf_op jit(solution)/shard_map/ppermute | solution.py:1167
  412.4 404.0 %reduce-scatter.7.cloned.1.call-start = ((), (), s32[]{:S(2)}) async-start(), calls=%async_computation.19 | async-start | bytes 10813440 | tf_op jit(solution)/shard_map/reduce_scatter | solution.py:1385
  529.6 437.9 %reduce-scatter.9.cloned.1.call-start = ((), (), s32[]{:S(2)}) async-start(), calls=%async_computation.20 | async-start | bytes 7208960 | tf_op jit(solution)/shard_map/reduce_scatter | solution.py:1385
  648.2 435.2 %reduce-scatter.11.cloned.1.call-start = ((), (), s32[]{:S(2)}) async-start(), calls=%async_computation.21 | async-start | bytes 7208960 | tf_op jit(solution)/shard_map/reduce_scatter | solution.py:1385
  757.2 56.1 %all-to-all-start.1 = ((f32[8,2,512]{2,1,0:T(2,128)}), f32[8,2,512]{2,1,0:T(2,128)S(1)}, u32[]{:S(2)}, u32[]{:S(2)}) async-start(f32[8,2,512]{2,1,0:T(2,128)} %gather_fusion.1), calls=%async_computation.2 | async-start | bytes 65536 | tf_op jit(solution)/shard_map/all_to_all | solution.py:1429
  760.7 400.0 %reduce-scatter.17.cloned.1.call-start = ((), (), s32[]{:S(2)}) async-start(), calls=%async_computation.24 | async-start | bytes 7208960 | tf_op jit(solution)/shard_map/reduce_scatter | solution.py:1385
  766.8 48.2 %collective-permute-start.8 = (bf16[512,2048]{1,0:T(8,128)(2,1)}, bf16[512,2048]{1,0:T(8,128)(2,1)S(1)}, u32[]{:S(2)}, u32[]{:S(2)}) collective-permute-start(bf16[512,2048]{1,0:T(8,128)(2,1)} %get-tuple-element.222), channel_id=1, source_target_pairs={{0,8},{8,0},{16,24},{24,16},{1,9},{9,1},{17,25},{25,17},{2,10},{10... | collective-permute-start | bytes 6291464 | tf_op jit(solution)/shard_map/ppermute | solution.py:1167
  943.0 231.8 %reduce-scatter.13.cloned.1.call-start = ((), (), s32[]{:S(2)}) async-start(), calls=%async_computation.22 | async-start | bytes 3932160 | tf_op jit(solution)/shard_map/reduce_scatter | solution.py:1474
  949.8 133.5 %collective-permute-start.14 = (bf16[512,2048]{1,0:T(8,128)(2,1)}, bf16[512,2048]{1,0:T(8,128)(2,1)}, u32[]{:S(2)}, u32[]{:S(2)}) collective-permute-start(bf16[512,2048]{1,0:T(8,128)(2,1)} %get-tuple-element.85), channel_id=1, source_target_pairs={{0,24},{8,16},{16,8},{24,0},{1,25},{9,17},{17,9},{25,1},{2,26},{10... | collective-permute-start | bytes 6291464 | tf_op jit(solution)/shard_map/ppermute | solution.py:1167
  964.1 72.6 %collective-permute-start.11 = (bf16[256,2048]{1,0:T(8,128)(2,1)}, bf16[256,2048]{1,0:T(8,128)(2,1)}, u32[]{:S(2)}, u32[]{:S(2)}) collective-permute-start(bf16[256,2048]{1,0:T(8,128)(2,1)} %get-tuple-element.218), channel_id=1, source_target_pairs={{0,8},{8,0},{16,24},{24,16},{1,9},{9,1},{17,25},{25,17},{2,10},{10... | collective-permute-start | bytes 3145736 | tf_op jit(solution)/shard_map/ppermute | solution.py:1167
  964.6 72.8 %collective-permute-start.12 = (bf16[256,2048]{1,0:T(8,128)(2,1)}, bf16[256,2048]{1,0:T(8,128)(2,1)}, u32[]{:S(2)}, u32[]{:S(2)}) collective-permute-start(bf16[256,2048]{1,0:T(8,128)(2,1)} %get-tuple-element.217), channel_id=1, source_target_pairs={{0,16},{8,24},{16,0},{24,8},{1,17},{9,25},{17,1},{25,9},{2,18},{10... | collective-permute-start | bytes 3145736 | tf_op jit(solution)/shard_map/ppermute | solution.py:1167
  965.1 94.5 %collective-permute-start.13 = (bf16[256,2048]{1,0:T(8,128)(2,1)}, bf16[256,2048]{1,0:T(8,128)(2,1)}, u32[]{:S(2)}, u32[]{:S(2)}) collective-permute-start(bf16[256,2048]{1,0:T(8,128)(2,1)} %get-tuple-element.216), channel_id=1, source_target_pairs={{0,24},{8,16},{16,8},{24,0},{1,25},{9,17},{17,9},{25,1},{2,26},{10... | collective-permute-start | bytes 3145736 | tf_op jit(solution)/shard_map/ppermute | solution.py:1167
  1180.1 49.1 %reduce-scatter.15.cloned.1.call-start = ((), (), s32[]{:S(2)}) async-start(), calls=%async_computation.23 | async-start | bytes 1310720 | tf_op jit(solution)/shard_map/reduce_scatter | solution.py:1385
  (69 other events, 1806.2 us)
Sparse Core Ops, SparseCore 0:
  18.8 92.0 all-gather.6
  113.1 105.1 all-gather.8
  220.5 57.4 all-gather.10
  279.4 105.3 all-gather.12
  386.2 104.9 all-gather.14
  492.7 105.0 all-gather.16
  600.1 146.8 reduce-scatter.6
  749.3 103.0 reduce-scatter.8
  854.7 102.7 reduce-scatter.10
  959.7 102.7 reduce-scatter.16
  1064.8 60.7 reduce-scatter.12
  1182.9 25.9 reduce-scatter.14

commit v9 on v8

--- a/solution.py
+++ b/solution.py
@@ -642,158 +642,6 @@
     )(*operands)
 
 
-def plane_scatter_kernel(relative, with_extra, *refs):
-    if with_extra:
-        part_ref, extra_ref, out_ref, *refs = refs
-        extra_out, refs = refs[:4], refs[4:]
-        extra_own, extra_got, extra_sems, refs = refs[0], refs[1], refs[2:5], refs[5:]
-    else:
-        part_ref, out_ref, *refs = refs
-    own, twin_got, x_got, y_got, x_last, y_last, send_sem, recv_sem, local_sem = refs
-    at, core, across, along, far = plane_places()
-    rows = part_ref.shape[1]
-    half = rows // 2
-    step = 64
-    greet(across, along, core)
-    started = []
-
-    def send(number, src, dst, target):
-        copy = pltpu.make_async_remote_copy(
-            src_ref=src,
-            dst_ref=dst,
-            send_sem=send_sem.at[number],
-            recv_sem=recv_sem.at[number],
-            device_id=target,
-            device_id_type=MESH_ID,
-        )
-        copy.start()
-        started.append(copy)
-        return copy
-
-    twins, heres = [], []
-    for j, (label, shift) in enumerate(((far, 3), (across, 1), (along, 2), (at, 0))):
-        theirs = shift + 4 if relative else label * 2 + 1 - core
-        ours = shift if relative else label * 2 + core
-        twins.append(send(j, part_ref.at[theirs], twin_got.at[j], {CTX: 1 - core}))
-        here = pltpu.make_async_copy(part_ref.at[ours], own.at[j], local_sem.at[j])
-        here.start()
-        heres.append(here)
-
-    def add_rows(target, t_first, count, source, s_first):
-        @pl.loop(0, count // step)
-        def _(i):
-            into = pl.ds(pl.multiple_of(t_first + i * step, step), step)
-            take = pl.ds(pl.multiple_of(s_first + i * step, step), step)
-            total = target[into].astype(jnp.float32) + source[take].astype(jnp.float32)
-            target[into] = total.astype(target.dtype)
-
-    top, bottom = pl.ds(0, half), pl.ds(half, half)
-    x_sent, y_sent = [], []
-    for j in range(4):
-        twins[j].wait_recv()
-        heres[j].wait()
-        add_rows(own.at[j], 0, rows, twin_got.at[j], 0)
-        if j < 2:
-            x_sent.append(send(4 + j, own.at[j, top], x_got.at[j], {EXP: across}))
-        if j == 0 or j == 2:
-            y_sent.append(send(6 + j // 2, own.at[j, bottom], y_got.at[j // 2], {EXP: along}))
-    if with_extra:
-        extra_here, extra_twin, extra_done = [], [], []
-        for k in range(4):
-            copy = pltpu.make_async_remote_copy(
-                src_ref=extra_ref.at[k + 4],
-                dst_ref=extra_got.at[k],
-                send_sem=extra_sems[0].at[k],
-                recv_sem=extra_sems[1].at[k],
-                device_id={CTX: 1 - core},
-                device_id_type=MESH_ID,
-            )
-            copy.start()
-            started.append(copy)
-            extra_twin.append(copy)
-            here = pltpu.make_async_copy(extra_ref.at[k], extra_own.at[k], extra_sems[2].at[k])
-            here.start()
-            extra_here.append(here)
-        for k in range(4):
-            extra_twin[k].wait_recv()
-            extra_here[k].wait()
-            add_rows(extra_own.at[k], 0, rows, extra_got.at[k], 0)
-            here = pltpu.make_async_copy(extra_own.at[k], extra_out[k], extra_sems[2].at[k])
-            here.start()
-            extra_done.append(here)
-    x_sent[0].wait_recv()
-    add_rows(own.at[2], 0, half, x_got.at[0], 0)
-    last_y = send(8, own.at[2, top], y_last, {EXP: along})
-    y_sent[0].wait_recv()
-    add_rows(own.at[1], half, half, y_got.at[0], 0)
-    last_x = send(9, own.at[1, bottom], x_last, {EXP: across})
-
-    def finish(first, near, later):
-        @pl.loop(0, half // step)
-        def _(i):
-            take = pl.ds(pl.multiple_of(i * step, step), step)
-            into = pl.ds(pl.multiple_of(first + i * step, step), step)
-            out_ref[into] = (
-                own[3, into].astype(jnp.float32)
-                + near[1, take].astype(jnp.float32)
-                + later[take].astype(jnp.float32)
-            ).astype(out_ref.dtype)
-
-    x_sent[1].wait_recv()
-    last_y.wait_recv()
-    finish(0, x_got, y_last)
-    y_sent[1].wait_recv()
-    last_x.wait_recv()
-    finish(half, y_got, x_last)
-    if with_extra:
-        for copy in extra_done:
-            copy.wait()
-    for copy in started:
-        copy.wait_send()
-
-
-def plane_scatter(parts, relative, number, out_type, extra=None):
-    plane, rows, cols = parts.shape
-    operands, extra_scratch = [parts], []
-    out_shape = [jax.ShapeDtypeStruct((rows, cols), out_type)]
-    out_specs = [pl.BlockSpec(memory_space=pltpu.VMEM)]
-    anywhere = pl.BlockSpec(memory_space=pl.ANY)
-    if extra is not None:
-        operands.append(extra)
-        out_shape += [jax.ShapeDtypeStruct((rows, cols), extra.dtype)] * 4
-        out_specs += [anywhere] * 4
-        extra_scratch = [pltpu.VMEM((4, rows, cols), extra.dtype)] * 2
-        extra_scratch += [pltpu.SemaphoreType.DMA((4,))] * 3
-    half = rows // 2
-    vmem = lambda *shape: pltpu.VMEM(shape, parts.dtype)
-    return pl.pallas_call(
-        partial(plane_scatter_kernel, relative, extra is not None),
-        out_shape=out_shape,
-        in_specs=[anywhere] * len(operands),
-        out_specs=out_specs,
-        scratch_shapes=extra_scratch
-        + [
-            vmem(4, rows, cols),
-            vmem(4, rows, cols),
-            vmem(2, half, cols),
-            vmem(2, half, cols),
-            vmem(half, cols),
-            vmem(half, cols),
-            pltpu.SemaphoreType.DMA((10,)),
-            pltpu.SemaphoreType.DMA((10,)),
-            pltpu.SemaphoreType.DMA((4,)),
-        ],
-        compiler_params=pltpu.CompilerParams(
-            collective_id=number,
-            has_side_effects=True,
-            vmem_limit_bytes=(36 if extra is None else 54) * 2**20,
-        ),
-        cost_estimate=pl.CostEstimate(
-            flops=0, bytes_accessed=rows * cols, transcendentals=0
-        ),
-    )(*operands)
-
-
 def norm_qkv_kernel(hidden_ref, gain_ref, w_ref, norm_ref, qkv_ref):
     values = hidden_ref[...].astype(jnp.float32)
     inv = lax.rsqrt(jnp.mean(values * values, axis=1, keepdims=True) + EPS)
@@ -834,6 +682,22 @@
     return (slots == lanes).astype(jnp.bfloat16)
 
 
+def hand_out(step_at, half, blocks, out_refs, sems):
+    copies = [
+        pltpu.make_async_copy(blocks.at[k], out_refs[k], sems.at[k]) for k in range(half)
+    ]
+    for k in range(half):
+
+        @pl.when(step_at == half + k)
+        def _():
+            copies[k].start()
+
+    @pl.when(step_at == 2 * half - 1)
+    def _():
+        for copy in copies:
+            copy.wait()
+
+
 def output_kernel(
     half,
     hidden_ref,
@@ -843,13 +707,10 @@
     sg_ref,
     gate_ref,
     cot_ref,
-    near_ref,
-    dots_ref,
-    given,
-    got,
-    send_sem,
-    recv_sem,
+    *refs,
 ):
+    near_refs, dots_ref, refs = refs[:half], refs[half], refs[half + 1 :]
+    given, got, send_sem, recv_sem, out_sem = refs
     step_at = pl.program_id(0)
     is_far = step_at < half
     slot = lax.rem(step_at, half)
@@ -906,9 +767,11 @@
         block_copy(slot).wait_recv()
 
         def store(cols, total):
-            near_ref[0, :, cols] = low(total + got[slot, :, cols].astype(jnp.float32))
+            got[slot, :, cols] = low(total + got[slot, :, cols].astype(jnp.float32))
 
         make(store)
+
+    hand_out(step_at, half, got, near_refs, out_sem)
 
     @pl.when(step_at == 2 * half - 1)
     def _():
@@ -935,16 +798,17 @@
             pl.BlockSpec((tokens, width), lambda i: (at(i), 0)),
         ],
         out_specs=[
-            pl.BlockSpec((1, tokens, width), lambda i: (jnp.maximum(i - half, 0), 0, 0)),
+            *[pl.BlockSpec(memory_space=pl.ANY)] * half,
             pl.BlockSpec((tokens, 128), lambda i: (at(i), 0)),
         ],
         out_shape=[
-            jax.ShapeDtypeStruct((half, tokens, width), jnp.bfloat16),
+            *[jax.ShapeDtypeStruct((tokens, width), jnp.bfloat16)] * half,
             jax.ShapeDtypeStruct((count, 128), jnp.float32),
         ],
         scratch_shapes=[
             pltpu.VMEM((half, tokens, width), jnp.bfloat16),
             pltpu.VMEM((half, tokens, width), jnp.bfloat16),
+            pltpu.SemaphoreType.DMA((half,)),
             pltpu.SemaphoreType.DMA((half,)),
             pltpu.SemaphoreType.DMA((half,)),
         ],
@@ -1157,6 +1021,115 @@
             transcendentals=0,
         ),
     )(hidden, dgate, dup, cots, n2)
+
+
+def n1_grad_kernel(half, grads_ref, w_ref, *refs):
+    near_refs, refs = refs[:half], refs[half:]
+    rows_in, given, got, load_sem, send_sem, recv_sem, out_sem = refs
+    place, core = lax.axis_index(EXP), lax.axis_index(CTX)
+    step_at = pl.program_id(0)
+    is_far = step_at < half
+    slot = lax.rem(step_at, half)
+    tokens = rows_in.shape[1]
+    twin_id = {CTX: 1 - core}
+
+    def load(step, k):
+        column, level = place % 2, place // 2
+        there = (column + k % 2) % 2 + 2 * ((level + k // 2) % 2)
+        owner = 1 - core if step < half else core
+        first = pl.multiple_of((there * 2 + owner) * tokens, tokens)
+        return pltpu.make_async_copy(
+            grads_ref.at[pl.ds(first, tokens)], rows_in.at[step], load_sem.at[step]
+        )
+
+    loads = [load(step, step % half) for step in range(2 * half)]
+
+    @pl.when(step_at == 0)
+    def _():
+        for copy in loads:
+            copy.start()
+        barrier = pltpu.get_barrier_semaphore()
+        pl.semaphore_signal(barrier, inc=1, device_id=twin_id, device_id_type=MESH_ID)
+        pl.semaphore_wait(barrier, 1)
+
+    for step in range(2 * half):
+
+        @pl.when(step_at == step)
+        def _():
+            loads[step].wait()
+
+    def block_copy(k):
+        return pltpu.make_async_remote_copy(
+            src_ref=given.at[k],
+            dst_ref=got.at[k],
+            send_sem=send_sem.at[k],
+            recv_sem=recv_sem.at[k],
+            device_id=twin_id,
+            device_id_type=MESH_ID,
+        )
+
+    def make(store):
+        step = 512
+        for first in range(0, w_ref.shape[0], step):
+            cols = pl.ds(first, step)
+            store(cols, mm(rows_in[step_at], w_ref[cols, :], ((1,), (1,))))
+
+    @pl.when(is_far)
+    def _():
+        def store(cols, total):
+            given[slot, :, cols] = low(total)
+
+        make(store)
+        block_copy(slot).start()
+
+    @pl.when(jnp.logical_not(is_far))
+    def _():
+        block_copy(slot).wait_recv()
+
+        def store(cols, total):
+            got[slot, :, cols] = low(total + got[slot, :, cols].astype(jnp.float32))
+
+        make(store)
+
+    hand_out(step_at, half, got, near_refs, out_sem)
+
+    @pl.when(step_at == 2 * half - 1)
+    def _():
+        for k in range(half):
+            block_copy(k).wait_send()
+
+
+def n1_grad_parts(grads, w, blocks):
+    rows, cols = grads.shape
+    width = w.shape[0]
+    tokens, half = rows // blocks, blocks // 2
+    return pl.pallas_call(
+        partial(n1_grad_kernel, half),
+        grid=(blocks,),
+        in_specs=[
+            pl.BlockSpec(memory_space=pl.ANY),
+            pl.BlockSpec((width, cols), lambda i: (0, 0)),
+        ],
+        out_specs=[pl.BlockSpec(memory_space=pl.ANY)] * half,
+        out_shape=[jax.ShapeDtypeStruct((tokens, width), jnp.bfloat16)] * half,
+        scratch_shapes=[
+            pltpu.VMEM((blocks, tokens, cols), jnp.bfloat16),
+            pltpu.VMEM((half, tokens, width), jnp.bfloat16),
+            pltpu.VMEM((half, tokens, width), jnp.bfloat16),
+            pltpu.SemaphoreType.DMA((blocks,)),
+            pltpu.SemaphoreType.DMA((half,)),
+            pltpu.SemaphoreType.DMA((half,)),
+            pltpu.SemaphoreType.DMA((half,)),
+        ],
+        compiler_params=pltpu.CompilerParams(
+            collective_id=1, has_side_effects=True, vmem_limit_bytes=48 * 2**20
+        ),
+        cost_estimate=pl.CostEstimate(
+            flops=2 * rows * width * cols,
+            bytes_accessed=4 * rows * width,
+            transcendentals=0,
+        ),
+    )(grads, w)
 
 
 def after(values, others):
@@ -1375,12 +1348,12 @@
     rows_out = width // (halves * depth)
 
     def shared_scatter(total):
-        first, second = total[:, :rows_out], total[:, rows_out:]
+        first, second = total[:, :, :rows_out], total[:, :, rows_out:]
         keep = jnp.where(core == 0, first, second)
         got = twin(jnp.where(core == 0, second, first))
-        both = jnp.where(core == 0, jnp.stack([keep, got]), jnp.stack([got, keep]))
-        both = both.reshape(halves, depth, part, rows_out).transpose(1, 0, 2, 3)
-        return both.reshape(units, rows_out).astype(jnp.float32)
+        both = [v.reshape(3, depth, part, rows_out) for v in (keep, got)]
+        both = jnp.where(core == 0, jnp.stack(both, axis=2), jnp.stack(both[::-1], axis=2))
+        return both.reshape(3, units, rows_out).astype(jnp.float32)
 
     scatter = lambda v, dim: lax.psum_scatter(v, DP, scatter_dimension=dim, tiled=True)
     shared_sums = unit_grads(
@@ -1398,7 +1371,7 @@
     grads_made = (grad_ex_down, grad_ex_gate, grad_ex_up)
     grads = [scatter(v, dim) for v, dim in zip(grads_made, (1, 0, 0))]
     slots = slots.reshape(all_tokens, 1)
-    out_near, dots = output_parts(
+    *out_near, dots = output_parts(
         shared_hidden,
         sh_down,
         result_e.reshape(plane, capacity, width),
@@ -1463,14 +1436,13 @@
         .transpose(1, 0, 2, 3)
         .reshape(width, 3 * head_cols)
     )
-    qkv_grad, grad_out, _ = lax.optimization_barrier((qkv_grad, hops(out_grad_sums), grad_qkv))
-    grad_out = low(sum_up(grad_out))
-    n1_grad = low(mm(qkv_grad, w_qkv, ((1,), (1,))))
-    n1_grad, out_far, _ = lax.optimization_barrier(
-        (n1_grad, out_far, (grad_qkv, grad_out, grads[1]))
-    )
+    out_grad_got = hops(out_grad_sums)
+    qkv_grad = after(qkv_grad, (grad_qkv, grads[1]))
+    n1_near = n1_grad_parts(qkv_grad, w_qkv, plane)
+    n1_near, out_far, out_grad_got = lax.optimization_barrier((n1_near, out_far, out_grad_got))
     output = low(output + out_far.astype(jnp.float32))
-    n1_grad = plane_scatter(n1_grad.reshape(plane, tokens, width), False, 1, jnp.float32)[0]
+    grad_out = low(sum_up(out_grad_got))
+    n1_got = hops(n1_near)
     grad_qkv = lax.psum_scatter(grad_qkv, DP, scatter_dimension=0, tiled=True)
     qkv_sum = grad_qkv
     w_rows = (
@@ -1501,17 +1473,15 @@
         .astype(jnp.float32)
     )
     grad_ex_down, grad_ex_gate, grad_ex_up = [
-        v.astype(jnp.float32)[None] for v in after(grads, n1_grad)
+        v.astype(jnp.float32)[None] for v in after(grads, n1_near)
     ]
-    grad_out = scatter(after(grad_out, (n1_grad, qkv_sum)), 0).astype(jnp.float32)
-    shared_sums = after(shared_sums, (n1_grad, qkv_sum))
-    grad_sh_down, grad_sh_gate, grad_sh_up = [
-        shared_scatter(v)
-        for v in shared_sums.reshape(3, units // halves, -1)
-    ]
+    grad_out = scatter(after(grad_out, qkv_sum), 0).astype(jnp.float32)
+    shared_sums = after(shared_sums, n1_near)
+    shared_sums = shared_scatter(shared_sums.reshape(3, units // halves, -1))
+    grad_sh_down, grad_sh_gate, grad_sh_up = [shared_sums[k] for k in range(3)]
     grad_sh_gate, grad_sh_up = grad_sh_gate.T, grad_sh_up.T
     dz_all = jnp.concatenate([logit_grad, sg_logit_grad], axis=1)
-    dz_all = after(dz_all, (n1_grad, qkv_sum))
+    dz_all = after(dz_all, n1_near)
     small_grads = mm(n2, dz_all, ((0,), (0,)))
     small_grads = jnp.concatenate([small_grads, grad_gain_two[:, None]], axis=1).T
     small_grads = jnp.pad(small_grads, ((0, 14 - experts_all), (0, 0)))
@@ -1523,6 +1493,7 @@
     small_grads = jnp.sum(
         lax.all_to_all(small_grads, DP, split_axis=0, concat_axis=0, tiled=True), axis=0
     )
+    n1_grad = sum_up(after(n1_got, qkv_sum))
     input_part, _ = norm_back(x_rows, inv_one, g_one, n1_grad)
     input_grad = low(residual_grad + input_part)
     return (

time: 1250 us -> 1240 us (level)
  Pallas kernels: 476 us -> 424 us
  waiting for transfers between devices: 117 us -> 160 us
  other arithmetic: 105 us -> 121 us
  matrix products: 362 us -> 348 us
    all_to_all x1, waiting for transfers between devices: 2.55 us -> 67.6 us  [local_plane(): lax.all_to_all(small_grads, PLANE, split_axis=0, concat_axis=0, tiled=True)]
    pallas_call x1, Pallas kernels: 75.3 us -> 20.2 us  [n1_grad_parts(): pl.pallas_call(partial(n1_grad_kernel, half), grid=(blocks,), in_specs=[p...]
    ppermute x12 -> x15, waiting for transfers between devices: 40.4 us -> 23.7 us  [swap(): return lax.ppermute(values, EXP, [(i, i ^ bits) for i in range(4)])]
    dot_general x21 -> x20, matrix products: 336 us -> 321 us  [mm(): lax.dot_general(left, right, (dims, ((), ())), preferred_element_type=jnp...]
    unnamed x129 -> x95, local copies, waits for them, and re-layouts: 36 us -> 36.7 us
  transfers between devices with their start and end apart: 37 -> 38, of which waited for: 14 -> 10; matrix products, arithmetic and copies ran while one was open for 45% -> 45% of each run, Pallas kernels for 38% -> 34%
where the time goes in v9:
time: 1240 us; the launch traced here: 1230 us
  Pallas kernels  424 us (34%)
  matrix products  348 us (28%)
  waiting for transfers between devices  160 us (13%)
  other arithmetic  121 us (10%)
  local copies, waits for them, and re-layouts  115 us (9%)
  starting transfers between devices  47.6 us (4%)
  between operations  15.4 us (1%)
    dot_general x20, matrix products, mm(): lax.dot_general(left, right, (dims, ((), ())), preferred_element_type=jnp...  321 us
    pallas_call x2, Pallas kernels, plane_gather(): pl.pallas_call(partial(plane_gather_kernel, info is not None, relative),...  155 us
    pallas_call x1, Pallas kernels, n2_grad_sum(): pl.pallas_call(n2_grad_kernel, grid=(blocks,), in_specs=[by_units, by_uni...  95.4 us
    all_to_all x1, waiting for transfers between devices, local_plane(): lax.all_to_all(small_grads, PLANE, split_axis=0, concat_axis=0, tiled=True)  67.6 us
    pallas_call x2, Pallas kernels, attention_call(): pl.pallas_call(partial(body, heads, step), grid=(rows // seq_len,), in_sp...  50.6 us
    pallas_call x1, Pallas kernels, unit_grads(): pl.pallas_call(unit_grad_kernel, grid=(depth * halves,), in_specs=[whole,...  44 us
    convert_element_type x7, other arithmetic, low(): return values.astype(jnp.bfloat16)  43.7 us
    unnamed x95, local copies, waits for them, and re-layouts  36.7 us
  transfers between devices with their start and end apart: 38, of which 10 were waited for; matrix products, arithmetic and copies ran while one was open for 45% of the time, Pallas kernels for 34%

profile of v9, /device:TPU:0, one launch (start us, length us, event | category | flops | bytes accessed | tf_op | source)
XLA Modules:
  0.0 1231.4 jit_solution(1851375707135680955)
XLA Ops:
  26.6 81.1 %shard_map.315 = (bf16[8,512,2048]{2,1,0:T(8,128)(2,1)}, s32[8,8,512]{2,1,0:T(8,128)}) custom-call(bf16[512,2048]{1,0:T(8,128)(2,1)} %bitcast.243, s32[8,512]{1,0:T(8,128)} %concatenate.50.refs_1_), custom_call_target="tpu_custom_call" | custom-call | bytes 1048576 | tf_op jit(solution)/shard_map/pallas_call | solution.py:628
  125.5 22.3 %shard_map.316 = (bf16[4096,2048]{1,0:T(8,128)(2,1)}, bf16[4096,768]{1,0:T(8,128)(2,1)}) custom-call(bf16[4096,2048]{1,0:T(8,128)(2,1)} %bitcast.299, f32[1,2048]{1,0:T(1,128)S(1)} %copy.192.gain_ref, bf16[2048,768]{1,0:T(8,128)(2,1)S(1)} %slice.152.w_ref), custom_call_target="tpu_custom_call" | custom-call | flops 12884901888 | bytes 33554432 | tf_op jit(solution)/shard_map/pallas_call | solution.py:655
  147.8 19.4 %shard_map.317 = bf16[4096,256]{1,0:T(8,128)(2,1)S(1)} custom-call(bf16[4096,768]{1,0:T(8,128)(2,1)} %get-tuple-element.72.qkv_ref, s32[4096,1]{1,0:T(8,128)S(1)} %copy.193.q_code_ref, s32[4,1,1024]{2,1,0:T(1,128)S(1)} %bitcast.240), custom_call_target="tpu_custom_call" | custom-call | flops 4294967296 | bytes 8388608 | tf_op jit(solution)/shard_map/pallas_call | solution.py:502
  232.3 74.2 %shard_map.318 = bf16[8,512,2048]{2,1,0:T(8,128)(2,1)} custom-call(bf16[512,2048]{1,0:T(8,128)(2,1)} %multiply_convert_fusion.7.refs_0_), custom_call_target="tpu_custom_call" | custom-call | bytes 1048576 | tf_op jit(solution)/shard_map/pallas_call | solution.py:628
  323.3 19.2 %fusion.11 = f32[704,4096]{1,0:T(8,128)} fusion(bf16[4096,2048]{1,0:T(8,128)(2,1)} %bitcast.249, bf16[2048,1408]{0,1:T(8,128)(2,1)} %all-gather.9.cloned.1.call-done), kind=kOutput, calls=%fused_computation.54 | convolution fusion | flops 11811160064 | bytes 31195136 | tf_op jit(solution)/shard_map/dot_general | solution.py:1161
  342.5 22.5 %multiply_convert_fusion.6 = (bf16[704,4096]{1,0:T(8,128)(2,1)}, f32[704,4096]{1,0:T(8,128)}) fusion(f32[704,4096]{1,0:T(8,128)} %fusion.11, bf16[4096,2048]{1,0:T(8,128)(2,1)} %bitcast.250, bf16[2048,1408]{0,1:T(8,128)(2,1)} %all-gather.9.cloned.1.call-done), kind=kOutput, calls=%fused_computation.13 | convolution fusion | flops 11828461568 | bytes 48496640 | tf_op jit(solution)/shard_map/dot_general | solution.py:1161
  365.0 21.4 %all-gather.13.cloned.1.call-done = bf16[2048,1408]{1,0:T(8,128)(2,1)} async-done(((bf16[512,1408]{1,0:T(8,128)(2,1)}), bf16[2048,1408]{1,0:T(8,128)(2,1)}) %all-gather.13.cloned.1.call-update) | async-done | bytes 5767184 | tf_op jit(solution)/shard_map/all_gather | solution.py:1292
  386.5 21.0 %fusion.52 = f32[2304,1408]{1,0:T(8,128)} fusion(bf16[2304,2048]{1,0:T(8,128)(2,1)} %bitcast.300, bf16[2048,1408]{1,0:T(8,128)(2,1)} %all-gather.13.cloned.1.call-done), kind=kOutput, calls=%fused_computation.176 | convolution fusion | flops 13287555072 | bytes 28180480 | tf_op jit(solution)/shard_map/dot_general | solution.py:1161
  461.4 25.1 %multiply_convert_fusion.4 = (bf16[704,4096]{1,0:T(8,128)(2,1)}, bf16[704,4096]{1,0:T(8,128)(2,1)}) fusion(f32[704,4096]{1,0:T(8,128)} %fusion.11, f32[704,4096]{1,0:T(8,128)} %get-tuple-element.279, bf16[704,2048]{1,0:T(8,128)(2,1)} %all-gather.11.cloned.1.call-done.down_ref, bf16[4096,2048]{1,0:T(8,128)(2,1)} %multiply_convert_fusion.cot_ref), kind=kOutput, calls=%fused_computation.11 | convolution fusion | flops 11848646656 | bytes 54263808 | tf_op jit(solution)/shard_map/dot_general | solution.py:1161
  489.2 44.0 %shard_map.320 = bf16[4,2112,512]{2,1,0:T(8,128)(2,1)} custom-call(bf16[704,4096]{1,0:T(8,128)(2,1)S(1)} %copy-done.5, bf16[704,4096]{1,0:T(8,128)(2,1)} %get-tuple-element.243.dgate_ref, bf16[704,4096]{1,0:T(8,128)(2,1)} %get-tuple-element.242.dup_ref, bf16[4096,2048]{1,0:T(8,128)(2,1)} %multiply_convert_fusion.cot_ref, bf16[4096,2048]{1,0:T(8,128)(2,1)} %bitcast.252), custom_call_target="tpu_custom_call" | custom-call | flops 35433480192 | bytes 59506688 | tf_op jit(solution)/shard_map/pallas_call | solution.py:1009
  541.5 20.8 %fusion.53 = f32[2304,1408]{1,0:T(8,128)} fusion(bf16[2304,2048]{1,0:T(8,128)(2,1)} %bitcast.301, bf16[2048,1408]{1,0:T(8,128)(2,1)} %all-gather.15.cloned.1.call-done), kind=kOutput, calls=%fused_computation.177 | convolution fusion | flops 13287555072 | bytes 28180480 | tf_op jit(solution)/shard_map/dot_general | solution.py:1161
  599.4 30.4 %multiply_convert_fusion.1 = (bf16[2304,1408]{1,0:T(8,128)(2,1)}, bf16[2304,1408]{1,0:T(8,128)(2,1)}, bf16[2304,1408]{1,0:T(8,128)(2,1)}) fusion(f32[2304,1408]{1,0:T(8,128)} %fusion.52, f32[2304,1408]{1,0:T(8,128)} %fusion.53, bf16[2304,2048]{1,0:T(8,128)(2,1)} %fusion, bf16[1408,2048]{1,0:T(8,128)(2,1)} %all-gather.17.cloned.1.call-done), kind=kOutput, calls=%fused_computation.6 | convolution fusion | flops 13336215552 | bytes 60620800 | tf_op jit(solution)/shard_map/dot_general | solution.py:1161
  629.8 19.8 %convolution_convert_fusion.4 = bf16[1408,2048]{1,0:T(8,128)(2,1)} fusion(bf16[2304,1408]{1,0:T(8,128)(2,1)} %get-tuple-element.241, bf16[2304,2048]{1,0:T(8,128)(2,1)} %fusion), kind=kOutput, calls=%fused_computation.23 | convolution fusion | flops 13290438656 | bytes 21692416 | tf_op jit(solution)/shard_map/dot_general | solution.py:1161
  649.7 20.6 %convolution_convert_fusion.3 = bf16[2048,1408]{1,0:T(8,128)(2,1)} fusion(bf16[2304,2048]{1,0:T(8,128)(2,1)} %bitcast.302, bf16[2304,1408]{1,0:T(8,128)(2,1)} %get-tuple-element.240), kind=kOutput, calls=%fused_computation.22 | convolution fusion | flops 13290438656 | bytes 21692416 | tf_op jit(solution)/shard_map/dot_general | solution.py:1161
  677.5 20.6 %convolution_convert_fusion.2 = bf16[2048,1408]{1,0:T(8,128)(2,1)} fusion(bf16[2304,2048]{1,0:T(8,128)(2,1)} %bitcast.303, bf16[2304,1408]{1,0:T(8,128)(2,1)} %get-tuple-element.239), kind=kOutput, calls=%fused_computation.21 | convolution fusion | flops 13290438656 | bytes 21692416 | tf_op jit(solution)/shard_map/dot_general | solution.py:1161
  700.1 20.0 %convolution_convert_fusion = bf16[2304,2048]{1,0:T(8,128)(2,1)} fusion(bf16[2304,1408]{1,0:T(8,128)(2,1)} %get-tuple-element.241, bf16[1408,2048]{1,0:T(8,128)(2,1)} %all-gather.17.cloned.1.call-done), kind=kOutput, calls=%fused_computation.16 | convolution fusion | flops 13292273664 | bytes 21692416 | tf_op jit(solution)/shard_map/dot_general | solution.py:1161
  720.1 35.9 %shard_map.319 = (bf16[512,2048]{1,0:T(8,128)(2,1)}, bf16[512,2048]{1,0:T(8,128)(2,1)}, bf16[512,2048]{1,0:T(8,128)(2,1)}, bf16[512,2048]{1,0:T(8,128)(2,1)}, f32[4096,128]{1,0:T(8,128)}) custom-call(bf16[704,4096]{1,0:T(8,128)(2,1)} %get-tuple-element.278.hidden_ref.hid_ref, bf16[704,2048]{1,0:T(8,128)(2,1)} %all-gather.11.cloned.1.call-done.down_ref, ...), custom_call_target="tpu_custom_call" | custom-call | flops 16642998272 | bytes 50331648 | tf_op jit(solution)/shard_map/pallas_call | solution.py:788
  766.3 21.0 %fusion.54 = f32[2304,2048]{1,0:T(8,128)} fusion(bf16[2304,1408]{1,0:T(8,128)(2,1)} %get-tuple-element.240, bf16[2048,1408]{1,0:T(8,128)(2,1)} %all-gather.13.cloned.1.call-done), kind=kOutput, calls=%fused_computation.178 | convolution fusion | flops 13287555072 | bytes 31129600 | tf_op jit(solution)/shard_map/dot_general | solution.py:1161
  787.2 21.9 %add_convert_fusion = bf16[2304,2048]{1,0:T(8,128)(2,1)} fusion(f32[2304,2048]{1,0:T(8,128)} %fusion.54, bf16[2304,1408]{1,0:T(8,128)(2,1)} %get-tuple-element.239, bf16[2048,1408]{1,0:T(8,128)(2,1)} %all-gather.15.cloned.1.call-done), kind=kOutput, calls=%fused_computation.5 | convolution fusion | flops 13296992256 | bytes 40566784 | tf_op jit(solution)/shard_map/dot_general | solution.py:1161
  811.3 95.4 %shard_map.321 = f32[512,2048]{1,0:T(8,128)} custom-call(bf16[704,4096]{1,0:T(8,128)(2,1)} %get-tuple-element.243.dgate_ref, bf16[704,4096]{1,0:T(8,128)(2,1)} %get-tuple-element.242.dup_ref, bf16[704,2048]{1,0:T(8,128)(2,1)} %get-tuple-element.253.gate_ref, bf16[704,2048]{1,0:T(8,128)(2,1)} %get-tuple-element.252.up_ref, bf16[8,288,2048]{2,1,0:T(8,128)(2,1)} %bitcast.304, ...), custom_call_target="tpu_custom_call" | custom-call | flops 28454158336 | bytes 33554432 | tf_op jit(solution)/shard_map/pallas_call | solution.py:971
  966.9 31.2 %shard_map.322.grads_ref = bf16[4096,768]{1,0:T(8,128)(2,1)} custom-call(bf16[4096,768]{1,0:T(8,128)(2,1)} %get-tuple-element.72.qkv_ref, bf16[4096,256]{1,0:T(8,128)(2,1)} %bitcast.54.grad_ref, s32[4096,1]{1,0:T(8,128)S(1)} %copy.193.q_code_ref, s32[4,1,1024]{2,1,0:T(1,128)S(1)} %bitcast.241), custom_call_target="tpu_custom_call" | custom-call | flops 10737418240 | bytes 12582912 | tf_op jit(solution)/shard_map/pallas_call | solution.py:502
  1026.6 20.2 %shard_map.323 = (bf16[512,2048]{1,0:T(8,128)(2,1)S(1)}, bf16[512,2048]{1,0:T(8,128)(2,1)}, bf16[512,2048]{1,0:T(8,128)(2,1)}, bf16[512,2048]{1,0:T(8,128)(2,1)}) custom-call(bf16[4096,768]{1,0:T(8,128)(2,1)} %shard_map.322.grads_ref, bf16[2048,768]{1,0:T(8,128)(2,1)} %copy-done.2), custom_call_target="tpu_custom_call" | custom-call | flops 12884901888 | bytes 33554432 | tf_op jit(solution)/shard_map/pallas_call | solution.py:1106
  1049.4 21.1 %collective-permute-done.13 = bf16[256,2048]{1,0:T(8,128)(2,1)} collective-permute-done((bf16[256,2048]{1,0:T(8,128)(2,1)}, bf16[256,2048]{1,0:T(8,128)(2,1)}, u32[]{:S(2)}, u32[]{:S(2)}) %collective-permute-start.13) | collective-permute-done | bytes 1048608 | tf_op jit(solution)/shard_map/ppermute | solution.py:1140
  1095.7 67.6 %all-to-all-done.5 = f32[8,16,256]{2,1,0:T(8,128)S(1)} async-done(((f32[8,16,256]{2,1,0:T(8,128)}), f32[8,16,256]{2,1,0:T(8,128)S(1)}, u32[]{:S(2)}, u32[]{:S(2)}) %all-to-all-start.5) | async-done | bytes 131104 | tf_op jit(solution)/shard_map/all_to_all | solution.py:1490
  (300 shorter events, 419.0 us)
Async XLA Ops:
  7.2 105.4 %all-gather.7.cloned.1.call-start = ((), (), s32[]{:S(2)}) async-start(), calls=%async_computation.13 | async-start | bytes 5898240 | tf_op jit(solution)/shard_map/all_gather | solution.py:1226
  20.4 211.9 %all-gather.9.cloned.1.call-start = ((), (), s32[]{:S(2)}) async-start(), calls=%async_computation.14 | async-start | bytes 7208960 | tf_op jit(solution)/shard_map/all_gather | solution.py:1283
  24.3 340.8 %all-gather.11.cloned.1.call-start = ((), (), s32[]{:S(2)}) async-start(), calls=%async_computation.15 | async-start | bytes 3604480 | tf_op jit(solution)/shard_map/all_gather | solution.py:1285
  25.8 360.6 %all-gather.13.cloned.1.call-start = ((), (), s32[]{:S(2)}) async-start(), calls=%async_computation.16 | async-start | bytes 7208960 | tf_op jit(solution)/shard_map/all_gather | solution.py:1292
  107.7 433.8 %all-gather.15.cloned.1.call-start = ((), (), s32[]{:S(2)}) async-start(), calls=%async_computation.17 | async-start | bytes 7208960 | tf_op jit(solution)/shard_map/all_gather | solution.py:1293
  115.2 58.1 %collective-permute-start = (bf16[4,64,2048]{2,1,0:T(8,128)(2,1)}, bf16[4,64,2048]{2,1,0:T(8,128)(2,1)}, u32[]{:S(2)}, u32[]{:S(2)}) collective-permute-start(bf16[4,64,2048]{2,1,0:T(8,128)(2,1)} %reshape.654), channel_id=1, source_target_pairs={{0,8},{8,0},{16,24},{24,16},{1,9},{9,1},{17,25},{25,17},{2,10},{10... | collective-permute-start | bytes 3145736 | tf_op jit(solution)/shard_map/ppermute | solution.py:1140
  116.8 56.6 %collective-permute-start.1 = (bf16[4,64,2048]{2,1,0:T(8,128)(2,1)}, bf16[4,64,2048]{2,1,0:T(8,128)(2,1)}, u32[]{:S(2)}, u32[]{:S(2)}) collective-permute-start(bf16[4,64,2048]{2,1,0:T(8,128)(2,1)} %reshape.654), channel_id=1, source_target_pairs={{0,16},{8,24},{16,0},{24,8},{1,17},{9,25},{17,1},{25,9},{2,18},{10... | collective-permute-start | bytes 3145736 | tf_op jit(solution)/shard_map/ppermute | solution.py:1140
  118.2 55.2 %collective-permute-start.2 = (bf16[4,64,2048]{2,1,0:T(8,128)(2,1)}, bf16[4,64,2048]{2,1,0:T(8,128)(2,1)}, u32[]{:S(2)}, u32[]{:S(2)}) collective-permute-start(bf16[4,64,2048]{2,1,0:T(8,128)(2,1)} %reshape.654), channel_id=1, source_target_pairs={{0,24},{8,16},{16,8},{24,0},{1,25},{9,17},{17,9},{25,1},{2,26},{10... | collective-permute-start | bytes 3145736 | tf_op jit(solution)/shard_map/ppermute | solution.py:1140
  188.9 410.4 %all-gather.17.cloned.1.call-start = ((), (), s32[]{:S(2)}) async-start(), calls=%async_computation.18 | async-start | bytes 7208960 | tf_op jit(solution)/shard_map/all_gather | solution.py:1294
  306.4 101.0 %collective-permute-start.4 = (bf16[512,2048]{1,0:T(8,128)(2,1)}, bf16[512,2048]{1,0:T(8,128)(2,1)}, u32[]{:S(2)}, u32[]{:S(2)}) collective-permute-start(bf16[512,2048]{1,0:T(8,128)(2,1)} %bitcast.244), channel_id=1, source_target_pairs={{0,8},{8,0},{16,24},{24,16},{1,9},{9,1},{17,25},{25,17},{2,10},{10... | collective-permute-start | bytes 6291464 | tf_op jit(solution)/shard_map/ppermute | solution.py:1140
  307.8 99.6 %collective-permute-start.5 = (bf16[512,2048]{1,0:T(8,128)(2,1)}, bf16[512,2048]{1,0:T(8,128)(2,1)}, u32[]{:S(2)}, u32[]{:S(2)}) collective-permute-start(bf16[512,2048]{1,0:T(8,128)(2,1)} %bitcast.245), channel_id=1, source_target_pairs={{0,16},{8,24},{16,0},{24,8},{1,17},{9,25},{17,1},{25,9},{2,18},{10... | collective-permute-start | bytes 6291464 | tf_op jit(solution)/shard_map/ppermute | solution.py:1140
  308.5 98.9 %collective-permute-start.6 = (bf16[512,2048]{1,0:T(8,128)(2,1)}, bf16[512,2048]{1,0:T(8,128)(2,1)}, u32[]{:S(2)}, u32[]{:S(2)}) collective-permute-start(bf16[512,2048]{1,0:T(8,128)(2,1)} %bitcast.246), channel_id=1, source_target_pairs={{0,24},{8,16},{16,8},{24,0},{1,25},{9,17},{17,9},{25,1},{2,26},{10... | collective-permute-start | bytes 6291464 | tf_op jit(solution)/shard_map/ppermute | solution.py:1140
  414.2 395.1 %reduce-scatter.7.cloned.1.call-start = ((), (), s32[]{:S(2)}) async-start(), calls=%async_computation.19 | async-start | bytes 10813440 | tf_op jit(solution)/shard_map/reduce_scatter | solution.py:1358
  533.3 424.2 %reduce-scatter.9.cloned.1.call-start = ((), (), s32[]{:S(2)}) async-start(), calls=%async_computation.20 | async-start | bytes 7208960 | tf_op jit(solution)/shard_map/reduce_scatter | solution.py:1358
  649.7 376.9 %reduce-scatter.11.cloned.1.call-start = ((), (), s32[]{:S(2)}) async-start(), calls=%async_computation.21 | async-start | bytes 7208960 | tf_op jit(solution)/shard_map/reduce_scatter | solution.py:1358
  756.0 53.3 %collective-permute-start.8 = (bf16[512,2048]{1,0:T(8,128)(2,1)}, bf16[512,2048]{1,0:T(8,128)(2,1)}, u32[]{:S(2)}, u32[]{:S(2)}) collective-permute-start(bf16[512,2048]{1,0:T(8,128)(2,1)} %get-tuple-element.89), channel_id=1, source_target_pairs={{0,8},{8,0},{16,24},{24,16},{1,9},{9,1},{17,25},{25,17},{2,10},{10... | collective-permute-start | bytes 6291464 | tf_op jit(solution)/shard_map/ppermute | solution.py:1140
  765.7 317.8 %reduce-scatter.17.cloned.1.call-start = ((), (), s32[]{:S(2)}) async-start(), calls=%async_computation.24 | async-start | bytes 7208960 | tf_op jit(solution)/shard_map/reduce_scatter | solution.py:1358
  939.7 244.0 %reduce-scatter.13.cloned.1.call-start = ((), (), s32[]{:S(2)}) async-start(), calls=%async_computation.22 | async-start | bytes 3932160 | tf_op jit(solution)/shard_map/reduce_scatter | solution.py:1446
  939.8 107.1 %collective-permute-start.11 = (bf16[512,2048]{1,0:T(8,128)(2,1)}, bf16[512,2048]{1,0:T(8,128)(2,1)}, u32[]{:S(2)}, u32[]{:S(2)}) collective-permute-start(bf16[512,2048]{1,0:T(8,128)(2,1)} %get-tuple-element.106), channel_id=1, source_target_pairs={{0,24},{8,16},{16,8},{24,0},{1,25},{9,17},{17,9},{25,1},{2,26},{10... | collective-permute-start | bytes 6291464 | tf_op jit(solution)/shard_map/ppermute | solution.py:1140
  1070.5 113.2 %collective-permute-start.15 = (bf16[512,2048]{1,0:T(8,128)(2,1)}, bf16[512,2048]{1,0:T(8,128)(2,1)}, u32[]{:S(2)}, u32[]{:S(2)}) collective-permute-start(bf16[512,2048]{1,0:T(8,128)(2,1)} %get-tuple-element.109), channel_id=1, source_target_pairs={{0,8},{8,0},{16,24},{24,16},{1,9},{9,1},{17,25},{25,17},{2,10},{10... | collective-permute-start | bytes 6291464 | tf_op jit(solution)/shard_map/ppermute | solution.py:1140
  1070.9 112.8 %collective-permute-start.16 = (bf16[512,2048]{1,0:T(8,128)(2,1)}, bf16[512,2048]{1,0:T(8,128)(2,1)}, u32[]{:S(2)}, u32[]{:S(2)}) collective-permute-start(bf16[512,2048]{1,0:T(8,128)(2,1)} %get-tuple-element.110), channel_id=1, source_target_pairs={{0,16},{8,24},{16,0},{24,8},{1,17},{9,25},{17,1},{25,9},{2,18},{10... | collective-permute-start | bytes 6291464 | tf_op jit(solution)/shard_map/ppermute | solution.py:1140
  1072.3 111.4 %collective-permute-start.17 = (bf16[512,2048]{1,0:T(8,128)(2,1)}, bf16[512,2048]{1,0:T(8,128)(2,1)}, u32[]{:S(2)}, u32[]{:S(2)}) collective-permute-start(bf16[512,2048]{1,0:T(8,128)(2,1)} %get-tuple-element.111), channel_id=1, source_target_pairs={{0,24},{8,16},{16,8},{24,0},{1,25},{9,17},{17,9},{25,1},{2,26},{10... | collective-permute-start | bytes 6291464 | tf_op jit(solution)/shard_map/ppermute | solution.py:1140
  1076.7 86.6 %all-to-all-start.5 = ((f32[8,16,256]{2,1,0:T(8,128)}), f32[8,16,256]{2,1,0:T(8,128)S(1)}, u32[]{:S(2)}, u32[]{:S(2)}) async-start(f32[8,16,256]{2,1,0:T(8,128)} %bitcast.234), calls=%async_computation.10 | async-start | bytes 262144 | tf_op jit(solution)/shard_map/all_to_all | solution.py:1490
  1083.0 92.3 %collective-permute-start.18 = (bf16[3,704,256]{2,1,0:T(8,128)(2,1)}, bf16[3,704,256]{2,1,0:T(8,128)(2,1)}, u32[]{:S(2)}, u32[]{:S(2)}) collective-permute-start(bf16[3,704,256]{2,1,0:T(8,128)(2,1)} %get-tuple-element.258), channel_id=1, source_target_pairs={{0,4},{4,0},{1,5},{5,1},{2,6},{6,2},{3,7},{7,3},{8,12},{12,8},{9,1... | collective-permute-start | bytes 3244040 | tf_op jit(solution)/shard_map/ppermute | solution.py:1144
  (53 other events, 1468.6 us)
Sparse Core Ops, SparseCore 0:
  20.5 92.0 all-gather.6
  114.8 105.1 all-gather.8
  222.1 57.4 all-gather.10
  281.0 105.3 all-gather.12
  387.9 104.9 all-gather.14
  494.3 104.9 all-gather.16
  601.7 146.8 reduce-scatter.6
  750.9 103.0 reduce-scatter.8
  856.4 102.7 reduce-scatter.10
  961.3 102.7 reduce-scatter.16
  1066.4 60.7 reduce-scatter.12
  1192.2 27.2 reduce-scatter.14

commit v10 on v9

--- a/solution.py
+++ b/solution.py
@@ -1375,7 +1375,7 @@
         shared_hidden,
         sh_down,
         result_e.reshape(plane, capacity, width),
-        after(slots, grads_made),
+        slots,
         sg_all,
         expert_gate,
         cot_all,
@@ -1384,8 +1384,8 @@
         mm(gate_grad_e, ex_gate, ((1,), (1,))) + mm(up_grad_e, ex_up, ((1,), (1,)))
     )
 
-    out_got = [swap(out_near[k], k) for k in (1, 2)]
-    slots, out_got, _ = lax.optimization_barrier((slots, out_got, shared_sums))
+    out_got = hops(out_near)
+    slots, out_got, _ = lax.optimization_barrier((slots, out_got, (shared_sums, grads_made)))
     n2_grad = n2_grad_sum(
         gate_grad_s,
         up_grad_s,
@@ -1394,7 +1394,6 @@
         rows_grad.reshape(plane, capacity, width),
         slots,
     )
-    out_far = swap(after(out_near[3], n2_grad), 3)
 
     dots = dots.reshape(plane, tokens, 128)[:, :, :2].transpose(0, 2, 1)
     back = jnp.arange(plane, dtype=jnp.int32) ^ me
@@ -1415,8 +1414,7 @@
 
     attended_grad = low(mm(low_residual, w_out_full, ((1,), (1,))))
     low_residual = after(low_residual, attended_grad)
-    out_got = after(out_got, attended_grad)
-    output = residual + out_near[0].astype(jnp.float32) + sum_up(out_got)
+    output = low(residual + sum_up(after(out_got, attended_grad)))
     attended_grad = to_columns(attended_grad)
     grad_out = low(mm(attended, low_residual, ((0,), (0,))))
     grad_out = grad_out.reshape(groups, halves, width // plane, width)
@@ -1427,6 +1425,16 @@
         [block_of(k, core) for k in range(4)],
         jnp.stack([block_of(k, 1 - core) for k in range(4)]),
     )
+    dz_all = jnp.concatenate([logit_grad, sg_logit_grad], axis=1)
+    dz_all = after(dz_all, out_grad_sums)
+    small_grads = mm(n2, dz_all, ((0,), (0,)))
+    small_grads = jnp.concatenate([small_grads, grad_gain_two[:, None]], axis=1).T
+    small_grads = jnp.pad(small_grads, ((0, 14 - experts_all), (0, 0)))
+    small_grads = small_grads.reshape(16, plane, width // plane).transpose(1, 0, 2)
+    attended_grad, small_grads = lax.optimization_barrier((attended_grad, small_grads))
+    small_grads = jnp.sum(
+        lax.all_to_all(small_grads, PLANE, split_axis=0, concat_axis=0, tiled=True), axis=0
+    )
     attended_grad = after(attended_grad, (out_grad_sums, output, grads[0]))
     qkv_grad = attention_call(qkv, attended_grad, q_codes, k_codes, seq_len)
     grad_qkv = low(mm(n1_all, qkv_grad, ((0,), (0,))))
@@ -1437,10 +1445,10 @@
         .reshape(width, 3 * head_cols)
     )
     out_grad_got = hops(out_grad_sums)
-    qkv_grad = after(qkv_grad, (grad_qkv, grads[1]))
+    qkv_grad, out_grad_got, small_grads, _ = lax.optimization_barrier(
+        (qkv_grad, out_grad_got, small_grads, (grad_qkv, grads[1]))
+    )
     n1_near = n1_grad_parts(qkv_grad, w_qkv, plane)
-    n1_near, out_far, out_grad_got = lax.optimization_barrier((n1_near, out_far, out_grad_got))
-    output = low(output + out_far.astype(jnp.float32))
     grad_out = low(sum_up(out_grad_got))
     n1_got = hops(n1_near)
     grad_qkv = lax.psum_scatter(grad_qkv, DP, scatter_dimension=0, tiled=True)
@@ -1480,15 +1488,7 @@
     shared_sums = shared_scatter(shared_sums.reshape(3, units // halves, -1))
     grad_sh_down, grad_sh_gate, grad_sh_up = [shared_sums[k] for k in range(3)]
     grad_sh_gate, grad_sh_up = grad_sh_gate.T, grad_sh_up.T
-    dz_all = jnp.concatenate([logit_grad, sg_logit_grad], axis=1)
-    dz_all = after(dz_all, n1_near)
-    small_grads = mm(n2, dz_all, ((0,), (0,)))
-    small_grads = jnp.concatenate([small_grads, grad_gain_two[:, None]], axis=1).T
-    small_grads = jnp.pad(small_grads, ((0, 14 - experts_all), (0, 0)))
-    small_grads = small_grads.reshape(16, plane, width // plane).transpose(1, 0, 2)
-    small_grads = jnp.sum(
-        lax.all_to_all(small_grads, PLANE, split_axis=0, concat_axis=0, tiled=True), axis=0
-    )
+    small_grads = after(small_grads, n1_near)
     small_grads = small_grads.reshape(16, depth, shard // plane).transpose(1, 0, 2)
     small_grads = jnp.sum(
         lax.all_to_all(small_grads, DP, split_axis=0, concat_axis=0, tiled=True), axis=0

time: 1240 us -> 1270 us (1.024)
  waiting for transfers between devices: 160 us -> 191 us
    ppermute x15, waiting for transfers between devices: 23.7 us -> 84.3 us  [swap(): return lax.ppermute(values, EXP, [(i, i ^ bits) for i in range(4)])]
    all_to_all x1, waiting for transfers between devices: 67.6 us -> 39.7 us  [local_plane(): lax.all_to_all(small_grads, PLANE, split_axis=0, concat_axis=0, tiled=True)]
    convert_element_type x7 -> x8, other arithmetic: 43.7 us -> 51.9 us  [low(): return values.astype(jnp.bfloat16)]
    unnamed x95 -> x93, local copies, waits for them, and re-layouts: 36.7 us -> 37.4 us
  transfers between devices with their start and end apart: 38 -> 38, of which waited for: 10 -> 11; matrix products, arithmetic and copies ran while one was open for 45% -> 44% of each run, Pallas kernels for 34% -> 34%
where the time goes in v10:
time: 1270 us; the launch traced here: 1260 us
  Pallas kernels  424 us (33%)
  matrix products  346 us (27%)
  waiting for transfers between devices  191 us (15%)
  other arithmetic  122 us (10%)
  local copies, waits for them, and re-layouts  114 us (9%)
  starting transfers between devices  45.8 us (4%)
  between operations  15.6 us (1%)
    dot_general x20, matrix products, mm(): lax.dot_general(left, right, (dims, ((), ())), preferred_element_type=jnp...  320 us
    pallas_call x2, Pallas kernels, plane_gather(): pl.pallas_call(partial(plane_gather_kernel, info is not None, relative),...  155 us
    pallas_call x1, Pallas kernels, n2_grad_sum(): pl.pallas_call(n2_grad_kernel, grid=(blocks,), in_specs=[by_units, by_uni...  95.2 us
    ppermute x15, waiting for transfers between devices, swap(): return lax.ppermute(values, EXP, [(i, i ^ bits) for i in range(4)])  84.3 us
    convert_element_type x8, other arithmetic, low(): return values.astype(jnp.bfloat16)  51.9 us
    pallas_call x2, Pallas kernels, attention_call(): pl.pallas_call(partial(body, heads, step), grid=(rows // seq_len,), in_sp...  50.1 us
    pallas_call x1, Pallas kernels, unit_grads(): pl.pallas_call(unit_grad_kernel, grid=(depth * halves,), in_specs=[whole,...  44 us
    all_to_all x1, waiting for transfers between devices, local_plane(): lax.all_to_all(small_grads, PLANE, split_axis=0, concat_axis=0, tiled=True)  39.7 us
  transfers between devices with their start and end apart: 38, of which 11 were waited for; matrix products, arithmetic and copies ran while one was open for 44% of the time, Pallas kernels for 34%

profile of v10, /device:TPU:0, one launch (start us, length us, event | category | flops | bytes accessed | tf_op | source)
XLA Modules:
  0.0 1258.1 jit_solution(18223514410254005025)
XLA Ops:
  24.9 81.1 %shard_map.315 = (bf16[8,512,2048]{2,1,0:T(8,128)(2,1)}, s32[8,8,512]{2,1,0:T(8,128)}) custom-call(bf16[512,2048]{1,0:T(8,128)(2,1)} %bitcast.242, s32[8,512]{1,0:T(8,128)} %concatenate.50.refs_1_), custom_call_target="tpu_custom_call" | custom-call | bytes 1048576 | tf_op jit(solution)/shard_map/pallas_call | solution.py:628
  123.8 22.3 %shard_map.316 = (bf16[4096,2048]{1,0:T(8,128)(2,1)}, bf16[4096,768]{1,0:T(8,128)(2,1)}) custom-call(bf16[4096,2048]{1,0:T(8,128)(2,1)} %bitcast.297, f32[1,2048]{1,0:T(1,128)S(1)} %copy.192.gain_ref, bf16[2048,768]{1,0:T(8,128)(2,1)S(1)} %slice.152.w_ref), custom_call_target="tpu_custom_call" | custom-call | flops 12884901888 | bytes 33554432 | tf_op jit(solution)/shard_map/pallas_call | solution.py:655
  146.1 19.4 %shard_map.317 = bf16[4096,256]{1,0:T(8,128)(2,1)S(1)} custom-call(bf16[4096,768]{1,0:T(8,128)(2,1)} %get-tuple-element.73.qkv_ref, s32[4096,1]{1,0:T(8,128)S(1)} %copy.193.q_code_ref, s32[4,1,1024]{2,1,0:T(1,128)S(1)} %bitcast.239), custom_call_target="tpu_custom_call" | custom-call | flops 4294967296 | bytes 8388608 | tf_op jit(solution)/shard_map/pallas_call | solution.py:502
  230.6 74.2 %shard_map.318 = bf16[8,512,2048]{2,1,0:T(8,128)(2,1)} custom-call(bf16[512,2048]{1,0:T(8,128)(2,1)} %multiply_convert_fusion.7.refs_0_), custom_call_target="tpu_custom_call" | custom-call | bytes 1048576 | tf_op jit(solution)/shard_map/pallas_call | solution.py:628
  340.9 22.5 %multiply_convert_fusion.6 = (bf16[704,4096]{1,0:T(8,128)(2,1)}, f32[704,4096]{1,0:T(8,128)}) fusion(f32[704,4096]{1,0:T(8,128)} %fusion.11, bf16[4096,2048]{1,0:T(8,128)(2,1)} %bitcast.249, bf16[2048,1408]{0,1:T(8,128)(2,1)} %all-gather.9.cloned.1.call-done), kind=kOutput, calls=%fused_computation.13 | convolution fusion | flops 11828461568 | bytes 48496640 | tf_op jit(solution)/shard_map/dot_general | solution.py:1161
  363.4 21.4 %all-gather.13.cloned.1.call-done = bf16[2048,1408]{1,0:T(8,128)(2,1)} async-done(((bf16[512,1408]{1,0:T(8,128)(2,1)}), bf16[2048,1408]{1,0:T(8,128)(2,1)}) %all-gather.13.cloned.1.call-update) | async-done | bytes 5767184 | tf_op jit(solution)/shard_map/all_gather | solution.py:1292
  384.8 21.0 %fusion.53 = f32[2304,1408]{1,0:T(8,128)} fusion(bf16[2304,2048]{1,0:T(8,128)(2,1)} %bitcast.298, bf16[2048,1408]{1,0:T(8,128)(2,1)} %all-gather.13.cloned.1.call-done), kind=kOutput, calls=%fused_computation.176 | convolution fusion | flops 13287555072 | bytes 28180480 | tf_op jit(solution)/shard_map/dot_general | solution.py:1161
  461.1 25.2 %multiply_convert_fusion.4 = (bf16[704,4096]{1,0:T(8,128)(2,1)}, bf16[704,4096]{1,0:T(8,128)(2,1)}) fusion(f32[704,4096]{1,0:T(8,128)} %fusion.11, f32[704,4096]{1,0:T(8,128)} %get-tuple-element.282, bf16[704,2048]{1,0:T(8,128)(2,1)} %all-gather.11.cloned.1.call-done.down_ref, bf16[4096,2048]{1,0:T(8,128)(2,1)} %multiply_convert_fusion.cot_ref), kind=kOutput, calls=%fused_computation.11 | convolution fusion | flops 11848646656 | bytes 54263808 | tf_op jit(solution)/shard_map/dot_general | solution.py:1161
  488.9 44.0 %shard_map.320 = bf16[4,2112,512]{2,1,0:T(8,128)(2,1)} custom-call(bf16[704,4096]{1,0:T(8,128)(2,1)S(1)} %copy-done.5, bf16[704,4096]{1,0:T(8,128)(2,1)} %get-tuple-element.246.dgate_ref, bf16[704,4096]{1,0:T(8,128)(2,1)} %get-tuple-element.245.dup_ref, bf16[4096,2048]{1,0:T(8,128)(2,1)} %multiply_convert_fusion.cot_ref, bf16[4096,2048]{1,0:T(8,128)(2,1)} %bitcast.251), custom_call_target="tpu_custom_call" | custom-call | flops 35433480192 | bytes 59506688 | tf_op jit(solution)/shard_map/pallas_call | solution.py:1009
  541.1 20.7 %fusion.54 = f32[2304,1408]{1,0:T(8,128)} fusion(bf16[2304,2048]{1,0:T(8,128)(2,1)} %bitcast.299, bf16[2048,1408]{1,0:T(8,128)(2,1)} %all-gather.15.cloned.1.call-done), kind=kOutput, calls=%fused_computation.177 | convolution fusion | flops 13287555072 | bytes 28180480 | tf_op jit(solution)/shard_map/dot_general | solution.py:1161
  597.7 30.5 %multiply_convert_fusion.1 = (bf16[2304,1408]{1,0:T(8,128)(2,1)}, bf16[2304,1408]{1,0:T(8,128)(2,1)}, bf16[2304,1408]{1,0:T(8,128)(2,1)}) fusion(f32[2304,1408]{1,0:T(8,128)} %fusion.53, f32[2304,1408]{1,0:T(8,128)} %fusion.54, bf16[2304,2048]{1,0:T(8,128)(2,1)} %fusion, bf16[1408,2048]{1,0:T(8,128)(2,1)} %all-gather.17.cloned.1.call-done), kind=kOutput, calls=%fused_computation.6 | convolution fusion | flops 13336215552 | bytes 60620800 | tf_op jit(solution)/shard_map/dot_general | solution.py:1161
  628.2 19.8 %convolution_convert_fusion.4 = bf16[1408,2048]{1,0:T(8,128)(2,1)} fusion(bf16[2304,1408]{1,0:T(8,128)(2,1)} %get-tuple-element.244, bf16[2304,2048]{1,0:T(8,128)(2,1)} %fusion), kind=kOutput, calls=%fused_computation.23 | convolution fusion | flops 13290438656 | bytes 21692416 | tf_op jit(solution)/shard_map/dot_general | solution.py:1161
  648.1 20.6 %convolution_convert_fusion.3 = bf16[2048,1408]{1,0:T(8,128)(2,1)} fusion(bf16[2304,2048]{1,0:T(8,128)(2,1)} %bitcast.300, bf16[2304,1408]{1,0:T(8,128)(2,1)} %get-tuple-element.243), kind=kOutput, calls=%fused_computation.22 | convolution fusion | flops 13290438656 | bytes 21692416 | tf_op jit(solution)/shard_map/dot_general | solution.py:1161
  678.1 20.1 %convolution_convert_fusion = bf16[2304,2048]{1,0:T(8,128)(2,1)} fusion(bf16[2304,1408]{1,0:T(8,128)(2,1)} %get-tuple-element.244, bf16[1408,2048]{1,0:T(8,128)(2,1)} %all-gather.17.cloned.1.call-done), kind=kOutput, calls=%fused_computation.16 | convolution fusion | flops 13292273664 | bytes 21692416 | tf_op jit(solution)/shard_map/dot_general | solution.py:1161
  698.1 35.9 %shard_map.319 = (bf16[512,2048]{1,0:T(8,128)(2,1)}, bf16[512,2048]{1,0:T(8,128)(2,1)}, bf16[512,2048]{1,0:T(8,128)(2,1)}, bf16[512,2048]{1,0:T(8,128)(2,1)}, f32[4096,128]{1,0:T(8,128)}) custom-call(bf16[704,4096]{1,0:T(8,128)(2,1)} %get-tuple-element.281.hidden_ref.hid_ref, bf16[704,2048]{1,0:T(8,128)(2,1)} %all-gather.11.cloned.1.call-done.down_ref, ...), custom_call_target="tpu_custom_call" | custom-call | flops 16642998272 | bytes 50331648 | tf_op jit(solution)/shard_map/pallas_call | solution.py:788
  744.8 20.5 %convolution_convert_fusion.2 = bf16[2048,1408]{1,0:T(8,128)(2,1)} fusion(bf16[2304,2048]{1,0:T(8,128)(2,1)} %bitcast.301, bf16[2304,1408]{1,0:T(8,128)(2,1)} %get-tuple-element.242), kind=kOutput, calls=%fused_computation.21 | convolution fusion | flops 13290438656 | bytes 21692416 | tf_op jit(solution)/shard_map/dot_general | solution.py:1161
  765.3 20.8 %fusion.55 = f32[2304,2048]{1,0:T(8,128)} fusion(bf16[2304,1408]{1,0:T(8,128)(2,1)} %get-tuple-element.243, bf16[2048,1408]{1,0:T(8,128)(2,1)} %all-gather.13.cloned.1.call-done), kind=kOutput, calls=%fused_computation.178 | convolution fusion | flops 13287555072 | bytes 31129600 | tf_op jit(solution)/shard_map/dot_general | solution.py:1161
  786.2 22.0 %add_convert_fusion = bf16[2304,2048]{1,0:T(8,128)(2,1)} fusion(f32[2304,2048]{1,0:T(8,128)} %fusion.55, bf16[2304,1408]{1,0:T(8,128)(2,1)} %get-tuple-element.242, bf16[2048,1408]{1,0:T(8,128)(2,1)} %all-gather.15.cloned.1.call-done), kind=kOutput, calls=%fused_computation.5 | convolution fusion | flops 13296992256 | bytes 40566784 | tf_op jit(solution)/shard_map/dot_general | solution.py:1161
  811.0 24.7 %collective-permute-done.8 = bf16[512,2048]{1,0:T(8,128)(2,1)} collective-permute-done((bf16[512,2048]{1,0:T(8,128)(2,1)}, bf16[512,2048]{1,0:T(8,128)(2,1)}, u32[]{:S(2)}, u32[]{:S(2)}) %collective-permute-start.8) | collective-permute-done | bytes 2097184 | tf_op jit(solution)/shard_map/ppermute | solution.py:1140
  837.6 95.2 %shard_map.321 = f32[512,2048]{1,0:T(8,128)} custom-call(bf16[704,4096]{1,0:T(8,128)(2,1)} %get-tuple-element.246.dgate_ref, bf16[704,4096]{1,0:T(8,128)(2,1)} %get-tuple-element.245.dup_ref, bf16[704,2048]{1,0:T(8,128)(2,1)} %get-tuple-element.256.gate_ref, bf16[704,2048]{1,0:T(8,128)(2,1)} %get-tuple-element.255.up_ref, bf16[8,288,2048]{2,1,0:T(8,128)(2,1)} %bitcast.302, ...), custom_call_target="tpu_custom_call" | custom-call | flops 28454158336 | bytes 33554432 | tf_op jit(solution)/shard_map/pallas_call | solution.py:971
  995.1 30.7 %shard_map.322.grads_ref = bf16[4096,768]{1,0:T(8,128)(2,1)} custom-call(bf16[4096,768]{1,0:T(8,128)(2,1)} %get-tuple-element.73.qkv_ref, bf16[4096,256]{1,0:T(8,128)(2,1)} %bitcast.55.grad_ref, s32[4096,1]{1,0:T(8,128)S(1)} %copy.193.q_code_ref, s32[4,1,1024]{2,1,0:T(1,128)S(1)} %bitcast.240), custom_call_target="tpu_custom_call" | custom-call | flops 10737418240 | bytes 12582912 | tf_op jit(solution)/shard_map/pallas_call | solution.py:502
  1056.8 39.7 %all-to-all-done.3 = f32[8,16,256]{2,1,0:T(8,128)S(1)} async-done(((f32[8,16,256]{2,1,0:T(8,128)}), f32[8,16,256]{2,1,0:T(8,128)S(1)}, u32[]{:S(2)}, u32[]{:S(2)}) %all-to-all-start.3) | async-done | bytes 131104 | tf_op jit(solution)/shard_map/all_to_all | solution.py:1436
  1096.6 21.0 %shard_map.323 = (bf16[512,2048]{1,0:T(8,128)(2,1)S(1)}, bf16[512,2048]{1,0:T(8,128)(2,1)}, bf16[512,2048]{1,0:T(8,128)(2,1)}, bf16[512,2048]{1,0:T(8,128)(2,1)}) custom-call(bf16[4096,768]{1,0:T(8,128)(2,1)} %shard_map.322.grads_ref, bf16[2048,768]{1,0:T(8,128)(2,1)} %copy-done.2), custom_call_target="tpu_custom_call" | custom-call | flops 12884901888 | bytes 33554432 | tf_op jit(solution)/shard_map/pallas_call | solution.py:1106
  1166.4 44.6 %collective-permute-done.16 = bf16[512,2048]{1,0:T(8,128)(2,1)} collective-permute-done((bf16[512,2048]{1,0:T(8,128)(2,1)}, bf16[512,2048]{1,0:T(8,128)(2,1)}, u32[]{:S(2)}, u32[]{:S(2)}) %collective-permute-start.16) | collective-permute-done | bytes 2097184 | tf_op jit(solution)/shard_map/ppermute | solution.py:1140
  (297 shorter events, 444.8 us)
Async XLA Ops:
  7.2 103.8 %all-gather.7.cloned.1.call-start = ((), (), s32[]{:S(2)}) async-start(), calls=%async_computation.13 | async-start | bytes 5898240 | tf_op jit(solution)/shard_map/all_gather | solution.py:1226
  18.7 211.9 %all-gather.9.cloned.1.call-start = ((), (), s32[]{:S(2)}) async-start(), calls=%async_computation.14 | async-start | bytes 7208960 | tf_op jit(solution)/shard_map/all_gather | solution.py:1283
  22.6 340.8 %all-gather.11.cloned.1.call-start = ((), (), s32[]{:S(2)}) async-start(), calls=%async_computation.15 | async-start | bytes 3604480 | tf_op jit(solution)/shard_map/all_gather | solution.py:1285
  24.2 360.6 %all-gather.13.cloned.1.call-start = ((), (), s32[]{:S(2)}) async-start(), calls=%async_computation.16 | async-start | bytes 7208960 | tf_op jit(solution)/shard_map/all_gather | solution.py:1292
  106.0 435.0 %all-gather.15.cloned.1.call-start = ((), (), s32[]{:S(2)}) async-start(), calls=%async_computation.17 | async-start | bytes 7208960 | tf_op jit(solution)/shard_map/all_gather | solution.py:1293
  113.6 58.1 %collective-permute-start.2 = (bf16[4,64,2048]{2,1,0:T(8,128)(2,1)}, bf16[4,64,2048]{2,1,0:T(8,128)(2,1)}, u32[]{:S(2)}, u32[]{:S(2)}) collective-permute-start(bf16[4,64,2048]{2,1,0:T(8,128)(2,1)} %reshape.654), channel_id=1, source_target_pairs={{0,24},{8,16},{16,8},{24,0},{1,25},{9,17},{17,9},{25,1},{2,26},{10... | collective-permute-start | bytes 3145736 | tf_op jit(solution)/shard_map/ppermute | solution.py:1140
  116.0 55.7 %collective-permute-start.1 = (bf16[4,64,2048]{2,1,0:T(8,128)(2,1)}, bf16[4,64,2048]{2,1,0:T(8,128)(2,1)}, u32[]{:S(2)}, u32[]{:S(2)}) collective-permute-start(bf16[4,64,2048]{2,1,0:T(8,128)(2,1)} %reshape.654), channel_id=1, source_target_pairs={{0,16},{8,24},{16,0},{24,8},{1,17},{9,25},{17,1},{25,9},{2,18},{10... | collective-permute-start | bytes 3145736 | tf_op jit(solution)/shard_map/ppermute | solution.py:1140
  116.6 55.2 %collective-permute-start = (bf16[4,64,2048]{2,1,0:T(8,128)(2,1)}, bf16[4,64,2048]{2,1,0:T(8,128)(2,1)}, u32[]{:S(2)}, u32[]{:S(2)}) collective-permute-start(bf16[4,64,2048]{2,1,0:T(8,128)(2,1)} %reshape.654), channel_id=1, source_target_pairs={{0,8},{8,0},{16,24},{24,16},{1,9},{9,1},{17,25},{25,17},{2,10},{10... | collective-permute-start | bytes 3145736 | tf_op jit(solution)/shard_map/ppermute | solution.py:1140
  187.3 410.5 %all-gather.17.cloned.1.call-start = ((), (), s32[]{:S(2)}) async-start(), calls=%async_computation.18 | async-start | bytes 7208960 | tf_op jit(solution)/shard_map/all_gather | solution.py:1294
  304.8 101.0 %collective-permute-start.6 = (bf16[512,2048]{1,0:T(8,128)(2,1)}, bf16[512,2048]{1,0:T(8,128)(2,1)}, u32[]{:S(2)}, u32[]{:S(2)}) collective-permute-start(bf16[512,2048]{1,0:T(8,128)(2,1)} %bitcast.243), channel_id=1, source_target_pairs={{0,24},{8,16},{16,8},{24,0},{1,25},{9,17},{17,9},{25,1},{2,26},{10... | collective-permute-start | bytes 6291464 | tf_op jit(solution)/shard_map/ppermute | solution.py:1140
  306.3 99.5 %collective-permute-start.5 = (bf16[512,2048]{1,0:T(8,128)(2,1)}, bf16[512,2048]{1,0:T(8,128)(2,1)}, u32[]{:S(2)}, u32[]{:S(2)}) collective-permute-start(bf16[512,2048]{1,0:T(8,128)(2,1)} %bitcast.244), channel_id=1, source_target_pairs={{0,16},{8,24},{16,0},{24,8},{1,17},{9,25},{17,1},{25,9},{2,18},{10... | collective-permute-start | bytes 6291464 | tf_op jit(solution)/shard_map/ppermute | solution.py:1140
  307.6 98.2 %collective-permute-start.4 = (bf16[512,2048]{1,0:T(8,128)(2,1)}, bf16[512,2048]{1,0:T(8,128)(2,1)}, u32[]{:S(2)}, u32[]{:S(2)}) collective-permute-start(bf16[512,2048]{1,0:T(8,128)(2,1)} %bitcast.245), channel_id=1, source_target_pairs={{0,8},{8,0},{16,24},{24,16},{1,9},{9,1},{17,25},{25,17},{2,10},{10... | collective-permute-start | bytes 6291464 | tf_op jit(solution)/shard_map/ppermute | solution.py:1140
  412.6 423.0 %reduce-scatter.7.cloned.1.call-start = ((), (), s32[]{:S(2)}) async-start(), calls=%async_computation.19 | async-start | bytes 10813440 | tf_op jit(solution)/shard_map/reduce_scatter | solution.py:1358
  532.9 462.2 %reduce-scatter.9.cloned.1.call-start = ((), (), s32[]{:S(2)}) async-start(), calls=%async_computation.20 | async-start | bytes 7208960 | tf_op jit(solution)/shard_map/reduce_scatter | solution.py:1358
  648.1 448.5 %reduce-scatter.11.cloned.1.call-start = ((), (), s32[]{:S(2)}) async-start(), calls=%async_computation.21 | async-start | bytes 7208960 | tf_op jit(solution)/shard_map/reduce_scatter | solution.py:1358
  737.6 70.5 %all-to-all-start.1 = ((f32[8,2,512]{2,1,0:T(2,128)}), f32[8,2,512]{2,1,0:T(2,128)S(1)}, u32[]{:S(2)}, u32[]{:S(2)}) async-start(f32[8,2,512]{2,1,0:T(2,128)} %gather_fusion.1), calls=%async_computation.2 | async-start | bytes 65536 | tf_op jit(solution)/shard_map/all_to_all | solution.py:1401
  741.2 379.9 %reduce-scatter.17.cloned.1.call-start = ((), (), s32[]{:S(2)}) async-start(), calls=%async_computation.24 | async-start | bytes 7208960 | tf_op jit(solution)/shard_map/reduce_scatter | solution.py:1358
  741.2 69.7 %collective-permute-start.10 = (bf16[512,2048]{1,0:T(8,128)(2,1)}, bf16[512,2048]{1,0:T(8,128)(2,1)}, u32[]{:S(2)}, u32[]{:S(2)}) collective-permute-start(bf16[512,2048]{1,0:T(8,128)(2,1)} %get-tuple-element.91), channel_id=1, source_target_pairs={{0,24},{8,16},{16,8},{24,0},{1,25},{9,17},{17,9},{25,1},{2,26},{10... | collective-permute-start | bytes 6291464 | tf_op jit(solution)/shard_map/ppermute | solution.py:1140
  744.1 91.5 %collective-permute-start.8 = (bf16[512,2048]{1,0:T(8,128)(2,1)}, bf16[512,2048]{1,0:T(8,128)(2,1)}, u32[]{:S(2)}, u32[]{:S(2)}) collective-permute-start(bf16[512,2048]{1,0:T(8,128)(2,1)} %get-tuple-element.89), channel_id=1, source_target_pairs={{0,8},{8,0},{16,24},{24,16},{1,9},{9,1},{17,25},{25,17},{2,10},{10... | collective-permute-start | bytes 6291464 | tf_op jit(solution)/shard_map/ppermute | solution.py:1140
  744.7 91.0 %collective-permute-start.9 = (bf16[512,2048]{1,0:T(8,128)(2,1)}, bf16[512,2048]{1,0:T(8,128)(2,1)}, u32[]{:S(2)}, u32[]{:S(2)}) collective-permute-start(bf16[512,2048]{1,0:T(8,128)(2,1)} %get-tuple-element.90), channel_id=1, source_target_pairs={{0,16},{8,24},{16,0},{24,8},{1,17},{9,25},{17,1},{25,9},{2,18},{10... | collective-permute-start | bytes 6291464 | tf_op jit(solution)/shard_map/ppermute | solution.py:1140
  968.4 183.0 %reduce-scatter.13.cloned.1.call-start = ((), (), s32[]{:S(2)}) async-start(), calls=%async_computation.22 | async-start | bytes 3932160 | tf_op jit(solution)/shard_map/reduce_scatter | solution.py:1454
  1117.9 93.0 %collective-permute-start.16 = (bf16[512,2048]{1,0:T(8,128)(2,1)}, bf16[512,2048]{1,0:T(8,128)(2,1)}, u32[]{:S(2)}, u32[]{:S(2)}) collective-permute-start(bf16[512,2048]{1,0:T(8,128)(2,1)} %get-tuple-element.111), channel_id=1, source_target_pairs={{0,16},{8,24},{16,0},{24,8},{1,17},{9,25},{17,1},{25,9},{2,18},{10... | collective-permute-start | bytes 6291464 | tf_op jit(solution)/shard_map/ppermute | solution.py:1140
  1118.8 92.2 %collective-permute-start.17 = (bf16[512,2048]{1,0:T(8,128)(2,1)}, bf16[512,2048]{1,0:T(8,128)(2,1)}, u32[]{:S(2)}, u32[]{:S(2)}) collective-permute-start(bf16[512,2048]{1,0:T(8,128)(2,1)} %get-tuple-element.112), channel_id=1, source_target_pairs={{0,24},{8,16},{16,8},{24,0},{1,25},{9,17},{17,9},{25,1},{2,26},{10... | collective-permute-start | bytes 6291464 | tf_op jit(solution)/shard_map/ppermute | solution.py:1140
  1135.0 114.1 %reduce-scatter.15.cloned.1.call-start = ((), (), s32[]{:S(2)}) async-start(), calls=%async_computation.23 | async-start | bytes 1310720 | tf_op jit(solution)/shard_map/reduce_scatter | solution.py:1358
  (52 other events, 1513.5 us)
Sparse Core Ops, SparseCore 0:
  18.8 92.0 all-gather.6
  113.1 105.1 all-gather.8
  220.5 57.4 all-gather.10
  279.4 105.3 all-gather.12
  386.2 104.9 all-gather.14
  492.7 105.0 all-gather.16
  600.1 146.8 reduce-scatter.6
  749.3 103.0 reduce-scatter.8
  854.7 102.7 reduce-scatter.10
  959.7 102.7 reduce-scatter.16
  1064.8 60.7 reduce-scatter.12
  1151.5 25.3 reduce-scatter.14

commit v11 on v10

--- a/solution.py
+++ b/solution.py
@@ -682,15 +682,18 @@
     return (slots == lanes).astype(jnp.bfloat16)
 
 
-def hand_out(step_at, half, blocks, out_refs, sems):
+def hand_out(step_at, half, blocks, pieces, sems):
     copies = [
-        pltpu.make_async_copy(blocks.at[k], out_refs[k], sems.at[k]) for k in range(half)
+        pltpu.make_async_copy(blocks.at[k, part], goal, sems.at[number])
+        for number, (k, part, goal) in enumerate(pieces)
     ]
     for k in range(half):
 
         @pl.when(step_at == half + k)
         def _():
-            copies[k].start()
+            for copy, piece in zip(copies, pieces):
+                if piece[0] == k:
+                    copy.start()
 
     @pl.when(step_at == 2 * half - 1)
     def _():
@@ -771,7 +774,9 @@
 
         make(store)
 
-    hand_out(step_at, half, got, near_refs, out_sem)
+    everything = pl.ds(0, got.shape[1])
+    pieces = [(k, everything, near_refs[k]) for k in range(half)]
+    hand_out(step_at, half, got, pieces, out_sem)
 
     @pl.when(step_at == 2 * half - 1)
     def _():
@@ -1091,7 +1096,18 @@
 
         make(store)
 
-    hand_out(step_at, half, got, near_refs, out_sem)
+    own, x_send, y_send, rest = near_refs
+    top, bottom = pl.ds(0, tokens // 2), pl.ds(tokens // 2, tokens // 2)
+    pieces = [
+        (0, pl.ds(0, tokens), own),
+        (1, top, x_send.at[bottom]),
+        (1, bottom, rest.at[bottom]),
+        (2, top, rest.at[top]),
+        (2, bottom, y_send.at[bottom]),
+        (3, top, x_send.at[top]),
+        (3, bottom, y_send.at[top]),
+    ]
+    hand_out(step_at, half, got, pieces, out_sem)
 
     @pl.when(step_at == 2 * half - 1)
     def _():
@@ -1119,7 +1135,7 @@
             pltpu.SemaphoreType.DMA((blocks,)),
             pltpu.SemaphoreType.DMA((half,)),
             pltpu.SemaphoreType.DMA((half,)),
-            pltpu.SemaphoreType.DMA((half,)),
+            pltpu.SemaphoreType.DMA((7,)),
         ],
         compiler_params=pltpu.CompilerParams(
             collective_id=1, has_side_effects=True, vmem_limit_bytes=48 * 2**20
@@ -1151,6 +1167,21 @@
 
 def hops(sums):
     return [sums[0]] + [swap(sums[k], k) for k in (1, 2, 3)]
+
+
+def two_stage_sum(own, x_send, y_send, rest, later):
+    half = own.shape[0] // 2
+    wide = lambda v: v.astype(jnp.float32)
+    x_got, y_got = swap(x_send, 1), swap(y_send, 2)
+    y_last = swap(low(wide(rest[:half]) + wide(x_got[:half])), 2)
+    x_last = swap(low(wide(rest[half:]) + wide(y_got[:half])), 1)
+    x_last, y_last = after((x_last, y_last), later)
+    return jnp.concatenate(
+        [
+            wide(own[:half]) + wide(x_got[half:]) + wide(y_last),
+            wide(own[half:]) + wide(y_got[half:]) + wide(x_last),
+        ]
+    )
 
 
 def sum_up(parts):
@@ -1366,10 +1397,6 @@
     up_grad_e = low(hgrad_e * act_e)
 
     grad_ex_down = low(mm(hidden_e, row_grads, ((0,), (0,))))
-    grad_ex_gate = low(mm(expert_rows, gate_grad_e, ((0,), (0,))))
-    grad_ex_up = low(mm(expert_rows, up_grad_e, ((0,), (0,))))
-    grads_made = (grad_ex_down, grad_ex_gate, grad_ex_up)
-    grads = [scatter(v, dim) for v, dim in zip(grads_made, (1, 0, 0))]
     slots = slots.reshape(all_tokens, 1)
     *out_near, dots = output_parts(
         shared_hidden,
@@ -1380,6 +1407,11 @@
         expert_gate,
         cot_all,
     )
+    expert_rows = after(expert_rows, out_near)
+    grad_ex_gate = low(mm(expert_rows, gate_grad_e, ((0,), (0,))))
+    grad_ex_up = low(mm(expert_rows, up_grad_e, ((0,), (0,))))
+    grads_made = (grad_ex_down, grad_ex_gate, grad_ex_up)
+    grads = [scatter(v, dim) for v, dim in zip(grads_made, (1, 0, 0))]
     rows_grad = low(
         mm(gate_grad_e, ex_gate, ((1,), (1,))) + mm(up_grad_e, ex_up, ((1,), (1,)))
     )
@@ -1432,11 +1464,14 @@
     small_grads = jnp.pad(small_grads, ((0, 14 - experts_all), (0, 0)))
     small_grads = small_grads.reshape(16, plane, width // plane).transpose(1, 0, 2)
     attended_grad, small_grads = lax.optimization_barrier((attended_grad, small_grads))
+    attended_grad = after(attended_grad, (out_grad_sums, output, grads[0]))
+    qkv_grad = attention_call(qkv, attended_grad, q_codes, k_codes, seq_len)
+    out_grad_got = hops(out_grad_sums)
+    qkv_grad, out_grad_got = lax.optimization_barrier((qkv_grad, out_grad_got))
+    small_grads = after(small_grads, qkv_grad)
     small_grads = jnp.sum(
         lax.all_to_all(small_grads, PLANE, split_axis=0, concat_axis=0, tiled=True), axis=0
     )
-    attended_grad = after(attended_grad, (out_grad_sums, output, grads[0]))
-    qkv_grad = attention_call(qkv, attended_grad, q_codes, k_codes, seq_len)
     grad_qkv = low(mm(n1_all, qkv_grad, ((0,), (0,))))
     fine = shard // plane
     grad_qkv = (
@@ -1444,13 +1479,11 @@
         .transpose(1, 0, 2, 3)
         .reshape(width, 3 * head_cols)
     )
-    out_grad_got = hops(out_grad_sums)
-    qkv_grad, out_grad_got, small_grads, _ = lax.optimization_barrier(
-        (qkv_grad, out_grad_got, small_grads, (grad_qkv, grads[1]))
+    qkv_grad, small_grads, _ = lax.optimization_barrier(
+        (qkv_grad, small_grads, (grad_qkv, grads[1]))
     )
     n1_near = n1_grad_parts(qkv_grad, w_qkv, plane)
     grad_out = low(sum_up(out_grad_got))
-    n1_got = hops(n1_near)
     grad_qkv = lax.psum_scatter(grad_qkv, DP, scatter_dimension=0, tiled=True)
     qkv_sum = grad_qkv
     w_rows = (
@@ -1493,7 +1526,7 @@
     small_grads = jnp.sum(
         lax.all_to_all(small_grads, DP, split_axis=0, concat_axis=0, tiled=True), axis=0
     )
-    n1_grad = sum_up(after(n1_got, qkv_sum))
+    n1_grad = two_stage_sum(*n1_near, grad_qkv)
     input_part, _ = norm_back(x_rows, inv_one, g_one, n1_grad)
     input_grad = low(residual_grad + input_part)
     return (

time: 1270 us -> 1230 us (0.969)
  waiting for transfers between devices: 191 us -> 149 us
    all_to_all x1, waiting for transfers between devices: 39.7 us -> 2.64 us  [local_plane(): lax.all_to_all(small_grads, PLANE, split_axis=0, concat_axis=0, tiled=True)]
    ppermute x15 -> x16, waiting for transfers between devices: 84.3 us -> 57.7 us  [swap(): return lax.ppermute(values, EXP, [(i, i ^ bits) for i in range(4)])]
    all_to_all x1, waiting for transfers between devices: 0.01 us -> 20.9 us  [local_plane(): dots = lax.all_to_all(dots, PLANE, split_axis=0, concat_axis=0, tiled=True)]
    convert_element_type x8 -> x9, other arithmetic: 51.9 us -> 55.7 us  [low(): return values.astype(jnp.bfloat16)]
    unnamed x93 -> x109, local copies, waits for them, and re-layouts: 37.4 us -> 38.8 us
  transfers between devices with their start and end apart: 38 -> 39, of which waited for: 11 -> 14; matrix products, arithmetic and copies ran while one was open for 44% -> 46% of each run, Pallas kernels for 34% -> 35%
where the time goes in v11:
time: 1230 us; the launch traced here: 1220 us
  Pallas kernels  423 us (34%)
  matrix products  347 us (28%)
  waiting for transfers between devices  149 us (12%)
  other arithmetic  123 us (10%)
  local copies, waits for them, and re-layouts  115 us (9%)
  starting transfers between devices  44.9 us (4%)
  between operations  15.4 us (1%)
    dot_general x20, matrix products, mm(): lax.dot_general(left, right, (dims, ((), ())), preferred_element_type=jnp...  320 us
    pallas_call x2, Pallas kernels, plane_gather(): pl.pallas_call(partial(plane_gather_kernel, info is not None, relative),...  155 us
    pallas_call x1, Pallas kernels, n2_grad_sum(): pl.pallas_call(n2_grad_kernel, grid=(blocks,), in_specs=[by_units, by_uni...  95.1 us
    ppermute x16, waiting for transfers between devices, swap(): return lax.ppermute(values, EXP, [(i, i ^ bits) for i in range(4)])  57.7 us
    convert_element_type x9, other arithmetic, low(): return values.astype(jnp.bfloat16)  55.7 us
    pallas_call x2, Pallas kernels, attention_call(): pl.pallas_call(partial(body, heads, step), grid=(rows // seq_len,), in_sp...  50 us
    pallas_call x1, Pallas kernels, unit_grads(): pl.pallas_call(unit_grad_kernel, grid=(depth * halves,), in_specs=[whole,...  44.1 us
    unnamed x109, local copies, waits for them, and re-layouts  38.8 us
  transfers between devices with their start and end apart: 39, of which 14 were waited for; matrix products, arithmetic and copies ran while one was open for 46% of the time, Pallas kernels for 35%

profile of v11, /device:TPU:0, one launch (start us, length us, event | category | flops | bytes accessed | tf_op | source)
XLA Modules:
  0.0 1217.8 jit_solution(12023396166409781347)
XLA Ops:
  24.9 81.1 %shard_map.315 = (bf16[8,512,2048]{2,1,0:T(8,128)(2,1)}, s32[8,8,512]{2,1,0:T(8,128)}) custom-call(bf16[512,2048]{1,0:T(8,128)(2,1)} %bitcast.242, s32[8,512]{1,0:T(8,128)} %concatenate.53.refs_1_), custom_call_target="tpu_custom_call" | custom-call | bytes 1048576 | tf_op jit(solution)/shard_map/pallas_call | solution.py:628
  123.8 22.3 %shard_map.316 = (bf16[4096,2048]{1,0:T(8,128)(2,1)}, bf16[4096,768]{1,0:T(8,128)(2,1)}) custom-call(bf16[4096,2048]{1,0:T(8,128)(2,1)} %bitcast.297, f32[1,2048]{1,0:T(1,128)S(1)} %copy.192.gain_ref, bf16[2048,768]{1,0:T(8,128)(2,1)S(1)} %slice.184.w_ref), custom_call_target="tpu_custom_call" | custom-call | flops 12884901888 | bytes 33554432 | tf_op jit(solution)/shard_map/pallas_call | solution.py:655
  230.5 74.2 %shard_map.318 = bf16[8,512,2048]{2,1,0:T(8,128)(2,1)} custom-call(bf16[512,2048]{1,0:T(8,128)(2,1)} %multiply_convert_fusion.7.refs_0_), custom_call_target="tpu_custom_call" | custom-call | bytes 1048576 | tf_op jit(solution)/shard_map/pallas_call | solution.py:628
  321.5 19.4 %fusion.11 = f32[704,4096]{1,0:T(8,128)} fusion(bf16[4096,2048]{1,0:T(8,128)(2,1)} %bitcast.248, bf16[2048,1408]{0,1:T(8,128)(2,1)} %all-gather.9.cloned.1.call-done), kind=kOutput, calls=%fused_computation.53 | convolution fusion | flops 11811160064 | bytes 31195136 | tf_op jit(solution)/shard_map/dot_general | solution.py:1192
  341.0 22.6 %multiply_convert_fusion.6 = (bf16[704,4096]{1,0:T(8,128)(2,1)}, f32[704,4096]{1,0:T(8,128)}) fusion(f32[704,4096]{1,0:T(8,128)} %fusion.11, bf16[4096,2048]{1,0:T(8,128)(2,1)} %bitcast.249, bf16[2048,1408]{0,1:T(8,128)(2,1)} %all-gather.9.cloned.1.call-done), kind=kOutput, calls=%fused_computation.13 | convolution fusion | flops 11828461568 | bytes 48496640 | tf_op jit(solution)/shard_map/dot_general | solution.py:1192
  363.5 21.3 %all-gather.13.cloned.1.call-done = bf16[2048,1408]{1,0:T(8,128)(2,1)} async-done(((bf16[512,1408]{1,0:T(8,128)(2,1)}), bf16[2048,1408]{1,0:T(8,128)(2,1)}) %all-gather.13.cloned.1.call-update) | async-done | bytes 5767184 | tf_op jit(solution)/shard_map/all_gather | solution.py:1323
  384.8 21.0 %fusion.53 = f32[2304,1408]{1,0:T(8,128)} fusion(bf16[2304,2048]{1,0:T(8,128)(2,1)} %bitcast.298, bf16[2048,1408]{1,0:T(8,128)(2,1)} %all-gather.13.cloned.1.call-done), kind=kOutput, calls=%fused_computation.180 | convolution fusion | flops 13287555072 | bytes 28180480 | tf_op jit(solution)/shard_map/dot_general | solution.py:1192
  460.8 25.1 %multiply_convert_fusion.4 = (bf16[704,4096]{1,0:T(8,128)(2,1)}, bf16[704,4096]{1,0:T(8,128)(2,1)}) fusion(f32[704,4096]{1,0:T(8,128)} %fusion.11, f32[704,4096]{1,0:T(8,128)} %get-tuple-element.288, bf16[704,2048]{1,0:T(8,128)(2,1)} %all-gather.11.cloned.1.call-done.down_ref, bf16[4096,2048]{1,0:T(8,128)(2,1)} %multiply_convert_fusion.cot_ref), kind=kOutput, calls=%fused_computation.11 | convolution fusion | flops 11848646656 | bytes 54263808 | tf_op jit(solution)/shard_map/dot_general | solution.py:1192
  488.6 44.1 %shard_map.320 = bf16[4,2112,512]{2,1,0:T(8,128)(2,1)} custom-call(bf16[704,4096]{1,0:T(8,128)(2,1)S(1)} %copy-done.5, bf16[704,4096]{1,0:T(8,128)(2,1)} %get-tuple-element.248.dgate_ref, bf16[704,4096]{1,0:T(8,128)(2,1)} %get-tuple-element.247.dup_ref, bf16[4096,2048]{1,0:T(8,128)(2,1)} %multiply_convert_fusion.cot_ref, bf16[4096,2048]{1,0:T(8,128)(2,1)} %bitcast.251), custom_call_target="tpu_custom_call" | custom-call | flops 35433480192 | bytes 59506688 | tf_op jit(solution)/shard_map/pallas_call | solution.py:1014
  540.9 20.8 %fusion.54 = f32[2304,1408]{1,0:T(8,128)} fusion(bf16[2304,2048]{1,0:T(8,128)(2,1)} %bitcast.299, bf16[2048,1408]{1,0:T(8,128)(2,1)} %all-gather.15.cloned.1.call-done), kind=kOutput, calls=%fused_computation.181 | convolution fusion | flops 13287555072 | bytes 28180480 | tf_op jit(solution)/shard_map/dot_general | solution.py:1192
  597.7 30.6 %multiply_convert_fusion.1 = (bf16[2304,1408]{1,0:T(8,128)(2,1)}, bf16[2304,1408]{1,0:T(8,128)(2,1)}, bf16[2304,1408]{1,0:T(8,128)(2,1)}) fusion(f32[2304,1408]{1,0:T(8,128)} %fusion.53, f32[2304,1408]{1,0:T(8,128)} %fusion.54, bf16[2304,2048]{1,0:T(8,128)(2,1)} %fusion, bf16[1408,2048]{1,0:T(8,128)(2,1)} %all-gather.17.cloned.1.call-done), kind=kOutput, calls=%fused_computation.6 | convolution fusion | flops 13336215552 | bytes 60620800 | tf_op jit(solution)/shard_map/dot_general | solution.py:1192
  628.4 19.8 %convolution_convert_fusion.4 = bf16[1408,2048]{1,0:T(8,128)(2,1)} fusion(bf16[2304,1408]{1,0:T(8,128)(2,1)} %get-tuple-element.246, bf16[2304,2048]{1,0:T(8,128)(2,1)} %fusion), kind=kOutput, calls=%fused_computation.23 | convolution fusion | flops 13290438656 | bytes 21692416 | tf_op jit(solution)/shard_map/dot_general | solution.py:1192
  650.4 20.1 %convolution_convert_fusion = bf16[2304,2048]{1,0:T(8,128)(2,1)} fusion(bf16[2304,1408]{1,0:T(8,128)(2,1)} %get-tuple-element.246, bf16[1408,2048]{1,0:T(8,128)(2,1)} %all-gather.17.cloned.1.call-done), kind=kOutput, calls=%fused_computation.16 | convolution fusion | flops 13292273664 | bytes 21692416 | tf_op jit(solution)/shard_map/dot_general | solution.py:1192
  670.5 36.0 %shard_map.319 = (bf16[512,2048]{1,0:T(8,128)(2,1)}, bf16[512,2048]{1,0:T(8,128)(2,1)}, bf16[512,2048]{1,0:T(8,128)(2,1)}, bf16[512,2048]{1,0:T(8,128)(2,1)}, f32[4096,128]{1,0:T(8,128)}) custom-call(bf16[704,4096]{1,0:T(8,128)(2,1)} %get-tuple-element.287.hidden_ref.hid_ref, bf16[704,2048]{1,0:T(8,128)(2,1)} %all-gather.11.cloned.1.call-done.down_ref, ...), custom_call_target="tpu_custom_call" | custom-call | flops 16642998272 | bytes 50331648 | tf_op jit(solution)/shard_map/pallas_call | solution.py:793
  706.5 20.7 %convolution_convert_fusion.3 = bf16[2048,1408]{1,0:T(8,128)(2,1)} fusion(bf16[2304,2048]{1,0:T(8,128)(2,1)} %bitcast.300, bf16[2304,1408]{1,0:T(8,128)(2,1)} %get-tuple-element.245), kind=kOutput, calls=%fused_computation.22 | convolution fusion | flops 13290438656 | bytes 21692416 | tf_op jit(solution)/shard_map/dot_general | solution.py:1192
  745.0 20.3 %convolution_convert_fusion.2 = bf16[2048,1408]{1,0:T(8,128)(2,1)} fusion(bf16[2304,2048]{1,0:T(8,128)(2,1)} %bitcast.301, bf16[2304,1408]{1,0:T(8,128)(2,1)} %get-tuple-element.244), kind=kOutput, calls=%fused_computation.21 | convolution fusion | flops 13290438656 | bytes 21692416 | tf_op jit(solution)/shard_map/dot_general | solution.py:1192
  765.3 20.8 %fusion.55 = f32[2304,2048]{1,0:T(8,128)} fusion(bf16[2304,1408]{1,0:T(8,128)(2,1)} %get-tuple-element.245, bf16[2048,1408]{1,0:T(8,128)(2,1)} %all-gather.13.cloned.1.call-done), kind=kOutput, calls=%fused_computation.182 | convolution fusion | flops 13287555072 | bytes 31129600 | tf_op jit(solution)/shard_map/dot_general | solution.py:1192
  786.1 22.0 %add_convert_fusion = bf16[2304,2048]{1,0:T(8,128)(2,1)} fusion(f32[2304,2048]{1,0:T(8,128)} %fusion.55, bf16[2304,1408]{1,0:T(8,128)(2,1)} %get-tuple-element.244, bf16[2048,1408]{1,0:T(8,128)(2,1)} %all-gather.15.cloned.1.call-done), kind=kOutput, calls=%fused_computation.5 | convolution fusion | flops 13296992256 | bytes 40566784 | tf_op jit(solution)/shard_map/dot_general | solution.py:1192
  808.1 20.9 %all-to-all-done.1 = f32[8,2,512]{2,1,0:T(2,128)S(1)} async-done(((f32[8,2,512]{2,1,0:T(2,128)}), f32[8,2,512]{2,1,0:T(2,128)S(1)}, u32[]{:S(2)}, u32[]{:S(2)}) %all-to-all-start.1) | async-done | bytes 32800 | tf_op jit(solution)/shard_map/all_to_all | solution.py:1433
  833.8 95.1 %shard_map.321 = f32[512,2048]{1,0:T(8,128)} custom-call(bf16[704,4096]{1,0:T(8,128)(2,1)} %get-tuple-element.248.dgate_ref, bf16[704,4096]{1,0:T(8,128)(2,1)} %get-tuple-element.247.dup_ref, bf16[704,2048]{1,0:T(8,128)(2,1)} %get-tuple-element.258.gate_ref, bf16[704,2048]{1,0:T(8,128)(2,1)} %get-tuple-element.257.up_ref, bf16[8,288,2048]{2,1,0:T(8,128)(2,1)} %bitcast.302, ...), custom_call_target="tpu_custom_call" | custom-call | flops 28454158336 | bytes 33554432 | tf_op jit(solution)/shard_map/pallas_call | solution.py:976
  991.5 30.7 %shard_map.322.grads_ref = bf16[4096,768]{1,0:T(8,128)(2,1)} custom-call(bf16[4096,768]{1,0:T(8,128)(2,1)} %get-tuple-element.74.qkv_ref, bf16[4096,256]{1,0:T(8,128)(2,1)} %bitcast.55.grad_ref, s32[4096,1]{1,0:T(8,128)S(1)} %copy.193.q_code_ref, s32[4,1,1024]{2,1,0:T(1,128)S(1)} %bitcast.240), custom_call_target="tpu_custom_call" | custom-call | flops 10737418240 | bytes 12582912 | tf_op jit(solution)/shard_map/pallas_call | solution.py:502
  1035.9 19.5 %convolution_convert_fusion.7 = bf16[2048,768]{1,0:T(8,128)(2,1)S(1)} fusion(bf16[4096,2048]{1,0:T(8,128)(2,1)} %get-tuple-element.111, bf16[4096,768]{1,0:T(8,128)(2,1)} %shard_map.322.grads_ref), kind=kOutput, calls=%fused_computation.47 | convolution fusion | flops 12886474752 | bytes 26214400 | tf_op jit(solution)/shard_map/dot_general | solution.py:1192
  1066.5 20.7 %shard_map.323 = (bf16[512,2048]{1,0:T(8,128)(2,1)S(1)}, bf16[512,2048]{1,0:T(8,128)(2,1)}, bf16[512,2048]{1,0:T(8,128)(2,1)}, bf16[512,2048]{1,0:T(8,128)(2,1)}) custom-call(bf16[4096,768]{1,0:T(8,128)(2,1)} %shard_map.322.grads_ref, bf16[2048,768]{1,0:T(8,128)(2,1)} %copy-done.2), custom_call_target="tpu_custom_call" | custom-call | flops 12884901888 | bytes 33554432 | tf_op jit(solution)/shard_map/pallas_call | solution.py:1122
  1104.2 31.8 %collective-permute-done.15 = bf16[512,2048]{1,0:T(8,128)(2,1)} collective-permute-done((bf16[512,2048]{1,0:T(8,128)(2,1)}, bf16[512,2048]{1,0:T(8,128)(2,1)}, u32[]{:S(2)}, u32[]{:S(2)}) %collective-permute-start.15) | collective-permute-done | bytes 2097184 | tf_op jit(solution)/shard_map/ppermute | solution.py:1156
  (317 shorter events, 441.8 us)
Async XLA Ops:
  7.2 103.8 %all-gather.7.cloned.1.call-start = ((), (), s32[]{:S(2)}) async-start(), calls=%async_computation.13 | async-start | bytes 5898240 | tf_op jit(solution)/shard_map/all_gather | solution.py:1257
  18.7 211.7 %all-gather.9.cloned.1.call-start = ((), (), s32[]{:S(2)}) async-start(), calls=%async_computation.14 | async-start | bytes 7208960 | tf_op jit(solution)/shard_map/all_gather | solution.py:1314
  22.6 340.9 %all-gather.11.cloned.1.call-start = ((), (), s32[]{:S(2)}) async-start(), calls=%async_computation.15 | async-start | bytes 3604480 | tf_op jit(solution)/shard_map/all_gather | solution.py:1316
  24.2 360.6 %all-gather.13.cloned.1.call-start = ((), (), s32[]{:S(2)}) async-start(), calls=%async_computation.16 | async-start | bytes 7208960 | tf_op jit(solution)/shard_map/all_gather | solution.py:1323
  106.0 434.8 %all-gather.15.cloned.1.call-start = ((), (), s32[]{:S(2)}) async-start(), calls=%async_computation.17 | async-start | bytes 7208960 | tf_op jit(solution)/shard_map/all_gather | solution.py:1324
  113.6 58.1 %collective-permute-start.2 = (bf16[4,64,2048]{2,1,0:T(8,128)(2,1)}, bf16[4,64,2048]{2,1,0:T(8,128)(2,1)}, u32[]{:S(2)}, u32[]{:S(2)}) collective-permute-start(bf16[4,64,2048]{2,1,0:T(8,128)(2,1)} %reshape.654), channel_id=1, source_target_pairs={{0,24},{8,16},{16,8},{24,0},{1,25},{9,17},{17,9},{25,1},{2,26},{10... | collective-permute-start | bytes 3145736 | tf_op jit(solution)/shard_map/ppermute | solution.py:1156
  116.0 55.7 %collective-permute-start.1 = (bf16[4,64,2048]{2,1,0:T(8,128)(2,1)}, bf16[4,64,2048]{2,1,0:T(8,128)(2,1)}, u32[]{:S(2)}, u32[]{:S(2)}) collective-permute-start(bf16[4,64,2048]{2,1,0:T(8,128)(2,1)} %reshape.654), channel_id=1, source_target_pairs={{0,16},{8,24},{16,0},{24,8},{1,17},{9,25},{17,1},{25,9},{2,18},{10... | collective-permute-start | bytes 3145736 | tf_op jit(solution)/shard_map/ppermute | solution.py:1156
  116.6 55.1 %collective-permute-start = (bf16[4,64,2048]{2,1,0:T(8,128)(2,1)}, bf16[4,64,2048]{2,1,0:T(8,128)(2,1)}, u32[]{:S(2)}, u32[]{:S(2)}) collective-permute-start(bf16[4,64,2048]{2,1,0:T(8,128)(2,1)} %reshape.654), channel_id=1, source_target_pairs={{0,8},{8,0},{16,24},{24,16},{1,9},{9,1},{17,25},{25,17},{2,10},{10... | collective-permute-start | bytes 3145736 | tf_op jit(solution)/shard_map/ppermute | solution.py:1156
  187.1 410.6 %all-gather.17.cloned.1.call-start = ((), (), s32[]{:S(2)}) async-start(), calls=%async_computation.18 | async-start | bytes 7208960 | tf_op jit(solution)/shard_map/all_gather | solution.py:1325
  304.7 101.1 %collective-permute-start.6 = (bf16[512,2048]{1,0:T(8,128)(2,1)}, bf16[512,2048]{1,0:T(8,128)(2,1)}, u32[]{:S(2)}, u32[]{:S(2)}) collective-permute-start(bf16[512,2048]{1,0:T(8,128)(2,1)} %bitcast.243), channel_id=1, source_target_pairs={{0,24},{8,16},{16,8},{24,0},{1,25},{9,17},{17,9},{25,1},{2,26},{10... | collective-permute-start | bytes 6291464 | tf_op jit(solution)/shard_map/ppermute | solution.py:1156
  306.2 99.6 %collective-permute-start.5 = (bf16[512,2048]{1,0:T(8,128)(2,1)}, bf16[512,2048]{1,0:T(8,128)(2,1)}, u32[]{:S(2)}, u32[]{:S(2)}) collective-permute-start(bf16[512,2048]{1,0:T(8,128)(2,1)} %bitcast.244), channel_id=1, source_target_pairs={{0,16},{8,24},{16,0},{24,8},{1,17},{9,25},{17,1},{25,9},{2,18},{10... | collective-permute-start | bytes 6291464 | tf_op jit(solution)/shard_map/ppermute | solution.py:1156
  307.5 98.3 %collective-permute-start.4 = (bf16[512,2048]{1,0:T(8,128)(2,1)}, bf16[512,2048]{1,0:T(8,128)(2,1)}, u32[]{:S(2)}, u32[]{:S(2)}) collective-permute-start(bf16[512,2048]{1,0:T(8,128)(2,1)} %bitcast.245), channel_id=1, source_target_pairs={{0,8},{8,0},{16,24},{24,16},{1,9},{9,1},{17,25},{25,17},{2,10},{10... | collective-permute-start | bytes 6291464 | tf_op jit(solution)/shard_map/ppermute | solution.py:1156
  412.6 419.3 %reduce-scatter.7.cloned.1.call-start = ((), (), s32[]{:S(2)}) async-start(), calls=%async_computation.19 | async-start | bytes 10813440 | tf_op jit(solution)/shard_map/reduce_scatter | solution.py:1389
  532.7 458.8 %reduce-scatter.9.cloned.1.call-start = ((), (), s32[]{:S(2)}) async-start(), calls=%async_computation.20 | async-start | bytes 7208960 | tf_op jit(solution)/shard_map/reduce_scatter | solution.py:1389
  648.2 418.3 %reduce-scatter.11.cloned.1.call-start = ((), (), s32[]{:S(2)}) async-start(), calls=%async_computation.21 | async-start | bytes 7208960 | tf_op jit(solution)/shard_map/reduce_scatter | solution.py:1389
  734.3 97.5 %collective-permute-start.10 = (bf16[512,2048]{1,0:T(8,128)(2,1)}, bf16[512,2048]{1,0:T(8,128)(2,1)}, u32[]{:S(2)}, u32[]{:S(2)}) collective-permute-start(bf16[512,2048]{1,0:T(8,128)(2,1)} %get-tuple-element.92), channel_id=1, source_target_pairs={{0,24},{8,16},{16,8},{24,0},{1,25},{9,17},{17,9},{25,1},{2,26},{10... | collective-permute-start | bytes 6291464 | tf_op jit(solution)/shard_map/ppermute | solution.py:1156
  736.6 95.2 %collective-permute-start.8 = (bf16[512,2048]{1,0:T(8,128)(2,1)}, bf16[512,2048]{1,0:T(8,128)(2,1)}, u32[]{:S(2)}, u32[]{:S(2)}) collective-permute-start(bf16[512,2048]{1,0:T(8,128)(2,1)} %get-tuple-element.90), channel_id=1, source_target_pairs={{0,8},{8,0},{16,24},{24,16},{1,9},{9,1},{17,25},{25,17},{2,10},{10... | collective-permute-start | bytes 6291464 | tf_op jit(solution)/shard_map/ppermute | solution.py:1156
  737.2 94.6 %collective-permute-start.9 = (bf16[512,2048]{1,0:T(8,128)(2,1)}, bf16[512,2048]{1,0:T(8,128)(2,1)}, u32[]{:S(2)}, u32[]{:S(2)}) collective-permute-start(bf16[512,2048]{1,0:T(8,128)(2,1)} %get-tuple-element.91), channel_id=1, source_target_pairs={{0,16},{8,24},{16,0},{24,8},{1,17},{9,25},{17,1},{25,9},{2,18},{10... | collective-permute-start | bytes 6291464 | tf_op jit(solution)/shard_map/ppermute | solution.py:1156
  741.4 87.6 %all-to-all-start.1 = ((f32[8,2,512]{2,1,0:T(2,128)}), f32[8,2,512]{2,1,0:T(2,128)S(1)}, u32[]{:S(2)}, u32[]{:S(2)}) async-start(f32[8,2,512]{2,1,0:T(2,128)} %gather_fusion.1), calls=%async_computation.2 | async-start | bytes 65536 | tf_op jit(solution)/shard_map/all_to_all | solution.py:1433
  744.9 346.9 %reduce-scatter.17.cloned.1.call-start = ((), (), s32[]{:S(2)}) async-start(), calls=%async_computation.24 | async-start | bytes 7208960 | tf_op jit(solution)/shard_map/reduce_scatter | solution.py:1389
  964.3 202.0 %reduce-scatter.13.cloned.1.call-start = ((), (), s32[]{:S(2)}) async-start(), calls=%async_computation.22 | async-start | bytes 3932160 | tf_op jit(solution)/shard_map/reduce_scatter | solution.py:1487
  984.1 51.9 %collective-permute-start.14 = (bf16[256,2048]{1,0:T(8,128)(2,1)}, bf16[256,2048]{1,0:T(8,128)(2,1)}, u32[]{:S(2)}, u32[]{:S(2)}) collective-permute-start(bf16[256,2048]{1,0:T(8,128)(2,1)} %get-tuple-element.249), channel_id=1, source_target_pairs={{0,24},{8,16},{16,8},{24,0},{1,25},{9,17},{17,9},{25,1},{2,26},{10... | collective-permute-start | bytes 3145736 | tf_op jit(solution)/shard_map/ppermute | solution.py:1156
  1094.5 51.6 %collective-permute-start.19 = (bf16[3,704,256]{2,1,0:T(8,128)(2,1)}, bf16[3,704,256]{2,1,0:T(8,128)(2,1)}, u32[]{:S(2)}, u32[]{:S(2)}) collective-permute-start(bf16[3,704,256]{2,1,0:T(8,128)(2,1)} %get-tuple-element.263), channel_id=1, source_target_pairs={{0,4},{4,0},{1,5},{5,1},{2,6},{6,2},{3,7},{7,3},{8,12},{12,8},{9,1... | collective-permute-start | bytes 3244040 | tf_op jit(solution)/shard_map/ppermute | solution.py:1160
  1098.7 110.3 %reduce-scatter.15.cloned.1.call-start = ((), (), s32[]{:S(2)}) async-start(), calls=%async_computation.23 | async-start | bytes 1310720 | tf_op jit(solution)/shard_map/reduce_scatter | solution.py:1389
  (61 other events, 1650.0 us)
Sparse Core Ops, SparseCore 0:
  18.8 92.0 all-gather.6
  113.1 105.1 all-gather.8
  220.5 57.4 all-gather.10
  279.4 105.3 all-gather.12
  386.2 104.9 all-gather.14
  492.7 105.0 all-gather.16
  600.1 146.8 reduce-scatter.6
  749.3 103.0 reduce-scatter.8
  854.7 102.7 reduce-scatter.10
  959.7 102.7 reduce-scatter.16
  1064.8 61.0 reduce-scatter.12
  1166.5 23.4 reduce-scatter.14

commit v12 on v11

--- a/solution.py
+++ b/solution.py
@@ -1169,10 +1169,10 @@
     return [sums[0]] + [swap(sums[k], k) for k in (1, 2, 3)]
 
 
-def two_stage_sum(own, x_send, y_send, rest, later):
+def two_stage_sum(own, x_send, y_send, rest, between, later):
     half = own.shape[0] // 2
     wide = lambda v: v.astype(jnp.float32)
-    x_got, y_got = swap(x_send, 1), swap(y_send, 2)
+    x_got, y_got = after((swap(x_send, 1), swap(y_send, 2)), between)
     y_last = swap(low(wide(rest[:half]) + wide(x_got[:half])), 2)
     x_last = swap(low(wide(rest[half:]) + wide(y_got[:half])), 1)
     x_last, y_last = after((x_last, y_last), later)
@@ -1416,7 +1416,7 @@
         mm(gate_grad_e, ex_gate, ((1,), (1,))) + mm(up_grad_e, ex_up, ((1,), (1,)))
     )
 
-    out_got = hops(out_near)
+    out_got = [out_near[0]] + [swap(out_near[k], k) for k in (1, 2)]
     slots, out_got, _ = lax.optimization_barrier((slots, out_got, (shared_sums, grads_made)))
     n2_grad = n2_grad_sum(
         gate_grad_s,
@@ -1426,6 +1426,7 @@
         rows_grad.reshape(plane, capacity, width),
         slots,
     )
+    out_far = swap(after(out_near[3], n2_grad), 3)
 
     dots = dots.reshape(plane, tokens, 128)[:, :, :2].transpose(0, 2, 1)
     back = jnp.arange(plane, dtype=jnp.int32) ^ me
@@ -1446,7 +1447,7 @@
 
     attended_grad = low(mm(low_residual, w_out_full, ((1,), (1,))))
     low_residual = after(low_residual, attended_grad)
-    output = low(residual + sum_up(after(out_got, attended_grad)))
+    output = residual + sum_up(after(out_got, attended_grad))
     attended_grad = to_columns(attended_grad)
     grad_out = low(mm(attended, low_residual, ((0,), (0,))))
     grad_out = grad_out.reshape(groups, halves, width // plane, width)
@@ -1479,9 +1480,10 @@
         .transpose(1, 0, 2, 3)
         .reshape(width, 3 * head_cols)
     )
-    qkv_grad, small_grads, _ = lax.optimization_barrier(
-        (qkv_grad, small_grads, (grad_qkv, grads[1]))
-    )
+    qkv_grad, small_grads, out_far, _ = lax.optimization_barrier(
+        (qkv_grad, small_grads, out_far, (grad_qkv, grads[1]))
+    )
+    output = low(output + out_far.astype(jnp.float32))
     n1_near = n1_grad_parts(qkv_grad, w_qkv, plane)
     grad_out = low(sum_up(out_grad_got))
     grad_qkv = lax.psum_scatter(grad_qkv, DP, scatter_dimension=0, tiled=True)
@@ -1493,22 +1495,22 @@
     )
     w_rows = lax.dynamic_index_in_dim(w_rows, lax.axis_index(DP), axis=0, keepdims=False)
     gain_dots = jnp.sum(grad_qkv.astype(jnp.float32) * w_rows.astype(jnp.float32), axis=1)
-    gain_dots = lax.all_to_all(
-        gain_dots.reshape(plane, 1, fine), PLANE, split_axis=0, concat_axis=0, tiled=True
-    )
     my_gain = lax.dynamic_slice(
         g_one, ((me * depth + lax.axis_index(DP)) * fine,), (fine,)
     )
-    grad_gain_one = jnp.sum(gain_dots[:, 0], axis=0) / my_gain
+    gain_dots = jnp.broadcast_to(low(gain_dots).reshape(plane, fine, 1), (plane, fine, 128))
     grad_qkv = lax.all_to_all(
-        grad_qkv.reshape(plane, fine, 3 * head_cols),
+        jnp.concatenate([grad_qkv.reshape(plane, fine, 3 * head_cols), gain_dots], axis=2),
         PLANE,
         split_axis=0,
         concat_axis=0,
         tiled=True,
     )
+    gain_dots = grad_qkv[:, :, 3 * head_cols].astype(jnp.float32)
+    grad_gain_one = jnp.sum(gain_dots, axis=0) / my_gain
     grad_qkv = (
-        grad_qkv.reshape(plane, fine, 3, head_cols)
+        grad_qkv[:, :, : 3 * head_cols]
+        .reshape(plane, fine, 3, head_cols)
         .transpose(2, 1, 0, 3)
         .reshape(3, fine, width)
         .astype(jnp.float32)
@@ -1526,7 +1528,7 @@
     small_grads = jnp.sum(
         lax.all_to_all(small_grads, DP, split_axis=0, concat_axis=0, tiled=True), axis=0
     )
-    n1_grad = two_stage_sum(*n1_near, grad_qkv)
+    n1_grad = two_stage_sum(*n1_near, qkv_sum, grad_qkv)
     input_part, _ = norm_back(x_rows, inv_one, g_one, n1_grad)
     input_grad = low(residual_grad + input_part)
     return (

time: 1230 us -> 1220 us (level)
  waiting for transfers between devices: 149 us -> 129 us
    all_to_all x1, waiting for transfers between devices: 20.9 us -> 0.01 us  [local_plane(): dots = lax.all_to_all(dots, PLANE, split_axis=0, concat_axis=0, tiled=True)]
    ppermute x16, waiting for transfers between devices: 57.7 us -> 71.9 us  [swap(): return lax.ppermute(values, EXP, [(i, i ^ bits) for i in range(4)])]
    convert_element_type x9 -> x8, other arithmetic: 55.7 us -> 48.3 us  [low(): return values.astype(jnp.bfloat16)]
    unnamed x109 -> x103, local copies, waits for them, and re-layouts: 38.8 us -> 39.7 us
  transfers between devices with their start and end apart: 39 -> 38, of which waited for: 14 -> 11; matrix products, arithmetic and copies ran while one was open for 46% -> 47% of each run, Pallas kernels for 35% -> 35%
where the time goes in v12:
time: 1220 us; the launch traced here: 1210 us
  Pallas kernels  424 us (35%)
  matrix products  345 us (28%)
  waiting for transfers between devices  129 us (11%)
  other arithmetic  129 us (11%)
  local copies, waits for them, and re-layouts  117 us (10%)
  starting transfers between devices  47.3 us (4%)
  between operations  15.7 us (1%)
    dot_general x20, matrix products, mm(): lax.dot_general(left, right, (dims, ((), ())), preferred_element_type=jnp...  319 us
    pallas_call x2, Pallas kernels, plane_gather(): pl.pallas_call(partial(plane_gather_kernel, info is not None, relative),...  155 us
    pallas_call x1, Pallas kernels, n2_grad_sum(): pl.pallas_call(n2_grad_kernel, grid=(blocks,), in_specs=[by_units, by_uni...  95.8 us
    ppermute x16, waiting for transfers between devices, swap(): return lax.ppermute(values, EXP, [(i, i ^ bits) for i in range(4)])  71.9 us
    pallas_call x2, Pallas kernels, attention_call(): pl.pallas_call(partial(body, heads, step), grid=(rows // seq_len,), in_sp...  50.1 us
    convert_element_type x8, other arithmetic, low(): return values.astype(jnp.bfloat16)  48.3 us
    pallas_call x1, Pallas kernels, unit_grads(): pl.pallas_call(unit_grad_kernel, grid=(depth * halves,), in_specs=[whole,...  44.1 us
    unnamed x103, local copies, waits for them, and re-layouts  39.7 us
  transfers between devices with their start and end apart: 38, of which 11 were waited for; matrix products, arithmetic and copies ran while one was open for 47% of the time, Pallas kernels for 35%

profile of v12, /device:TPU:0, one launch (start us, length us, event | category | flops | bytes accessed | tf_op | source)
XLA Modules:
  0.0 1207.4 jit_solution(10353672586868554238)
XLA Ops:
  24.9 81.1 %shard_map.315 = (bf16[8,512,2048]{2,1,0:T(8,128)(2,1)}, s32[8,8,512]{2,1,0:T(8,128)}) custom-call(bf16[512,2048]{1,0:T(8,128)(2,1)} %bitcast.242, s32[8,512]{1,0:T(8,128)} %concatenate.56.refs_1_), custom_call_target="tpu_custom_call" | custom-call | bytes 1048576 | tf_op jit(solution)/shard_map/pallas_call | solution.py:628
  123.8 22.3 %shard_map.316 = (bf16[4096,2048]{1,0:T(8,128)(2,1)}, bf16[4096,768]{1,0:T(8,128)(2,1)}) custom-call(bf16[4096,2048]{1,0:T(8,128)(2,1)} %bitcast.298, f32[1,2048]{1,0:T(1,128)S(1)} %copy.161.gain_ref, bf16[2048,768]{1,0:T(8,128)(2,1)S(1)} %slice.192.w_ref), custom_call_target="tpu_custom_call" | custom-call | flops 12884901888 | bytes 33554432 | tf_op jit(solution)/shard_map/pallas_call | solution.py:655
  146.1 19.4 %shard_map.317 = bf16[4096,256]{1,0:T(8,128)(2,1)S(1)} custom-call(bf16[4096,768]{1,0:T(8,128)(2,1)} %get-tuple-element.76.qkv_ref, s32[4096,1]{1,0:T(8,128)S(1)} %copy.162.q_code_ref, s32[4,1,1024]{2,1,0:T(1,128)S(1)} %bitcast.239), custom_call_target="tpu_custom_call" | custom-call | flops 4294967296 | bytes 8388608 | tf_op jit(solution)/shard_map/pallas_call | solution.py:502
  230.6 74.2 %shard_map.318 = bf16[8,512,2048]{2,1,0:T(8,128)(2,1)} custom-call(bf16[512,2048]{1,0:T(8,128)(2,1)} %multiply_convert_fusion.7.refs_0_), custom_call_target="tpu_custom_call" | custom-call | bytes 1048576 | tf_op jit(solution)/shard_map/pallas_call | solution.py:628
  321.7 19.5 %fusion.11 = f32[704,4096]{1,0:T(8,128)} fusion(bf16[4096,2048]{1,0:T(8,128)(2,1)} %bitcast.248, bf16[2048,1408]{0,1:T(8,128)(2,1)} %all-gather.9.cloned.1.call-done), kind=kOutput, calls=%fused_computation.54 | convolution fusion | flops 11811160064 | bytes 31195136 | tf_op jit(solution)/shard_map/dot_general | solution.py:1192
  341.1 22.4 %multiply_convert_fusion.6 = (bf16[704,4096]{1,0:T(8,128)(2,1)}, f32[704,4096]{1,0:T(8,128)}) fusion(f32[704,4096]{1,0:T(8,128)} %fusion.11, bf16[4096,2048]{1,0:T(8,128)(2,1)} %bitcast.249, bf16[2048,1408]{0,1:T(8,128)(2,1)} %all-gather.9.cloned.1.call-done), kind=kOutput, calls=%fused_computation.13 | convolution fusion | flops 11828461568 | bytes 48496640 | tf_op jit(solution)/shard_map/dot_general | solution.py:1192
  363.6 21.2 %all-gather.13.cloned.1.call-done = bf16[2048,1408]{1,0:T(8,128)(2,1)} async-done(((bf16[512,1408]{1,0:T(8,128)(2,1)}), bf16[2048,1408]{1,0:T(8,128)(2,1)}) %all-gather.13.cloned.1.call-update) | async-done | bytes 5767184 | tf_op jit(solution)/shard_map/all_gather | solution.py:1323
  384.8 21.0 %fusion.52 = f32[2304,1408]{1,0:T(8,128)} fusion(bf16[2304,2048]{1,0:T(8,128)(2,1)} %bitcast.299, bf16[2048,1408]{1,0:T(8,128)(2,1)} %all-gather.13.cloned.1.call-done), kind=kOutput, calls=%fused_computation.183 | convolution fusion | flops 13287555072 | bytes 28180480 | tf_op jit(solution)/shard_map/dot_general | solution.py:1192
  460.9 25.1 %multiply_convert_fusion.4 = (bf16[704,4096]{1,0:T(8,128)(2,1)}, bf16[704,4096]{1,0:T(8,128)(2,1)}) fusion(f32[704,4096]{1,0:T(8,128)} %fusion.11, f32[704,4096]{1,0:T(8,128)} %get-tuple-element.275, bf16[704,2048]{1,0:T(8,128)(2,1)} %all-gather.11.cloned.1.call-done.down_ref, bf16[4096,2048]{1,0:T(8,128)(2,1)} %multiply_convert_fusion.cot_ref), kind=kOutput, calls=%fused_computation.11 | convolution fusion | flops 11848646656 | bytes 54263808 | tf_op jit(solution)/shard_map/dot_general | solution.py:1192
  488.6 44.1 %shard_map.320 = bf16[4,2112,512]{2,1,0:T(8,128)(2,1)} custom-call(bf16[704,4096]{1,0:T(8,128)(2,1)S(1)} %copy-done.5, bf16[704,4096]{1,0:T(8,128)(2,1)} %get-tuple-element.235.dgate_ref, bf16[704,4096]{1,0:T(8,128)(2,1)} %get-tuple-element.234.dup_ref, bf16[4096,2048]{1,0:T(8,128)(2,1)} %multiply_convert_fusion.cot_ref, bf16[4096,2048]{1,0:T(8,128)(2,1)} %bitcast.251), custom_call_target="tpu_custom_call" | custom-call | flops 35433480192 | bytes 59506688 | tf_op jit(solution)/shard_map/pallas_call | solution.py:1014
  540.9 20.7 %fusion.53 = f32[2304,1408]{1,0:T(8,128)} fusion(bf16[2304,2048]{1,0:T(8,128)(2,1)} %bitcast.300, bf16[2048,1408]{1,0:T(8,128)(2,1)} %all-gather.15.cloned.1.call-done), kind=kOutput, calls=%fused_computation.184 | convolution fusion | flops 13287555072 | bytes 28180480 | tf_op jit(solution)/shard_map/dot_general | solution.py:1192
  597.7 30.6 %multiply_convert_fusion.1 = (bf16[2304,1408]{1,0:T(8,128)(2,1)}, bf16[2304,1408]{1,0:T(8,128)(2,1)}, bf16[2304,1408]{1,0:T(8,128)(2,1)}) fusion(f32[2304,1408]{1,0:T(8,128)} %fusion.52, f32[2304,1408]{1,0:T(8,128)} %fusion.53, bf16[2304,2048]{1,0:T(8,128)(2,1)} %fusion, bf16[1408,2048]{1,0:T(8,128)(2,1)} %all-gather.17.cloned.1.call-done), kind=kOutput, calls=%fused_computation.6 | convolution fusion | flops 13336215552 | bytes 60620800 | tf_op jit(solution)/shard_map/dot_general | solution.py:1192
  628.4 19.8 %convolution_convert_fusion.4 = bf16[1408,2048]{1,0:T(8,128)(2,1)} fusion(bf16[2304,1408]{1,0:T(8,128)(2,1)} %get-tuple-element.233, bf16[2304,2048]{1,0:T(8,128)(2,1)} %fusion), kind=kOutput, calls=%fused_computation.23 | convolution fusion | flops 13290438656 | bytes 21692416 | tf_op jit(solution)/shard_map/dot_general | solution.py:1192
  650.4 20.1 %convolution_convert_fusion = bf16[2304,2048]{1,0:T(8,128)(2,1)} fusion(bf16[2304,1408]{1,0:T(8,128)(2,1)} %get-tuple-element.233, bf16[1408,2048]{1,0:T(8,128)(2,1)} %all-gather.17.cloned.1.call-done), kind=kOutput, calls=%fused_computation.16 | convolution fusion | flops 13292273664 | bytes 21692416 | tf_op jit(solution)/shard_map/dot_general | solution.py:1192
  670.5 35.9 %shard_map.319 = (bf16[512,2048]{1,0:T(8,128)(2,1)}, bf16[512,2048]{1,0:T(8,128)(2,1)}, bf16[512,2048]{1,0:T(8,128)(2,1)}, bf16[512,2048]{1,0:T(8,128)(2,1)}, f32[4096,128]{1,0:T(8,128)}) custom-call(bf16[704,4096]{1,0:T(8,128)(2,1)} %get-tuple-element.274.hidden_ref.hid_ref, bf16[704,2048]{1,0:T(8,128)(2,1)} %all-gather.11.cloned.1.call-done.down_ref, ...), custom_call_target="tpu_custom_call" | custom-call | flops 16642998272 | bytes 50331648 | tf_op jit(solution)/shard_map/pallas_call | solution.py:793
  706.4 20.5 %convolution_convert_fusion.3 = bf16[2048,1408]{1,0:T(8,128)(2,1)} fusion(bf16[2304,2048]{1,0:T(8,128)(2,1)} %bitcast.301, bf16[2304,1408]{1,0:T(8,128)(2,1)} %get-tuple-element.232), kind=kOutput, calls=%fused_computation.22 | convolution fusion | flops 13290438656 | bytes 21692416 | tf_op jit(solution)/shard_map/dot_general | solution.py:1192
  743.8 20.3 %convolution_convert_fusion.2 = bf16[2048,1408]{1,0:T(8,128)(2,1)} fusion(bf16[2304,2048]{1,0:T(8,128)(2,1)} %bitcast.302, bf16[2304,1408]{1,0:T(8,128)(2,1)} %get-tuple-element.231), kind=kOutput, calls=%fused_computation.21 | convolution fusion | flops 13290438656 | bytes 21692416 | tf_op jit(solution)/shard_map/dot_general | solution.py:1192
  764.1 20.7 %fusion.54 = f32[2304,2048]{1,0:T(8,128)} fusion(bf16[2304,1408]{1,0:T(8,128)(2,1)} %get-tuple-element.232, bf16[2048,1408]{1,0:T(8,128)(2,1)} %all-gather.13.cloned.1.call-done), kind=kOutput, calls=%fused_computation.185 | convolution fusion | flops 13287555072 | bytes 31129600 | tf_op jit(solution)/shard_map/dot_general | solution.py:1192
  784.8 21.9 %add_convert_fusion = bf16[2304,2048]{1,0:T(8,128)(2,1)} fusion(f32[2304,2048]{1,0:T(8,128)} %fusion.54, bf16[2304,1408]{1,0:T(8,128)(2,1)} %get-tuple-element.231, bf16[2048,1408]{1,0:T(8,128)(2,1)} %all-gather.15.cloned.1.call-done), kind=kOutput, calls=%fused_computation.5 | convolution fusion | flops 13296992256 | bytes 40566784 | tf_op jit(solution)/shard_map/dot_general | solution.py:1192
  808.9 95.8 %shard_map.321 = f32[512,2048]{1,0:T(8,128)} custom-call(bf16[704,4096]{1,0:T(8,128)(2,1)} %get-tuple-element.235.dgate_ref, bf16[704,4096]{1,0:T(8,128)(2,1)} %get-tuple-element.234.dup_ref, bf16[704,2048]{1,0:T(8,128)(2,1)} %get-tuple-element.245.gate_ref, bf16[704,2048]{1,0:T(8,128)(2,1)} %get-tuple-element.244.up_ref, bf16[8,288,2048]{2,1,0:T(8,128)(2,1)} %bitcast.303, ...), custom_call_target="tpu_custom_call" | custom-call | flops 28454158336 | bytes 33554432 | tf_op jit(solution)/shard_map/pallas_call | solution.py:976
  964.5 30.7 %shard_map.322.grads_ref = bf16[4096,768]{1,0:T(8,128)(2,1)} custom-call(bf16[4096,768]{1,0:T(8,128)(2,1)} %get-tuple-element.76.qkv_ref, bf16[4096,256]{1,0:T(8,128)(2,1)} %bitcast.54.grad_ref, s32[4096,1]{1,0:T(8,128)S(1)} %copy.162.q_code_ref, s32[4,1,1024]{2,1,0:T(1,128)S(1)} %bitcast.240), custom_call_target="tpu_custom_call" | custom-call | flops 10737418240 | bytes 12582912 | tf_op jit(solution)/shard_map/pallas_call | solution.py:502
  995.1 35.6 %collective-permute-done.11 = bf16[256,2048]{1,0:T(8,128)(2,1)S(1)} collective-permute-done((bf16[256,2048]{1,0:T(8,128)(2,1)}, bf16[256,2048]{1,0:T(8,128)(2,1)S(1)}, u32[]{:S(2)}, u32[]{:S(2)}) %collective-permute-start.11) | collective-permute-done | bytes 1048608 | tf_op jit(solution)/shard_map/ppermute | solution.py:1156
  1031.1 22.8 %collective-permute-done.13 = bf16[256,2048]{1,0:T(8,128)(2,1)} collective-permute-done((bf16[256,2048]{1,0:T(8,128)(2,1)}, bf16[256,2048]{1,0:T(8,128)(2,1)}, u32[]{:S(2)}, u32[]{:S(2)}) %collective-permute-start.13) | collective-permute-done | bytes 1048608 | tf_op jit(solution)/shard_map/ppermute | solution.py:1156
  1087.8 20.8 %shard_map.323 = (bf16[512,2048]{1,0:T(8,128)(2,1)S(1)}, bf16[512,2048]{1,0:T(8,128)(2,1)}, bf16[512,2048]{1,0:T(8,128)(2,1)}, bf16[512,2048]{1,0:T(8,128)(2,1)}) custom-call(bf16[4096,768]{1,0:T(8,128)(2,1)} %shard_map.322.grads_ref, bf16[2048,768]{1,0:T(8,128)(2,1)} %copy-done.2), custom_call_target="tpu_custom_call" | custom-call | flops 12884901888 | bytes 33554432 | tf_op jit(solution)/shard_map/pallas_call | solution.py:1122
  (313 shorter events, 425.2 us)
Async XLA Ops:
  7.2 103.8 %all-gather.7.cloned.1.call-start = ((), (), s32[]{:S(2)}) async-start(), calls=%async_computation.12 | async-start | bytes 5898240 | tf_op jit(solution)/shard_map/all_gather | solution.py:1257
  18.7 211.9 %all-gather.9.cloned.1.call-start = ((), (), s32[]{:S(2)}) async-start(), calls=%async_computation.13 | async-start | bytes 7208960 | tf_op jit(solution)/shard_map/all_gather | solution.py:1314
  22.6 341.0 %all-gather.11.cloned.1.call-start = ((), (), s32[]{:S(2)}) async-start(), calls=%async_computation.14 | async-start | bytes 3604480 | tf_op jit(solution)/shard_map/all_gather | solution.py:1316
  24.2 360.6 %all-gather.13.cloned.1.call-start = ((), (), s32[]{:S(2)}) async-start(), calls=%async_computation.15 | async-start | bytes 7208960 | tf_op jit(solution)/shard_map/all_gather | solution.py:1323
  106.0 434.9 %all-gather.15.cloned.1.call-start = ((), (), s32[]{:S(2)}) async-start(), calls=%async_computation.16 | async-start | bytes 7208960 | tf_op jit(solution)/shard_map/all_gather | solution.py:1324
  113.6 58.1 %collective-permute-start.2 = (bf16[4,64,2048]{2,1,0:T(8,128)(2,1)}, bf16[4,64,2048]{2,1,0:T(8,128)(2,1)}, u32[]{:S(2)}, u32[]{:S(2)}) collective-permute-start(bf16[4,64,2048]{2,1,0:T(8,128)(2,1)} %reshape.659), channel_id=1, source_target_pairs={{0,24},{8,16},{16,8},{24,0},{1,25},{9,17},{17,9},{25,1},{2,26},{10... | collective-permute-start | bytes 3145736 | tf_op jit(solution)/shard_map/ppermute | solution.py:1156
  116.0 55.7 %collective-permute-start.1 = (bf16[4,64,2048]{2,1,0:T(8,128)(2,1)}, bf16[4,64,2048]{2,1,0:T(8,128)(2,1)}, u32[]{:S(2)}, u32[]{:S(2)}) collective-permute-start(bf16[4,64,2048]{2,1,0:T(8,128)(2,1)} %reshape.659), channel_id=1, source_target_pairs={{0,16},{8,24},{16,0},{24,8},{1,17},{9,25},{17,1},{25,9},{2,18},{10... | collective-permute-start | bytes 3145736 | tf_op jit(solution)/shard_map/ppermute | solution.py:1156
  116.6 55.1 %collective-permute-start = (bf16[4,64,2048]{2,1,0:T(8,128)(2,1)}, bf16[4,64,2048]{2,1,0:T(8,128)(2,1)}, u32[]{:S(2)}, u32[]{:S(2)}) collective-permute-start(bf16[4,64,2048]{2,1,0:T(8,128)(2,1)} %reshape.659), channel_id=1, source_target_pairs={{0,8},{8,0},{16,24},{24,16},{1,9},{9,1},{17,25},{25,17},{2,10},{10... | collective-permute-start | bytes 3145736 | tf_op jit(solution)/shard_map/ppermute | solution.py:1156
  187.3 410.4 %all-gather.17.cloned.1.call-start = ((), (), s32[]{:S(2)}) async-start(), calls=%async_computation.17 | async-start | bytes 7208960 | tf_op jit(solution)/shard_map/all_gather | solution.py:1325
  304.8 101.0 %collective-permute-start.6 = (bf16[512,2048]{1,0:T(8,128)(2,1)}, bf16[512,2048]{1,0:T(8,128)(2,1)}, u32[]{:S(2)}, u32[]{:S(2)}) collective-permute-start(bf16[512,2048]{1,0:T(8,128)(2,1)} %bitcast.243), channel_id=1, source_target_pairs={{0,24},{8,16},{16,8},{24,0},{1,25},{9,17},{17,9},{25,1},{2,26},{10... | collective-permute-start | bytes 6291464 | tf_op jit(solution)/shard_map/ppermute | solution.py:1156
  306.3 99.5 %collective-permute-start.5 = (bf16[512,2048]{1,0:T(8,128)(2,1)}, bf16[512,2048]{1,0:T(8,128)(2,1)}, u32[]{:S(2)}, u32[]{:S(2)}) collective-permute-start(bf16[512,2048]{1,0:T(8,128)(2,1)} %bitcast.244), channel_id=1, source_target_pairs={{0,16},{8,24},{16,0},{24,8},{1,17},{9,25},{17,1},{25,9},{2,18},{10... | collective-permute-start | bytes 6291464 | tf_op jit(solution)/shard_map/ppermute | solution.py:1156
  307.6 98.1 %collective-permute-start.4 = (bf16[512,2048]{1,0:T(8,128)(2,1)}, bf16[512,2048]{1,0:T(8,128)(2,1)}, u32[]{:S(2)}, u32[]{:S(2)}) collective-permute-start(bf16[512,2048]{1,0:T(8,128)(2,1)} %bitcast.245), channel_id=1, source_target_pairs={{0,8},{8,0},{16,24},{24,16},{1,9},{9,1},{17,25},{25,17},{2,10},{10... | collective-permute-start | bytes 6291464 | tf_op jit(solution)/shard_map/ppermute | solution.py:1156
  412.6 394.4 %reduce-scatter.7.cloned.1.call-start = ((), (), s32[]{:S(2)}) async-start(), calls=%async_computation.18 | async-start | bytes 10813440 | tf_op jit(solution)/shard_map/reduce_scatter | solution.py:1389
  532.7 431.8 %reduce-scatter.9.cloned.1.call-start = ((), (), s32[]{:S(2)}) async-start(), calls=%async_computation.19 | async-start | bytes 7208960 | tf_op jit(solution)/shard_map/reduce_scatter | solution.py:1389
  648.2 439.6 %reduce-scatter.11.cloned.1.call-start = ((), (), s32[]{:S(2)}) async-start(), calls=%async_computation.20 | async-start | bytes 7208960 | tf_op jit(solution)/shard_map/reduce_scatter | solution.py:1389
  734.0 72.9 %collective-permute-start.8 = (bf16[512,2048]{1,0:T(8,128)(2,1)}, bf16[512,2048]{1,0:T(8,128)(2,1)}, u32[]{:S(2)}, u32[]{:S(2)}) collective-permute-start(bf16[512,2048]{1,0:T(8,128)(2,1)} %get-tuple-element.92), channel_id=1, source_target_pairs={{0,8},{8,0},{16,24},{24,16},{1,9},{9,1},{17,25},{25,17},{2,10},{10... | collective-permute-start | bytes 6291464 | tf_op jit(solution)/shard_map/ppermute | solution.py:1156
  735.4 71.5 %collective-permute-start.9 = (bf16[512,2048]{1,0:T(8,128)(2,1)}, bf16[512,2048]{1,0:T(8,128)(2,1)}, u32[]{:S(2)}, u32[]{:S(2)}) collective-permute-start(bf16[512,2048]{1,0:T(8,128)(2,1)} %get-tuple-element.93), channel_id=1, source_target_pairs={{0,16},{8,24},{16,0},{24,8},{1,17},{9,25},{17,1},{25,9},{2,18},{10... | collective-permute-start | bytes 6291464 | tf_op jit(solution)/shard_map/ppermute | solution.py:1156
  740.4 66.4 %all-to-all-start.1 = ((f32[8,2,512]{2,1,0:T(2,128)}), f32[8,2,512]{2,1,0:T(2,128)S(1)}, u32[]{:S(2)}, u32[]{:S(2)}) async-start(f32[8,2,512]{2,1,0:T(2,128)} %gather_fusion.1), calls=%async_computation.2 | async-start | bytes 65536 | tf_op jit(solution)/shard_map/all_to_all | solution.py:1434
  743.8 367.1 %reduce-scatter.17.cloned.1.call-start = ((), (), s32[]{:S(2)}) async-start(), calls=%async_computation.23 | async-start | bytes 7208960 | tf_op jit(solution)/shard_map/reduce_scatter | solution.py:1389
  937.2 199.3 %reduce-scatter.13.cloned.1.call-start = ((), (), s32[]{:S(2)}) async-start(), calls=%async_computation.21 | async-start | bytes 3932160 | tf_op jit(solution)/shard_map/reduce_scatter | solution.py:1489
  937.3 150.5 %collective-permute-start.14 = (bf16[512,2048]{1,0:T(8,128)(2,1)}, bf16[512,2048]{1,0:T(8,128)(2,1)}, u32[]{:S(2)}, u32[]{:S(2)}) collective-permute-start(bf16[512,2048]{1,0:T(8,128)(2,1)} %get-tuple-element.111), channel_id=1, source_target_pairs={{0,24},{8,16},{16,8},{24,0},{1,25},{9,17},{17,9},{25,1},{2,26},{10... | collective-permute-start | bytes 6291464 | tf_op jit(solution)/shard_map/ppermute | solution.py:1156
  955.0 75.7 %collective-permute-start.11 = (bf16[256,2048]{1,0:T(8,128)(2,1)}, bf16[256,2048]{1,0:T(8,128)(2,1)S(1)}, u32[]{:S(2)}, u32[]{:S(2)}) collective-permute-start(bf16[256,2048]{1,0:T(8,128)(2,1)} %get-tuple-element.238), channel_id=1, source_target_pairs={{0,8},{8,0},{16,24},{24,16},{1,9},{9,1},{17,25},{25,17},{2,10},{10... | collective-permute-start | bytes 3145736 | tf_op jit(solution)/shard_map/ppermute | solution.py:1156
  955.6 75.5 %collective-permute-start.12 = (bf16[256,2048]{1,0:T(8,128)(2,1)}, bf16[256,2048]{1,0:T(8,128)(2,1)}, u32[]{:S(2)}, u32[]{:S(2)}) collective-permute-start(bf16[256,2048]{1,0:T(8,128)(2,1)} %get-tuple-element.237), channel_id=1, source_target_pairs={{0,16},{8,24},{16,0},{24,8},{1,17},{9,25},{17,1},{25,9},{2,18},{10... | collective-permute-start | bytes 3145736 | tf_op jit(solution)/shard_map/ppermute | solution.py:1156
  955.6 98.2 %collective-permute-start.13 = (bf16[256,2048]{1,0:T(8,128)(2,1)}, bf16[256,2048]{1,0:T(8,128)(2,1)}, u32[]{:S(2)}, u32[]{:S(2)}) collective-permute-start(bf16[256,2048]{1,0:T(8,128)(2,1)} %get-tuple-element.236), channel_id=1, source_target_pairs={{0,24},{8,16},{16,8},{24,0},{1,25},{9,17},{17,9},{25,1},{2,26},{10... | collective-permute-start | bytes 3145736 | tf_op jit(solution)/shard_map/ppermute | solution.py:1156
  (57 other events, 1488.5 us)
Sparse Core Ops, SparseCore 0:
  18.8 92.0 all-gather.6
  113.1 105.1 all-gather.8
  220.5 57.4 all-gather.10
  279.4 105.3 all-gather.12
  386.2 104.9 all-gather.14
  492.7 104.9 all-gather.16
  600.1 146.8 reduce-scatter.6
  749.3 103.0 reduce-scatter.8
  854.7 102.7 reduce-scatter.10
  959.6 102.7 reduce-scatter.16
  1075.1 56.8 reduce-scatter.12
  1173.7 24.2 reduce-scatter.14

commit v13 on v12

--- a/solution.py
+++ b/solution.py
@@ -1416,7 +1416,7 @@
         mm(gate_grad_e, ex_gate, ((1,), (1,))) + mm(up_grad_e, ex_up, ((1,), (1,)))
     )
 
-    out_got = [out_near[0]] + [swap(out_near[k], k) for k in (1, 2)]
+    out_got = hops(out_near)
     slots, out_got, _ = lax.optimization_barrier((slots, out_got, (shared_sums, grads_made)))
     n2_grad = n2_grad_sum(
         gate_grad_s,
@@ -1426,7 +1426,6 @@
         rows_grad.reshape(plane, capacity, width),
         slots,
     )
-    out_far = swap(after(out_near[3], n2_grad), 3)
 
     dots = dots.reshape(plane, tokens, 128)[:, :, :2].transpose(0, 2, 1)
     back = jnp.arange(plane, dtype=jnp.int32) ^ me
@@ -1447,7 +1446,7 @@
 
     attended_grad = low(mm(low_residual, w_out_full, ((1,), (1,))))
     low_residual = after(low_residual, attended_grad)
-    output = residual + sum_up(after(out_got, attended_grad))
+    output = low(residual + sum_up(after(out_got, attended_grad)))
     attended_grad = to_columns(attended_grad)
     grad_out = low(mm(attended, low_residual, ((0,), (0,))))
     grad_out = grad_out.reshape(groups, halves, width // plane, width)
@@ -1480,10 +1479,9 @@
         .transpose(1, 0, 2, 3)
         .reshape(width, 3 * head_cols)
     )
-    qkv_grad, small_grads, out_far, _ = lax.optimization_barrier(
-        (qkv_grad, small_grads, out_far, (grad_qkv, grads[1]))
-    )
-    output = low(output + out_far.astype(jnp.float32))
+    qkv_grad, small_grads, _ = lax.optimization_barrier(
+        (qkv_grad, small_grads, (grad_qkv, grads[1]))
+    )
     n1_near = n1_grad_parts(qkv_grad, w_qkv, plane)
     grad_out = low(sum_up(out_grad_got))
     grad_qkv = lax.psum_scatter(grad_qkv, DP, scatter_dimension=0, tiled=True)

time: 1220 us -> 1200 us (0.984)
  waiting for transfers between devices: 129 us -> 111 us
    ppermute x16, waiting for transfers between devices: 71.9 us -> 21.9 us  [swap(): return lax.ppermute(values, EXP, [(i, i ^ bits) for i in range(4)])]
    all_to_all x1, waiting for transfers between devices: 0.01 us -> 20.9 us  [local_plane(): dots = lax.all_to_all(dots, PLANE, split_axis=0, concat_axis=0, tiled=True)]
    convert_element_type x8 -> x9, other arithmetic: 48.3 us -> 57.2 us  [low(): return values.astype(jnp.bfloat16)]
    unnamed x103 -> x99, local copies, waits for them, and re-layouts: 39.7 us -> 39.6 us
  transfers between devices with their start and end apart: 38 -> 38, of which waited for: 11 -> 13; matrix products, arithmetic and copies ran while one was open for 47% -> 48% of each run, Pallas kernels for 35% -> 36%
where the time goes in v13:
time: 1200 us; the launch traced here: 1190 us
  Pallas kernels  424 us (35%)
  matrix products  347 us (29%)
  other arithmetic  131 us (11%)
  local copies, waits for them, and re-layouts  117 us (10%)
  waiting for transfers between devices  111 us (9%)
  starting transfers between devices  45.5 us (4%)
  between operations  15.4 us (1%)
    dot_general x20, matrix products, mm(): lax.dot_general(left, right, (dims, ((), ())), preferred_element_type=jnp...  320 us
    pallas_call x2, Pallas kernels, plane_gather(): pl.pallas_call(partial(plane_gather_kernel, info is not None, relative),...  155 us
    pallas_call x1, Pallas kernels, n2_grad_sum(): pl.pallas_call(n2_grad_kernel, grid=(blocks,), in_specs=[by_units, by_uni...  95.1 us
    convert_element_type x9, other arithmetic, low(): return values.astype(jnp.bfloat16)  57.2 us
    pallas_call x2, Pallas kernels, attention_call(): pl.pallas_call(partial(body, heads, step), grid=(rows // seq_len,), in_sp...  50 us
    pallas_call x1, Pallas kernels, unit_grads(): pl.pallas_call(unit_grad_kernel, grid=(depth * halves,), in_specs=[whole,...  44.1 us
    unnamed x99, local copies, waits for them, and re-layouts  39.6 us
    pallas_call x1, Pallas kernels, output_parts(): pl.pallas_call(partial(output_kernel, half), grid=(blocks,), in_specs=[pl...  35.9 us
  transfers between devices with their start and end apart: 38, of which 13 were waited for; matrix products, arithmetic and copies ran while one was open for 48% of the time, Pallas kernels for 36%

profile of v13, /device:TPU:0, one launch (start us, length us, event | category | flops | bytes accessed | tf_op | source)
XLA Modules:
  0.0 1191.0 jit_solution(14054216025207426995)
XLA Ops:
  24.9 81.1 %shard_map.315 = (bf16[8,512,2048]{2,1,0:T(8,128)(2,1)}, s32[8,8,512]{2,1,0:T(8,128)}) custom-call(bf16[512,2048]{1,0:T(8,128)(2,1)} %bitcast.241, s32[8,512]{1,0:T(8,128)} %concatenate.56.refs_1_), custom_call_target="tpu_custom_call" | custom-call | bytes 1048576 | tf_op jit(solution)/shard_map/pallas_call | solution.py:628
  123.8 22.3 %shard_map.316 = (bf16[4096,2048]{1,0:T(8,128)(2,1)}, bf16[4096,768]{1,0:T(8,128)(2,1)}) custom-call(bf16[4096,2048]{1,0:T(8,128)(2,1)} %bitcast.296, f32[1,2048]{1,0:T(1,128)S(1)} %copy.161.gain_ref, bf16[2048,768]{1,0:T(8,128)(2,1)S(1)} %slice.192.w_ref), custom_call_target="tpu_custom_call" | custom-call | flops 12884901888 | bytes 33554432 | tf_op jit(solution)/shard_map/pallas_call | solution.py:655
  146.1 19.4 %shard_map.317 = bf16[4096,256]{1,0:T(8,128)(2,1)S(1)} custom-call(bf16[4096,768]{1,0:T(8,128)(2,1)} %get-tuple-element.76.qkv_ref, s32[4096,1]{1,0:T(8,128)S(1)} %copy.162.q_code_ref, s32[4,1,1024]{2,1,0:T(1,128)S(1)} %bitcast.238), custom_call_target="tpu_custom_call" | custom-call | flops 4294967296 | bytes 8388608 | tf_op jit(solution)/shard_map/pallas_call | solution.py:502
  230.7 74.2 %shard_map.318 = bf16[8,512,2048]{2,1,0:T(8,128)(2,1)} custom-call(bf16[512,2048]{1,0:T(8,128)(2,1)} %multiply_convert_fusion.7.refs_0_), custom_call_target="tpu_custom_call" | custom-call | bytes 1048576 | tf_op jit(solution)/shard_map/pallas_call | solution.py:628
  321.7 19.5 %fusion.11 = f32[704,4096]{1,0:T(8,128)} fusion(bf16[4096,2048]{1,0:T(8,128)(2,1)} %bitcast.247, bf16[2048,1408]{0,1:T(8,128)(2,1)} %all-gather.9.cloned.1.call-done), kind=kOutput, calls=%fused_computation.53 | convolution fusion | flops 11811160064 | bytes 31195136 | tf_op jit(solution)/shard_map/dot_general | solution.py:1192
  341.2 22.5 %multiply_convert_fusion.6 = (bf16[704,4096]{1,0:T(8,128)(2,1)}, f32[704,4096]{1,0:T(8,128)}) fusion(f32[704,4096]{1,0:T(8,128)} %fusion.11, bf16[4096,2048]{1,0:T(8,128)(2,1)} %bitcast.248, bf16[2048,1408]{0,1:T(8,128)(2,1)} %all-gather.9.cloned.1.call-done), kind=kOutput, calls=%fused_computation.13 | convolution fusion | flops 11828461568 | bytes 48496640 | tf_op jit(solution)/shard_map/dot_general | solution.py:1192
  363.6 21.2 %all-gather.13.cloned.1.call-done = bf16[2048,1408]{1,0:T(8,128)(2,1)} async-done(((bf16[512,1408]{1,0:T(8,128)(2,1)}), bf16[2048,1408]{1,0:T(8,128)(2,1)}) %all-gather.13.cloned.1.call-update) | async-done | bytes 5767184 | tf_op jit(solution)/shard_map/all_gather | solution.py:1323
  384.8 21.0 %fusion.53 = f32[2304,1408]{1,0:T(8,128)} fusion(bf16[2304,2048]{1,0:T(8,128)(2,1)} %bitcast.297, bf16[2048,1408]{1,0:T(8,128)(2,1)} %all-gather.13.cloned.1.call-done), kind=kOutput, calls=%fused_computation.183 | convolution fusion | flops 13287555072 | bytes 28180480 | tf_op jit(solution)/shard_map/dot_general | solution.py:1192
  460.8 25.1 %multiply_convert_fusion.4 = (bf16[704,4096]{1,0:T(8,128)(2,1)}, bf16[704,4096]{1,0:T(8,128)(2,1)}) fusion(f32[704,4096]{1,0:T(8,128)} %fusion.11, f32[704,4096]{1,0:T(8,128)} %get-tuple-element.276, bf16[704,2048]{1,0:T(8,128)(2,1)} %all-gather.11.cloned.1.call-done.down_ref, bf16[4096,2048]{1,0:T(8,128)(2,1)} %multiply_convert_fusion.cot_ref), kind=kOutput, calls=%fused_computation.11 | convolution fusion | flops 11848646656 | bytes 54263808 | tf_op jit(solution)/shard_map/dot_general | solution.py:1192
  488.6 44.1 %shard_map.320 = bf16[4,2112,512]{2,1,0:T(8,128)(2,1)} custom-call(bf16[704,4096]{1,0:T(8,128)(2,1)S(1)} %copy-done.5, bf16[704,4096]{1,0:T(8,128)(2,1)} %get-tuple-element.236.dgate_ref, bf16[704,4096]{1,0:T(8,128)(2,1)} %get-tuple-element.235.dup_ref, bf16[4096,2048]{1,0:T(8,128)(2,1)} %multiply_convert_fusion.cot_ref, bf16[4096,2048]{1,0:T(8,128)(2,1)} %bitcast.250), custom_call_target="tpu_custom_call" | custom-call | flops 35433480192 | bytes 59506688 | tf_op jit(solution)/shard_map/pallas_call | solution.py:1014
  540.8 20.8 %fusion.54 = f32[2304,1408]{1,0:T(8,128)} fusion(bf16[2304,2048]{1,0:T(8,128)(2,1)} %bitcast.298, bf16[2048,1408]{1,0:T(8,128)(2,1)} %all-gather.15.cloned.1.call-done), kind=kOutput, calls=%fused_computation.184 | convolution fusion | flops 13287555072 | bytes 28180480 | tf_op jit(solution)/shard_map/dot_general | solution.py:1192
  597.7 30.7 %multiply_convert_fusion.1 = (bf16[2304,1408]{1,0:T(8,128)(2,1)}, bf16[2304,1408]{1,0:T(8,128)(2,1)}, bf16[2304,1408]{1,0:T(8,128)(2,1)}) fusion(f32[2304,1408]{1,0:T(8,128)} %fusion.53, f32[2304,1408]{1,0:T(8,128)} %fusion.54, bf16[2304,2048]{1,0:T(8,128)(2,1)} %fusion, bf16[1408,2048]{1,0:T(8,128)(2,1)} %all-gather.17.cloned.1.call-done), kind=kOutput, calls=%fused_computation.6 | convolution fusion | flops 13336215552 | bytes 60620800 | tf_op jit(solution)/shard_map/dot_general | solution.py:1192
  628.4 19.8 %convolution_convert_fusion.4 = bf16[1408,2048]{1,0:T(8,128)(2,1)} fusion(bf16[2304,1408]{1,0:T(8,128)(2,1)} %get-tuple-element.234, bf16[2304,2048]{1,0:T(8,128)(2,1)} %fusion), kind=kOutput, calls=%fused_computation.23 | convolution fusion | flops 13290438656 | bytes 21692416 | tf_op jit(solution)/shard_map/dot_general | solution.py:1192
  650.4 20.1 %convolution_convert_fusion = bf16[2304,2048]{1,0:T(8,128)(2,1)} fusion(bf16[2304,1408]{1,0:T(8,128)(2,1)} %get-tuple-element.234, bf16[1408,2048]{1,0:T(8,128)(2,1)} %all-gather.17.cloned.1.call-done), kind=kOutput, calls=%fused_computation.16 | convolution fusion | flops 13292273664 | bytes 21692416 | tf_op jit(solution)/shard_map/dot_general | solution.py:1192
  670.6 35.9 %shard_map.319 = (bf16[512,2048]{1,0:T(8,128)(2,1)}, bf16[512,2048]{1,0:T(8,128)(2,1)}, bf16[512,2048]{1,0:T(8,128)(2,1)}, bf16[512,2048]{1,0:T(8,128)(2,1)}, f32[4096,128]{1,0:T(8,128)}) custom-call(bf16[704,4096]{1,0:T(8,128)(2,1)} %get-tuple-element.275.hidden_ref.hid_ref, bf16[704,2048]{1,0:T(8,128)(2,1)} %all-gather.11.cloned.1.call-done.down_ref, ...), custom_call_target="tpu_custom_call" | custom-call | flops 16642998272 | bytes 50331648 | tf_op jit(solution)/shard_map/pallas_call | solution.py:793
  706.5 20.7 %convolution_convert_fusion.3 = bf16[2048,1408]{1,0:T(8,128)(2,1)} fusion(bf16[2304,2048]{1,0:T(8,128)(2,1)} %bitcast.299, bf16[2304,1408]{1,0:T(8,128)(2,1)} %get-tuple-element.233), kind=kOutput, calls=%fused_computation.22 | convolution fusion | flops 13290438656 | bytes 21692416 | tf_op jit(solution)/shard_map/dot_general | solution.py:1192
  745.0 20.3 %convolution_convert_fusion.2 = bf16[2048,1408]{1,0:T(8,128)(2,1)} fusion(bf16[2304,2048]{1,0:T(8,128)(2,1)} %bitcast.300, bf16[2304,1408]{1,0:T(8,128)(2,1)} %get-tuple-element.232), kind=kOutput, calls=%fused_computation.21 | convolution fusion | flops 13290438656 | bytes 21692416 | tf_op jit(solution)/shard_map/dot_general | solution.py:1192
  765.3 20.8 %fusion.55 = f32[2304,2048]{1,0:T(8,128)} fusion(bf16[2304,1408]{1,0:T(8,128)(2,1)} %get-tuple-element.233, bf16[2048,1408]{1,0:T(8,128)(2,1)} %all-gather.13.cloned.1.call-done), kind=kOutput, calls=%fused_computation.185 | convolution fusion | flops 13287555072 | bytes 31129600 | tf_op jit(solution)/shard_map/dot_general | solution.py:1192
  786.1 22.0 %add_convert_fusion = bf16[2304,2048]{1,0:T(8,128)(2,1)} fusion(f32[2304,2048]{1,0:T(8,128)} %fusion.55, bf16[2304,1408]{1,0:T(8,128)(2,1)} %get-tuple-element.232, bf16[2048,1408]{1,0:T(8,128)(2,1)} %all-gather.15.cloned.1.call-done), kind=kOutput, calls=%fused_computation.5 | convolution fusion | flops 13296992256 | bytes 40566784 | tf_op jit(solution)/shard_map/dot_general | solution.py:1192
  808.1 20.9 %all-to-all-done.1 = f32[8,2,512]{2,1,0:T(2,128)S(1)} async-done(((f32[8,2,512]{2,1,0:T(2,128)}), f32[8,2,512]{2,1,0:T(2,128)S(1)}, u32[]{:S(2)}, u32[]{:S(2)}) %all-to-all-start.1) | async-done | bytes 32800 | tf_op jit(solution)/shard_map/all_to_all | solution.py:1433
  833.8 95.1 %shard_map.321 = f32[512,2048]{1,0:T(8,128)} custom-call(bf16[704,4096]{1,0:T(8,128)(2,1)} %get-tuple-element.236.dgate_ref, bf16[704,4096]{1,0:T(8,128)(2,1)} %get-tuple-element.235.dup_ref, bf16[704,2048]{1,0:T(8,128)(2,1)} %get-tuple-element.246.gate_ref, bf16[704,2048]{1,0:T(8,128)(2,1)} %get-tuple-element.245.up_ref, bf16[8,288,2048]{2,1,0:T(8,128)(2,1)} %bitcast.301, ...), custom_call_target="tpu_custom_call" | custom-call | flops 28454158336 | bytes 33554432 | tf_op jit(solution)/shard_map/pallas_call | solution.py:976
  991.5 30.6 %shard_map.322.grads_ref = bf16[4096,768]{1,0:T(8,128)(2,1)} custom-call(bf16[4096,768]{1,0:T(8,128)(2,1)} %get-tuple-element.76.qkv_ref, bf16[4096,256]{1,0:T(8,128)(2,1)} %bitcast.55.grad_ref, s32[4096,1]{1,0:T(8,128)S(1)} %copy.162.q_code_ref, s32[4,1,1024]{2,1,0:T(1,128)S(1)} %bitcast.239), custom_call_target="tpu_custom_call" | custom-call | flops 10737418240 | bytes 12582912 | tf_op jit(solution)/shard_map/pallas_call | solution.py:502
  1036.0 19.5 %convolution_convert_fusion.7 = bf16[2048,768]{1,0:T(8,128)(2,1)S(1)} fusion(bf16[4096,2048]{1,0:T(8,128)(2,1)} %get-tuple-element.113, bf16[4096,768]{1,0:T(8,128)(2,1)} %shard_map.322.grads_ref), kind=kOutput, calls=%fused_computation.47 | convolution fusion | flops 12886474752 | bytes 26214400 | tf_op jit(solution)/shard_map/dot_general | solution.py:1192
  1070.3 20.9 %shard_map.323 = (bf16[512,2048]{1,0:T(8,128)(2,1)S(1)}, bf16[512,2048]{1,0:T(8,128)(2,1)}, bf16[512,2048]{1,0:T(8,128)(2,1)}, bf16[512,2048]{1,0:T(8,128)(2,1)}) custom-call(bf16[4096,768]{1,0:T(8,128)(2,1)} %shard_map.322.grads_ref, bf16[2048,768]{1,0:T(8,128)(2,1)} %copy-done.2), custom_call_target="tpu_custom_call" | custom-call | flops 12884901888 | bytes 33554432 | tf_op jit(solution)/shard_map/pallas_call | solution.py:1122
  (308 shorter events, 427.4 us)
Async XLA Ops:
  7.2 103.8 %all-gather.7.cloned.1.call-start = ((), (), s32[]{:S(2)}) async-start(), calls=%async_computation.12 | async-start | bytes 5898240 | tf_op jit(solution)/shard_map/all_gather | solution.py:1257
  18.7 211.9 %all-gather.9.cloned.1.call-start = ((), (), s32[]{:S(2)}) async-start(), calls=%async_computation.13 | async-start | bytes 7208960 | tf_op jit(solution)/shard_map/all_gather | solution.py:1314
  22.6 341.0 %all-gather.11.cloned.1.call-start = ((), (), s32[]{:S(2)}) async-start(), calls=%async_computation.14 | async-start | bytes 3604480 | tf_op jit(solution)/shard_map/all_gather | solution.py:1316
  24.2 360.6 %all-gather.13.cloned.1.call-start = ((), (), s32[]{:S(2)}) async-start(), calls=%async_computation.15 | async-start | bytes 7208960 | tf_op jit(solution)/shard_map/all_gather | solution.py:1323
  106.0 434.8 %all-gather.15.cloned.1.call-start = ((), (), s32[]{:S(2)}) async-start(), calls=%async_computation.16 | async-start | bytes 7208960 | tf_op jit(solution)/shard_map/all_gather | solution.py:1324
  113.6 58.1 %collective-permute-start.2 = (bf16[4,64,2048]{2,1,0:T(8,128)(2,1)}, bf16[4,64,2048]{2,1,0:T(8,128)(2,1)}, u32[]{:S(2)}, u32[]{:S(2)}) collective-permute-start(bf16[4,64,2048]{2,1,0:T(8,128)(2,1)} %reshape.659), channel_id=1, source_target_pairs={{0,24},{8,16},{16,8},{24,0},{1,25},{9,17},{17,9},{25,1},{2,26},{10... | collective-permute-start | bytes 3145736 | tf_op jit(solution)/shard_map/ppermute | solution.py:1156
  116.0 55.7 %collective-permute-start.1 = (bf16[4,64,2048]{2,1,0:T(8,128)(2,1)}, bf16[4,64,2048]{2,1,0:T(8,128)(2,1)}, u32[]{:S(2)}, u32[]{:S(2)}) collective-permute-start(bf16[4,64,2048]{2,1,0:T(8,128)(2,1)} %reshape.659), channel_id=1, source_target_pairs={{0,16},{8,24},{16,0},{24,8},{1,17},{9,25},{17,1},{25,9},{2,18},{10... | collective-permute-start | bytes 3145736 | tf_op jit(solution)/shard_map/ppermute | solution.py:1156
  116.6 55.2 %collective-permute-start = (bf16[4,64,2048]{2,1,0:T(8,128)(2,1)}, bf16[4,64,2048]{2,1,0:T(8,128)(2,1)}, u32[]{:S(2)}, u32[]{:S(2)}) collective-permute-start(bf16[4,64,2048]{2,1,0:T(8,128)(2,1)} %reshape.659), channel_id=1, source_target_pairs={{0,8},{8,0},{16,24},{24,16},{1,9},{9,1},{17,25},{25,17},{2,10},{10... | collective-permute-start | bytes 3145736 | tf_op jit(solution)/shard_map/ppermute | solution.py:1156
  187.3 410.4 %all-gather.17.cloned.1.call-start = ((), (), s32[]{:S(2)}) async-start(), calls=%async_computation.17 | async-start | bytes 7208960 | tf_op jit(solution)/shard_map/all_gather | solution.py:1325
  304.8 101.0 %collective-permute-start.6 = (bf16[512,2048]{1,0:T(8,128)(2,1)}, bf16[512,2048]{1,0:T(8,128)(2,1)}, u32[]{:S(2)}, u32[]{:S(2)}) collective-permute-start(bf16[512,2048]{1,0:T(8,128)(2,1)} %bitcast.242), channel_id=1, source_target_pairs={{0,24},{8,16},{16,8},{24,0},{1,25},{9,17},{17,9},{25,1},{2,26},{10... | collective-permute-start | bytes 6291464 | tf_op jit(solution)/shard_map/ppermute | solution.py:1156
  306.4 99.4 %collective-permute-start.5 = (bf16[512,2048]{1,0:T(8,128)(2,1)}, bf16[512,2048]{1,0:T(8,128)(2,1)}, u32[]{:S(2)}, u32[]{:S(2)}) collective-permute-start(bf16[512,2048]{1,0:T(8,128)(2,1)} %bitcast.243), channel_id=1, source_target_pairs={{0,16},{8,24},{16,0},{24,8},{1,17},{9,25},{17,1},{25,9},{2,18},{10... | collective-permute-start | bytes 6291464 | tf_op jit(solution)/shard_map/ppermute | solution.py:1156
  307.7 98.1 %collective-permute-start.4 = (bf16[512,2048]{1,0:T(8,128)(2,1)}, bf16[512,2048]{1,0:T(8,128)(2,1)}, u32[]{:S(2)}, u32[]{:S(2)}) collective-permute-start(bf16[512,2048]{1,0:T(8,128)(2,1)} %bitcast.244), channel_id=1, source_target_pairs={{0,8},{8,0},{16,24},{24,16},{1,9},{9,1},{17,25},{25,17},{2,10},{10... | collective-permute-start | bytes 6291464 | tf_op jit(solution)/shard_map/ppermute | solution.py:1156
  412.6 419.3 %reduce-scatter.7.cloned.1.call-start = ((), (), s32[]{:S(2)}) async-start(), calls=%async_computation.18 | async-start | bytes 10813440 | tf_op jit(solution)/shard_map/reduce_scatter | solution.py:1389
  532.7 458.9 %reduce-scatter.9.cloned.1.call-start = ((), (), s32[]{:S(2)}) async-start(), calls=%async_computation.19 | async-start | bytes 7208960 | tf_op jit(solution)/shard_map/reduce_scatter | solution.py:1389
  648.2 422.0 %reduce-scatter.11.cloned.1.call-start = ((), (), s32[]{:S(2)}) async-start(), calls=%async_computation.20 | async-start | bytes 7208960 | tf_op jit(solution)/shard_map/reduce_scatter | solution.py:1389
  734.4 97.5 %collective-permute-start.10 = (bf16[512,2048]{1,0:T(8,128)(2,1)}, bf16[512,2048]{1,0:T(8,128)(2,1)}, u32[]{:S(2)}, u32[]{:S(2)}) collective-permute-start(bf16[512,2048]{1,0:T(8,128)(2,1)} %get-tuple-element.94), channel_id=1, source_target_pairs={{0,24},{8,16},{16,8},{24,0},{1,25},{9,17},{17,9},{25,1},{2,26},{10... | collective-permute-start | bytes 6291464 | tf_op jit(solution)/shard_map/ppermute | solution.py:1156
  736.6 95.2 %collective-permute-start.8 = (bf16[512,2048]{1,0:T(8,128)(2,1)}, bf16[512,2048]{1,0:T(8,128)(2,1)}, u32[]{:S(2)}, u32[]{:S(2)}) collective-permute-start(bf16[512,2048]{1,0:T(8,128)(2,1)} %get-tuple-element.92), channel_id=1, source_target_pairs={{0,8},{8,0},{16,24},{24,16},{1,9},{9,1},{17,25},{25,17},{2,10},{10... | collective-permute-start | bytes 6291464 | tf_op jit(solution)/shard_map/ppermute | solution.py:1156
  737.2 94.6 %collective-permute-start.9 = (bf16[512,2048]{1,0:T(8,128)(2,1)}, bf16[512,2048]{1,0:T(8,128)(2,1)}, u32[]{:S(2)}, u32[]{:S(2)}) collective-permute-start(bf16[512,2048]{1,0:T(8,128)(2,1)} %get-tuple-element.93), channel_id=1, source_target_pairs={{0,16},{8,24},{16,0},{24,8},{1,17},{9,25},{17,1},{25,9},{2,18},{10... | collective-permute-start | bytes 6291464 | tf_op jit(solution)/shard_map/ppermute | solution.py:1156
  741.4 87.5 %all-to-all-start.1 = ((f32[8,2,512]{2,1,0:T(2,128)}), f32[8,2,512]{2,1,0:T(2,128)S(1)}, u32[]{:S(2)}, u32[]{:S(2)}) async-start(f32[8,2,512]{2,1,0:T(2,128)} %gather_fusion.1), calls=%async_computation.2 | async-start | bytes 65536 | tf_op jit(solution)/shard_map/all_to_all | solution.py:1433
  744.9 348.6 %reduce-scatter.17.cloned.1.call-start = ((), (), s32[]{:S(2)}) async-start(), calls=%async_computation.23 | async-start | bytes 7208960 | tf_op jit(solution)/shard_map/reduce_scatter | solution.py:1389
  964.4 161.5 %reduce-scatter.13.cloned.1.call-start = ((), (), s32[]{:S(2)}) async-start(), calls=%async_computation.21 | async-start | bytes 3932160 | tf_op jit(solution)/shard_map/reduce_scatter | solution.py:1487
  984.1 51.9 %collective-permute-start.14 = (bf16[256,2048]{1,0:T(8,128)(2,1)}, bf16[256,2048]{1,0:T(8,128)(2,1)}, u32[]{:S(2)}, u32[]{:S(2)}) collective-permute-start(bf16[256,2048]{1,0:T(8,128)(2,1)} %get-tuple-element.237), channel_id=1, source_target_pairs={{0,24},{8,16},{16,8},{24,0},{1,25},{9,17},{17,9},{25,1},{2,26},{10... | collective-permute-start | bytes 3145736 | tf_op jit(solution)/shard_map/ppermute | solution.py:1156
  1091.1 48.7 %collective-permute-start.15 = (bf16[512,2048]{1,0:T(8,128)(2,1)}, bf16[512,2048]{1,0:T(8,128)(2,1)}, u32[]{:S(2)}, u32[]{:S(2)}) collective-permute-start(bf16[512,2048]{1,0:T(8,128)(2,1)} %get-tuple-element.116), channel_id=1, source_target_pairs={{0,8},{8,0},{16,24},{24,16},{1,9},{9,1},{17,25},{25,17},{2,10},{10... | collective-permute-start | bytes 6291464 | tf_op jit(solution)/shard_map/ppermute | solution.py:1156
  1092.0 48.8 %collective-permute-start.16 = (bf16[512,2048]{1,0:T(8,128)(2,1)}, bf16[512,2048]{1,0:T(8,128)(2,1)}, u32[]{:S(2)}, u32[]{:S(2)}) collective-permute-start(bf16[512,2048]{1,0:T(8,128)(2,1)} %get-tuple-element.117), channel_id=1, source_target_pairs={{0,16},{8,24},{16,0},{24,8},{1,17},{9,25},{17,1},{25,9},{2,18},{10... | collective-permute-start | bytes 6291464 | tf_op jit(solution)/shard_map/ppermute | solution.py:1156
  (55 other events, 1461.4 us)
Sparse Core Ops, SparseCore 0:
  18.8 92.0 all-gather.6
  113.1 105.1 all-gather.8
  220.5 57.4 all-gather.10
  279.4 105.3 all-gather.12
  386.2 104.9 all-gather.14
  492.7 104.9 all-gather.16
  600.1 146.8 reduce-scatter.6
  749.3 103.0 reduce-scatter.8
  854.7 102.7 reduce-scatter.10
  959.7 102.7 reduce-scatter.16
  1064.8 61.0 reduce-scatter.12
  1156.3 24.1 reduce-scatter.14
